TPU v7x, 128 devices: a whole 4x4x4 slice. The times are simulated.
128 devices in a mesh: tm: 4 (over x), vox: 32 (over y, z, core).
Axes of the slice: x: 4, y: 4, z: 4, core: 2. Of those that a mesh axis runs over, the one named last changes fastest.
Arguments:
- u_train: bfloat16 [3072, 4096], P('tm'), may hold values from -0.109375 to 0.109375
- y_train: bfloat16 [3072, 12288], P('tm', 'vox'), may hold values from -6 to 6
- sing: float32 [4096], replicated, may hold values from 0.5 to 8
- lambdas: float32 [20], replicated, may hold values from 0.1 to 100
- lam_index: int32 [96], P('vox'), may hold values from 0 to 19
- live: int32 [96], P('vox'), may hold values from 0 to 1, as said below
- v_basis: bfloat16 [4096, 4096], P('tm', 'vox'), may hold values from -0.09375 to 0.09375
- x_test: bfloat16 [1024, 4096], P(None, 'tm'), may hold values from -0.09375 to 0.09375
Outputs:
- weights: bfloat16 [4096, 12288], P('tm', 'vox')
- predictions: bfloat16 [1024, 12288], P('tm', 'vox')
Inputs may be any that keep to these rules, and one draw needn't show every extreme that they name: Of the 3 voxel blocks that one device along vox holds, at most 2 are live, and some device holds exactly 2.
All inputs are finite; a program needn't handle non-finite values.
Results may differ from a plain program's by a relative error of at most 0.0058.
Values may be sent and summed in bfloat16 or wider, within the bound.
No kernel may reach another device: no remote copies, remote signals or barrier semaphores. Data moves between devices by JAX's collectives and lax.ppermute only.
A program may use at most 128 MiB of HBM per device.

v0:
```python
import jax
import jax.numpy as jnp
from jax import lax
from jax.sharding import PartitionSpec as P

BLK = 128


def body(u_train, y_train, sing, lambdas, lam_index, live, v_basis, x_test):
    penalty_count = lambdas.shape[0]
    selector = (lam_index[:, None] == jnp.arange(penalty_count, dtype=jnp.int32)[None, :]).astype(
        jnp.float32
    )
    selector = selector * live[:, None].astype(jnp.float32)
    used_columns = y_train.shape[1]
    used_blocks = selector.shape[0]
    partial_value = lax.dot_general(
        u_train, y_train, (((0,), (0,)), ((), ())), preferred_element_type=jnp.float32
    )
    products = lax.psum(partial_value, "tm")
    filters = sing[None, :] / (sing[None, :] * sing[None, :] + lambdas[:, None])
    row_count = products.shape[0]
    blocks = (
        products.reshape(row_count, used_blocks, BLK)
        * jnp.dot(selector, filters, precision=lax.Precision.HIGHEST).T[:, :, None]
    )
    filtered = blocks.reshape(row_count, used_columns).astype(jnp.bfloat16)
    weight_sum = jnp.dot(
        lax.all_gather(v_basis, "vox", axis=1, tiled=True),
        filtered,
        preferred_element_type=jnp.float32,
    )
    weight_cols = weight_sum.astype(jnp.bfloat16)
    partial_test = jnp.dot(x_test, weight_cols, preferred_element_type=jnp.float32)
    predicted = lax.psum_scatter(partial_test, "tm", scatter_dimension=0, tiled=True).astype(
        jnp.bfloat16
    )
    return (weight_cols, predicted)


def solution(mesh):
    placed = (
        P("tm", None),
        P("tm", "vox"),
        P(),
        P(),
        P("vox"),
        P("vox"),
        P("tm", "vox"),
        P(None, "tm"),
    )
    return jax.shard_map(
        body,
        mesh=mesh,
        in_specs=placed,
        out_specs=(P("tm", "vox"), P("tm", "vox")),
        check_vma=False,
    )
```

profile of v0, /device:TPU:0, one launch (start us, length us, event | category | flops | bytes accessed | tf_op | source)
XLA Modules:
  0.0 195.9 jit_solution(1191638270185912026)
XLA Ops:
  8.0 0.0 copy-start
  8.0 0.0 all-reduce.2.cloned.1.call-start
  8.1 8.3 %fusion.10 = f32[4096,384]{0,1:T(8,128)} fusion(bf16[768,4096]{1,0:T(8,128)(2,1)} %param.8, bf16[768,384]{1,0:T(8,128)(2,1)} %param.9), kind=kOutput, calls=%fused_computation.15 | convolution fusion | flops 2415919104 | bytes 13172736 | tf_op jit(solution)/shard_map/dot_general | solution.py:17
  16.3 0.0 copy-start.1
  16.3 0.0 copy-start.2
  16.3 0.0 copy-start.3
  16.3 0.0 copy-start.4
  16.3 0.0 all-reduce.2.cloned.1.call-update
  16.3 0.0 all-gather.2.cloned.1.call-start
  16.4 0.5 all-gather.2.cloned.1.call-update
  16.9 0.0 reduce-scatter.2.cloned.1.call-start
  17.0 0.0 copy-done.1
  17.0 0.0 copy-done.2
  17.0 0.0 copy-done.3
  17.1 0.0 copy-done.4
  17.1 0.5 fusion.1
  17.5 128.3 %all-reduce.2.cloned.1.call-done = f32[4096,384]{0,1:T(8,128)} async-done(((f32[4096,384]{0,1:T(8,128)}), f32[4096,384]{0,1:T(8,128)}) %all-reduce.2.cloned.1.call-update) | async-done | bytes 6291472 | tf_op jit(solution)/shard_map/psum | solution.py:20
  145.8 5.0 %fusion = bf16[4096,384]{0,1:T(8,128)(2,1)} fusion(f32[4096,384]{0,1:T(8,128)} %all-reduce.2.cloned.1.call-done, f32[4096,3]{0,1:T(4,128)S(1)} %fusion.1), kind=kLoop, calls=%fused_computation.1 | loop fusion | flops 3145728 | bytes 9486336 | tf_op jit(solution)/shard_map/convert_element_type | solution.py:27
  150.9 0.0 all-gather.2.cloned.1.call-done
  150.9 7.8 %convolution_convert_fusion = bf16[384,1024]{1,0:T(8,128)(2,1)S(1)} fusion(bf16[4096,384]{0,1:T(8,128)(2,1)} %fusion, bf16[1024,4096]{1,0:T(8,128)(2,1)} %all-gather.2.cloned.1.call-done), kind=kOutput, calls=%fused_computation.3 | convolution fusion | flops 3221618688 | bytes 12320768 | tf_op jit(solution)/shard_map/dot_general | solution.py:28
  158.6 0.0 copy-done
  158.6 2.2 %convolution_bitcast_fusion = f32[1024,384]{0,1:T(8,128)} fusion(bf16[384,1024]{1,0:T(8,128)(2,1)S(1)} %convolution_convert_fusion, bf16[1024,1024]{1,0:T(8,128)(2,1)S(1)} %copy-done), kind=kOutput, calls=%fused_computation.2 | convolution fusion | flops 805306368 | bytes 4456448 | tf_op jit(solution)/shard_map/dot_general | solution.py:34
  160.8 0.0 reduce-scatter.2.cloned.1.call-update
  160.8 1.2 copy.13
  162.0 24.6 %reduce-scatter.2.cloned.1.call-done = f32[256,384]{0,1:T(8,128)} async-done(((f32[1024,384]{0,1:T(8,128)}), f32[256,384]{0,1:T(8,128)}) %reduce-scatter.2.cloned.1.call-update) | async-done | bytes 393232 | tf_op jit(solution)/shard_map/reduce_scatter | solution.py:35
  186.6 1.0 convert_element_type.21
  187.6 0.8 copy.14
  (2 shorter events, 0.0 us)
Async XLA Ops:
  8.0 150.6 %copy-start = (bf16[1024,1024]{1,0:T(8,128)(2,1)S(1)}, bf16[1024,1024]{1,0:T(8,128)(2,1)}, u32[]{:S(2)}) copy-start(bf16[1024,1024]{1,0:T(8,128)(2,1)} %param.15) | copy-start | bytes 6291460
  8.0 137.8 %all-reduce.2.cloned.1.call-start = ((), (), s32[]{:S(2)}) async-start(), calls=%async_computation.1 | async-start | bytes 12582912 | tf_op jit(solution)/shard_map/psum | solution.py:20
  16.3 0.7 copy-start.1
  16.3 0.7 copy-start.2
  16.3 0.7 copy-start.3
  16.3 0.7 copy-start.4
  16.3 134.5 %all-gather.2.cloned.1.call-start = ((), (), s32[]{:S(2)}) async-start(), calls=%async_computation.2 | async-start | bytes 8650752 | tf_op jit(solution)/shard_map/all_gather | solution.py:29
  16.9 169.7 %reduce-scatter.2.cloned.1.call-start = ((), (), s32[]{:S(2)}) async-start(), calls=%async_computation.3 | async-start | bytes 1966080 | tf_op jit(solution)/shard_map/reduce_scatter | solution.py:35
Sparse Core Ops, SparseCore 0:
  16.5 129.2 all-reduce.1
  161.0 25.5 reduce-scatter.1
Sparse Core Ops, SparseCore 1:
  19.0 61.7 all-gather.1
where the time goes:
time: 196 us
  waiting for transfers between devices  153 us (78%)
  matrix products  18.7 us (10%)
  between operations  15.5 us (8%)
  other arithmetic  6.07 us (3%)
  local copies, waits for them, and re-layouts  2.04 us (1%)
    psum x1, waiting for transfers between devices, body(): products = lax.psum(partial_value, 'tm')  128 us
    reduce_scatter x1, waiting for transfers between devices, body(): lax.psum_scatter(partial_test, 'tm', scatter_dimension=0, tiled=True)  24.6 us
    dot_general x1, matrix products, body(): lax.dot_general(u_train, y_train, (((0,), (0,)), ((), ())), preferred_ele...  8.25 us
    dot_general x1, matrix products, body(): jnp.dot(lax.all_gather(v_basis, 'vox', axis=1, tiled=True), filtered, pre...  7.77 us
    convert_element_type x1, other arithmetic, body(): filtered = blocks.reshape(row_count, used_columns).astype(jnp.bfloat16)  5.05 us
  transfers between devices with their start and end apart: 3, of which 2 were waited for; matrix products, arithmetic and copies ran while one was open for 3% of the time, Pallas kernels for 0%

commit v1 on v0

v1 whole, which is shorter than its diff:
```python
import functools

import jax
import jax.numpy as jnp
from jax import lax
from jax.experimental import pallas as pl
from jax.experimental.pallas import tpu as pltpu
from jax.sharding import PartitionSpec as P

F32 = jnp.float32
BF16 = jnp.bfloat16
F = 4096
NLAM = 20
BLK = 128
VD = 384
NB = 3
NS = 2
TEST = 1024
T = 768
Q = 1024
W = NS * BLK
NX = NY = NZ = 4
NC = 2
SMEM = pl.BlockSpec(memory_space=pltpu.SMEM)
VMEM = pl.BlockSpec(memory_space=pltpu.VMEM)
ANY = pl.BlockSpec(memory_space=pl.ANY)


def moves(target):
    pairs = []
    for x in range(NX):
        for y in range(NY):
            for z in range(NZ):
                for c in range(NC):
                    tx, ty, tz, tc = target(x, y, z, c)
                    source = ((x * NY + y) * NZ + z) * NC + c
                    goal = (((tx % NX) * NY + ty % NY) * NZ + tz % NZ) * NC + tc % NC
                    pairs.append((source, goal))
    return pairs


PRIMARY = moves(lambda x, y, z, c: (x + 1 - 2 * c, y, z, c))
SECONDARY = moves(lambda x, y, z, c: (x - 1 + 2 * c, y, z, c))
OPPOSITE = moves(lambda x, y, z, c: (x + 2, y, z, c))
SWAP = moves(lambda x, y, z, c: (x, y, z, c + 1))
FIRST = [moves(lambda x, y, z, c, d=d: (x, y + d * (1 - c), z + d * c, c)) for d in (1, 2, 3)]
SECOND = [moves(lambda x, y, z, c, d=d: (x, y + d * c, z + d * (1 - c), c)) for d in (1, 2, 3)]


def send(value, pairs):
    return lax.ppermute(value, ("tm", "vox"), pairs)


def place():
    x = lax.axis_index("tm")
    v = lax.axis_index("vox")
    return x, v // (NZ * NC), (v // NC) % NZ, v % NC


def slots(live):
    first = jnp.where(live[0] > 0, 0, jnp.where(live[1] > 0, 1, 2))
    second = jnp.where(live[2] > 0, 2, jnp.where(live[1] > 0, 1, 0))
    return first, second


def quarter(which, x, c):
    step = 1 - 2 * c
    if which == "primary":
        return (x + step + NX) % NX
    if which == "secondary":
        return (x - step + NX) % NX
    if which == "opposite":
        return (x + 2) % NX
    return x


def partial_kernel(which, lambdas, lam_index, live, sing, u, y, *rest):
    n = len(which)
    outs, (ys, us, sems) = rest[:n], rest[n:]
    x, _, _, c = place()
    picked = slots(live)
    copies = []
    for i, slot in enumerate(picked):
        source = y.at[:, pl.ds(pl.multiple_of(slot * BLK, BLK), BLK)]
        copies.append(pltpu.make_async_copy(source, ys.at[i], sems.at[i]))
    where = [quarter(name, x, c) for name in which]
    for i, q in enumerate(where):
        source = u.at[:, pl.ds(pl.multiple_of(q * Q, Q), Q)]
        copies.append(pltpu.make_async_copy(source, us.at[i], sems.at[NS + i]))
    for copy in copies:
        copy.start()
    copies[0].wait()
    copies[1].wait()
    yt = jnp.concatenate([ys[0], ys[1]], axis=1).T
    for i, q in enumerate(where):
        copies[NS + i].wait()
        total = jnp.dot(yt, us[i], preferred_element_type=F32)
        s = sing[:, pl.ds(pl.multiple_of(q * Q, Q), Q)]
        for j, slot in enumerate(picked):
            scale = s / (s * s + lambdas[lam_index[slot]]) * live[slot].astype(F32)
            rows = slice(j * BLK, (j + 1) * BLK)
            outs[i][rows, :] = (total[rows, :] * scale).astype(outs[i].dtype)


def partial_call(which, dtypes, lambdas, lam_index, live, sing, u, y):
    n = len(which)
    return pl.pallas_call(
        functools.partial(partial_kernel, which),
        out_shape=[jax.ShapeDtypeStruct((W, Q), d) for d in dtypes],
        in_specs=[SMEM, SMEM, SMEM, VMEM, ANY, ANY],
        out_specs=[VMEM] * n,
        scratch_shapes=[
            pltpu.VMEM((NS, T, BLK), BF16),
            pltpu.VMEM((n, T, Q), BF16),
            pltpu.SemaphoreType.DMA((NS + n,)),
        ],
        compiler_params=pltpu.CompilerParams(vmem_limit_bytes=24 << 20),
        cost_estimate=pl.CostEstimate(
            flops=2 * W * T * Q * n, bytes_accessed=2 * T * Q * n + 4 * W * Q * n, transcendentals=0
        ),
    )(lambdas, lam_index, live, sing, u, y)


def shard_copies(q, slot, own, other, held, sems):
    _, y, z, c = place()
    back = (y - q + NY) % NY
    found = []
    for core in range(NC):
        for same in range(2):
            blocks = own if same else other
            mine = (c == core) if same else (c != core)
            for k in range(NZ):
                at = (slot * NZ + (z - k + NZ) % NZ) * NC + core
                if core == 0:
                    copy = pltpu.make_async_copy(blocks[k].at[back], held.at[at], sems.at[at])
                    found.append((mine, copy))
                else:
                    for i in range(NY):
                        copy = pltpu.make_async_copy(blocks[i].at[k], held.at[at], sems.at[at])
                        found.append((mine & (back == i), copy))
    return found


def start_all(found):
    for condition, copy in found:
        pl.when(condition)(copy.start)


def wait_shards(slot, own, held, sems):
    for i in range(NZ * NC):
        at = slot * NZ * NC + i
        pltpu.make_async_copy(own[0].at[0], held.at[at], sems.at[at]).wait()


def multiply(slot, held, features):
    total = None
    for z in range(NZ):
        at = slot * NZ * NC + z * NC
        left = jnp.concatenate([held[at], held[at + 1]], axis=1)
        right = features[:, z * NC * BLK : (z + 1) * NC * BLK]
        part = lax.dot_general(left, right, (((1,), (1,)), ((), ())), preferred_element_type=F32)
        total = part if total is None else total + part
    return total


def three_kernel(*refs):
    own, other, features = refs[:4], refs[4:8], refs[8:11]
    out, held, sems = refs[11:]
    x, _, _, c = place()
    names = ("own", "primary", "secondary")
    for i, name in enumerate(names):
        start_all(shard_copies(quarter(name, x, c), i, own, other, held, sems))
    for i in range(3):
        wait_shards(i, own, held, sems)
        part = multiply(i, held, features[i])
        if i == 0:
            out[...] = part
        else:
            out[...] += part


def three_call(own, other, features):
    return pl.pallas_call(
        three_kernel,
        out_shape=jax.ShapeDtypeStruct((Q, W), F32),
        in_specs=[ANY] * 8 + [VMEM] * 3,
        out_specs=VMEM,
        scratch_shapes=[
            pltpu.VMEM((3 * NZ * NC, Q, BLK), BF16),
            pltpu.SemaphoreType.DMA((3 * NZ * NC,)),
        ],
        compiler_params=pltpu.CompilerParams(vmem_limit_bytes=32 << 20),
        cost_estimate=pl.CostEstimate(
            flops=2 * W * 3 * Q * Q, bytes_accessed=2 * Q * 3 * Q, transcendentals=0
        ),
    )(*own, *other, *features)


def spread(out, values, live):
    first, second = slots(live)
    left, right = values[:, :BLK], values[:, BLK:]
    for b in range(NB):
        alive = live[b] > 0
        block = jnp.where(first == b, left, right)
        out[:, b * BLK : (b + 1) * BLK] = jnp.where(alive, block, jnp.zeros_like(block)).astype(
            out.dtype
        )


def last_kernel(live, *refs):
    own, other = refs[:4], refs[4:8]
    features, so_far, tests = refs[8:11]
    weights, mine, primary, secondary, opposite, held, sems = refs[11:]
    x, _, _, c = place()
    start_all(shard_copies(quarter("opposite", x, c), 0, own, other, held, sems))
    wait_shards(0, own, held, sems)
    total = (so_far[...] + multiply(0, held, features)).astype(BF16)
    spread(weights, total, live)
    rows = TEST // NX
    for name, out in (
        ("opposite", opposite),
        ("primary", primary),
        ("secondary", secondary),
        ("own", mine),
    ):
        q = quarter(name, x, c)
        part = tests[pl.ds(pl.multiple_of(q * rows, rows), rows), :]
        out[...] = jnp.dot(part, total, preferred_element_type=F32).astype(out.dtype)


def last_call(live, own, other, features, so_far, tests):
    rows = TEST // NX
    return pl.pallas_call(
        last_kernel,
        out_shape=[
            jax.ShapeDtypeStruct((Q, VD), BF16),
            jax.ShapeDtypeStruct((rows, W), F32),
            jax.ShapeDtypeStruct((rows, W), BF16),
            jax.ShapeDtypeStruct((rows, W), BF16),
            jax.ShapeDtypeStruct((rows, W), BF16),
        ],
        in_specs=[SMEM] + [ANY] * 8 + [VMEM] * 3,
        out_specs=[VMEM] * 5,
        scratch_shapes=[
            pltpu.VMEM((NZ * NC, Q, BLK), BF16),
            pltpu.SemaphoreType.DMA((NZ * NC,)),
        ],
        compiler_params=pltpu.CompilerParams(vmem_limit_bytes=32 << 20),
        cost_estimate=pl.CostEstimate(
            flops=4 * W * Q * Q, bytes_accessed=4 * Q * Q, transcendentals=0
        ),
    )(live, *own, *other, features, so_far, tests)


def end_kernel(live, mine, a, b, c, out):
    total = mine[...] + a[...].astype(F32) + b[...].astype(F32) + c[...].astype(F32)
    spread(out, total.astype(BF16), live)


def end_call(live, mine, a, b, c):
    return pl.pallas_call(
        end_kernel,
        out_shape=jax.ShapeDtypeStruct((TEST // NX, VD), BF16),
        in_specs=[SMEM] + [VMEM] * 4,
        out_specs=VMEM,
    )(live, mine, a, b, c)


def body(u_train, y_train, sing, lambdas, lam_index, live, v_basis, x_test):
    sing = sing.reshape(1, F)
    small = (lambdas, lam_index, live, sing, u_train, y_train)
    near = [send(v_basis, pairs) for pairs in FIRST]
    (p_opposite,) = partial_call(("opposite",), (BF16,), *small)
    come = send(p_opposite, PRIMARY)
    p_primary, p_secondary, p_own = partial_call(
        ("primary", "secondary", "own"), (F32, BF16, F32), *small
    )
    row = jnp.stack([v_basis, *near])
    own = [row] + [send(row, pairs) for pairs in SECOND]
    other = [send(block, SWAP) for block in own]
    onward = (p_primary + come.astype(F32)).astype(BF16)
    from_secondary = send(onward, PRIMARY)
    from_primary = send(p_secondary, SECONDARY)
    filtered = (p_own + from_secondary.astype(F32) + from_primary.astype(F32)).astype(BF16)
    f_secondary = send(filtered, PRIMARY)
    f_primary = send(filtered, SECONDARY)
    f_opposite = send(f_secondary, PRIMARY)
    so_far = three_call(own, other, (filtered, f_primary, f_secondary))
    weights, mine, primary, secondary, opposite = last_call(
        live, own, other, f_opposite, so_far, x_test
    )
    predictions = end_call(
        live, mine, send(opposite, OPPOSITE), send(primary, PRIMARY), send(secondary, SECONDARY)
    )
    return weights, predictions


def solution(mesh):
    placed = (
        P("tm", None),
        P("tm", "vox"),
        P(),
        P(),
        P("vox"),
        P("vox"),
        P("tm", "vox"),
        P(None, "tm"),
    )
    return jax.shard_map(
        body,
        mesh=mesh,
        in_specs=placed,
        out_specs=(P("tm", "vox"), P("tm", "vox")),
        check_vma=False,
    )
```

time: 196 us -> 88.1 us (0.45)
  waiting for transfers between devices: 153 us -> 39.4 us
  starting transfers between devices: 0.12 us -> 24.3 us
  matrix products: 18.7 us -> 0 us
  Pallas kernels: 0 us -> 15 us
  between operations: 15.5 us -> 0.75 us
  local copies, waits for them, and re-layouts: 2.04 us -> 7.91 us
  other arithmetic: 6.07 us -> 0.53 us
    psum x1 -> x0, waiting for transfers between devices: 128 us -> none  [body(): products = lax.psum(partial_value, 'tm')]
    ppermute x0 -> x19, waiting for transfers between devices: none -> 39.4 us  [send(): return lax.ppermute(value, ('tm', 'vox'), pairs)]
    reduce_scatter x1 -> x0, waiting for transfers between devices: 24.6 us -> none  [body(): lax.psum_scatter(partial_test, 'tm', scatter_dimension=0, tiled=True)]
    ppermute x0 -> x19, starting transfers between devices: none -> 24.3 us  [send(): return lax.ppermute(value, ('tm', 'vox'), pairs)]
    dot_general x4 -> x0, matrix products: 18.7 us -> none  [the longest x1 8.25 us: body(): lax.dot_general(u_train, y_train, (((0,), (0,)), ((), ())), preferred_ele...]
    pallas_call x0 -> x5, Pallas kernels: none -> 15 us  [the longest x2 4.8 us: partial_call(): pl.pallas_call(functools.partial(partial_kernel, which), out_shape=[jax.S...]
    unnamed x12 -> x26, local copies, waits for them, and re-layouts: 2.04 us -> 7.91 us
    convert_element_type x3 -> x2, other arithmetic: 6.06 us -> 0.4 us  [the longest x1 0.25 us: body(): (p_own + from_secondary.astype(F32) + from_primary.astype(F32)).astype(BF16)]
  transfers between devices with their start and end apart: 3 -> 19, of which waited for: 2 -> 6; matrix products, arithmetic and copies ran while one was open for 3% -> 1% of each run, Pallas kernels for 0% -> 11%
where the time goes in v1:
time: 88.1 us; the launch traced here: 87.8 us
  waiting for transfers between devices  39.4 us (45%)
  starting transfers between devices  24.3 us (28%)
  Pallas kernels  15 us (17%)
  local copies, waits for them, and re-layouts  7.91 us (9%)
    ppermute x19, waiting for transfers between devices, send(): return lax.ppermute(value, ('tm', 'vox'), pairs)  39.4 us
    ppermute x19, starting transfers between devices, send(): return lax.ppermute(value, ('tm', 'vox'), pairs)  24.3 us
    unnamed x26, local copies, waits for them, and re-layouts  7.91 us
    pallas_call x2, Pallas kernels, partial_call(): pl.pallas_call(functools.partial(partial_kernel, which), out_shape=[jax.S...  4.8 us
    pallas_call x1, Pallas kernels, three_call(): pl.pallas_call(three_kernel, out_shape=jax.ShapeDtypeStruct((Q, W), F32),...  4.48 us
    pallas_call x1, Pallas kernels, last_call(): pl.pallas_call(last_kernel, out_shape=[jax.ShapeDtypeStruct((Q, VD), BF16...  3.83 us
    pallas_call x1, Pallas kernels, end_call(): pl.pallas_call(end_kernel, out_shape=jax.ShapeDtypeStruct((TEST // NX, VD...  1.89 us
  transfers between devices with their start and end apart: 19, of which 6 were waited for; matrix products, arithmetic and copies ran while one was open for 1% of the time, Pallas kernels for 11%

profile of v1, /device:TPU:0, one launch (start us, length us, event | category | flops | bytes accessed | tf_op | source)
XLA Modules:
  0.0 87.8 jit_solution(7089606443344557754)
XLA Ops:
  0.6 1.7 %collective-permute-start = (bf16[1024,128]{1,0:T(8,128)(2,1)}, bf16[1024,128]{1,0:T(8,128)(2,1)S(1)}, u32[]{:S(2)}, u32[]{:S(2)}) collective-permute-start(bf16[1024,128]{1,0:T(8,128)(2,1)} %param.14), channel_id=1, source_target_pairs={{0,8},{1,3},{2,10},{3,5},{4,12},{5,7},{6,14},{7,1},{8,16},{9,11},{... | collective-permute-start | bytes 786440 | tf_op jit(solution)/shard_map/ppermute | solution.py:51
  2.4 2.9 %collective-permute-start.1 = (bf16[1024,128]{1,0:T(8,128)(2,1)}, bf16[1024,128]{1,0:T(8,128)(2,1)S(1)}, u32[]{:S(2)}, u32[]{:S(2)}) collective-permute-start(bf16[1024,128]{1,0:T(8,128)(2,1)} %param.14), channel_id=1, source_target_pairs={{0,16},{1,5},{2,18},{3,7},{4,20},{5,1},{6,22},{7,3},{8,24},{9,13},... | collective-permute-start | bytes 786440 | tf_op jit(solution)/shard_map/ppermute | solution.py:51
  5.3 1.3 %collective-permute-start.2 = (bf16[1024,128]{1,0:T(8,128)(2,1)}, bf16[1024,128]{1,0:T(8,128)(2,1)S(1)}, u32[]{:S(2)}, u32[]{:S(2)}) collective-permute-start(bf16[1024,128]{1,0:T(8,128)(2,1)} %param.14), channel_id=1, source_target_pairs={{0,24},{1,7},{2,26},{3,1},{4,28},{5,3},{6,30},{7,5},{8,0},{9,15},{... | collective-permute-start | bytes 786440 | tf_op jit(solution)/shard_map/ppermute | solution.py:51
  6.6 0.0 copy-start
  6.6 2.8 %copy-done = bf16[768,4096]{1,0:T(8,128)(2,1)S(1)} copy-done((bf16[768,4096]{1,0:T(8,128)(2,1)S(1)}, bf16[768,4096]{1,0:T(8,128)(2,1)}, u32[]{:S(2)}) %copy-start) | copy-done | bytes 6291480
  9.4 0.0 copy-start.1
  9.4 1.1 %copy-done.1 = bf16[768,384]{1,0:T(8,128)(2,1)S(1)} copy-done((bf16[768,384]{1,0:T(8,128)(2,1)S(1)}, bf16[768,384]{1,0:T(8,128)(2,1)}, u32[]{:S(2)}) %copy-start.1) | copy-done | bytes 589848
  10.5 0.0 copy-start.4
  10.5 0.7 copy-done.4
  11.2 0.0 copy-start.5
  11.2 0.7 copy-done.5
  11.8 0.7 copy-done.7
  12.5 0.7 copy-done.8
  13.1 1.6 %shard_map.96 = bf16[256,1024]{1,0:T(8,128)(2,1)S(1)} custom-call(f32[20]{0:T(128)S(1)} %copy-done.7, s32[3]{0:T(128)S(1)} %copy-done.8, s32[3]{0:T(128)S(1)} %copy-done.5, f32[1,4096]{1,0:T(1,128)S(1)} %bitcast.5, bf16[768,4096]{1,0:T(8,128)(2,1)S(1)} %copy-done, bf16[768,384]{1,0:T(8,128)(2,1)S(1)} %copy-done.1), custom_call_target="tpu_custom_call" | custom-call | flops 402653184 | bytes 2621440 | tf_op jit(solution)/shard_map/pallas_call | solution.py:107
  14.8 1.6 %collective-permute-start.10 = (bf16[256,1024]{1,0:T(8,128)(2,1)S(1)}, bf16[256,1024]{1,0:T(8,128)(2,1)S(1)}, u32[]{:S(2)}, u32[]{:S(2)}) collective-permute-start(bf16[256,1024]{1,0:T(8,128)(2,1)S(1)} %shard_map.96), channel_id=1, source_target_pairs={{0,32},{1,97},{2,34},{3,99},{4,36},{5,101},{6,38},{7,103},{8,40},{... | collective-permute-start | bytes 1572872 | tf_op jit(solution)/shard_map/ppermute | solution.py:51
  16.3 0.0 collective-permute-done
  16.3 0.0 collective-permute-done.1
  16.3 0.0 collective-permute-done.2
  16.3 0.0 copy-done.9
  16.3 0.1 pad_maximum_fusion.refs_0_
  16.5 2.0 %collective-permute-start.3 = (bf16[4,1024,128]{2,1,0:T(8,128)(2,1)S(1)}, bf16[4,1024,128]{2,1,0:T(8,128)(2,1)S(1)}, u32[]{:S(2)}, u32[]{:S(2)}) collective-permute-start(bf16[4,1024,128]{2,1,0:T(8,128)(2,1)S(1)} %pad_maximum_fusion.refs_0_), channel_id=1, source_target_pairs={{0,2},{1,9},{2,4},{3,11},{4,6},{5,13},{6,0},{7,15},{8,10},{9,17},{... | collective-permute-start | bytes 3145736 | tf_op jit(solution)/shard_map/ppermute | solution.py:51
  18.5 3.6 %collective-permute-start.4 = (bf16[4,1024,128]{2,1,0:T(8,128)(2,1)S(1)}, bf16[4,1024,128]{2,1,0:T(8,128)(2,1)S(1)}, u32[]{:S(2)}, u32[]{:S(2)}) collective-permute-start(bf16[4,1024,128]{2,1,0:T(8,128)(2,1)S(1)} %pad_maximum_fusion.refs_0_), channel_id=1, source_target_pairs={{0,4},{1,17},{2,6},{3,19},{4,0},{5,21},{6,2},{7,23},{8,12},{9,25},... | collective-permute-start | bytes 3145736 | tf_op jit(solution)/shard_map/ppermute | solution.py:51
  22.1 1.0 %collective-permute-start.5 = (bf16[4,1024,128]{2,1,0:T(8,128)(2,1)S(1)}, bf16[4,1024,128]{2,1,0:T(8,128)(2,1)S(1)}, u32[]{:S(2)}, u32[]{:S(2)}) collective-permute-start(bf16[4,1024,128]{2,1,0:T(8,128)(2,1)S(1)} %pad_maximum_fusion.refs_0_), channel_id=1, source_target_pairs={{0,6},{1,25},{2,0},{3,27},{4,2},{5,29},{6,4},{7,31},{8,14},{9,1},{... | collective-permute-start | bytes 3145736 | tf_op jit(solution)/shard_map/ppermute | solution.py:51
  23.1 3.2 %shard_map.95 = (f32[256,1024]{1,0:T(8,128)S(1)}, bf16[256,1024]{1,0:T(8,128)(2,1)S(1)}, f32[256,1024]{1,0:T(8,128)S(1)}) custom-call(f32[20]{0:T(128)S(1)} %copy-done.7, s32[3]{0:T(128)S(1)} %copy-done.8, s32[3]{0:T(128)S(1)} %copy-done.5, f32[1,4096]{1,0:T(1,128)S(1)} %bitcast.6, bf16[768,4096]{1,0:T(8,128)(2,1)S(1)} %copy-done, bf16[768,384]{1,0:T(8,128)(2,1)S(1)} %copy-done.1), custom_call_target="tpu_custom_call" | custom-call | flops 1207959552 | bytes 7864320 | tf_op jit(solution)/shard_map/pallas_call | solution.py:107
  26.3 1.8 %collective-permute-start.12 = (bf16[256,1024]{1,0:T(8,128)(2,1)S(1)}, bf16[256,1024]{1,0:T(8,128)(2,1)S(1)}, u32[]{:S(2)}, u32[]{:S(2)}) collective-permute-start(bf16[256,1024]{1,0:T(8,128)(2,1)S(1)} %get-tuple-element.12), channel_id=1, source_target_pairs={{0,96},{1,33},{2,98},{3,35},{4,100},{5,37},{6,102},{7,39},{8,104},... | collective-permute-start | bytes 1572872 | tf_op jit(solution)/shard_map/ppermute | solution.py:51
  28.1 0.0 collective-permute-done.10
  28.1 0.1 add_convert_fusion.1
  28.2 0.3 collective-permute-start.11
  28.6 11.4 %collective-permute-done.12 = bf16[256,1024]{1,0:T(8,128)(2,1)S(1)} collective-permute-done((bf16[256,1024]{1,0:T(8,128)(2,1)S(1)}, bf16[256,1024]{1,0:T(8,128)(2,1)S(1)}, u32[]{:S(2)}, u32[]{:S(2)}) %collective-permute-start.12) | collective-permute-done | bytes 524320 | tf_op jit(solution)/shard_map/ppermute | solution.py:51
  40.0 0.0 collective-permute-start.6
  40.0 0.0 collective-permute-done.3.refs_1_
  40.0 0.5 collective-permute-start.7
  40.5 5.5 %collective-permute-done.4.refs_2_ = bf16[4,1024,128]{2,1,0:T(8,128)(2,1)S(1)} collective-permute-done((bf16[4,1024,128]{2,1,0:T(8,128)(2,1)S(1)}, bf16[4,1024,128]{2,1,0:T(8,128)(2,1)S(1)}, u32[]{:S(2)}, u32[]{:S(2)}) %collective-permute-start.4) | collective-permute-done | bytes 1048608 | tf_op jit(solution)/shard_map/ppermute | solution.py:51
  46.1 0.0 collective-permute-start.8
  46.1 0.0 collective-permute-done.5.refs_3_
  46.1 0.5 collective-permute-start.9
  46.6 0.0 collective-permute-done.11
  46.6 0.3 add_convert_fusion.refs_8_
  46.8 1.6 %collective-permute-start.13 = (bf16[256,1024]{1,0:T(8,128)(2,1)S(1)}, bf16[256,1024]{1,0:T(8,128)(2,1)S(1)}, u32[]{:S(2)}, u32[]{:S(2)}) collective-permute-start(bf16[256,1024]{1,0:T(8,128)(2,1)S(1)} %add_convert_fusion.refs_8_), channel_id=1, source_target_pairs={{0,32},{1,97},{2,34},{3,99},{4,36},{5,101},{6,38},{7,103},{8,40},{... | collective-permute-start | bytes 1572872 | tf_op jit(solution)/shard_map/ppermute | solution.py:51
  48.4 0.0 collective-permute-done.6.refs_4_
  48.4 1.7 %collective-permute-start.15 = (bf16[256,1024]{1,0:T(8,128)(2,1)S(1)}, bf16[256,1024]{1,0:T(8,128)(2,1)S(1)}, u32[]{:S(2)}, u32[]{:S(2)}) collective-permute-start(bf16[256,1024]{1,0:T(8,128)(2,1)S(1)} %add_convert_fusion.refs_8_), channel_id=1, source_target_pairs={{0,96},{1,33},{2,98},{3,35},{4,100},{5,37},{6,102},{7,39},{8,104},... | collective-permute-start | bytes 1572872 | tf_op jit(solution)/shard_map/ppermute | solution.py:51
  50.1 12.3 %collective-permute-done.13.refs_10_ = bf16[256,1024]{1,0:T(8,128)(2,1)S(1)} collective-permute-done((bf16[256,1024]{1,0:T(8,128)(2,1)S(1)}, bf16[256,1024]{1,0:T(8,128)(2,1)S(1)}, u32[]{:S(2)}, u32[]{:S(2)}) %collective-permute-start.13) | collective-permute-done | bytes 524320 | tf_op jit(solution)/shard_map/ppermute | solution.py:51
  62.5 0.1 collective-permute-start.14
  62.5 0.0 collective-permute-done.15.refs_9_
  62.5 0.0 collective-permute-done.7.refs_5_
  62.5 0.0 collective-permute-done.8.refs_6_
  62.5 0.0 collective-permute-done.9.refs_7_
  62.5 4.5 %shard_map.97.refs_9_ = f32[1024,256]{1,0:T(8,128)S(1)} custom-call(bf16[4,1024,128]{2,1,0:T(8,128)(2,1)S(1)} %pad_maximum_fusion.refs_0_, bf16[4,1024,128]{2,1,0:T(8,128)(2,1)S(1)} %collective-permute-done.3.refs_1_, bf16[4,1024,128]{2,1,0:T(8,128)(2,1)S(1)} %collective-permute-done.4.refs_2_, bf16[4,1024,128]{2,1,0:T(8,128)(2,1)S(1)} %collective-permute-done.5.refs_3_, ...), custom_call_target="tpu_custom_call" | custom-call | flops 1610612736 | bytes 6291456 | tf_op jit(solution)/shard_map/pallas_call | solution.py:183
  67.0 5.8 %collective-permute-done.14.refs_8_ = bf16[256,1024]{1,0:T(8,128)(2,1)S(1)} collective-permute-done((bf16[256,1024]{1,0:T(8,128)(2,1)S(1)}, bf16[256,1024]{1,0:T(8,128)(2,1)S(1)}, u32[]{:S(2)}, u32[]{:S(2)}) %collective-permute-start.14) | collective-permute-done | bytes 524320 | tf_op jit(solution)/shard_map/ppermute | solution.py:51
  72.9 0.0 copy-done.2
  72.9 0.0 copy-done.6
  72.9 3.8 %shard_map.98 = (bf16[1024,384]{1,0:T(8,128)(2,1)}, f32[256,256]{1,0:T(8,128)S(1)}, bf16[256,256]{1,0:T(8,128)(2,1)S(1)}, bf16[256,256]{1,0:T(8,128)(2,1)S(1)}, bf16[256,256]{1,0:T(8,128)(2,1)S(1)}) custom-call(s32[3]{0:T(128)S(1)} %copy-done.6, bf16[4,1024,128]{2,1,0:T(8,128)(2,1)S(1)} %pad_maximum_fusion.refs_0_, ...), custom_call_target="tpu_custom_call" | custom-call | flops 1073741824 | bytes 4194304 | tf_op jit(solution)/shard_map/pallas_call | solution.py:233
  76.7 0.0 copy-start.3
  76.7 0.7 copy-done.3
  77.4 0.4 collective-permute-start.16
  77.8 0.0 collective-permute-start.17
  77.8 3.2 %collective-permute-start.18 = (bf16[256,256]{1,0:T(8,128)(2,1)S(1)}, bf16[256,256]{1,0:T(8,128)(2,1)S(1)}, u32[]{:S(2)}, u32[]{:S(2)}) collective-permute-start(bf16[256,256]{1,0:T(8,128)(2,1)S(1)} %get-tuple-element.17), channel_id=1, source_target_pairs={{0,96},{1,33},{2,98},{3,35},{4,100},{5,37},{6,102},{7,39},{8,104},... | collective-permute-start | bytes 393224 | tf_op jit(solution)/shard_map/ppermute | solution.py:51
  81.0 3.0 %collective-permute-done.16.a = bf16[256,256]{1,0:T(8,128)(2,1)S(1)} collective-permute-done((bf16[256,256]{1,0:T(8,128)(2,1)S(1)}, bf16[256,256]{1,0:T(8,128)(2,1)S(1)}, u32[]{:S(2)}, u32[]{:S(2)}) %collective-permute-start.16) | collective-permute-done | bytes 131104 | tf_op jit(solution)/shard_map/ppermute | solution.py:51
  84.0 1.3 %collective-permute-done.17.b = bf16[256,256]{1,0:T(8,128)(2,1)S(1)} collective-permute-done((bf16[256,256]{1,0:T(8,128)(2,1)S(1)}, bf16[256,256]{1,0:T(8,128)(2,1)S(1)}, u32[]{:S(2)}, u32[]{:S(2)}) %collective-permute-start.17) | collective-permute-done | bytes 131104 | tf_op jit(solution)/shard_map/ppermute | solution.py:51
  85.3 0.0 collective-permute-done.18.c
  85.3 0.0 copy-done.10
  85.3 0.6 copy-done.11
  85.9 0.0 copy-done.12
  86.0 1.9 %shard_map.99 = bf16[256,384]{1,0:T(8,128)(2,1)} custom-call(s32[3]{0:T(128)} %live.7, f32[256,256]{1,0:T(8,128)} %copy-done.3, bf16[256,256]{1,0:T(8,128)(2,1)} %copy-done.10, bf16[256,256]{1,0:T(8,128)(2,1)} %copy-done.11, bf16[256,256]{1,0:T(8,128)(2,1)} %copy-done.12), custom_call_target="tpu_custom_call" | custom-call | tf_op jit(solution)/shard_map/pallas_call | solution.py:261
  (8 shorter events, 0.0 us)
Async XLA Ops:
  0.6 15.7 %collective-permute-start = (bf16[1024,128]{1,0:T(8,128)(2,1)}, bf16[1024,128]{1,0:T(8,128)(2,1)S(1)}, u32[]{:S(2)}, u32[]{:S(2)}) collective-permute-start(bf16[1024,128]{1,0:T(8,128)(2,1)} %param.14), channel_id=1, source_target_pairs={{0,8},{1,3},{2,10},{3,5},{4,12},{5,7},{6,14},{7,1},{8,16},{9,11},{... | collective-permute-start | bytes 786440 | tf_op jit(solution)/shard_map/ppermute | solution.py:51
  2.4 14.0 %collective-permute-start.1 = (bf16[1024,128]{1,0:T(8,128)(2,1)}, bf16[1024,128]{1,0:T(8,128)(2,1)S(1)}, u32[]{:S(2)}, u32[]{:S(2)}) collective-permute-start(bf16[1024,128]{1,0:T(8,128)(2,1)} %param.14), channel_id=1, source_target_pairs={{0,16},{1,5},{2,18},{3,7},{4,20},{5,1},{6,22},{7,3},{8,24},{9,13},... | collective-permute-start | bytes 786440 | tf_op jit(solution)/shard_map/ppermute | solution.py:51
  5.3 11.1 %collective-permute-start.2 = (bf16[1024,128]{1,0:T(8,128)(2,1)}, bf16[1024,128]{1,0:T(8,128)(2,1)S(1)}, u32[]{:S(2)}, u32[]{:S(2)}) collective-permute-start(bf16[1024,128]{1,0:T(8,128)(2,1)} %param.14), channel_id=1, source_target_pairs={{0,24},{1,7},{2,26},{3,1},{4,28},{5,3},{6,30},{7,5},{8,0},{9,15},{... | collective-permute-start | bytes 786440 | tf_op jit(solution)/shard_map/ppermute | solution.py:51
  6.6 2.8 %copy-start = (bf16[768,4096]{1,0:T(8,128)(2,1)S(1)}, bf16[768,4096]{1,0:T(8,128)(2,1)}, u32[]{:S(2)}) copy-start(bf16[768,4096]{1,0:T(8,128)(2,1)} %u.3) | copy-start | bytes 18874372
  9.4 1.1 %copy-start.1 = (bf16[768,384]{1,0:T(8,128)(2,1)S(1)}, bf16[768,384]{1,0:T(8,128)(2,1)}, u32[]{:S(2)}) copy-start(bf16[768,384]{1,0:T(8,128)(2,1)} %y.3) | copy-start | bytes 1769476
  10.5 0.7 copy-start.4
  11.2 0.7 copy-start.5
  11.8 0.7 copy-start.7
  12.5 0.7 copy-start.8
  13.1 3.2 %copy-start.9 = (bf16[1024,128]{1,0:T(8,128)(2,1)S(1)}, bf16[1024,128]{1,0:T(8,128)(2,1)}, u32[]{:S(2)}) copy-start(bf16[1024,128]{1,0:T(8,128)(2,1)} %param.14) | copy-start | bytes 786436
  14.8 13.3 %collective-permute-start.10 = (bf16[256,1024]{1,0:T(8,128)(2,1)S(1)}, bf16[256,1024]{1,0:T(8,128)(2,1)S(1)}, u32[]{:S(2)}, u32[]{:S(2)}) collective-permute-start(bf16[256,1024]{1,0:T(8,128)(2,1)S(1)} %shard_map.96), channel_id=1, source_target_pairs={{0,32},{1,97},{2,34},{3,99},{4,36},{5,101},{6,38},{7,103},{8,40},{... | collective-permute-start | bytes 1572872 | tf_op jit(solution)/shard_map/ppermute | solution.py:51
  16.5 23.5 %collective-permute-start.3 = (bf16[4,1024,128]{2,1,0:T(8,128)(2,1)S(1)}, bf16[4,1024,128]{2,1,0:T(8,128)(2,1)S(1)}, u32[]{:S(2)}, u32[]{:S(2)}) collective-permute-start(bf16[4,1024,128]{2,1,0:T(8,128)(2,1)S(1)} %pad_maximum_fusion.refs_0_), channel_id=1, source_target_pairs={{0,2},{1,9},{2,4},{3,11},{4,6},{5,13},{6,0},{7,15},{8,10},{9,17},{... | collective-permute-start | bytes 3145736 | tf_op jit(solution)/shard_map/ppermute | solution.py:51
  18.5 27.6 %collective-permute-start.4 = (bf16[4,1024,128]{2,1,0:T(8,128)(2,1)S(1)}, bf16[4,1024,128]{2,1,0:T(8,128)(2,1)S(1)}, u32[]{:S(2)}, u32[]{:S(2)}) collective-permute-start(bf16[4,1024,128]{2,1,0:T(8,128)(2,1)S(1)} %pad_maximum_fusion.refs_0_), channel_id=1, source_target_pairs={{0,4},{1,17},{2,6},{3,19},{4,0},{5,21},{6,2},{7,23},{8,12},{9,25},... | collective-permute-start | bytes 3145736 | tf_op jit(solution)/shard_map/ppermute | solution.py:51
  22.1 24.0 %collective-permute-start.5 = (bf16[4,1024,128]{2,1,0:T(8,128)(2,1)S(1)}, bf16[4,1024,128]{2,1,0:T(8,128)(2,1)S(1)}, u32[]{:S(2)}, u32[]{:S(2)}) collective-permute-start(bf16[4,1024,128]{2,1,0:T(8,128)(2,1)S(1)} %pad_maximum_fusion.refs_0_), channel_id=1, source_target_pairs={{0,6},{1,25},{2,0},{3,27},{4,2},{5,29},{6,4},{7,31},{8,14},{9,1},{... | collective-permute-start | bytes 3145736 | tf_op jit(solution)/shard_map/ppermute | solution.py:51
  26.3 13.7 %collective-permute-start.12 = (bf16[256,1024]{1,0:T(8,128)(2,1)S(1)}, bf16[256,1024]{1,0:T(8,128)(2,1)S(1)}, u32[]{:S(2)}, u32[]{:S(2)}) collective-permute-start(bf16[256,1024]{1,0:T(8,128)(2,1)S(1)} %get-tuple-element.12), channel_id=1, source_target_pairs={{0,96},{1,33},{2,98},{3,35},{4,100},{5,37},{6,102},{7,39},{8,104},... | collective-permute-start | bytes 1572872 | tf_op jit(solution)/shard_map/ppermute | solution.py:51
  28.2 18.3 %collective-permute-start.11 = (bf16[256,1024]{1,0:T(8,128)(2,1)S(1)}, bf16[256,1024]{1,0:T(8,128)(2,1)S(1)}, u32[]{:S(2)}, u32[]{:S(2)}) collective-permute-start(bf16[256,1024]{1,0:T(8,128)(2,1)S(1)} %add_convert_fusion.1), channel_id=1, source_target_pairs={{0,32},{1,97},{2,34},{3,99},{4,36},{5,101},{6,38},{7,103},{8,40},{... | collective-permute-start | bytes 1572872 | tf_op jit(solution)/shard_map/ppermute | solution.py:51
  40.0 8.4 %collective-permute-start.6 = (bf16[4,1024,128]{2,1,0:T(8,128)(2,1)S(1)}, bf16[4,1024,128]{2,1,0:T(8,128)(2,1)S(1)}, u32[]{:S(2)}, u32[]{:S(2)}) collective-permute-start(bf16[4,1024,128]{2,1,0:T(8,128)(2,1)S(1)} %pad_maximum_fusion.refs_0_), channel_id=1, source_target_pairs={{0,1},{1,0},{2,3},{3,2},{4,5},{5,4},{6,7},{7,6},{8,9},{9,8},{10,11... | collective-permute-start | bytes 3145736 | tf_op jit(solution)/shard_map/ppermute | solution.py:51
  40.0 22.5 %collective-permute-start.7 = (bf16[4,1024,128]{2,1,0:T(8,128)(2,1)S(1)}, bf16[4,1024,128]{2,1,0:T(8,128)(2,1)S(1)}, u32[]{:S(2)}, u32[]{:S(2)}) collective-permute-start(bf16[4,1024,128]{2,1,0:T(8,128)(2,1)S(1)} %collective-permute-done.3.refs_1_), channel_id=1, source_target_pairs={{0,1},{1,0},{2,3},{3,2},{4,5},{5,4},{6,7},{7,6},{8,9},{9,8},{10,11... | collective-permute-start | bytes 3145736 | tf_op jit(solution)/shard_map/ppermute | solution.py:51
  46.1 16.5 %collective-permute-start.8 = (bf16[4,1024,128]{2,1,0:T(8,128)(2,1)S(1)}, bf16[4,1024,128]{2,1,0:T(8,128)(2,1)S(1)}, u32[]{:S(2)}, u32[]{:S(2)}) collective-permute-start(bf16[4,1024,128]{2,1,0:T(8,128)(2,1)S(1)} %collective-permute-done.4.refs_2_), channel_id=1, source_target_pairs={{0,1},{1,0},{2,3},{3,2},{4,5},{5,4},{6,7},{7,6},{8,9},{9,8},{10,11... | collective-permute-start | bytes 3145736 | tf_op jit(solution)/shard_map/ppermute | solution.py:51
  46.1 16.5 %collective-permute-start.9 = (bf16[4,1024,128]{2,1,0:T(8,128)(2,1)S(1)}, bf16[4,1024,128]{2,1,0:T(8,128)(2,1)S(1)}, u32[]{:S(2)}, u32[]{:S(2)}) collective-permute-start(bf16[4,1024,128]{2,1,0:T(8,128)(2,1)S(1)} %collective-permute-done.5.refs_3_), channel_id=1, source_target_pairs={{0,1},{1,0},{2,3},{3,2},{4,5},{5,4},{6,7},{7,6},{8,9},{9,8},{10,11... | collective-permute-start | bytes 3145736 | tf_op jit(solution)/shard_map/ppermute | solution.py:51
  46.6 26.3 %copy-start.2 = (bf16[1024,1024]{1,0:T(8,128)(2,1)S(1)}, bf16[1024,1024]{1,0:T(8,128)(2,1)}, u32[]{:S(2)}) copy-start(bf16[1024,1024]{1,0:T(8,128)(2,1)} %refs_10_.1) | copy-start | bytes 6291460
  46.6 26.3 %copy-start.6 = (s32[3]{0:T(128)S(1)}, s32[3]{0:T(128)}, u32[]{:S(2)}) copy-start(s32[3]{0:T(128)} %live.7) | copy-start | bytes 40
  46.8 15.6 %collective-permute-start.13 = (bf16[256,1024]{1,0:T(8,128)(2,1)S(1)}, bf16[256,1024]{1,0:T(8,128)(2,1)S(1)}, u32[]{:S(2)}, u32[]{:S(2)}) collective-permute-start(bf16[256,1024]{1,0:T(8,128)(2,1)S(1)} %add_convert_fusion.refs_8_), channel_id=1, source_target_pairs={{0,32},{1,97},{2,34},{3,99},{4,36},{5,101},{6,38},{7,103},{8,40},{... | collective-permute-start | bytes 1572872 | tf_op jit(solution)/shard_map/ppermute | solution.py:51
  48.4 14.1 %collective-permute-start.15 = (bf16[256,1024]{1,0:T(8,128)(2,1)S(1)}, bf16[256,1024]{1,0:T(8,128)(2,1)S(1)}, u32[]{:S(2)}, u32[]{:S(2)}) collective-permute-start(bf16[256,1024]{1,0:T(8,128)(2,1)S(1)} %add_convert_fusion.refs_8_), channel_id=1, source_target_pairs={{0,96},{1,33},{2,98},{3,35},{4,100},{5,37},{6,102},{7,39},{8,104},... | collective-permute-start | bytes 1572872 | tf_op jit(solution)/shard_map/ppermute | solution.py:51
  62.5 10.4 %collective-permute-start.14 = (bf16[256,1024]{1,0:T(8,128)(2,1)S(1)}, bf16[256,1024]{1,0:T(8,128)(2,1)S(1)}, u32[]{:S(2)}, u32[]{:S(2)}) collective-permute-start(bf16[256,1024]{1,0:T(8,128)(2,1)S(1)} %collective-permute-done.13.refs_10_), channel_id=1, source_target_pairs={{0,32},{1,97},{2,34},{3,99},{4,36},{5,101},{6,38},{7,103},{8,40},{... | collective-permute-start | bytes 1572872 | tf_op jit(solution)/shard_map/ppermute | solution.py:51
  76.7 0.7 copy-start.3
  77.4 6.6 %collective-permute-start.16 = (bf16[256,256]{1,0:T(8,128)(2,1)S(1)}, bf16[256,256]{1,0:T(8,128)(2,1)S(1)}, u32[]{:S(2)}, u32[]{:S(2)}) collective-permute-start(bf16[256,256]{1,0:T(8,128)(2,1)S(1)} %get-tuple-element.15), channel_id=1, source_target_pairs={{0,64},{1,65},{2,66},{3,67},{4,68},{5,69},{6,70},{7,71},{8,72},{9,... | collective-permute-start | bytes 393224 | tf_op jit(solution)/shard_map/ppermute | solution.py:51
  77.8 7.5 %collective-permute-start.17 = (bf16[256,256]{1,0:T(8,128)(2,1)S(1)}, bf16[256,256]{1,0:T(8,128)(2,1)S(1)}, u32[]{:S(2)}, u32[]{:S(2)}) collective-permute-start(bf16[256,256]{1,0:T(8,128)(2,1)S(1)} %get-tuple-element.16), channel_id=1, source_target_pairs={{0,32},{1,97},{2,34},{3,99},{4,36},{5,101},{6,38},{7,103},{8,40},{... | collective-permute-start | bytes 393224 | tf_op jit(solution)/shard_map/ppermute | solution.py:51
  77.8 7.5 %collective-permute-start.18 = (bf16[256,256]{1,0:T(8,128)(2,1)S(1)}, bf16[256,256]{1,0:T(8,128)(2,1)S(1)}, u32[]{:S(2)}, u32[]{:S(2)}) collective-permute-start(bf16[256,256]{1,0:T(8,128)(2,1)S(1)} %get-tuple-element.17), channel_id=1, source_target_pairs={{0,96},{1,33},{2,98},{3,35},{4,100},{5,37},{6,102},{7,39},{8,104},... | collective-permute-start | bytes 393224 | tf_op jit(solution)/shard_map/ppermute | solution.py:51
  84.0 1.3 %copy-start.10 = (bf16[256,256]{1,0:T(8,128)(2,1)}, bf16[256,256]{1,0:T(8,128)(2,1)S(1)}, u32[]{:S(2)}) copy-start(bf16[256,256]{1,0:T(8,128)(2,1)S(1)} %collective-permute-done.16.a) | copy-start | bytes 393220
  85.3 0.7 copy-start.11
  85.3 0.7 copy-start.12

commit v2 on v1

v2 whole, which is shorter than its diff:
```python
import functools

import jax
import jax.numpy as jnp
from jax import lax
from jax.experimental import pallas as pl
from jax.experimental.pallas import tpu as pltpu
from jax.sharding import PartitionSpec as P

F32 = jnp.float32
BF16 = jnp.bfloat16
F = 4096
NLAM = 20
BLK = 128
VD = 384
NB = 3
NS = 2
TEST = 1024
T = 768
Q = 1024
W = NS * BLK
NX = NY = NZ = 4
NC = 2
SMEM = pl.BlockSpec(memory_space=pltpu.SMEM)
VMEM = pl.BlockSpec(memory_space=pltpu.VMEM)
HBM = pl.BlockSpec(memory_space=pltpu.HBM)


def moves(target):
    pairs = []
    for x in range(NX):
        for y in range(NY):
            for z in range(NZ):
                for c in range(NC):
                    tx, ty, tz, tc = target(x, y, z, c)
                    source = ((x * NY + y) * NZ + z) * NC + c
                    goal = (((tx % NX) * NY + ty % NY) * NZ + tz % NZ) * NC + tc % NC
                    pairs.append((source, goal))
    return pairs


PRIMARY = moves(lambda x, y, z, c: (x + 1 - 2 * c, y, z, c))
SECONDARY = moves(lambda x, y, z, c: (x - 1 + 2 * c, y, z, c))
OPPOSITE = moves(lambda x, y, z, c: (x + 2, y, z, c))
SWAP = moves(lambda x, y, z, c: (x, y, z, c + 1))
FIRST = [moves(lambda x, y, z, c, d=d: (x, y + d * (1 - c), z + d * c, c)) for d in (1, 2, 3)]
UP = moves(lambda x, y, z, c: (x, y + c, z + 1 - c, c))
DOWN = moves(lambda x, y, z, c: (x, y - c, z - 1 + c, c))


def pin(*arrays):
    return [pltpu.with_memory_space_constraint(a, pltpu.HBM) for a in arrays]


def send(value, pairs):
    return lax.ppermute(value, ("tm", "vox"), pairs)


def place():
    x = lax.axis_index("tm")
    v = lax.axis_index("vox")
    return x, v // (NZ * NC), (v // NC) % NZ, v % NC


def slots(live):
    first = jnp.where(live[0] > 0, 0, jnp.where(live[1] > 0, 1, 2))
    second = jnp.where(live[2] > 0, 2, jnp.where(live[1] > 0, 1, 0))
    return first, second


def quarter(which, x, c):
    step = 1 - 2 * c
    if which == "primary":
        return (x + step + NX) % NX
    if which == "secondary":
        return (x - step + NX) % NX
    if which == "opposite":
        return (x + 2) % NX
    return x


SMALL = [
    pltpu.SMEM((NLAM,), F32),
    pltpu.SMEM((NB,), jnp.int32),
    pltpu.SMEM((NB,), jnp.int32),
    pltpu.VMEM((1, F), F32),
]


def scaled(total, q, picked, lambdas, lam_index, live, sing):
    s = sing[:, pl.ds(pl.multiple_of(q * Q, Q), Q)]
    parts = []
    for j, slot in enumerate(picked):
        scale = s / (s * s + lambdas[lam_index[slot]]) * live[slot].astype(F32)
        parts.append(total[j * BLK : (j + 1) * BLK, :] * scale)
    return parts


def start_kernel(lambdas_h, lam_index_h, live_h, sing_h, u, y, *rest):
    out, yt_out, lambdas, lam_index, live, sing, ys, us, sems = rest
    x, _, _, c = place()
    q = quarter("opposite", x, c)
    held = (lambdas, lam_index, live, sing)
    copies = [
        pltpu.make_async_copy(r, h, sems.at[i])
        for i, (r, h) in enumerate(zip((lambdas_h, lam_index_h, live_h, sing_h), held))
    ]
    for copy in copies:
        copy.start()
    wide = pltpu.make_async_copy(u.at[:, pl.ds(pl.multiple_of(q * Q, Q), Q)], us, sems.at[4])
    whole = pltpu.make_async_copy(y, ys, sems.at[5])
    whole.start()
    wide.start()
    for copy in copies:
        copy.wait()
    picked = slots(live)
    whole.wait()
    for j, slot in enumerate(picked):
        block = ys[:, pl.ds(pl.multiple_of(slot * BLK, BLK), BLK)]
        yt_out[j * BLK : (j + 1) * BLK, :] = block.T
    wide.wait()
    total = jnp.dot(yt_out[...], us[...], preferred_element_type=F32)
    for j, part in enumerate(scaled(total, q, picked, *held)):
        out[j * BLK : (j + 1) * BLK, :] = part.astype(out.dtype)


def start_call(lambdas, lam_index, live, sing, u, y):
    return pl.pallas_call(
        start_kernel,
        out_shape=[jax.ShapeDtypeStruct((W, Q), BF16), jax.ShapeDtypeStruct((W, T), BF16)],
        in_specs=[HBM] * 6,
        out_specs=[VMEM] * 2,
        scratch_shapes=SMALL
        + [pltpu.VMEM((T, VD), BF16), pltpu.VMEM((T, Q), BF16), pltpu.SemaphoreType.DMA((6,))],
        compiler_params=pltpu.CompilerParams(vmem_limit_bytes=8 << 20),
        cost_estimate=pl.CostEstimate(
            flops=2 * W * T * Q, bytes_accessed=2 * T * Q, transcendentals=0
        ),
    )(*pin(lambdas, lam_index, live, sing, u, y))


def rest_kernel(lambdas_h, lam_index_h, live_h, sing_h, u, yt, *rest):
    outs, (lambdas, lam_index, live, sing, us, sems) = rest[:3], rest[3:]
    x, _, _, c = place()
    where = [quarter(name, x, c) for name in ("primary", "secondary", "own")]
    held = (lambdas, lam_index, live, sing)
    copies = [
        pltpu.make_async_copy(r, h, sems.at[i])
        for i, (r, h) in enumerate(zip((lambdas_h, lam_index_h, live_h, sing_h), held))
    ]
    wide = [
        pltpu.make_async_copy(u.at[:, pl.ds(pl.multiple_of(q * Q, Q), Q)], us.at[i], sems.at[4 + i])
        for i, q in enumerate(where)
    ]
    for copy in copies + wide:
        copy.start()
    for copy in copies:
        copy.wait()
    picked = slots(live)
    for i, q in enumerate(where):
        wide[i].wait()
        total = jnp.dot(yt[...], us[i], preferred_element_type=F32)
        for j, part in enumerate(scaled(total, q, picked, *held)):
            outs[i][j * BLK : (j + 1) * BLK, :] = part.astype(outs[i].dtype)


def rest_call(lambdas, lam_index, live, sing, u, yt):
    return pl.pallas_call(
        rest_kernel,
        out_shape=[jax.ShapeDtypeStruct((W, Q), d) for d in (F32, BF16, F32)],
        in_specs=[HBM] * 5 + [VMEM],
        out_specs=[VMEM] * 3,
        scratch_shapes=SMALL + [pltpu.VMEM((3, T, Q), BF16), pltpu.SemaphoreType.DMA((7,))],
        compiler_params=pltpu.CompilerParams(vmem_limit_bytes=12 << 20),
        cost_estimate=pl.CostEstimate(
            flops=6 * W * T * Q, bytes_accessed=6 * T * Q, transcendentals=0
        ),
    )(*pin(lambdas, lam_index, live, sing, u), yt)


CHUNK = 256


def multiply(q, rows, shards, features):
    _, y, z0, c = place()
    back = (y - q + NY) % NY
    total = None
    for z in range(NZ):
        deep = (z0 - z + NZ) % NZ
        first = c * NY * NZ + deep * NY + back
        second = (1 - c) * NY * NZ + back * NZ + deep
        left = jnp.concatenate([shards[first, rows, :], shards[second, rows, :]], axis=1)
        right = features[:, z * NC * BLK : (z + 1) * NC * BLK]
        part = lax.dot_general(left, right, (((1,), (1,)), ((), ())), preferred_element_type=F32)
        total = part if total is None else total + part
    return total


def three_kernel(shards, own, primary, secondary, out):
    x, _, _, c = place()
    features = (own, primary, secondary)
    for r in range(Q // CHUNK):
        rows = slice(r * CHUNK, (r + 1) * CHUNK)
        total = None
        for i, name in enumerate(("own", "primary", "secondary")):
            part = multiply(quarter(name, x, c), rows, shards, features[i])
            total = part if total is None else total + part
        out[rows, :] = total


def three_call(shards, features):
    return pl.pallas_call(
        three_kernel,
        out_shape=jax.ShapeDtypeStruct((Q, W), F32),
        in_specs=[VMEM] * 4,
        out_specs=VMEM,
        compiler_params=pltpu.CompilerParams(vmem_limit_bytes=8 << 20),
        cost_estimate=pl.CostEstimate(
            flops=2 * W * 3 * Q * Q, bytes_accessed=2 * Q * 3 * Q, transcendentals=0
        ),
    )(shards, *features)


def spread(out, rows, values, live):
    first, second = slots(live)
    left, right = values[:, :BLK], values[:, BLK:]
    for b in range(NB):
        block = jnp.where(first == b, left, right)
        block = jnp.where(live[b] > 0, block, jnp.zeros_like(block))
        out[rows, b * BLK : (b + 1) * BLK] = block.astype(out.dtype)


def last_kernel(live_h, shards, features, so_far, tests, *rest):
    weights, mine, primary, secondary, opposite, live, packed, sem = rest
    copy = pltpu.make_async_copy(live_h, live, sem)
    copy.start()
    x, _, _, c = place()
    q = quarter("opposite", x, c)
    copy.wait()
    for r in range(Q // CHUNK):
        rows = slice(r * CHUNK, (r + 1) * CHUNK)
        total = (so_far[rows, :] + multiply(q, rows, shards, features)).astype(BF16)
        packed[rows, :] = total
        spread(weights, rows, total, live)
    count = TEST // NX
    for name, out in (
        ("opposite", opposite),
        ("primary", primary),
        ("secondary", secondary),
        ("own", mine),
    ):
        q = quarter(name, x, c)
        part = tests[pl.ds(pl.multiple_of(q * count, count), count), :]
        out[...] = jnp.dot(part, packed[...], preferred_element_type=F32).astype(out.dtype)


def last_call(live, shards, features, so_far, tests):
    rows = TEST // NX
    return pl.pallas_call(
        last_kernel,
        out_shape=[
            jax.ShapeDtypeStruct((Q, VD), BF16),
            jax.ShapeDtypeStruct((rows, W), F32),
            jax.ShapeDtypeStruct((rows, W), BF16),
            jax.ShapeDtypeStruct((rows, W), BF16),
            jax.ShapeDtypeStruct((rows, W), BF16),
        ],
        in_specs=[HBM] + [VMEM] * 4,
        out_specs=[VMEM] * 5,
        scratch_shapes=[
            pltpu.SMEM((NB,), jnp.int32),
            pltpu.VMEM((Q, W), BF16),
            pltpu.SemaphoreType.DMA,
        ],
        compiler_params=pltpu.CompilerParams(vmem_limit_bytes=8 << 20),
        cost_estimate=pl.CostEstimate(
            flops=4 * W * Q * Q, bytes_accessed=4 * Q * Q, transcendentals=0
        ),
    )(*pin(live), shards, features, so_far, tests)


def end_kernel(live_h, mine, a, b, c, out, live, sem):
    copy = pltpu.make_async_copy(live_h, live, sem)
    copy.start()
    total = mine[...] + a[...].astype(F32) + b[...].astype(F32) + c[...].astype(F32)
    copy.wait()
    spread(out, slice(0, TEST // NX), total, live)


def end_call(live, mine, a, b, c):
    return pl.pallas_call(
        end_kernel,
        out_shape=jax.ShapeDtypeStruct((TEST // NX, VD), BF16),
        in_specs=[HBM] + [VMEM] * 4,
        out_specs=VMEM,
        scratch_shapes=[pltpu.SMEM((NB,), jnp.int32), pltpu.SemaphoreType.DMA],
        compiler_params=pltpu.CompilerParams(vmem_limit_bytes=4 << 20),
    )(*pin(live), mine, a, b, c)


def body(u_train, y_train, sing, lambdas, lam_index, live, v_basis, x_test):
    sing = sing.reshape(1, F)
    small = (lambdas, lam_index, live, sing)
    p_opposite, yt = start_call(*small, u_train, y_train)
    come = send(p_opposite, PRIMARY)
    v_basis, yt = lax.optimization_barrier((v_basis, yt))
    near = [send(v_basis, pairs) for pairs in FIRST]
    p_primary, p_secondary, p_own = rest_call(*small, u_train, yt)
    row = jnp.stack([v_basis, *near])
    below = send(row, UP)
    above = send(row, DOWN)
    far_a = send(below[:2], UP)
    far_b = send(above[2:], DOWN)
    own = [row, below, far_a, far_b, above]
    other = [send(block, SWAP) for block in own]
    shards = jnp.concatenate(own + other)
    onward = (p_primary + come.astype(F32)).astype(BF16)
    from_secondary = send(onward, PRIMARY)
    from_primary = send(p_secondary, SECONDARY)
    filtered = (p_own + from_secondary.astype(F32) + from_primary.astype(F32)).astype(BF16)
    f_secondary = send(filtered, PRIMARY)
    f_primary = send(filtered, SECONDARY)
    f_opposite = send(f_secondary, PRIMARY)
    so_far = three_call(shards, (filtered, f_primary, f_secondary))
    weights, mine, primary, secondary, opposite = last_call(
        live, shards, f_opposite, so_far, x_test
    )
    predictions = end_call(
        live, mine, send(opposite, OPPOSITE), send(primary, PRIMARY), send(secondary, SECONDARY)
    )
    return weights, predictions


def solution(mesh):
    placed = (
        P("tm", None),
        P("tm", "vox"),
        P(),
        P(),
        P("vox"),
        P("vox"),
        P("tm", "vox"),
        P(None, "tm"),
    )
    return jax.shard_map(
        body,
        mesh=mesh,
        in_specs=placed,
        out_specs=(P("tm", "vox"), P("tm", "vox")),
        check_vma=False,
    )
```

time: 88.1 us -> 81.8 us (0.928)
  local copies, waits for them, and re-layouts: 7.91 us -> 1.17 us
  Pallas kernels: 15 us -> 11.4 us
  starting transfers between devices: 24.3 us -> 27.9 us
  waiting for transfers between devices: 39.4 us -> 38.2 us
  other arithmetic: 0.53 us -> 1.46 us
    unnamed x26 -> x16, local copies, waits for them, and re-layouts: 7.91 us -> 0.96 us
    ppermute x19 -> x21, starting transfers between devices: 24.3 us -> 27.9 us  [send(): return lax.ppermute(value, ('tm', 'vox'), pairs)]
    pallas_call x1, Pallas kernels: 4.48 us -> 1.8 us  [three_call(): pl.pallas_call(three_kernel, out_shape=jax.ShapeDtypeStruct((Q, W), F32),...]
    ppermute x19 -> x21, waiting for transfers between devices: 39.4 us -> 38.2 us  [send(): return lax.ppermute(value, ('tm', 'vox'), pairs)]
    pallas_call x1, Pallas kernels: 3.83 us -> 2.73 us  [last_call(): pl.pallas_call(last_kernel, out_shape=[jax.ShapeDtypeStruct((Q, VD), BF16...]
    another operation x1, other arithmetic: 0.13 us -> 1.08 us  [body(): row = jnp.stack([v_basis, *near])]
  transfers between devices with their start and end apart: 19 -> 21, of which waited for: 6 -> 9; matrix products, arithmetic and copies ran while one was open for 1% -> 3% of each run, Pallas kernels for 11% -> 6%
where the time goes in v2:
time: 81.8 us; the launch traced here: 81.1 us
  waiting for transfers between devices  38.2 us (47%)
  starting transfers between devices  27.9 us (34%)
  Pallas kernels  11.4 us (14%)
  other arithmetic  1.46 us (2%)
  local copies, waits for them, and re-layouts  1.17 us (1%)
  between operations  0.9 us (1%)
    ppermute x21, waiting for transfers between devices, send(): return lax.ppermute(value, ('tm', 'vox'), pairs)  38.2 us
    ppermute x21, starting transfers between devices, send(): return lax.ppermute(value, ('tm', 'vox'), pairs)  27.9 us
    pallas_call x1, Pallas kernels, rest_call(): pl.pallas_call(rest_kernel, out_shape=[jax.ShapeDtypeStruct((W, Q), d) fo...  3.22 us
    pallas_call x1, Pallas kernels, last_call(): pl.pallas_call(last_kernel, out_shape=[jax.ShapeDtypeStruct((Q, VD), BF16...  2.73 us
    pallas_call x1, Pallas kernels, start_call(): pl.pallas_call(start_kernel, out_shape=[jax.ShapeDtypeStruct((W, Q), BF16...  2.28 us
    pallas_call x1, Pallas kernels, three_call(): pl.pallas_call(three_kernel, out_shape=jax.ShapeDtypeStruct((Q, W), F32),...  1.8 us
  transfers between devices with their start and end apart: 21, of which 9 were waited for; matrix products, arithmetic and copies ran while one was open for 3% of the time, Pallas kernels for 6%

profile of v2, /device:TPU:0, one launch (start us, length us, event | category | flops | bytes accessed | tf_op | source)
XLA Modules:
  0.0 81.1 jit_solution(4871992935309578797)
XLA Ops:
  0.6 0.0 copy-start.1
  0.6 2.3 %shard_map.95 = (bf16[256,1024]{1,0:T(8,128)(2,1)S(1)}, bf16[256,768]{1,0:T(8,128)(2,1)S(1)}) custom-call(f32[20]{0:T(128)} %lambdas_h.3, s32[3]{0:T(128)} %lam_index_h.3, s32[3]{0:T(128)} %live_h.7, f32[1,4096]{1,0:T(1,128)} %bitcast.13, bf16[768,4096]{1,0:T(8,128)(2,1)} %u.3, bf16[768,384]{1,0:T(8,128)(2,1)} %y.1), custom_call_target="tpu_custom_call" | custom-call | flops 402653184 | bytes 1572864 | tf_op jit(solution)/shard_map/pallas_call | solution.py:128
  2.9 1.7 %collective-permute-start = (bf16[1024,128]{1,0:T(8,128)(2,1)}, bf16[1024,128]{1,0:T(8,128)(2,1)S(1)}, u32[]{:S(2)}, u32[]{:S(2)}) collective-permute-start(bf16[1024,128]{1,0:T(8,128)(2,1)} %param.14), channel_id=1, source_target_pairs={{0,8},{1,3},{2,10},{3,5},{4,12},{5,7},{6,14},{7,1},{8,16},{9,11},{... | collective-permute-start | bytes 786440 | tf_op jit(solution)/shard_map/ppermute | solution.py:56
  4.7 2.9 %collective-permute-start.1 = (bf16[1024,128]{1,0:T(8,128)(2,1)}, bf16[1024,128]{1,0:T(8,128)(2,1)S(1)}, u32[]{:S(2)}, u32[]{:S(2)}) collective-permute-start(bf16[1024,128]{1,0:T(8,128)(2,1)} %param.14), channel_id=1, source_target_pairs={{0,16},{1,5},{2,18},{3,7},{4,20},{5,1},{6,22},{7,3},{8,24},{9,13},... | collective-permute-start | bytes 786440 | tf_op jit(solution)/shard_map/ppermute | solution.py:56
  7.6 1.3 %collective-permute-start.2 = (bf16[1024,128]{1,0:T(8,128)(2,1)}, bf16[1024,128]{1,0:T(8,128)(2,1)S(1)}, u32[]{:S(2)}, u32[]{:S(2)}) collective-permute-start(bf16[1024,128]{1,0:T(8,128)(2,1)} %param.14), channel_id=1, source_target_pairs={{0,24},{1,7},{2,26},{3,1},{4,28},{5,3},{6,30},{7,5},{8,0},{9,15},{... | collective-permute-start | bytes 786440 | tf_op jit(solution)/shard_map/ppermute | solution.py:56
  8.9 1.5 %collective-permute-start.12 = (bf16[256,1024]{1,0:T(8,128)(2,1)S(1)}, bf16[256,1024]{1,0:T(8,128)(2,1)S(1)}, u32[]{:S(2)}, u32[]{:S(2)}) collective-permute-start(bf16[256,1024]{1,0:T(8,128)(2,1)S(1)} %get-tuple-element.19), channel_id=1, source_target_pairs={{0,32},{1,97},{2,34},{3,99},{4,36},{5,101},{6,38},{7,103},{8,40},{... | collective-permute-start | bytes 1572872 | tf_op jit(solution)/shard_map/ppermute | solution.py:56
  10.4 0.4 collective-permute-done
  10.8 4.1 %collective-permute-done.1 = bf16[1024,128]{1,0:T(8,128)(2,1)S(1)} collective-permute-done((bf16[1024,128]{1,0:T(8,128)(2,1)}, bf16[1024,128]{1,0:T(8,128)(2,1)S(1)}, u32[]{:S(2)}, u32[]{:S(2)}) %collective-permute-start.1) | collective-permute-done | bytes 262176 | tf_op jit(solution)/shard_map/ppermute | solution.py:56
  14.9 0.0 collective-permute-done.2
  14.9 1.1 %pad_maximum_fusion = bf16[4,1024,128]{2,1,0:T(8,128)(2,1)S(1)} fusion(bf16[1,1024,128]{2,1,0:T(8,128)(2,1)S(1)} %bitcast.10, bf16[1,1024,128]{2,1,0:T(8,128)(2,1)S(1)} %bitcast.12, bf16[1,1024,128]{2,1,0:T(8,128)(2,1)S(1)} %bitcast.11, bf16[1,1024,128]{2,1,0:T(8,128)(2,1)} %bitcast.9), kind=kLoop, calls=%fused_computation | loop fusion | flops 1572864 | bytes 2097152 | tf_op jit(solution)/shard_map/stack | solution.py:309
  16.0 2.0 %collective-permute-start.3 = (bf16[4,1024,128]{2,1,0:T(8,128)(2,1)S(1)}, bf16[4,1024,128]{2,1,0:T(8,128)(2,1)S(1)}, u32[]{:S(2)}, u32[]{:S(2)}) collective-permute-start(bf16[4,1024,128]{2,1,0:T(8,128)(2,1)S(1)} %pad_maximum_fusion), channel_id=1, source_target_pairs={{0,2},{1,9},{2,4},{3,11},{4,6},{5,13},{6,0},{7,15},{8,10},{9,17},{... | collective-permute-start | bytes 3145736 | tf_op jit(solution)/shard_map/ppermute | solution.py:56
  18.0 2.2 %collective-permute-start.5 = (bf16[4,1024,128]{2,1,0:T(8,128)(2,1)S(1)}, bf16[4,1024,128]{2,1,0:T(8,128)(2,1)S(1)}, u32[]{:S(2)}, u32[]{:S(2)}) collective-permute-start(bf16[4,1024,128]{2,1,0:T(8,128)(2,1)S(1)} %pad_maximum_fusion), channel_id=1, source_target_pairs={{0,6},{1,25},{2,0},{3,27},{4,2},{5,29},{6,4},{7,31},{8,14},{9,1},{... | collective-permute-start | bytes 3145736 | tf_op jit(solution)/shard_map/ppermute | solution.py:56
  20.2 3.2 %shard_map.96 = (f32[256,1024]{1,0:T(8,128)S(1)}, bf16[256,1024]{1,0:T(8,128)(2,1)S(1)}, f32[256,1024]{1,0:T(8,128)S(1)}) custom-call(f32[20]{0:T(128)} %lambdas_h.3, s32[3]{0:T(128)} %lam_index_h.3, s32[3]{0:T(128)} %live_h.7, f32[1,4096]{1,0:T(1,128)} %bitcast.14, bf16[768,4096]{1,0:T(8,128)(2,1)} %u.3, bf16[256,768]{1,0:T(8,128)(2,1)S(1)} %get-tuple-element.16.yt), custom_call_target="tpu_custom_call" | custom-call | flops 1207959552 | bytes 4718592 | tf_op jit(solution)/shard_map/pallas_call | solution.py:168
  23.4 2.8 %collective-permute-start.14 = (bf16[256,1024]{1,0:T(8,128)(2,1)S(1)}, bf16[256,1024]{1,0:T(8,128)(2,1)S(1)}, u32[]{:S(2)}, u32[]{:S(2)}) collective-permute-start(bf16[256,1024]{1,0:T(8,128)(2,1)S(1)} %get-tuple-element.20), channel_id=1, source_target_pairs={{0,96},{1,33},{2,98},{3,35},{4,100},{5,37},{6,102},{7,39},{8,104},... | collective-permute-start | bytes 1572872 | tf_op jit(solution)/shard_map/ppermute | solution.py:56
  26.3 0.0 copy-done.1
  26.3 0.1 collective-permute-start.7
  26.4 0.0 collective-permute-done.12
  26.4 0.1 add_convert_fusion.1
  26.5 0.1 collective-permute-start.13
  26.7 6.2 %collective-permute-done.3 = bf16[4,1024,128]{2,1,0:T(8,128)(2,1)S(1)} collective-permute-done((bf16[4,1024,128]{2,1,0:T(8,128)(2,1)S(1)}, bf16[4,1024,128]{2,1,0:T(8,128)(2,1)S(1)}, u32[]{:S(2)}, u32[]{:S(2)}) %collective-permute-start.3) | collective-permute-done | bytes 1048608 | tf_op jit(solution)/shard_map/ppermute | solution.py:56
  32.9 0.1 collective-permute-start.4
  33.0 0.0 collective-permute-done.5
  33.0 0.1 collective-permute-start.8
  33.2 4.7 %collective-permute-done.14 = bf16[256,1024]{1,0:T(8,128)(2,1)S(1)} collective-permute-done((bf16[256,1024]{1,0:T(8,128)(2,1)S(1)}, bf16[256,1024]{1,0:T(8,128)(2,1)S(1)}, u32[]{:S(2)}, u32[]{:S(2)}) %collective-permute-start.14) | collective-permute-done | bytes 524320 | tf_op jit(solution)/shard_map/ppermute | solution.py:56
  37.9 1.9 %collective-permute-start.6 = (bf16[2,1024,128]{2,1,0:T(8,128)(2,1)S(1)}, bf16[2,1024,128]{2,1,0:T(8,128)(2,1)S(1)}, u32[]{:S(2)}, u32[]{:S(2)}) collective-permute-start(bf16[2,1024,128]{2,1,0:T(8,128)(2,1)S(1)} %slice.9), channel_id=1, source_target_pairs={{0,6},{1,25},{2,0},{3,27},{4,2},{5,29},{6,4},{7,31},{8,14},{9,1},{... | collective-permute-start | bytes 1572872 | tf_op jit(solution)/shard_map/ppermute | solution.py:56
  39.9 0.0 collective-permute-done.13
  39.9 0.2 add_convert_fusion.own
  40.1 0.1 collective-permute-start.11
  40.2 0.1 constant_dynamic-update-slice_fusion.8
  40.4 3.0 %collective-permute-done.4 = bf16[2,1024,128]{2,1,0:T(8,128)(2,1)S(1)} collective-permute-done((bf16[2,1024,128]{2,1,0:T(8,128)(2,1)S(1)}, bf16[2,1024,128]{2,1,0:T(8,128)(2,1)S(1)}, u32[]{:S(2)}, u32[]{:S(2)}) %collective-permute-start.4) | collective-permute-done | bytes 524320 | tf_op jit(solution)/shard_map/ppermute | solution.py:56
  43.4 1.5 %collective-permute-start.15 = (bf16[256,1024]{1,0:T(8,128)(2,1)S(1)}, bf16[256,1024]{1,0:T(8,128)(2,1)S(1)}, u32[]{:S(2)}, u32[]{:S(2)}) collective-permute-start(bf16[256,1024]{1,0:T(8,128)(2,1)S(1)} %add_convert_fusion.own), channel_id=1, source_target_pairs={{0,32},{1,97},{2,34},{3,99},{4,36},{5,101},{6,38},{7,103},{8,40},{... | collective-permute-start | bytes 1572872 | tf_op jit(solution)/shard_map/ppermute | solution.py:56
  44.9 0.1 constant_dynamic-update-slice_fusion.7
  45.0 2.1 %collective-permute-done.6 = bf16[2,1024,128]{2,1,0:T(8,128)(2,1)S(1)} collective-permute-done((bf16[2,1024,128]{2,1,0:T(8,128)(2,1)S(1)}, bf16[2,1024,128]{2,1,0:T(8,128)(2,1)S(1)}, u32[]{:S(2)}, u32[]{:S(2)}) %collective-permute-start.6) | collective-permute-done | bytes 524320 | tf_op jit(solution)/shard_map/ppermute | solution.py:56
  47.1 0.0 collective-permute-start.9
  47.1 0.1 constant_dynamic-update-slice_fusion.6
  47.2 0.0 collective-permute-done.7
  47.2 0.6 collective-permute-start.10
  47.8 0.1 constant_dynamic-update-slice_fusion.5
  47.9 0.1 constant_dynamic-update-slice_fusion.4
  48.1 0.0 copy-start
  48.1 5.7 %collective-permute-done.15.secondary = bf16[256,1024]{1,0:T(8,128)(2,1)S(1)} collective-permute-done((bf16[256,1024]{1,0:T(8,128)(2,1)S(1)}, bf16[256,1024]{1,0:T(8,128)(2,1)S(1)}, u32[]{:S(2)}, u32[]{:S(2)}) %collective-permute-start.15) | collective-permute-done | bytes 524320 | tf_op jit(solution)/shard_map/ppermute | solution.py:56
  53.8 1.5 %collective-permute-start.17 = (bf16[256,1024]{1,0:T(8,128)(2,1)S(1)}, bf16[256,1024]{1,0:T(8,128)(2,1)S(1)}, u32[]{:S(2)}, u32[]{:S(2)}) collective-permute-start(bf16[256,1024]{1,0:T(8,128)(2,1)S(1)} %add_convert_fusion.own), channel_id=1, source_target_pairs={{0,96},{1,33},{2,98},{3,35},{4,100},{5,37},{6,102},{7,39},{8,104},... | collective-permute-start | bytes 1572872 | tf_op jit(solution)/shard_map/ppermute | solution.py:56
  55.3 0.0 collective-permute-done.8
  55.3 0.5 collective-permute-start.16
  55.8 0.1 constant_dynamic-update-slice_fusion.3
  56.0 0.0 collective-permute-done.9
  56.0 0.1 constant_dynamic-update-slice_fusion.2
  56.1 0.0 collective-permute-done.10
  56.1 0.1 constant_dynamic-update-slice_fusion.1
  56.1 0.0 collective-permute-done.11
  56.1 0.1 constant_dynamic-update-slice_fusion.shards
  56.3 8.9 %collective-permute-done.17.primary = bf16[256,1024]{1,0:T(8,128)(2,1)S(1)} collective-permute-done((bf16[256,1024]{1,0:T(8,128)(2,1)S(1)}, bf16[256,1024]{1,0:T(8,128)(2,1)S(1)}, u32[]{:S(2)}, u32[]{:S(2)}) %collective-permute-start.17) | collective-permute-done | bytes 524320 | tf_op jit(solution)/shard_map/ppermute | solution.py:56
  65.2 1.8 %shard_map.97.so_far = f32[1024,256]{1,0:T(8,128)S(1)} custom-call(bf16[32,1024,128]{2,1,0:T(8,128)(2,1)S(1)} %constant_dynamic-update-slice_fusion.shards, bf16[256,1024]{1,0:T(8,128)(2,1)S(1)} %add_convert_fusion.own, bf16[256,1024]{1,0:T(8,128)(2,1)S(1)} %collective-permute-done.17.primary, bf16[256,1024]{1,0:T(8,128)(2,1)S(1)} %collective-permute-done.15.secondary), custom_call_target="tpu_custom_call" | custom-call | flops 1610612736 | bytes 6291456 | tf_op jit(solution)/shard_map/pallas_call | solution.py:212
  67.0 0.0 collective-permute-done.16.features
  67.0 0.0 copy-done
  67.0 2.7 %shard_map.98 = (bf16[1024,384]{1,0:T(8,128)(2,1)}, f32[256,256]{1,0:T(8,128)S(1)}, bf16[256,256]{1,0:T(8,128)(2,1)S(1)}, bf16[256,256]{1,0:T(8,128)(2,1)S(1)}, bf16[256,256]{1,0:T(8,128)(2,1)S(1)}) custom-call(s32[3]{0:T(128)} %live_h.7, bf16[32,1024,128]{2,1,0:T(8,128)(2,1)S(1)} %constant_dynamic-update-slice_fusion.shards, ...), custom_call_target="tpu_custom_call" | custom-call | flops 1073741824 | bytes 4194304 | tf_op jit(solution)/shard_map/pallas_call | solution.py:259
  69.8 3.7 %collective-permute-start.18 = (bf16[256,256]{1,0:T(8,128)(2,1)S(1)}, bf16[256,256]{1,0:T(8,128)(2,1)S(1)}, u32[]{:S(2)}, u32[]{:S(2)}) collective-permute-start(bf16[256,256]{1,0:T(8,128)(2,1)S(1)} %get-tuple-element.23), channel_id=1, source_target_pairs={{0,64},{1,65},{2,66},{3,67},{4,68},{5,69},{6,70},{7,71},{8,72},{9,... | collective-permute-start | bytes 393224 | tf_op jit(solution)/shard_map/ppermute | solution.py:56
  73.5 0.9 %collective-permute-start.19 = (bf16[256,256]{1,0:T(8,128)(2,1)S(1)}, bf16[256,256]{1,0:T(8,128)(2,1)S(1)}, u32[]{:S(2)}, u32[]{:S(2)}) collective-permute-start(bf16[256,256]{1,0:T(8,128)(2,1)S(1)} %get-tuple-element.24), channel_id=1, source_target_pairs={{0,32},{1,97},{2,34},{3,99},{4,36},{5,101},{6,38},{7,103},{8,40},{... | collective-permute-start | bytes 393224 | tf_op jit(solution)/shard_map/ppermute | solution.py:56
  74.4 2.3 %collective-permute-start.20 = (bf16[256,256]{1,0:T(8,128)(2,1)S(1)}, bf16[256,256]{1,0:T(8,128)(2,1)S(1)}, u32[]{:S(2)}, u32[]{:S(2)}) collective-permute-start(bf16[256,256]{1,0:T(8,128)(2,1)S(1)} %get-tuple-element.25), channel_id=1, source_target_pairs={{0,96},{1,33},{2,98},{3,35},{4,100},{5,37},{6,102},{7,39},{8,104},... | collective-permute-start | bytes 393224 | tf_op jit(solution)/shard_map/ppermute | solution.py:56
  76.7 0.0 collective-permute-done.18.a
  76.8 2.9 %collective-permute-done.19.b = bf16[256,256]{1,0:T(8,128)(2,1)S(1)} collective-permute-done((bf16[256,256]{1,0:T(8,128)(2,1)S(1)}, bf16[256,256]{1,0:T(8,128)(2,1)S(1)}, u32[]{:S(2)}, u32[]{:S(2)}) %collective-permute-start.19) | collective-permute-done | bytes 131104 | tf_op jit(solution)/shard_map/ppermute | solution.py:56
  79.7 0.0 collective-permute-done.20.c
  79.7 1.4 %shard_map.99 = bf16[256,384]{1,0:T(8,128)(2,1)} custom-call(s32[3]{0:T(128)} %live_h.7, f32[256,256]{1,0:T(8,128)S(1)} %get-tuple-element.22.mine, bf16[256,256]{1,0:T(8,128)(2,1)S(1)} %collective-permute-done.18.a, bf16[256,256]{1,0:T(8,128)(2,1)S(1)} %collective-permute-done.19.b, bf16[256,256]{1,0:T(8,128)(2,1)S(1)} %collective-permute-done.20.c), custom_call_target="tpu_custom_call" | custom-call | tf_op jit(solution)/shard_map/pallas_call | solution.py:291
  (6 shorter events, 0.2 us)
Async XLA Ops:
  0.6 25.6 %copy-start.1 = (bf16[1024,128]{1,0:T(8,128)(2,1)S(1)}, bf16[1024,128]{1,0:T(8,128)(2,1)}, u32[]{:S(2)}) copy-start(bf16[1024,128]{1,0:T(8,128)(2,1)} %param.14) | copy-start | bytes 786436
  2.9 7.9 %collective-permute-start = (bf16[1024,128]{1,0:T(8,128)(2,1)}, bf16[1024,128]{1,0:T(8,128)(2,1)S(1)}, u32[]{:S(2)}, u32[]{:S(2)}) collective-permute-start(bf16[1024,128]{1,0:T(8,128)(2,1)} %param.14), channel_id=1, source_target_pairs={{0,8},{1,3},{2,10},{3,5},{4,12},{5,7},{6,14},{7,1},{8,16},{9,11},{... | collective-permute-start | bytes 786440 | tf_op jit(solution)/shard_map/ppermute | solution.py:56
  4.7 10.3 %collective-permute-start.1 = (bf16[1024,128]{1,0:T(8,128)(2,1)}, bf16[1024,128]{1,0:T(8,128)(2,1)S(1)}, u32[]{:S(2)}, u32[]{:S(2)}) collective-permute-start(bf16[1024,128]{1,0:T(8,128)(2,1)} %param.14), channel_id=1, source_target_pairs={{0,16},{1,5},{2,18},{3,7},{4,20},{5,1},{6,22},{7,3},{8,24},{9,13},... | collective-permute-start | bytes 786440 | tf_op jit(solution)/shard_map/ppermute | solution.py:56
  7.6 7.4 %collective-permute-start.2 = (bf16[1024,128]{1,0:T(8,128)(2,1)}, bf16[1024,128]{1,0:T(8,128)(2,1)S(1)}, u32[]{:S(2)}, u32[]{:S(2)}) collective-permute-start(bf16[1024,128]{1,0:T(8,128)(2,1)} %param.14), channel_id=1, source_target_pairs={{0,24},{1,7},{2,26},{3,1},{4,28},{5,3},{6,30},{7,5},{8,0},{9,15},{... | collective-permute-start | bytes 786440 | tf_op jit(solution)/shard_map/ppermute | solution.py:56
  8.9 17.5 %collective-permute-start.12 = (bf16[256,1024]{1,0:T(8,128)(2,1)S(1)}, bf16[256,1024]{1,0:T(8,128)(2,1)S(1)}, u32[]{:S(2)}, u32[]{:S(2)}) collective-permute-start(bf16[256,1024]{1,0:T(8,128)(2,1)S(1)} %get-tuple-element.19), channel_id=1, source_target_pairs={{0,32},{1,97},{2,34},{3,99},{4,36},{5,101},{6,38},{7,103},{8,40},{... | collective-permute-start | bytes 1572872 | tf_op jit(solution)/shard_map/ppermute | solution.py:56
  16.0 16.9 %collective-permute-start.3 = (bf16[4,1024,128]{2,1,0:T(8,128)(2,1)S(1)}, bf16[4,1024,128]{2,1,0:T(8,128)(2,1)S(1)}, u32[]{:S(2)}, u32[]{:S(2)}) collective-permute-start(bf16[4,1024,128]{2,1,0:T(8,128)(2,1)S(1)} %pad_maximum_fusion), channel_id=1, source_target_pairs={{0,2},{1,9},{2,4},{3,11},{4,6},{5,13},{6,0},{7,15},{8,10},{9,17},{... | collective-permute-start | bytes 3145736 | tf_op jit(solution)/shard_map/ppermute | solution.py:56
  18.0 15.0 %collective-permute-start.5 = (bf16[4,1024,128]{2,1,0:T(8,128)(2,1)S(1)}, bf16[4,1024,128]{2,1,0:T(8,128)(2,1)S(1)}, u32[]{:S(2)}, u32[]{:S(2)}) collective-permute-start(bf16[4,1024,128]{2,1,0:T(8,128)(2,1)S(1)} %pad_maximum_fusion), channel_id=1, source_target_pairs={{0,6},{1,25},{2,0},{3,27},{4,2},{5,29},{6,4},{7,31},{8,14},{9,1},{... | collective-permute-start | bytes 3145736 | tf_op jit(solution)/shard_map/ppermute | solution.py:56
  23.4 14.5 %collective-permute-start.14 = (bf16[256,1024]{1,0:T(8,128)(2,1)S(1)}, bf16[256,1024]{1,0:T(8,128)(2,1)S(1)}, u32[]{:S(2)}, u32[]{:S(2)}) collective-permute-start(bf16[256,1024]{1,0:T(8,128)(2,1)S(1)} %get-tuple-element.20), channel_id=1, source_target_pairs={{0,96},{1,33},{2,98},{3,35},{4,100},{5,37},{6,102},{7,39},{8,104},... | collective-permute-start | bytes 1572872 | tf_op jit(solution)/shard_map/ppermute | solution.py:56
  26.3 20.9 %collective-permute-start.7 = (bf16[4,1024,128]{2,1,0:T(8,128)(2,1)S(1)}, bf16[4,1024,128]{2,1,0:T(8,128)(2,1)S(1)}, u32[]{:S(2)}, u32[]{:S(2)}) collective-permute-start(bf16[4,1024,128]{2,1,0:T(8,128)(2,1)S(1)} %pad_maximum_fusion), channel_id=1, source_target_pairs={{0,1},{1,0},{2,3},{3,2},{4,5},{5,4},{6,7},{7,6},{8,9},{9,8},{10,11... | collective-permute-start | bytes 3145736 | tf_op jit(solution)/shard_map/ppermute | solution.py:56
  26.5 13.3 %collective-permute-start.13 = (bf16[256,1024]{1,0:T(8,128)(2,1)S(1)}, bf16[256,1024]{1,0:T(8,128)(2,1)S(1)}, u32[]{:S(2)}, u32[]{:S(2)}) collective-permute-start(bf16[256,1024]{1,0:T(8,128)(2,1)S(1)} %add_convert_fusion.1), channel_id=1, source_target_pairs={{0,32},{1,97},{2,34},{3,99},{4,36},{5,101},{6,38},{7,103},{8,40},{... | collective-permute-start | bytes 1572872 | tf_op jit(solution)/shard_map/ppermute | solution.py:56
  32.9 10.5 %collective-permute-start.4 = (bf16[2,1024,128]{2,1,0:T(8,128)(2,1)S(1)}, bf16[2,1024,128]{2,1,0:T(8,128)(2,1)S(1)}, u32[]{:S(2)}, u32[]{:S(2)}) collective-permute-start(bf16[2,1024,128]{2,1,0:T(8,128)(2,1)S(1)} %slice.8), channel_id=1, source_target_pairs={{0,2},{1,9},{2,4},{3,11},{4,6},{5,13},{6,0},{7,15},{8,10},{9,17},{... | collective-permute-start | bytes 1572872 | tf_op jit(solution)/shard_map/ppermute | solution.py:56
  33.0 22.3 %collective-permute-start.8 = (bf16[4,1024,128]{2,1,0:T(8,128)(2,1)S(1)}, bf16[4,1024,128]{2,1,0:T(8,128)(2,1)S(1)}, u32[]{:S(2)}, u32[]{:S(2)}) collective-permute-start(bf16[4,1024,128]{2,1,0:T(8,128)(2,1)S(1)} %collective-permute-done.3), channel_id=1, source_target_pairs={{0,1},{1,0},{2,3},{3,2},{4,5},{5,4},{6,7},{7,6},{8,9},{9,8},{10,11... | collective-permute-start | bytes 3145736 | tf_op jit(solution)/shard_map/ppermute | solution.py:56
  37.9 9.2 %collective-permute-start.6 = (bf16[2,1024,128]{2,1,0:T(8,128)(2,1)S(1)}, bf16[2,1024,128]{2,1,0:T(8,128)(2,1)S(1)}, u32[]{:S(2)}, u32[]{:S(2)}) collective-permute-start(bf16[2,1024,128]{2,1,0:T(8,128)(2,1)S(1)} %slice.9), channel_id=1, source_target_pairs={{0,6},{1,25},{2,0},{3,27},{4,2},{5,29},{6,4},{7,31},{8,14},{9,1},{... | collective-permute-start | bytes 1572872 | tf_op jit(solution)/shard_map/ppermute | solution.py:56
  40.1 16.0 %collective-permute-start.11 = (bf16[4,1024,128]{2,1,0:T(8,128)(2,1)S(1)}, bf16[4,1024,128]{2,1,0:T(8,128)(2,1)S(1)}, u32[]{:S(2)}, u32[]{:S(2)}) collective-permute-start(bf16[4,1024,128]{2,1,0:T(8,128)(2,1)S(1)} %collective-permute-done.5), channel_id=1, source_target_pairs={{0,1},{1,0},{2,3},{3,2},{4,5},{5,4},{6,7},{7,6},{8,9},{9,8},{10,11... | collective-permute-start | bytes 3145736 | tf_op jit(solution)/shard_map/ppermute | solution.py:56
  43.4 10.4 %collective-permute-start.15 = (bf16[256,1024]{1,0:T(8,128)(2,1)S(1)}, bf16[256,1024]{1,0:T(8,128)(2,1)S(1)}, u32[]{:S(2)}, u32[]{:S(2)}) collective-permute-start(bf16[256,1024]{1,0:T(8,128)(2,1)S(1)} %add_convert_fusion.own), channel_id=1, source_target_pairs={{0,32},{1,97},{2,34},{3,99},{4,36},{5,101},{6,38},{7,103},{8,40},{... | collective-permute-start | bytes 1572872 | tf_op jit(solution)/shard_map/ppermute | solution.py:56
  47.1 8.9 %collective-permute-start.9 = (bf16[2,1024,128]{2,1,0:T(8,128)(2,1)S(1)}, bf16[2,1024,128]{2,1,0:T(8,128)(2,1)S(1)}, u32[]{:S(2)}, u32[]{:S(2)}) collective-permute-start(bf16[2,1024,128]{2,1,0:T(8,128)(2,1)S(1)} %collective-permute-done.4), channel_id=1, source_target_pairs={{0,1},{1,0},{2,3},{3,2},{4,5},{5,4},{6,7},{7,6},{8,9},{9,8},{10,11... | collective-permute-start | bytes 1572872 | tf_op jit(solution)/shard_map/ppermute | solution.py:56
  47.2 8.9 %collective-permute-start.10 = (bf16[2,1024,128]{2,1,0:T(8,128)(2,1)S(1)}, bf16[2,1024,128]{2,1,0:T(8,128)(2,1)S(1)}, u32[]{:S(2)}, u32[]{:S(2)}) collective-permute-start(bf16[2,1024,128]{2,1,0:T(8,128)(2,1)S(1)} %collective-permute-done.6), channel_id=1, source_target_pairs={{0,1},{1,0},{2,3},{3,2},{4,5},{5,4},{6,7},{7,6},{8,9},{9,8},{10,11... | collective-permute-start | bytes 1572872 | tf_op jit(solution)/shard_map/ppermute | solution.py:56
  48.1 19.0 %copy-start = (bf16[1024,1024]{1,0:T(8,128)(2,1)S(1)}, bf16[1024,1024]{1,0:T(8,128)(2,1)}, u32[]{:S(2)}) copy-start(bf16[1024,1024]{1,0:T(8,128)(2,1)} %tests.1) | copy-start | bytes 6291460
  53.8 11.4 %collective-permute-start.17 = (bf16[256,1024]{1,0:T(8,128)(2,1)S(1)}, bf16[256,1024]{1,0:T(8,128)(2,1)S(1)}, u32[]{:S(2)}, u32[]{:S(2)}) collective-permute-start(bf16[256,1024]{1,0:T(8,128)(2,1)S(1)} %add_convert_fusion.own), channel_id=1, source_target_pairs={{0,96},{1,33},{2,98},{3,35},{4,100},{5,37},{6,102},{7,39},{8,104},... | collective-permute-start | bytes 1572872 | tf_op jit(solution)/shard_map/ppermute | solution.py:56
  55.3 11.7 %collective-permute-start.16 = (bf16[256,1024]{1,0:T(8,128)(2,1)S(1)}, bf16[256,1024]{1,0:T(8,128)(2,1)S(1)}, u32[]{:S(2)}, u32[]{:S(2)}) collective-permute-start(bf16[256,1024]{1,0:T(8,128)(2,1)S(1)} %collective-permute-done.15.secondary), channel_id=1, source_target_pairs={{0,32},{1,97},{2,34},{3,99},{4,36},{5,101},{6,38},{7,103},{8,40},{... | collective-permute-start | bytes 1572872 | tf_op jit(solution)/shard_map/ppermute | solution.py:56
  69.8 7.0 %collective-permute-start.18 = (bf16[256,256]{1,0:T(8,128)(2,1)S(1)}, bf16[256,256]{1,0:T(8,128)(2,1)S(1)}, u32[]{:S(2)}, u32[]{:S(2)}) collective-permute-start(bf16[256,256]{1,0:T(8,128)(2,1)S(1)} %get-tuple-element.23), channel_id=1, source_target_pairs={{0,64},{1,65},{2,66},{3,67},{4,68},{5,69},{6,70},{7,71},{8,72},{9,... | collective-permute-start | bytes 393224 | tf_op jit(solution)/shard_map/ppermute | solution.py:56
  73.5 6.2 %collective-permute-start.19 = (bf16[256,256]{1,0:T(8,128)(2,1)S(1)}, bf16[256,256]{1,0:T(8,128)(2,1)S(1)}, u32[]{:S(2)}, u32[]{:S(2)}) collective-permute-start(bf16[256,256]{1,0:T(8,128)(2,1)S(1)} %get-tuple-element.24), channel_id=1, source_target_pairs={{0,32},{1,97},{2,34},{3,99},{4,36},{5,101},{6,38},{7,103},{8,40},{... | collective-permute-start | bytes 393224 | tf_op jit(solution)/shard_map/ppermute | solution.py:56
  74.4 5.3 %collective-permute-start.20 = (bf16[256,256]{1,0:T(8,128)(2,1)S(1)}, bf16[256,256]{1,0:T(8,128)(2,1)S(1)}, u32[]{:S(2)}, u32[]{:S(2)}) collective-permute-start(bf16[256,256]{1,0:T(8,128)(2,1)S(1)} %get-tuple-element.25), channel_id=1, source_target_pairs={{0,96},{1,33},{2,98},{3,35},{4,100},{5,37},{6,102},{7,39},{8,104},... | collective-permute-start | bytes 393224 | tf_op jit(solution)/shard_map/ppermute | solution.py:56

commit v3 on v2

--- a/solution.py
+++ b/solution.py
@@ -181,14 +181,18 @@
 CHUNK = 256
 
 
+def block_of(distance):
+    return jnp.where(distance == 3, 2, jnp.where(distance == 2, 3, distance))
+
+
 def multiply(q, rows, shards, features):
     _, y, z0, c = place()
     back = (y - q + NY) % NY
     total = None
     for z in range(NZ):
         deep = (z0 - z + NZ) % NZ
-        first = c * NY * NZ + deep * NY + back
-        second = (1 - c) * NY * NZ + back * NZ + deep
+        first = c * NY * NZ + block_of(deep) * NY + back
+        second = (1 - c) * NY * NZ + block_of(back) * NZ + deep
         left = jnp.concatenate([shards[first, rows, :], shards[second, rows, :]], axis=1)
         right = features[:, z * NC * BLK : (z + 1) * NC * BLK]
         part = lax.dot_general(left, right, (((1,), (1,)), ((), ())), preferred_element_type=F32)
@@ -303,24 +307,30 @@
     small = (lambdas, lam_index, live, sing)
     p_opposite, yt = start_call(*small, u_train, y_train)
     come = send(p_opposite, PRIMARY)
-    v_basis, yt = lax.optimization_barrier((v_basis, yt))
+    p_primary, p_secondary, p_own = rest_call(*small, u_train, yt)
+    v_basis, _ = lax.optimization_barrier((v_basis, yt))
     near = [send(v_basis, pairs) for pairs in FIRST]
-    p_primary, p_secondary, p_own = rest_call(*small, u_train, yt)
     row = jnp.stack([v_basis, *near])
     below = send(row, UP)
     above = send(row, DOWN)
-    far_a = send(below[:2], UP)
-    far_b = send(above[2:], DOWN)
-    own = [row, below, far_a, far_b, above]
-    other = [send(block, SWAP) for block in own]
-    shards = jnp.concatenate(own + other)
     onward = (p_primary + come.astype(F32)).astype(BF16)
     from_secondary = send(onward, PRIMARY)
     from_primary = send(p_secondary, SECONDARY)
     filtered = (p_own + from_secondary.astype(F32) + from_primary.astype(F32)).astype(BF16)
     f_secondary = send(filtered, PRIMARY)
     f_primary = send(filtered, SECONDARY)
+    below, above, _ = lax.optimization_barrier((below, above, filtered))
+    far_a = send(below[:2], UP)
+    far_b = send(above[2:], DOWN)
+    early = jnp.concatenate([row, below, above])
+    early_other = send(early, SWAP)
+    f_secondary, f_primary, far_a, far_b = lax.optimization_barrier(
+        (f_secondary, f_primary, far_a, far_b)
+    )
     f_opposite = send(f_secondary, PRIMARY)
+    late = jnp.concatenate([far_a, far_b])
+    late_other = send(late, SWAP)
+    shards = jnp.concatenate([early, late, early_other, late_other])
     so_far = three_call(shards, (filtered, f_primary, f_secondary))
     weights, mine, primary, secondary, opposite = last_call(
         live, shards, f_opposite, so_far, x_test

time: 81.8 us -> 74.3 us (0.908)
  waiting for transfers between devices: 38.2 us -> 32.2 us
  starting transfers between devices: 27.9 us -> 26.9 us
  other arithmetic: 1.46 us -> 0.63 us
    ppermute x21 -> x18, waiting for transfers between devices: 38.2 us -> 32.2 us  [send(): return lax.ppermute(value, ('tm', 'vox'), pairs)]
    ppermute x21 -> x18, starting transfers between devices: 27.9 us -> 26.9 us  [send(): return lax.ppermute(value, ('tm', 'vox'), pairs)]
    another operation x1, other arithmetic: 1.08 us -> 0.13 us  [body(): row = jnp.stack([v_basis, *near])]
  transfers between devices with their start and end apart: 21 -> 18, of which waited for: 9 -> 9; matrix products, arithmetic and copies ran while one was open for 3% -> 2% of each run, Pallas kernels for 6% -> 7%
where the time goes in v3:
time: 74.3 us; the launch traced here: 73.8 us
  waiting for transfers between devices  32.2 us (43%)
  starting transfers between devices  26.9 us (36%)
  Pallas kernels  11.4 us (15%)
  local copies, waits for them, and re-layouts  1.85 us (2%)
  between operations  0.81 us (1%)
    ppermute x18, waiting for transfers between devices, send(): return lax.ppermute(value, ('tm', 'vox'), pairs)  32.2 us
    ppermute x18, starting transfers between devices, send(): return lax.ppermute(value, ('tm', 'vox'), pairs)  26.9 us
    pallas_call x1, Pallas kernels, rest_call(): pl.pallas_call(rest_kernel, out_shape=[jax.ShapeDtypeStruct((W, Q), d) fo...  3.22 us
    pallas_call x1, Pallas kernels, last_call(): pl.pallas_call(last_kernel, out_shape=[jax.ShapeDtypeStruct((Q, VD), BF16...  2.72 us
    pallas_call x1, Pallas kernels, start_call(): pl.pallas_call(start_kernel, out_shape=[jax.ShapeDtypeStruct((W, Q), BF16...  2.28 us
    pallas_call x1, Pallas kernels, three_call(): pl.pallas_call(three_kernel, out_shape=jax.ShapeDtypeStruct((Q, W), F32),...  1.81 us
  transfers between devices with their start and end apart: 18, of which 9 were waited for; matrix products, arithmetic and copies ran while one was open for 2% of the time, Pallas kernels for 7%

profile of v3, /device:TPU:0, one launch (start us, length us, event | category | flops | bytes accessed | tf_op | source)
XLA Modules:
  0.0 73.8 jit_solution(11047328190269949386)
XLA Ops:
  0.6 0.0 copy-start.1
  0.6 2.3 %shard_map.95 = (bf16[256,1024]{1,0:T(8,128)(2,1)S(1)}, bf16[256,768]{1,0:T(8,128)(2,1)S(1)}) custom-call(f32[20]{0:T(128)} %lambdas_h.3, s32[3]{0:T(128)} %lam_index_h.3, s32[3]{0:T(128)} %live_h.7, f32[1,4096]{1,0:T(1,128)} %bitcast.17, bf16[768,4096]{1,0:T(8,128)(2,1)} %u.3, bf16[768,384]{1,0:T(8,128)(2,1)} %y.1), custom_call_target="tpu_custom_call" | custom-call | flops 402653184 | bytes 1572864 | tf_op jit(solution)/shard_map/pallas_call | solution.py:128
  2.9 1.6 %collective-permute-start.5 = (bf16[256,1024]{1,0:T(8,128)(2,1)S(1)}, bf16[256,1024]{1,0:T(8,128)(2,1)S(1)}, u32[]{:S(2)}, u32[]{:S(2)}) collective-permute-start(bf16[256,1024]{1,0:T(8,128)(2,1)S(1)} %get-tuple-element.23), channel_id=1, source_target_pairs={{0,32},{1,97},{2,34},{3,99},{4,36},{5,101},{6,38},{7,103},{8,40},{... | collective-permute-start | bytes 1572872 | tf_op jit(solution)/shard_map/ppermute | solution.py:56
  4.6 1.6 %collective-permute-start = (bf16[1024,128]{1,0:T(8,128)(2,1)}, bf16[1024,128]{1,0:T(8,128)(2,1)S(1)}, u32[]{:S(2)}, u32[]{:S(2)}) collective-permute-start(bf16[1024,128]{1,0:T(8,128)(2,1)} %param.14), channel_id=1, source_target_pairs={{0,8},{1,3},{2,10},{3,5},{4,12},{5,7},{6,14},{7,1},{8,16},{9,11},{... | collective-permute-start | bytes 786440 | tf_op jit(solution)/shard_map/ppermute | solution.py:56
  6.2 2.9 %collective-permute-start.1 = (bf16[1024,128]{1,0:T(8,128)(2,1)}, bf16[1024,128]{1,0:T(8,128)(2,1)S(1)}, u32[]{:S(2)}, u32[]{:S(2)}) collective-permute-start(bf16[1024,128]{1,0:T(8,128)(2,1)} %param.14), channel_id=1, source_target_pairs={{0,16},{1,5},{2,18},{3,7},{4,20},{5,1},{6,22},{7,3},{8,24},{9,13},... | collective-permute-start | bytes 786440 | tf_op jit(solution)/shard_map/ppermute | solution.py:56
  9.1 1.3 %collective-permute-start.2 = (bf16[1024,128]{1,0:T(8,128)(2,1)}, bf16[1024,128]{1,0:T(8,128)(2,1)S(1)}, u32[]{:S(2)}, u32[]{:S(2)}) collective-permute-start(bf16[1024,128]{1,0:T(8,128)(2,1)} %param.14), channel_id=1, source_target_pairs={{0,24},{1,7},{2,26},{3,1},{4,28},{5,3},{6,30},{7,5},{8,0},{9,15},{... | collective-permute-start | bytes 786440 | tf_op jit(solution)/shard_map/ppermute | solution.py:56
  10.4 3.2 %shard_map.96 = (f32[256,1024]{1,0:T(8,128)S(1)}, bf16[256,1024]{1,0:T(8,128)(2,1)S(1)}, f32[256,1024]{1,0:T(8,128)S(1)}) custom-call(f32[20]{0:T(128)} %lambdas_h.3, s32[3]{0:T(128)} %lam_index_h.3, s32[3]{0:T(128)} %live_h.7, f32[1,4096]{1,0:T(1,128)} %bitcast.18, bf16[768,4096]{1,0:T(8,128)(2,1)} %u.3, bf16[256,768]{1,0:T(8,128)(2,1)S(1)} %get-tuple-element.19.yt), custom_call_target="tpu_custom_call" | custom-call | flops 1207959552 | bytes 4718592 | tf_op jit(solution)/shard_map/pallas_call | solution.py:168
  13.6 1.8 %collective-permute-start.7 = (bf16[256,1024]{1,0:T(8,128)(2,1)S(1)}, bf16[256,1024]{1,0:T(8,128)(2,1)S(1)}, u32[]{:S(2)}, u32[]{:S(2)}) collective-permute-start(bf16[256,1024]{1,0:T(8,128)(2,1)S(1)} %get-tuple-element.24), channel_id=1, source_target_pairs={{0,96},{1,33},{2,98},{3,35},{4,100},{5,37},{6,102},{7,39},{8,104},... | collective-permute-start | bytes 1572872 | tf_op jit(solution)/shard_map/ppermute | solution.py:56
  15.4 0.0 copy-done.1
  15.5 0.0 collective-permute-done
  15.5 0.9 %collective-permute-done.1 = bf16[1024,128]{1,0:T(8,128)(2,1)S(1)} collective-permute-done((bf16[1024,128]{1,0:T(8,128)(2,1)}, bf16[1024,128]{1,0:T(8,128)(2,1)S(1)}, u32[]{:S(2)}, u32[]{:S(2)}) %collective-permute-start.1) | collective-permute-done | bytes 262176 | tf_op jit(solution)/shard_map/ppermute | solution.py:56
  16.4 0.0 collective-permute-done.2
  16.4 0.1 pad_maximum_fusion
  16.6 2.0 %collective-permute-start.3 = (bf16[4,1024,128]{2,1,0:T(8,128)(2,1)S(1)}, bf16[4,1024,128]{2,1,0:T(8,128)(2,1)S(1)}, u32[]{:S(2)}, u32[]{:S(2)}) collective-permute-start(bf16[4,1024,128]{2,1,0:T(8,128)(2,1)S(1)} %pad_maximum_fusion), channel_id=1, source_target_pairs={{0,2},{1,9},{2,4},{3,11},{4,6},{5,13},{6,0},{7,15},{8,10},{9,17},{... | collective-permute-start | bytes 3145736 | tf_op jit(solution)/shard_map/ppermute | solution.py:56
  18.5 2.2 %collective-permute-start.4 = (bf16[4,1024,128]{2,1,0:T(8,128)(2,1)S(1)}, bf16[4,1024,128]{2,1,0:T(8,128)(2,1)S(1)}, u32[]{:S(2)}, u32[]{:S(2)}) collective-permute-start(bf16[4,1024,128]{2,1,0:T(8,128)(2,1)S(1)} %pad_maximum_fusion), channel_id=1, source_target_pairs={{0,6},{1,25},{2,0},{3,27},{4,2},{5,29},{6,4},{7,31},{8,14},{9,1},{... | collective-permute-start | bytes 3145736 | tf_op jit(solution)/shard_map/ppermute | solution.py:56
  20.7 0.0 collective-permute-done.5
  20.7 0.2 add_convert_fusion.1
  20.9 1.6 %collective-permute-start.6 = (bf16[256,1024]{1,0:T(8,128)(2,1)S(1)}, bf16[256,1024]{1,0:T(8,128)(2,1)S(1)}, u32[]{:S(2)}, u32[]{:S(2)}) collective-permute-start(bf16[256,1024]{1,0:T(8,128)(2,1)S(1)} %add_convert_fusion.1), channel_id=1, source_target_pairs={{0,32},{1,97},{2,34},{3,99},{4,36},{5,101},{6,38},{7,103},{8,40},{... | collective-permute-start | bytes 1572872 | tf_op jit(solution)/shard_map/ppermute | solution.py:56
  22.5 0.1 constant_dynamic-update-slice_fusion.4
  22.5 0.1 constant_dynamic-update-slice_fusion.3
  22.6 0.1 constant_dynamic-update-slice_fusion.2
  22.7 0.2 collective-permute-done.7
  22.9 8.5 %collective-permute-done.6 = bf16[256,1024]{1,0:T(8,128)(2,1)S(1)} collective-permute-done((bf16[256,1024]{1,0:T(8,128)(2,1)S(1)}, bf16[256,1024]{1,0:T(8,128)(2,1)S(1)}, u32[]{:S(2)}, u32[]{:S(2)}) %collective-permute-start.6) | collective-permute-done | bytes 524320 | tf_op jit(solution)/shard_map/ppermute | solution.py:56
  31.4 0.3 add_convert_fusion.own
  31.6 1.8 %collective-permute-done.3 = bf16[4,1024,128]{2,1,0:T(8,128)(2,1)S(1)} collective-permute-done((bf16[4,1024,128]{2,1,0:T(8,128)(2,1)S(1)}, bf16[4,1024,128]{2,1,0:T(8,128)(2,1)S(1)}, u32[]{:S(2)}, u32[]{:S(2)}) %collective-permute-start.3) | collective-permute-done | bytes 1048608 | tf_op jit(solution)/shard_map/ppermute | solution.py:56
  33.4 0.0 collective-permute-done.4
  33.4 0.4 constant_dynamic-update-slice_fusion.1
  33.9 0.4 constant_dynamic-update-slice_fusion
  34.3 0.1 collective-permute-start.12
  34.4 1.6 %collective-permute-start.8 = (bf16[256,1024]{1,0:T(8,128)(2,1)S(1)}, bf16[256,1024]{1,0:T(8,128)(2,1)S(1)}, u32[]{:S(2)}, u32[]{:S(2)}) collective-permute-start(bf16[256,1024]{1,0:T(8,128)(2,1)S(1)} %add_convert_fusion.own), channel_id=1, source_target_pairs={{0,32},{1,97},{2,34},{3,99},{4,36},{5,101},{6,38},{7,103},{8,40},{... | collective-permute-start | bytes 1572872 | tf_op jit(solution)/shard_map/ppermute | solution.py:56
  35.9 1.7 %collective-permute-start.9 = (bf16[256,1024]{1,0:T(8,128)(2,1)S(1)}, bf16[256,1024]{1,0:T(8,128)(2,1)S(1)}, u32[]{:S(2)}, u32[]{:S(2)}) collective-permute-start(bf16[256,1024]{1,0:T(8,128)(2,1)S(1)} %add_convert_fusion.own), channel_id=1, source_target_pairs={{0,96},{1,33},{2,98},{3,35},{4,100},{5,37},{6,102},{7,39},{8,104},... | collective-permute-start | bytes 1572872 | tf_op jit(solution)/shard_map/ppermute | solution.py:56
  37.8 1.9 %collective-permute-start.10 = (bf16[2,1024,128]{2,1,0:T(8,128)(2,1)S(1)}, bf16[2,1024,128]{2,1,0:T(8,128)(2,1)S(1)}, u32[]{:S(2)}, u32[]{:S(2)}) collective-permute-start(bf16[2,1024,128]{2,1,0:T(8,128)(2,1)S(1)} %slice.6), channel_id=1, source_target_pairs={{0,2},{1,9},{2,4},{3,11},{4,6},{5,13},{6,0},{7,15},{8,10},{9,17},{... | collective-permute-start | bytes 1572872 | tf_op jit(solution)/shard_map/ppermute | solution.py:56
  39.6 1.6 %collective-permute-start.11 = (bf16[2,1024,128]{2,1,0:T(8,128)(2,1)S(1)}, bf16[2,1024,128]{2,1,0:T(8,128)(2,1)S(1)}, u32[]{:S(2)}, u32[]{:S(2)}) collective-permute-start(bf16[2,1024,128]{2,1,0:T(8,128)(2,1)S(1)} %slice.7), channel_id=1, source_target_pairs={{0,6},{1,25},{2,0},{3,27},{4,2},{5,29},{6,4},{7,31},{8,14},{9,1},{... | collective-permute-start | bytes 1572872 | tf_op jit(solution)/shard_map/ppermute | solution.py:56
  41.2 8.3 %collective-permute-done.8.secondary = bf16[256,1024]{1,0:T(8,128)(2,1)S(1)} collective-permute-done((bf16[256,1024]{1,0:T(8,128)(2,1)S(1)}, bf16[256,1024]{1,0:T(8,128)(2,1)S(1)}, u32[]{:S(2)}, u32[]{:S(2)}) %collective-permute-start.8) | collective-permute-done | bytes 524320 | tf_op jit(solution)/shard_map/ppermute | solution.py:56
  49.5 0.0 collective-permute-done.9.primary
  49.5 0.0 collective-permute-done.10
  49.5 0.0 collective-permute-done.11
  49.5 0.1 pad_maximum_fusion.1
  49.6 0.8 %collective-permute-start.13 = (bf16[4,1024,128]{2,1,0:T(8,128)(2,1)S(1)}, bf16[4,1024,128]{2,1,0:T(8,128)(2,1)S(1)}, u32[]{:S(2)}, u32[]{:S(2)}) collective-permute-start(bf16[4,1024,128]{2,1,0:T(8,128)(2,1)S(1)} %pad_maximum_fusion.1), channel_id=1, source_target_pairs={{0,1},{1,0},{2,3},{3,2},{4,5},{5,4},{6,7},{7,6},{8,9},{9,8},{10,11... | collective-permute-start | bytes 3145736 | tf_op jit(solution)/shard_map/ppermute | solution.py:56
  50.4 0.3 collective-permute-start.14
  50.7 0.1 constant_dynamic-update-slice_fusion.9
  50.8 0.1 constant_dynamic-update-slice_fusion.8
  50.9 0.0 copy-start
  50.9 0.0 collective-permute-done.12
  50.9 0.4 constant_dynamic-update-slice_fusion.7
  51.3 1.4 %collective-permute-done.13 = bf16[4,1024,128]{2,1,0:T(8,128)(2,1)S(1)} collective-permute-done((bf16[4,1024,128]{2,1,0:T(8,128)(2,1)S(1)}, bf16[4,1024,128]{2,1,0:T(8,128)(2,1)S(1)}, u32[]{:S(2)}, u32[]{:S(2)}) %collective-permute-start.13) | collective-permute-done | bytes 1048608 | tf_op jit(solution)/shard_map/ppermute | solution.py:56
  52.7 0.1 constant_dynamic-update-slice_fusion.6.shards
  52.9 1.8 %shard_map.97.so_far = f32[1024,256]{1,0:T(8,128)S(1)} custom-call(bf16[32,1024,128]{2,1,0:T(8,128)(2,1)S(1)} %constant_dynamic-update-slice_fusion.6.shards, bf16[256,1024]{1,0:T(8,128)(2,1)S(1)} %add_convert_fusion.own, bf16[256,1024]{1,0:T(8,128)(2,1)S(1)} %collective-permute-done.9.primary, bf16[256,1024]{1,0:T(8,128)(2,1)S(1)} %collective-permute-done.8.secondary), custom_call_target="tpu_custom_call" | custom-call | flops 1610612736 | bytes 6291456 | tf_op jit(solution)/shard_map/pallas_call | solution.py:216
  54.7 6.1 %collective-permute-done.14.features = bf16[256,1024]{1,0:T(8,128)(2,1)S(1)} collective-permute-done((bf16[256,1024]{1,0:T(8,128)(2,1)S(1)}, bf16[256,1024]{1,0:T(8,128)(2,1)S(1)}, u32[]{:S(2)}, u32[]{:S(2)}) %collective-permute-start.14) | collective-permute-done | bytes 524320 | tf_op jit(solution)/shard_map/ppermute | solution.py:56
  60.8 0.0 copy-done
  60.8 2.7 %shard_map.98 = (bf16[1024,384]{1,0:T(8,128)(2,1)}, f32[256,256]{1,0:T(8,128)S(1)}, bf16[256,256]{1,0:T(8,128)(2,1)S(1)}, bf16[256,256]{1,0:T(8,128)(2,1)S(1)}, bf16[256,256]{1,0:T(8,128)(2,1)S(1)}) custom-call(s32[3]{0:T(128)} %live_h.7, bf16[32,1024,128]{2,1,0:T(8,128)(2,1)S(1)} %constant_dynamic-update-slice_fusion.6.shards, ...), custom_call_target="tpu_custom_call" | custom-call | flops 1073741824 | bytes 4194304 | tf_op jit(solution)/shard_map/pallas_call | solution.py:263
  63.6 0.7 collective-permute-start.15
  64.2 0.5 collective-permute-start.16
  64.8 2.7 %collective-permute-start.17 = (bf16[256,256]{1,0:T(8,128)(2,1)S(1)}, bf16[256,256]{1,0:T(8,128)(2,1)S(1)}, u32[]{:S(2)}, u32[]{:S(2)}) collective-permute-start(bf16[256,256]{1,0:T(8,128)(2,1)S(1)} %get-tuple-element.35), channel_id=1, source_target_pairs={{0,96},{1,33},{2,98},{3,35},{4,100},{5,37},{6,102},{7,39},{8,104},... | collective-permute-start | bytes 393224 | tf_op jit(solution)/shard_map/ppermute | solution.py:56
  67.5 3.0 %collective-permute-done.15.a = bf16[256,256]{1,0:T(8,128)(2,1)S(1)} collective-permute-done((bf16[256,256]{1,0:T(8,128)(2,1)S(1)}, bf16[256,256]{1,0:T(8,128)(2,1)S(1)}, u32[]{:S(2)}, u32[]{:S(2)}) %collective-permute-start.15) | collective-permute-done | bytes 131104 | tf_op jit(solution)/shard_map/ppermute | solution.py:56
  70.5 1.9 %collective-permute-done.16.b = bf16[256,256]{1,0:T(8,128)(2,1)S(1)} collective-permute-done((bf16[256,256]{1,0:T(8,128)(2,1)S(1)}, bf16[256,256]{1,0:T(8,128)(2,1)S(1)}, u32[]{:S(2)}, u32[]{:S(2)}) %collective-permute-start.16) | collective-permute-done | bytes 131104 | tf_op jit(solution)/shard_map/ppermute | solution.py:56
  72.4 0.0 collective-permute-done.17.c
  72.4 1.4 %shard_map.99 = bf16[256,384]{1,0:T(8,128)(2,1)} custom-call(s32[3]{0:T(128)} %live_h.7, f32[256,256]{1,0:T(8,128)S(1)} %get-tuple-element.32.mine, bf16[256,256]{1,0:T(8,128)(2,1)S(1)} %collective-permute-done.15.a, bf16[256,256]{1,0:T(8,128)(2,1)S(1)} %collective-permute-done.16.b, bf16[256,256]{1,0:T(8,128)(2,1)S(1)} %collective-permute-done.17.c), custom_call_target="tpu_custom_call" | custom-call | tf_op jit(solution)/shard_map/pallas_call | solution.py:295
  (3 shorter events, 0.1 us)
Async XLA Ops:
  0.6 14.8 %copy-start.1 = (bf16[1024,128]{1,0:T(8,128)(2,1)S(1)}, bf16[1024,128]{1,0:T(8,128)(2,1)}, u32[]{:S(2)}) copy-start(bf16[1024,128]{1,0:T(8,128)(2,1)} %param.14) | copy-start | bytes 786436
  2.9 17.8 %collective-permute-start.5 = (bf16[256,1024]{1,0:T(8,128)(2,1)S(1)}, bf16[256,1024]{1,0:T(8,128)(2,1)S(1)}, u32[]{:S(2)}, u32[]{:S(2)}) collective-permute-start(bf16[256,1024]{1,0:T(8,128)(2,1)S(1)} %get-tuple-element.23), channel_id=1, source_target_pairs={{0,32},{1,97},{2,34},{3,99},{4,36},{5,101},{6,38},{7,103},{8,40},{... | collective-permute-start | bytes 1572872 | tf_op jit(solution)/shard_map/ppermute | solution.py:56
  4.6 10.9 %collective-permute-start = (bf16[1024,128]{1,0:T(8,128)(2,1)}, bf16[1024,128]{1,0:T(8,128)(2,1)S(1)}, u32[]{:S(2)}, u32[]{:S(2)}) collective-permute-start(bf16[1024,128]{1,0:T(8,128)(2,1)} %param.14), channel_id=1, source_target_pairs={{0,8},{1,3},{2,10},{3,5},{4,12},{5,7},{6,14},{7,1},{8,16},{9,11},{... | collective-permute-start | bytes 786440 | tf_op jit(solution)/shard_map/ppermute | solution.py:56
  6.2 10.3 %collective-permute-start.1 = (bf16[1024,128]{1,0:T(8,128)(2,1)}, bf16[1024,128]{1,0:T(8,128)(2,1)S(1)}, u32[]{:S(2)}, u32[]{:S(2)}) collective-permute-start(bf16[1024,128]{1,0:T(8,128)(2,1)} %param.14), channel_id=1, source_target_pairs={{0,16},{1,5},{2,18},{3,7},{4,20},{5,1},{6,22},{7,3},{8,24},{9,13},... | collective-permute-start | bytes 786440 | tf_op jit(solution)/shard_map/ppermute | solution.py:56
  9.1 7.4 %collective-permute-start.2 = (bf16[1024,128]{1,0:T(8,128)(2,1)}, bf16[1024,128]{1,0:T(8,128)(2,1)S(1)}, u32[]{:S(2)}, u32[]{:S(2)}) collective-permute-start(bf16[1024,128]{1,0:T(8,128)(2,1)} %param.14), channel_id=1, source_target_pairs={{0,24},{1,7},{2,26},{3,1},{4,28},{5,3},{6,30},{7,5},{8,0},{9,15},{... | collective-permute-start | bytes 786440 | tf_op jit(solution)/shard_map/ppermute | solution.py:56
  13.6 9.2 %collective-permute-start.7 = (bf16[256,1024]{1,0:T(8,128)(2,1)S(1)}, bf16[256,1024]{1,0:T(8,128)(2,1)S(1)}, u32[]{:S(2)}, u32[]{:S(2)}) collective-permute-start(bf16[256,1024]{1,0:T(8,128)(2,1)S(1)} %get-tuple-element.24), channel_id=1, source_target_pairs={{0,96},{1,33},{2,98},{3,35},{4,100},{5,37},{6,102},{7,39},{8,104},... | collective-permute-start | bytes 1572872 | tf_op jit(solution)/shard_map/ppermute | solution.py:56
  16.6 16.9 %collective-permute-start.3 = (bf16[4,1024,128]{2,1,0:T(8,128)(2,1)S(1)}, bf16[4,1024,128]{2,1,0:T(8,128)(2,1)S(1)}, u32[]{:S(2)}, u32[]{:S(2)}) collective-permute-start(bf16[4,1024,128]{2,1,0:T(8,128)(2,1)S(1)} %pad_maximum_fusion), channel_id=1, source_target_pairs={{0,2},{1,9},{2,4},{3,11},{4,6},{5,13},{6,0},{7,15},{8,10},{9,17},{... | collective-permute-start | bytes 3145736 | tf_op jit(solution)/shard_map/ppermute | solution.py:56
  18.5 14.9 %collective-permute-start.4 = (bf16[4,1024,128]{2,1,0:T(8,128)(2,1)S(1)}, bf16[4,1024,128]{2,1,0:T(8,128)(2,1)S(1)}, u32[]{:S(2)}, u32[]{:S(2)}) collective-permute-start(bf16[4,1024,128]{2,1,0:T(8,128)(2,1)S(1)} %pad_maximum_fusion), channel_id=1, source_target_pairs={{0,6},{1,25},{2,0},{3,27},{4,2},{5,29},{6,4},{7,31},{8,14},{9,1},{... | collective-permute-start | bytes 3145736 | tf_op jit(solution)/shard_map/ppermute | solution.py:56
  20.9 10.5 %collective-permute-start.6 = (bf16[256,1024]{1,0:T(8,128)(2,1)S(1)}, bf16[256,1024]{1,0:T(8,128)(2,1)S(1)}, u32[]{:S(2)}, u32[]{:S(2)}) collective-permute-start(bf16[256,1024]{1,0:T(8,128)(2,1)S(1)} %add_convert_fusion.1), channel_id=1, source_target_pairs={{0,32},{1,97},{2,34},{3,99},{4,36},{5,101},{6,38},{7,103},{8,40},{... | collective-permute-start | bytes 1572872 | tf_op jit(solution)/shard_map/ppermute | solution.py:56
  34.3 16.6 %collective-permute-start.12 = (bf16[12,1024,128]{2,1,0:T(8,128)(2,1)S(1)}, bf16[12,1024,128]{2,1,0:T(8,128)(2,1)S(1)}, u32[]{:S(2)}, u32[]{:S(2)}) collective-permute-start(bf16[12,1024,128]{2,1,0:T(8,128)(2,1)S(1)} %get-tuple-element.36), channel_id=1, source_target_pairs={{0,1},{1,0},{2,3},{3,2},{4,5},{5,4},{6,7},{7,6},{8,9},{9,8},{10,11... | collective-permute-start | bytes 9437192 | tf_op jit(solution)/shard_map/ppermute | solution.py:56
  34.4 15.2 %collective-permute-start.8 = (bf16[256,1024]{1,0:T(8,128)(2,1)S(1)}, bf16[256,1024]{1,0:T(8,128)(2,1)S(1)}, u32[]{:S(2)}, u32[]{:S(2)}) collective-permute-start(bf16[256,1024]{1,0:T(8,128)(2,1)S(1)} %add_convert_fusion.own), channel_id=1, source_target_pairs={{0,32},{1,97},{2,34},{3,99},{4,36},{5,101},{6,38},{7,103},{8,40},{... | collective-permute-start | bytes 1572872 | tf_op jit(solution)/shard_map/ppermute | solution.py:56
  35.9 13.6 %collective-permute-start.9 = (bf16[256,1024]{1,0:T(8,128)(2,1)S(1)}, bf16[256,1024]{1,0:T(8,128)(2,1)S(1)}, u32[]{:S(2)}, u32[]{:S(2)}) collective-permute-start(bf16[256,1024]{1,0:T(8,128)(2,1)S(1)} %add_convert_fusion.own), channel_id=1, source_target_pairs={{0,96},{1,33},{2,98},{3,35},{4,100},{5,37},{6,102},{7,39},{8,104},... | collective-permute-start | bytes 1572872 | tf_op jit(solution)/shard_map/ppermute | solution.py:56
  37.8 11.8 %collective-permute-start.10 = (bf16[2,1024,128]{2,1,0:T(8,128)(2,1)S(1)}, bf16[2,1024,128]{2,1,0:T(8,128)(2,1)S(1)}, u32[]{:S(2)}, u32[]{:S(2)}) collective-permute-start(bf16[2,1024,128]{2,1,0:T(8,128)(2,1)S(1)} %slice.6), channel_id=1, source_target_pairs={{0,2},{1,9},{2,4},{3,11},{4,6},{5,13},{6,0},{7,15},{8,10},{9,17},{... | collective-permute-start | bytes 1572872 | tf_op jit(solution)/shard_map/ppermute | solution.py:56
  39.6 9.9 %collective-permute-start.11 = (bf16[2,1024,128]{2,1,0:T(8,128)(2,1)S(1)}, bf16[2,1024,128]{2,1,0:T(8,128)(2,1)S(1)}, u32[]{:S(2)}, u32[]{:S(2)}) collective-permute-start(bf16[2,1024,128]{2,1,0:T(8,128)(2,1)S(1)} %slice.7), channel_id=1, source_target_pairs={{0,6},{1,25},{2,0},{3,27},{4,2},{5,29},{6,4},{7,31},{8,14},{9,1},{... | collective-permute-start | bytes 1572872 | tf_op jit(solution)/shard_map/ppermute | solution.py:56
  49.6 3.1 %collective-permute-start.13 = (bf16[4,1024,128]{2,1,0:T(8,128)(2,1)S(1)}, bf16[4,1024,128]{2,1,0:T(8,128)(2,1)S(1)}, u32[]{:S(2)}, u32[]{:S(2)}) collective-permute-start(bf16[4,1024,128]{2,1,0:T(8,128)(2,1)S(1)} %pad_maximum_fusion.1), channel_id=1, source_target_pairs={{0,1},{1,0},{2,3},{3,2},{4,5},{5,4},{6,7},{7,6},{8,9},{9,8},{10,11... | collective-permute-start | bytes 3145736 | tf_op jit(solution)/shard_map/ppermute | solution.py:56
  50.4 10.4 %collective-permute-start.14 = (bf16[256,1024]{1,0:T(8,128)(2,1)S(1)}, bf16[256,1024]{1,0:T(8,128)(2,1)S(1)}, u32[]{:S(2)}, u32[]{:S(2)}) collective-permute-start(bf16[256,1024]{1,0:T(8,128)(2,1)S(1)} %collective-permute-done.8.secondary), channel_id=1, source_target_pairs={{0,32},{1,97},{2,34},{3,99},{4,36},{5,101},{6,38},{7,103},{8,40},{... | collective-permute-start | bytes 1572872 | tf_op jit(solution)/shard_map/ppermute | solution.py:56
  50.9 10.0 %copy-start = (bf16[1024,1024]{1,0:T(8,128)(2,1)S(1)}, bf16[1024,1024]{1,0:T(8,128)(2,1)}, u32[]{:S(2)}) copy-start(bf16[1024,1024]{1,0:T(8,128)(2,1)} %tests.1) | copy-start | bytes 6291460
  63.6 6.9 %collective-permute-start.15 = (bf16[256,256]{1,0:T(8,128)(2,1)S(1)}, bf16[256,256]{1,0:T(8,128)(2,1)S(1)}, u32[]{:S(2)}, u32[]{:S(2)}) collective-permute-start(bf16[256,256]{1,0:T(8,128)(2,1)S(1)} %get-tuple-element.33), channel_id=1, source_target_pairs={{0,64},{1,65},{2,66},{3,67},{4,68},{5,69},{6,70},{7,71},{8,72},{9,... | collective-permute-start | bytes 393224 | tf_op jit(solution)/shard_map/ppermute | solution.py:56
  64.2 8.2 %collective-permute-start.16 = (bf16[256,256]{1,0:T(8,128)(2,1)S(1)}, bf16[256,256]{1,0:T(8,128)(2,1)S(1)}, u32[]{:S(2)}, u32[]{:S(2)}) collective-permute-start(bf16[256,256]{1,0:T(8,128)(2,1)S(1)} %get-tuple-element.34), channel_id=1, source_target_pairs={{0,32},{1,97},{2,34},{3,99},{4,36},{5,101},{6,38},{7,103},{8,40},{... | collective-permute-start | bytes 393224 | tf_op jit(solution)/shard_map/ppermute | solution.py:56
  64.8 7.6 %collective-permute-start.17 = (bf16[256,256]{1,0:T(8,128)(2,1)S(1)}, bf16[256,256]{1,0:T(8,128)(2,1)S(1)}, u32[]{:S(2)}, u32[]{:S(2)}) collective-permute-start(bf16[256,256]{1,0:T(8,128)(2,1)S(1)} %get-tuple-element.35), channel_id=1, source_target_pairs={{0,96},{1,33},{2,98},{3,35},{4,100},{5,37},{6,102},{7,39},{8,104},... | collective-permute-start | bytes 393224 | tf_op jit(solution)/shard_map/ppermute | solution.py:56

commit v4 on v3

--- a/solution.py
+++ b/solution.py
@@ -19,6 +19,8 @@
 T = 768
 Q = 1024
 W = NS * BLK
+ROW_COST = 10_000_000_000
+PASS_COST = 50_000_000_000
 NX = NY = NZ = 4
 NC = 2
 SMEM = pl.BlockSpec(memory_space=pltpu.SMEM)
@@ -39,8 +41,8 @@
     return pairs
 
 
-PRIMARY = moves(lambda x, y, z, c: (x + 1 - 2 * c, y, z, c))
-SECONDARY = moves(lambda x, y, z, c: (x - 1 + 2 * c, y, z, c))
+PAIR_A = moves(lambda x, y, z, c: (3 - x if c else x ^ 1, y, z, c))
+PAIR_B = moves(lambda x, y, z, c: (x ^ 1 if c else 3 - x, y, z, c))
 OPPOSITE = moves(lambda x, y, z, c: (x + 2, y, z, c))
 SWAP = moves(lambda x, y, z, c: (x, y, z, c + 1))
 FIRST = [moves(lambda x, y, z, c, d=d: (x, y + d * (1 - c), z + d * c, c)) for d in (1, 2, 3)]
@@ -69,11 +71,12 @@
 
 
 def quarter(which, x, c):
-    step = 1 - 2 * c
-    if which == "primary":
-        return (x + step + NX) % NX
-    if which == "secondary":
-        return (x - step + NX) % NX
+    flipped = x + 1 - 2 * (x % 2)
+    mirrored = NX - 1 - x
+    if which == "a":
+        return jnp.where(c == 0, flipped, mirrored)
+    if which == "b":
+        return jnp.where(c == 0, mirrored, flipped)
     if which == "opposite":
         return (x + 2) % NX
     return x
@@ -96,21 +99,30 @@
     return parts
 
 
+def products(where, outs, yt, us, wide, picked, held):
+    for i, q in enumerate(where):
+        wide[i].wait()
+        total = jnp.dot(yt[...], us[i], preferred_element_type=F32)
+        for j, part in enumerate(scaled(total, q, picked, *held)):
+            outs[i][j * BLK : (j + 1) * BLK, :] = part.astype(outs[i].dtype)
+
+
 def start_kernel(lambdas_h, lam_index_h, live_h, sing_h, u, y, *rest):
     out, yt_out, lambdas, lam_index, live, sing, ys, us, sems = rest
     x, _, _, c = place()
-    q = quarter("opposite", x, c)
+    where = [quarter(name, x, c) for name in ("a", "opposite")]
     held = (lambdas, lam_index, live, sing)
     copies = [
         pltpu.make_async_copy(r, h, sems.at[i])
         for i, (r, h) in enumerate(zip((lambdas_h, lam_index_h, live_h, sing_h), held))
     ]
-    for copy in copies:
+    whole = pltpu.make_async_copy(y, ys, sems.at[4])
+    wide = [
+        pltpu.make_async_copy(u.at[:, pl.ds(pl.multiple_of(q * Q, Q), Q)], us.at[i], sems.at[5 + i])
+        for i, q in enumerate(where)
+    ]
+    for copy in copies + [whole] + wide:
         copy.start()
-    wide = pltpu.make_async_copy(u.at[:, pl.ds(pl.multiple_of(q * Q, Q), Q)], us, sems.at[4])
-    whole = pltpu.make_async_copy(y, ys, sems.at[5])
-    whole.start()
-    wide.start()
     for copy in copies:
         copy.wait()
     picked = slots(live)
@@ -118,31 +130,28 @@
     for j, slot in enumerate(picked):
         block = ys[:, pl.ds(pl.multiple_of(slot * BLK, BLK), BLK)]
         yt_out[j * BLK : (j + 1) * BLK, :] = block.T
-    wide.wait()
-    total = jnp.dot(yt_out[...], us[...], preferred_element_type=F32)
-    for j, part in enumerate(scaled(total, q, picked, *held)):
-        out[j * BLK : (j + 1) * BLK, :] = part.astype(out.dtype)
+    products(where, [out.at[0], out.at[1]], yt_out, us, wide, picked, held)
 
 
 def start_call(lambdas, lam_index, live, sing, u, y):
     return pl.pallas_call(
         start_kernel,
-        out_shape=[jax.ShapeDtypeStruct((W, Q), BF16), jax.ShapeDtypeStruct((W, T), BF16)],
+        out_shape=[jax.ShapeDtypeStruct((2, W, Q), BF16), jax.ShapeDtypeStruct((W, T), BF16)],
         in_specs=[HBM] * 6,
         out_specs=[VMEM] * 2,
         scratch_shapes=SMALL
-        + [pltpu.VMEM((T, VD), BF16), pltpu.VMEM((T, Q), BF16), pltpu.SemaphoreType.DMA((6,))],
-        compiler_params=pltpu.CompilerParams(vmem_limit_bytes=8 << 20),
-        cost_estimate=pl.CostEstimate(
-            flops=2 * W * T * Q, bytes_accessed=2 * T * Q, transcendentals=0
+        + [pltpu.VMEM((T, VD), BF16), pltpu.VMEM((2, T, Q), BF16), pltpu.SemaphoreType.DMA((7,))],
+        compiler_params=pltpu.CompilerParams(vmem_limit_bytes=10 << 20),
+        cost_estimate=pl.CostEstimate(
+            flops=4 * W * T * Q, bytes_accessed=4 * T * Q, transcendentals=0
         ),
     )(*pin(lambdas, lam_index, live, sing, u, y))
 
 
 def rest_kernel(lambdas_h, lam_index_h, live_h, sing_h, u, yt, *rest):
-    outs, (lambdas, lam_index, live, sing, us, sems) = rest[:3], rest[3:]
+    outs, (lambdas, lam_index, live, sing, us, sems) = rest[:2], rest[2:]
     x, _, _, c = place()
-    where = [quarter(name, x, c) for name in ("primary", "secondary", "own")]
+    where = [quarter(name, x, c) for name in ("b", "own")]
     held = (lambdas, lam_index, live, sing)
     copies = [
         pltpu.make_async_copy(r, h, sems.at[i])
@@ -156,26 +165,57 @@
         copy.start()
     for copy in copies:
         copy.wait()
-    picked = slots(live)
-    for i, q in enumerate(where):
-        wide[i].wait()
-        total = jnp.dot(yt[...], us[i], preferred_element_type=F32)
-        for j, part in enumerate(scaled(total, q, picked, *held)):
-            outs[i][j * BLK : (j + 1) * BLK, :] = part.astype(outs[i].dtype)
+    products(where, outs, yt, us, wide, slots(live), held)
 
 
 def rest_call(lambdas, lam_index, live, sing, u, yt):
     return pl.pallas_call(
         rest_kernel,
-        out_shape=[jax.ShapeDtypeStruct((W, Q), d) for d in (F32, BF16, F32)],
+        out_shape=[jax.ShapeDtypeStruct((W, Q), F32)] * 2,
         in_specs=[HBM] * 5 + [VMEM],
-        out_specs=[VMEM] * 3,
-        scratch_shapes=SMALL + [pltpu.VMEM((3, T, Q), BF16), pltpu.SemaphoreType.DMA((7,))],
-        compiler_params=pltpu.CompilerParams(vmem_limit_bytes=12 << 20),
-        cost_estimate=pl.CostEstimate(
-            flops=6 * W * T * Q, bytes_accessed=6 * T * Q, transcendentals=0
+        out_specs=[VMEM] * 2,
+        scratch_shapes=SMALL + [pltpu.VMEM((2, T, Q), BF16), pltpu.SemaphoreType.DMA((6,))],
+        compiler_params=pltpu.CompilerParams(vmem_limit_bytes=10 << 20),
+        cost_estimate=pl.CostEstimate(
+            flops=4 * W * T * Q, bytes_accessed=4 * T * Q, transcendentals=0
         ),
     )(*pin(lambdas, lam_index, live, sing, u), yt)
+
+
+def row_kernel(a, b, c, d, out):
+    for i, block in enumerate((a, b, c, d)):
+        out[i] = block[...]
+
+
+def row_call(*blocks):
+    return pl.pallas_call(
+        row_kernel,
+        out_shape=jax.ShapeDtypeStruct((NY, Q, BLK), BF16),
+        in_specs=[VMEM] * 4,
+        out_specs=VMEM,
+        compiler_params=pltpu.CompilerParams(vmem_limit_bytes=2 << 20),
+        cost_estimate=pl.CostEstimate(
+            flops=ROW_COST, bytes_accessed=4 * Q * Q, transcendentals=0
+        ),
+    )(*blocks)
+
+
+def pass_kernel(value, out):
+    pass
+
+
+def pass_call(value):
+    return pl.pallas_call(
+        pass_kernel,
+        out_shape=jax.ShapeDtypeStruct(value.shape, value.dtype),
+        in_specs=[VMEM],
+        out_specs=VMEM,
+        input_output_aliases={0: 0},
+        compiler_params=pltpu.CompilerParams(vmem_limit_bytes=1 << 20),
+        cost_estimate=pl.CostEstimate(
+            flops=PASS_COST, bytes_accessed=4 * Q * Q, transcendentals=0
+        ),
+    )(value)
 
 
 CHUNK = 256
@@ -200,29 +240,26 @@
     return total
 
 
-def three_kernel(shards, own, primary, secondary, out):
+def half_kernel(shards, own, other, out):
     x, _, _, c = place()
-    features = (own, primary, secondary)
     for r in range(Q // CHUNK):
         rows = slice(r * CHUNK, (r + 1) * CHUNK)
-        total = None
-        for i, name in enumerate(("own", "primary", "secondary")):
-            part = multiply(quarter(name, x, c), rows, shards, features[i])
-            total = part if total is None else total + part
-        out[rows, :] = total
-
-
-def three_call(shards, features):
-    return pl.pallas_call(
-        three_kernel,
+        out[rows, :] = multiply(x, rows, shards, own) + multiply(
+            quarter("b", x, c), rows, shards, other
+        )
+
+
+def half_call(shards, own, other):
+    return pl.pallas_call(
+        half_kernel,
         out_shape=jax.ShapeDtypeStruct((Q, W), F32),
-        in_specs=[VMEM] * 4,
+        in_specs=[VMEM] * 3,
         out_specs=VMEM,
         compiler_params=pltpu.CompilerParams(vmem_limit_bytes=8 << 20),
         cost_estimate=pl.CostEstimate(
-            flops=2 * W * 3 * Q * Q, bytes_accessed=2 * Q * 3 * Q, transcendentals=0
-        ),
-    )(shards, *features)
+            flops=2 * W * 2 * Q * Q, bytes_accessed=2 * Q * 2 * Q, transcendentals=0
+        ),
+    )(shards, own, other)
 
 
 def spread(out, rows, values, live):
@@ -235,22 +272,24 @@
 
 
 def last_kernel(live_h, shards, features, so_far, tests, *rest):
-    weights, mine, primary, secondary, opposite, live, packed, sem = rest
+    weights, mine, to_a, to_b, opposite, live, packed, sem = rest
     copy = pltpu.make_async_copy(live_h, live, sem)
     copy.start()
     x, _, _, c = place()
-    q = quarter("opposite", x, c)
     copy.wait()
     for r in range(Q // CHUNK):
         rows = slice(r * CHUNK, (r + 1) * CHUNK)
-        total = (so_far[rows, :] + multiply(q, rows, shards, features)).astype(BF16)
+        total = so_far[rows, :]
+        for i, name in enumerate(("a", "opposite")):
+            total = total + multiply(quarter(name, x, c), rows, shards, features.at[i])
+        total = total.astype(BF16)
         packed[rows, :] = total
         spread(weights, rows, total, live)
     count = TEST // NX
     for name, out in (
         ("opposite", opposite),
-        ("primary", primary),
-        ("secondary", secondary),
+        ("a", to_a),
+        ("b", to_b),
         ("own", mine),
     ):
         q = quarter(name, x, c)
@@ -305,38 +344,29 @@
 def body(u_train, y_train, sing, lambdas, lam_index, live, v_basis, x_test):
     sing = sing.reshape(1, F)
     small = (lambdas, lam_index, live, sing)
-    p_opposite, yt = start_call(*small, u_train, y_train)
-    come = send(p_opposite, PRIMARY)
-    p_primary, p_secondary, p_own = rest_call(*small, u_train, yt)
-    v_basis, _ = lax.optimization_barrier((v_basis, yt))
+    p_send, yt = start_call(*small, u_train, y_train)
+    come = send(p_send, PAIR_A)
+    p_b, p_own = rest_call(*small, u_train, yt)
     near = [send(v_basis, pairs) for pairs in FIRST]
-    row = jnp.stack([v_basis, *near])
+    row = row_call(v_basis, *near)
     below = send(row, UP)
     above = send(row, DOWN)
-    onward = (p_primary + come.astype(F32)).astype(BF16)
-    from_secondary = send(onward, PRIMARY)
-    from_primary = send(p_secondary, SECONDARY)
-    filtered = (p_own + from_secondary.astype(F32) + from_primary.astype(F32)).astype(BF16)
-    f_secondary = send(filtered, PRIMARY)
-    f_primary = send(filtered, SECONDARY)
-    below, above, _ = lax.optimization_barrier((below, above, filtered))
+    from_b = send((p_b + come[1].astype(F32)).astype(BF16), PAIR_B)
+    filtered = (p_own + come[0].astype(F32) + from_b.astype(F32)).astype(BF16)
+    f_b = send(filtered, PAIR_B)
+    below, above, f_b = lax.optimization_barrier((below, above, f_b))
+    f_far = pass_call(send(jnp.stack([filtered, f_b]), PAIR_A))
     far_a = send(below[:2], UP)
     far_b = send(above[2:], DOWN)
     early = jnp.concatenate([row, below, above])
     early_other = send(early, SWAP)
-    f_secondary, f_primary, far_a, far_b = lax.optimization_barrier(
-        (f_secondary, f_primary, far_a, far_b)
-    )
-    f_opposite = send(f_secondary, PRIMARY)
     late = jnp.concatenate([far_a, far_b])
     late_other = send(late, SWAP)
     shards = jnp.concatenate([early, late, early_other, late_other])
-    so_far = three_call(shards, (filtered, f_primary, f_secondary))
-    weights, mine, primary, secondary, opposite = last_call(
-        live, shards, f_opposite, so_far, x_test
-    )
+    so_far = half_call(shards, filtered, f_b)
+    weights, mine, to_a, to_b, opposite = last_call(live, shards, f_far, so_far, x_test)
     predictions = end_call(
-        live, mine, send(opposite, OPPOSITE), send(primary, PRIMARY), send(secondary, SECONDARY)
+        live, mine, send(opposite, OPPOSITE), send(to_a, PAIR_A), send(to_b, PAIR_B)
     )
     return weights, predictions
 

time: 74.3 us -> 71.6 us (0.964)
  waiting for transfers between devices: 32.2 us -> 30.9 us
  starting transfers between devices: 26.9 us -> 26.1 us
    ppermute x18 -> x16, waiting for transfers between devices: 32.2 us -> 30.9 us  [send(): return lax.ppermute(value, ('tm', 'vox'), pairs)]
    ppermute x18 -> x16, starting transfers between devices: 26.9 us -> 26.1 us  [send(): return lax.ppermute(value, ('tm', 'vox'), pairs)]
    pallas_call x3 -> x5, Pallas kernels: 7.31 us -> 6.84 us  [the longest x1 2.87 us: start_call(): pl.pallas_call(start_kernel, out_shape=[jax.ShapeDtypeStruct((2, W, Q), B...]
  transfers between devices with their start and end apart: 18 -> 16, of which waited for: 9 -> 9; matrix products, arithmetic and copies ran while one was open for 2% -> 3% of each run, Pallas kernels for 7% -> 4%
where the time goes in v4:
time: 71.6 us; the launch traced here: 71.4 us
  waiting for transfers between devices  30.9 us (43%)
  starting transfers between devices  26.1 us (36%)
  Pallas kernels  11.5 us (16%)
  local copies, waits for them, and re-layouts  1.12 us (2%)
  other arithmetic  0.96 us (1%)
  between operations  0.83 us (1%)
    ppermute x16, waiting for transfers between devices, send(): return lax.ppermute(value, ('tm', 'vox'), pairs)  30.9 us
    ppermute x16, starting transfers between devices, send(): return lax.ppermute(value, ('tm', 'vox'), pairs)  26.1 us
    pallas_call x1, Pallas kernels, last_call(): pl.pallas_call(last_kernel, out_shape=[jax.ShapeDtypeStruct((Q, VD), BF16...  3.27 us
    pallas_call x1, Pallas kernels, start_call(): pl.pallas_call(start_kernel, out_shape=[jax.ShapeDtypeStruct((2, W, Q), B...  2.87 us
    pallas_call x1, Pallas kernels, rest_call(): pl.pallas_call(rest_kernel, out_shape=[jax.ShapeDtypeStruct((W, Q), F32)]...  2.63 us
  transfers between devices with their start and end apart: 16, of which 9 were waited for; matrix products, arithmetic and copies ran while one was open for 3% of the time, Pallas kernels for 4%

profile of v4, /device:TPU:0, one launch (start us, length us, event | category | flops | bytes accessed | tf_op | source)
XLA Modules:
  0.0 71.4 jit_solution(14097936536179531044)
XLA Ops:
  0.6 0.0 copy-start.1
  0.6 2.9 %shard_map.96 = (bf16[2,256,1024]{2,1,0:T(8,128)(2,1)S(1)}, bf16[256,768]{1,0:T(8,128)(2,1)S(1)}) custom-call(f32[20]{0:T(128)} %lambdas_h.3, s32[3]{0:T(128)} %lam_index_h.3, s32[3]{0:T(128)} %live_h.7, f32[1,4096]{1,0:T(1,128)} %bitcast.15, bf16[768,4096]{1,0:T(8,128)(2,1)} %u.3, bf16[768,384]{1,0:T(8,128)(2,1)} %y.1), custom_call_target="tpu_custom_call" | custom-call | flops 805306368 | bytes 3145728 | tf_op jit(solution)/shard_map/pallas_call | solution.py:137
  3.5 1.7 %collective-permute-start.5 = (bf16[2,256,1024]{2,1,0:T(8,128)(2,1)S(1)}, bf16[2,256,1024]{2,1,0:T(8,128)(2,1)S(1)}, u32[]{:S(2)}, u32[]{:S(2)}) collective-permute-start(bf16[2,256,1024]{2,1,0:T(8,128)(2,1)S(1)} %get-tuple-element.16), channel_id=1, source_target_pairs={{0,32},{1,97},{2,34},{3,99},{4,36},{5,101},{6,38},{7,103},{8,40},{... | collective-permute-start | bytes 3145736 | tf_op jit(solution)/shard_map/ppermute | solution.py:58
  5.2 1.6 %collective-permute-start = (bf16[1024,128]{1,0:T(8,128)(2,1)}, bf16[1024,128]{1,0:T(8,128)(2,1)S(1)}, u32[]{:S(2)}, u32[]{:S(2)}) collective-permute-start(bf16[1024,128]{1,0:T(8,128)(2,1)} %a.1), channel_id=1, source_target_pairs={{0,8},{1,3},{2,10},{3,5},{4,12},{5,7},{6,14},{7,1},{8,16},{9,11},{... | collective-permute-start | bytes 786440 | tf_op jit(solution)/shard_map/ppermute | solution.py:58
  6.7 2.9 %collective-permute-start.1 = (bf16[1024,128]{1,0:T(8,128)(2,1)}, bf16[1024,128]{1,0:T(8,128)(2,1)S(1)}, u32[]{:S(2)}, u32[]{:S(2)}) collective-permute-start(bf16[1024,128]{1,0:T(8,128)(2,1)} %a.1), channel_id=1, source_target_pairs={{0,16},{1,5},{2,18},{3,7},{4,20},{5,1},{6,22},{7,3},{8,24},{9,13},... | collective-permute-start | bytes 786440 | tf_op jit(solution)/shard_map/ppermute | solution.py:58
  9.7 1.3 %collective-permute-start.2 = (bf16[1024,128]{1,0:T(8,128)(2,1)}, bf16[1024,128]{1,0:T(8,128)(2,1)S(1)}, u32[]{:S(2)}, u32[]{:S(2)}) collective-permute-start(bf16[1024,128]{1,0:T(8,128)(2,1)} %a.1), channel_id=1, source_target_pairs={{0,24},{1,7},{2,26},{3,1},{4,28},{5,3},{6,30},{7,5},{8,0},{9,15},{... | collective-permute-start | bytes 786440 | tf_op jit(solution)/shard_map/ppermute | solution.py:58
  11.0 2.6 %shard_map.97 = (f32[256,1024]{1,0:T(8,128)S(1)}, f32[256,1024]{1,0:T(8,128)S(1)}) custom-call(f32[20]{0:T(128)} %lambdas_h.3, s32[3]{0:T(128)} %lam_index_h.3, s32[3]{0:T(128)} %live_h.7, f32[1,4096]{1,0:T(1,128)} %bitcast.16, bf16[768,4096]{1,0:T(8,128)(2,1)} %u.3, bf16[256,768]{1,0:T(8,128)(2,1)S(1)} %get-tuple-element.14.yt), custom_call_target="tpu_custom_call" | custom-call | flops 805306368 | bytes 3145728 | tf_op jit(solution)/shard_map/pallas_call | solution.py:172
  13.6 4.8 %collective-permute-done.5 = bf16[2,256,1024]{2,1,0:T(8,128)(2,1)S(1)} collective-permute-done((bf16[2,256,1024]{2,1,0:T(8,128)(2,1)S(1)}, bf16[2,256,1024]{2,1,0:T(8,128)(2,1)S(1)}, u32[]{:S(2)}, u32[]{:S(2)}) %collective-permute-start.5) | collective-permute-done | bytes 1048608 | tf_op jit(solution)/shard_map/ppermute | solution.py:58
  18.4 0.1 fusion
  18.5 2.9 %collective-permute-start.6 = (bf16[256,1024]{1,0:T(8,128)(2,1)S(1)}, bf16[256,1024]{1,0:T(8,128)(2,1)S(1)}, u32[]{:S(2)}, u32[]{:S(2)}) collective-permute-start(bf16[256,1024]{1,0:T(8,128)(2,1)S(1)} %fusion), channel_id=1, source_target_pairs={{0,96},{1,33},{2,98},{3,35},{4,100},{5,37},{6,102},{7,39},{8,104},... | collective-permute-start | bytes 1572872 | tf_op jit(solution)/shard_map/ppermute | solution.py:58
  21.5 0.0 collective-permute-done.b
  21.5 0.0 collective-permute-done.1.c
  21.5 0.0 collective-permute-done.2.d
  21.5 0.0 copy-done.1
  21.5 0.1 shard_map.95
  21.6 2.0 %collective-permute-start.3 = (bf16[4,1024,128]{2,1,0:T(8,128)(2,1)S(1)}, bf16[4,1024,128]{2,1,0:T(8,128)(2,1)S(1)}, u32[]{:S(2)}, u32[]{:S(2)}) collective-permute-start(bf16[4,1024,128]{2,1,0:T(8,128)(2,1)S(1)} %shard_map.95), channel_id=1, source_target_pairs={{0,2},{1,9},{2,4},{3,11},{4,6},{5,13},{6,0},{7,15},{8,10},{9,17},{... | collective-permute-start | bytes 3145736 | tf_op jit(solution)/shard_map/ppermute | solution.py:58
  23.6 2.2 %collective-permute-start.4 = (bf16[4,1024,128]{2,1,0:T(8,128)(2,1)S(1)}, bf16[4,1024,128]{2,1,0:T(8,128)(2,1)S(1)}, u32[]{:S(2)}, u32[]{:S(2)}) collective-permute-start(bf16[4,1024,128]{2,1,0:T(8,128)(2,1)S(1)} %shard_map.95), channel_id=1, source_target_pairs={{0,6},{1,25},{2,0},{3,27},{4,2},{5,29},{6,4},{7,31},{8,14},{9,1},{... | collective-permute-start | bytes 3145736 | tf_op jit(solution)/shard_map/ppermute | solution.py:58
  25.8 3.3 %collective-permute-done.6 = bf16[256,1024]{1,0:T(8,128)(2,1)S(1)} collective-permute-done((bf16[256,1024]{1,0:T(8,128)(2,1)S(1)}, bf16[256,1024]{1,0:T(8,128)(2,1)S(1)}, u32[]{:S(2)}, u32[]{:S(2)}) %collective-permute-start.6) | collective-permute-done | bytes 524320 | tf_op jit(solution)/shard_map/ppermute | solution.py:58
  29.0 0.2 fusion.2.own
  29.3 2.9 %collective-permute-start.7 = (bf16[256,1024]{1,0:T(8,128)(2,1)S(1)}, bf16[256,1024]{1,0:T(8,128)(2,1)S(1)}, u32[]{:S(2)}, u32[]{:S(2)}) collective-permute-start(bf16[256,1024]{1,0:T(8,128)(2,1)S(1)} %fusion.2.own), channel_id=1, source_target_pairs={{0,96},{1,33},{2,98},{3,35},{4,100},{5,37},{6,102},{7,39},{8,104},... | collective-permute-start | bytes 1572872 | tf_op jit(solution)/shard_map/ppermute | solution.py:58
  32.2 6.3 %collective-permute-done.3 = bf16[4,1024,128]{2,1,0:T(8,128)(2,1)S(1)} collective-permute-done((bf16[4,1024,128]{2,1,0:T(8,128)(2,1)S(1)}, bf16[4,1024,128]{2,1,0:T(8,128)(2,1)S(1)}, u32[]{:S(2)}, u32[]{:S(2)}) %collective-permute-start.3) | collective-permute-done | bytes 1048608 | tf_op jit(solution)/shard_map/ppermute | solution.py:58
  38.5 0.0 collective-permute-done.4
  38.5 1.6 %collective-permute-done.7.other = bf16[256,1024]{1,0:T(8,128)(2,1)S(1)} collective-permute-done((bf16[256,1024]{1,0:T(8,128)(2,1)S(1)}, bf16[256,1024]{1,0:T(8,128)(2,1)S(1)}, u32[]{:S(2)}, u32[]{:S(2)}) %collective-permute-start.7) | collective-permute-done | bytes 524320 | tf_op jit(solution)/shard_map/ppermute | solution.py:58
  40.0 0.1 pad_maximum_fusion.2
  40.1 0.1 collective-permute-start.12
  40.3 2.0 %collective-permute-start.8 = (bf16[2,1024,128]{2,1,0:T(8,128)(2,1)S(1)}, bf16[2,1024,128]{2,1,0:T(8,128)(2,1)S(1)}, u32[]{:S(2)}, u32[]{:S(2)}) collective-permute-start(bf16[2,1024,128]{2,1,0:T(8,128)(2,1)S(1)} %slice.14), channel_id=1, source_target_pairs={{0,2},{1,9},{2,4},{3,11},{4,6},{5,13},{6,0},{7,15},{8,10},{9,17},{... | collective-permute-start | bytes 1572872 | tf_op jit(solution)/shard_map/ppermute | solution.py:58
  42.3 2.2 %collective-permute-start.9 = (bf16[2,1024,128]{2,1,0:T(8,128)(2,1)S(1)}, bf16[2,1024,128]{2,1,0:T(8,128)(2,1)S(1)}, u32[]{:S(2)}, u32[]{:S(2)}) collective-permute-start(bf16[2,1024,128]{2,1,0:T(8,128)(2,1)S(1)} %slice.15), channel_id=1, source_target_pairs={{0,6},{1,25},{2,0},{3,27},{4,2},{5,29},{6,4},{7,31},{8,14},{9,1},{... | collective-permute-start | bytes 1572872 | tf_op jit(solution)/shard_map/ppermute | solution.py:58
  44.5 0.1 constant_dynamic-update-slice_fusion.6
  44.5 0.4 pad_maximum_fusion
  44.9 0.1 collective-permute-start.10
  45.0 0.1 constant_dynamic-update-slice_fusion.5
  45.2 0.1 constant_dynamic-update-slice_fusion.4
  45.3 6.2 %collective-permute-done.8 = bf16[2,1024,128]{2,1,0:T(8,128)(2,1)S(1)} collective-permute-done((bf16[2,1024,128]{2,1,0:T(8,128)(2,1)S(1)}, bf16[2,1024,128]{2,1,0:T(8,128)(2,1)S(1)}, u32[]{:S(2)}, u32[]{:S(2)}) %collective-permute-start.8) | collective-permute-done | bytes 524320 | tf_op jit(solution)/shard_map/ppermute | solution.py:58
  51.5 0.0 collective-permute-done.9
  51.5 0.1 pad_maximum_fusion.1
  51.6 0.1 collective-permute-start.11
  51.7 0.1 constant_dynamic-update-slice_fusion.3
  51.8 0.1 constant_dynamic-update-slice_fusion.2
  51.9 3.1 %collective-permute-done.12.value = bf16[2,256,1024]{2,1,0:T(8,128)(2,1)S(1)} collective-permute-done((bf16[2,256,1024]{2,1,0:T(8,128)(2,1)S(1)}, bf16[2,256,1024]{2,1,0:T(8,128)(2,1)S(1)}, u32[]{:S(2)}, u32[]{:S(2)}) %collective-permute-start.12) | collective-permute-done | bytes 1048608 | tf_op jit(solution)/shard_map/ppermute | solution.py:58
  55.0 0.0 copy-start
  55.0 0.0 collective-permute-done.10
  55.0 0.4 constant_dynamic-update-slice_fusion.1
  55.4 0.0 collective-permute-done.11
  55.4 0.1 constant_dynamic-update-slice_fusion.shards
  55.6 1.3 %shard_map.99.so_far = f32[1024,256]{1,0:T(8,128)S(1)} custom-call(bf16[32,1024,128]{2,1,0:T(8,128)(2,1)S(1)} %constant_dynamic-update-slice_fusion.shards, bf16[256,1024]{1,0:T(8,128)(2,1)S(1)} %fusion.2.own, bf16[256,1024]{1,0:T(8,128)(2,1)S(1)} %collective-permute-done.7.other), custom_call_target="tpu_custom_call" | custom-call | flops 1073741824 | bytes 4194304 | tf_op jit(solution)/shard_map/pallas_call | solution.py:253
  56.9 0.0 copy-done
  56.9 3.3 %shard_map.100 = (bf16[1024,384]{1,0:T(8,128)(2,1)}, f32[256,256]{1,0:T(8,128)S(1)}, bf16[256,256]{1,0:T(8,128)(2,1)S(1)}, bf16[256,256]{1,0:T(8,128)(2,1)S(1)}, bf16[256,256]{1,0:T(8,128)(2,1)S(1)}) custom-call(s32[3]{0:T(128)} %live_h.7, bf16[32,1024,128]{2,1,0:T(8,128)(2,1)S(1)} %constant_dynamic-update-slice_fusion.shards, ...), custom_call_target="tpu_custom_call" | custom-call | flops 1073741824 | bytes 4194304 | tf_op jit(solution)/shard_map/pallas_call | solution.py:302
  60.2 3.2 %collective-permute-start.13 = (bf16[256,256]{1,0:T(8,128)(2,1)S(1)}, bf16[256,256]{1,0:T(8,128)(2,1)S(1)}, u32[]{:S(2)}, u32[]{:S(2)}) collective-permute-start(bf16[256,256]{1,0:T(8,128)(2,1)S(1)} %get-tuple-element.23), channel_id=1, source_target_pairs={{0,64},{1,65},{2,66},{3,67},{4,68},{5,69},{6,70},{7,71},{8,72},{9,... | collective-permute-start | bytes 393224 | tf_op jit(solution)/shard_map/ppermute | solution.py:58
  63.3 0.5 collective-permute-start.14
  63.8 0.5 collective-permute-start.15
  64.3 2.9 %collective-permute-done.13.a = bf16[256,256]{1,0:T(8,128)(2,1)S(1)} collective-permute-done((bf16[256,256]{1,0:T(8,128)(2,1)S(1)}, bf16[256,256]{1,0:T(8,128)(2,1)S(1)}, u32[]{:S(2)}, u32[]{:S(2)}) %collective-permute-start.13) | collective-permute-done | bytes 131104 | tf_op jit(solution)/shard_map/ppermute | solution.py:58
  67.2 2.4 %collective-permute-done.14.b = bf16[256,256]{1,0:T(8,128)(2,1)S(1)} collective-permute-done((bf16[256,256]{1,0:T(8,128)(2,1)S(1)}, bf16[256,256]{1,0:T(8,128)(2,1)S(1)}, u32[]{:S(2)}, u32[]{:S(2)}) %collective-permute-start.14) | collective-permute-done | bytes 131104 | tf_op jit(solution)/shard_map/ppermute | solution.py:58
  69.6 0.4 collective-permute-done.15.c
  70.0 1.4 %shard_map.101 = bf16[256,384]{1,0:T(8,128)(2,1)} custom-call(s32[3]{0:T(128)} %live_h.7, f32[256,256]{1,0:T(8,128)S(1)} %get-tuple-element.22.mine, bf16[256,256]{1,0:T(8,128)(2,1)S(1)} %collective-permute-done.13.a, bf16[256,256]{1,0:T(8,128)(2,1)S(1)} %collective-permute-done.14.b, bf16[256,256]{1,0:T(8,128)(2,1)S(1)} %collective-permute-done.15.c), custom_call_target="tpu_custom_call" | custom-call | tf_op jit(solution)/shard_map/pallas_call | solution.py:334
  (3 shorter events, 0.1 us)
Async XLA Ops:
  0.6 20.9 %copy-start.1 = (bf16[1024,128]{1,0:T(8,128)(2,1)S(1)}, bf16[1024,128]{1,0:T(8,128)(2,1)}, u32[]{:S(2)}) copy-start(bf16[1024,128]{1,0:T(8,128)(2,1)} %a.1) | copy-start | bytes 786436
  3.5 14.9 %collective-permute-start.5 = (bf16[2,256,1024]{2,1,0:T(8,128)(2,1)S(1)}, bf16[2,256,1024]{2,1,0:T(8,128)(2,1)S(1)}, u32[]{:S(2)}, u32[]{:S(2)}) collective-permute-start(bf16[2,256,1024]{2,1,0:T(8,128)(2,1)S(1)} %get-tuple-element.16), channel_id=1, source_target_pairs={{0,32},{1,97},{2,34},{3,99},{4,36},{5,101},{6,38},{7,103},{8,40},{... | collective-permute-start | bytes 3145736 | tf_op jit(solution)/shard_map/ppermute | solution.py:58
  5.2 16.3 %collective-permute-start = (bf16[1024,128]{1,0:T(8,128)(2,1)}, bf16[1024,128]{1,0:T(8,128)(2,1)S(1)}, u32[]{:S(2)}, u32[]{:S(2)}) collective-permute-start(bf16[1024,128]{1,0:T(8,128)(2,1)} %a.1), channel_id=1, source_target_pairs={{0,8},{1,3},{2,10},{3,5},{4,12},{5,7},{6,14},{7,1},{8,16},{9,11},{... | collective-permute-start | bytes 786440 | tf_op jit(solution)/shard_map/ppermute | solution.py:58
  6.7 14.7 %collective-permute-start.1 = (bf16[1024,128]{1,0:T(8,128)(2,1)}, bf16[1024,128]{1,0:T(8,128)(2,1)S(1)}, u32[]{:S(2)}, u32[]{:S(2)}) collective-permute-start(bf16[1024,128]{1,0:T(8,128)(2,1)} %a.1), channel_id=1, source_target_pairs={{0,16},{1,5},{2,18},{3,7},{4,20},{5,1},{6,22},{7,3},{8,24},{9,13},... | collective-permute-start | bytes 786440 | tf_op jit(solution)/shard_map/ppermute | solution.py:58
  9.7 11.8 %collective-permute-start.2 = (bf16[1024,128]{1,0:T(8,128)(2,1)}, bf16[1024,128]{1,0:T(8,128)(2,1)S(1)}, u32[]{:S(2)}, u32[]{:S(2)}) collective-permute-start(bf16[1024,128]{1,0:T(8,128)(2,1)} %a.1), channel_id=1, source_target_pairs={{0,24},{1,7},{2,26},{3,1},{4,28},{5,3},{6,30},{7,5},{8,0},{9,15},{... | collective-permute-start | bytes 786440 | tf_op jit(solution)/shard_map/ppermute | solution.py:58
  18.5 10.5 %collective-permute-start.6 = (bf16[256,1024]{1,0:T(8,128)(2,1)S(1)}, bf16[256,1024]{1,0:T(8,128)(2,1)S(1)}, u32[]{:S(2)}, u32[]{:S(2)}) collective-permute-start(bf16[256,1024]{1,0:T(8,128)(2,1)S(1)} %fusion), channel_id=1, source_target_pairs={{0,96},{1,33},{2,98},{3,35},{4,100},{5,37},{6,102},{7,39},{8,104},... | collective-permute-start | bytes 1572872 | tf_op jit(solution)/shard_map/ppermute | solution.py:58
  21.6 16.9 %collective-permute-start.3 = (bf16[4,1024,128]{2,1,0:T(8,128)(2,1)S(1)}, bf16[4,1024,128]{2,1,0:T(8,128)(2,1)S(1)}, u32[]{:S(2)}, u32[]{:S(2)}) collective-permute-start(bf16[4,1024,128]{2,1,0:T(8,128)(2,1)S(1)} %shard_map.95), channel_id=1, source_target_pairs={{0,2},{1,9},{2,4},{3,11},{4,6},{5,13},{6,0},{7,15},{8,10},{9,17},{... | collective-permute-start | bytes 3145736 | tf_op jit(solution)/shard_map/ppermute | solution.py:58
  23.6 14.9 %collective-permute-start.4 = (bf16[4,1024,128]{2,1,0:T(8,128)(2,1)S(1)}, bf16[4,1024,128]{2,1,0:T(8,128)(2,1)S(1)}, u32[]{:S(2)}, u32[]{:S(2)}) collective-permute-start(bf16[4,1024,128]{2,1,0:T(8,128)(2,1)S(1)} %shard_map.95), channel_id=1, source_target_pairs={{0,6},{1,25},{2,0},{3,27},{4,2},{5,29},{6,4},{7,31},{8,14},{9,1},{... | collective-permute-start | bytes 3145736 | tf_op jit(solution)/shard_map/ppermute | solution.py:58
  29.3 10.8 %collective-permute-start.7 = (bf16[256,1024]{1,0:T(8,128)(2,1)S(1)}, bf16[256,1024]{1,0:T(8,128)(2,1)S(1)}, u32[]{:S(2)}, u32[]{:S(2)}) collective-permute-start(bf16[256,1024]{1,0:T(8,128)(2,1)S(1)} %fusion.2.own), channel_id=1, source_target_pairs={{0,96},{1,33},{2,98},{3,35},{4,100},{5,37},{6,102},{7,39},{8,104},... | collective-permute-start | bytes 1572872 | tf_op jit(solution)/shard_map/ppermute | solution.py:58
  40.1 14.9 %collective-permute-start.12 = (bf16[2,256,1024]{2,1,0:T(8,128)(2,1)S(1)}, bf16[2,256,1024]{2,1,0:T(8,128)(2,1)S(1)}, u32[]{:S(2)}, u32[]{:S(2)}) collective-permute-start(bf16[2,256,1024]{2,1,0:T(8,128)(2,1)S(1)} %pad_maximum_fusion.2), channel_id=1, source_target_pairs={{0,32},{1,97},{2,34},{3,99},{4,36},{5,101},{6,38},{7,103},{8,40},{... | collective-permute-start | bytes 3145736 | tf_op jit(solution)/shard_map/ppermute | solution.py:58
  40.3 11.2 %collective-permute-start.8 = (bf16[2,1024,128]{2,1,0:T(8,128)(2,1)S(1)}, bf16[2,1024,128]{2,1,0:T(8,128)(2,1)S(1)}, u32[]{:S(2)}, u32[]{:S(2)}) collective-permute-start(bf16[2,1024,128]{2,1,0:T(8,128)(2,1)S(1)} %slice.14), channel_id=1, source_target_pairs={{0,2},{1,9},{2,4},{3,11},{4,6},{5,13},{6,0},{7,15},{8,10},{9,17},{... | collective-permute-start | bytes 1572872 | tf_op jit(solution)/shard_map/ppermute | solution.py:58
  42.3 9.3 %collective-permute-start.9 = (bf16[2,1024,128]{2,1,0:T(8,128)(2,1)S(1)}, bf16[2,1024,128]{2,1,0:T(8,128)(2,1)S(1)}, u32[]{:S(2)}, u32[]{:S(2)}) collective-permute-start(bf16[2,1024,128]{2,1,0:T(8,128)(2,1)S(1)} %slice.15), channel_id=1, source_target_pairs={{0,6},{1,25},{2,0},{3,27},{4,2},{5,29},{6,4},{7,31},{8,14},{9,1},{... | collective-permute-start | bytes 1572872 | tf_op jit(solution)/shard_map/ppermute | solution.py:58
  44.9 10.1 %collective-permute-start.10 = (bf16[12,1024,128]{2,1,0:T(8,128)(2,1)S(1)}, bf16[12,1024,128]{2,1,0:T(8,128)(2,1)S(1)}, u32[]{:S(2)}, u32[]{:S(2)}) collective-permute-start(bf16[12,1024,128]{2,1,0:T(8,128)(2,1)S(1)} %pad_maximum_fusion), channel_id=1, source_target_pairs={{0,1},{1,0},{2,3},{3,2},{4,5},{5,4},{6,7},{7,6},{8,9},{9,8},{10,11... | collective-permute-start | bytes 9437192 | tf_op jit(solution)/shard_map/ppermute | solution.py:58
  51.6 3.8 %collective-permute-start.11 = (bf16[4,1024,128]{2,1,0:T(8,128)(2,1)S(1)}, bf16[4,1024,128]{2,1,0:T(8,128)(2,1)S(1)}, u32[]{:S(2)}, u32[]{:S(2)}) collective-permute-start(bf16[4,1024,128]{2,1,0:T(8,128)(2,1)S(1)} %pad_maximum_fusion.1), channel_id=1, source_target_pairs={{0,1},{1,0},{2,3},{3,2},{4,5},{5,4},{6,7},{7,6},{8,9},{9,8},{10,11... | collective-permute-start | bytes 3145736 | tf_op jit(solution)/shard_map/ppermute | solution.py:58
  55.0 1.9 %copy-start = (bf16[1024,1024]{1,0:T(8,128)(2,1)S(1)}, bf16[1024,1024]{1,0:T(8,128)(2,1)}, u32[]{:S(2)}) copy-start(bf16[1024,1024]{1,0:T(8,128)(2,1)} %tests.1) | copy-start | bytes 6291460
  60.2 7.0 %collective-permute-start.13 = (bf16[256,256]{1,0:T(8,128)(2,1)S(1)}, bf16[256,256]{1,0:T(8,128)(2,1)S(1)}, u32[]{:S(2)}, u32[]{:S(2)}) collective-permute-start(bf16[256,256]{1,0:T(8,128)(2,1)S(1)} %get-tuple-element.23), channel_id=1, source_target_pairs={{0,64},{1,65},{2,66},{3,67},{4,68},{5,69},{6,70},{7,71},{8,72},{9,... | collective-permute-start | bytes 393224 | tf_op jit(solution)/shard_map/ppermute | solution.py:58
  63.3 6.2 %collective-permute-start.14 = (bf16[256,256]{1,0:T(8,128)(2,1)S(1)}, bf16[256,256]{1,0:T(8,128)(2,1)S(1)}, u32[]{:S(2)}, u32[]{:S(2)}) collective-permute-start(bf16[256,256]{1,0:T(8,128)(2,1)S(1)} %get-tuple-element.24), channel_id=1, source_target_pairs={{0,32},{1,97},{2,34},{3,99},{4,36},{5,101},{6,38},{7,103},{8,40},{... | collective-permute-start | bytes 393224 | tf_op jit(solution)/shard_map/ppermute | solution.py:58
  63.8 6.2 %collective-permute-start.15 = (bf16[256,256]{1,0:T(8,128)(2,1)S(1)}, bf16[256,256]{1,0:T(8,128)(2,1)S(1)}, u32[]{:S(2)}, u32[]{:S(2)}) collective-permute-start(bf16[256,256]{1,0:T(8,128)(2,1)S(1)} %get-tuple-element.25), channel_id=1, source_target_pairs={{0,96},{1,33},{2,98},{3,35},{4,100},{5,37},{6,102},{7,39},{8,104},... | collective-permute-start | bytes 393224 | tf_op jit(solution)/shard_map/ppermute | solution.py:58

commit v5 on v4

--- a/solution.py
+++ b/solution.py
@@ -21,6 +21,7 @@
 W = NS * BLK
 ROW_COST = 10_000_000_000
 PASS_COST = 50_000_000_000
+LITTLE_COST = 500_000_000
 NX = NY = NZ = 4
 NC = 2
 SMEM = pl.BlockSpec(memory_space=pltpu.SMEM)
@@ -58,6 +59,10 @@
     return lax.ppermute(value, ("tm", "vox"), pairs)
 
 
+def after(value, other):
+    return lax.optimization_barrier((value, other))[0]
+
+
 def place():
     x = lax.axis_index("tm")
     v = lax.axis_index("vox")
@@ -104,11 +109,11 @@
         wide[i].wait()
         total = jnp.dot(yt[...], us[i], preferred_element_type=F32)
         for j, part in enumerate(scaled(total, q, picked, *held)):
-            outs[i][j * BLK : (j + 1) * BLK, :] = part.astype(outs[i].dtype)
+            outs[i][j][...] = part.astype(outs[i][j].dtype)
 
 
 def start_kernel(lambdas_h, lam_index_h, live_h, sing_h, u, y, *rest):
-    out, yt_out, lambdas, lam_index, live, sing, ys, us, sems = rest
+    out_0, out_1, yt_out, lambdas, lam_index, live, sing, ys, us, sems = rest
     x, _, _, c = place()
     where = [quarter(name, x, c) for name in ("a", "opposite")]
     held = (lambdas, lam_index, live, sing)
@@ -130,15 +135,17 @@
     for j, slot in enumerate(picked):
         block = ys[:, pl.ds(pl.multiple_of(slot * BLK, BLK), BLK)]
         yt_out[j * BLK : (j + 1) * BLK, :] = block.T
-    products(where, [out.at[0], out.at[1]], yt_out, us, wide, picked, held)
+    outs = [[out_0.at[i], out_1.at[i]] for i in range(2)]
+    products(where, outs, yt_out, us, wide, picked, held)
 
 
 def start_call(lambdas, lam_index, live, sing, u, y):
     return pl.pallas_call(
         start_kernel,
-        out_shape=[jax.ShapeDtypeStruct((2, W, Q), BF16), jax.ShapeDtypeStruct((W, T), BF16)],
+        out_shape=[jax.ShapeDtypeStruct((2, BLK, Q), BF16)] * 2
+        + [jax.ShapeDtypeStruct((W, T), BF16)],
         in_specs=[HBM] * 6,
-        out_specs=[VMEM] * 2,
+        out_specs=[VMEM] * 3,
         scratch_shapes=SMALL
         + [pltpu.VMEM((T, VD), BF16), pltpu.VMEM((2, T, Q), BF16), pltpu.SemaphoreType.DMA((7,))],
         compiler_params=pltpu.CompilerParams(vmem_limit_bytes=10 << 20),
@@ -149,7 +156,7 @@
 
 
 def rest_kernel(lambdas_h, lam_index_h, live_h, sing_h, u, yt, *rest):
-    outs, (lambdas, lam_index, live, sing, us, sems) = rest[:2], rest[2:]
+    outs, (lambdas, lam_index, live, sing, us, sems) = rest[:4], rest[4:]
     x, _, _, c = place()
     where = [quarter(name, x, c) for name in ("b", "own")]
     held = (lambdas, lam_index, live, sing)
@@ -165,15 +172,15 @@
         copy.start()
     for copy in copies:
         copy.wait()
-    products(where, outs, yt, us, wide, slots(live), held)
+    products(where, [outs[:2], outs[2:]], yt, us, wide, slots(live), held)
 
 
 def rest_call(lambdas, lam_index, live, sing, u, yt):
     return pl.pallas_call(
         rest_kernel,
-        out_shape=[jax.ShapeDtypeStruct((W, Q), F32)] * 2,
+        out_shape=[jax.ShapeDtypeStruct((BLK, Q), F32)] * 4,
         in_specs=[HBM] * 5 + [VMEM],
-        out_specs=[VMEM] * 2,
+        out_specs=[VMEM] * 4,
         scratch_shapes=SMALL + [pltpu.VMEM((2, T, Q), BF16), pltpu.SemaphoreType.DMA((6,))],
         compiler_params=pltpu.CompilerParams(vmem_limit_bytes=10 << 20),
         cost_estimate=pl.CostEstimate(
@@ -200,22 +207,21 @@
     )(*blocks)
 
 
-def pass_kernel(value, out):
+def pass_kernel(*refs):
     pass
 
 
-def pass_call(value):
+def pass_call(cost, *values):
+    n = len(values)
     return pl.pallas_call(
         pass_kernel,
-        out_shape=jax.ShapeDtypeStruct(value.shape, value.dtype),
-        in_specs=[VMEM],
-        out_specs=VMEM,
-        input_output_aliases={0: 0},
+        out_shape=[jax.ShapeDtypeStruct(v.shape, v.dtype) for v in values],
+        in_specs=[VMEM] * n,
+        out_specs=[VMEM] * n,
+        input_output_aliases={i: i for i in range(n)},
         compiler_params=pltpu.CompilerParams(vmem_limit_bytes=1 << 20),
-        cost_estimate=pl.CostEstimate(
-            flops=PASS_COST, bytes_accessed=4 * Q * Q, transcendentals=0
-        ),
-    )(value)
+        cost_estimate=pl.CostEstimate(flops=cost, bytes_accessed=1 << 20, transcendentals=0),
+    )(*values)
 
 
 CHUNK = 256
@@ -234,32 +240,33 @@
         first = c * NY * NZ + block_of(deep) * NY + back
         second = (1 - c) * NY * NZ + block_of(back) * NZ + deep
         left = jnp.concatenate([shards[first, rows, :], shards[second, rows, :]], axis=1)
-        right = features[:, z * NC * BLK : (z + 1) * NC * BLK]
+        columns = slice(z * NC * BLK, (z + 1) * NC * BLK)
+        right = jnp.concatenate([f[:, columns] for f in features], axis=0)
         part = lax.dot_general(left, right, (((1,), (1,)), ((), ())), preferred_element_type=F32)
         total = part if total is None else total + part
     return total
 
 
-def half_kernel(shards, own, other, out):
+def half_kernel(shards, own_0, own_1, other_0, other_1, out):
     x, _, _, c = place()
     for r in range(Q // CHUNK):
         rows = slice(r * CHUNK, (r + 1) * CHUNK)
-        out[rows, :] = multiply(x, rows, shards, own) + multiply(
-            quarter("b", x, c), rows, shards, other
+        out[rows, :] = multiply(x, rows, shards, (own_0, own_1)) + multiply(
+            quarter("b", x, c), rows, shards, (other_0, other_1)
         )
 
 
-def half_call(shards, own, other):
+def half_call(shards, *features):
     return pl.pallas_call(
         half_kernel,
         out_shape=jax.ShapeDtypeStruct((Q, W), F32),
-        in_specs=[VMEM] * 3,
+        in_specs=[VMEM] * 5,
         out_specs=VMEM,
         compiler_params=pltpu.CompilerParams(vmem_limit_bytes=8 << 20),
         cost_estimate=pl.CostEstimate(
             flops=2 * W * 2 * Q * Q, bytes_accessed=2 * Q * 2 * Q, transcendentals=0
         ),
-    )(shards, own, other)
+    )(shards, *features)
 
 
 def spread(out, rows, values, live):
@@ -271,7 +278,7 @@
         out[rows, b * BLK : (b + 1) * BLK] = block.astype(out.dtype)
 
 
-def last_kernel(live_h, shards, features, so_far, tests, *rest):
+def last_kernel(live_h, shards, far_0, far_1, so_far, tests, *rest):
     weights, mine, to_a, to_b, opposite, live, packed, sem = rest
     copy = pltpu.make_async_copy(live_h, live, sem)
     copy.start()
@@ -281,7 +288,9 @@
         rows = slice(r * CHUNK, (r + 1) * CHUNK)
         total = so_far[rows, :]
         for i, name in enumerate(("a", "opposite")):
-            total = total + multiply(quarter(name, x, c), rows, shards, features.at[i])
+            total = total + multiply(
+                quarter(name, x, c), rows, shards, (far_0.at[i], far_1.at[i])
+            )
         total = total.astype(BF16)
         packed[rows, :] = total
         spread(weights, rows, total, live)
@@ -297,7 +306,7 @@
         out[...] = jnp.dot(part, packed[...], preferred_element_type=F32).astype(out.dtype)
 
 
-def last_call(live, shards, features, so_far, tests):
+def last_call(live, shards, far, so_far, tests):
     rows = TEST // NX
     return pl.pallas_call(
         last_kernel,
@@ -308,7 +317,7 @@
             jax.ShapeDtypeStruct((rows, W), BF16),
             jax.ShapeDtypeStruct((rows, W), BF16),
         ],
-        in_specs=[HBM] + [VMEM] * 4,
+        in_specs=[HBM] + [VMEM] * 5,
         out_specs=[VMEM] * 5,
         scratch_shapes=[
             pltpu.SMEM((NB,), jnp.int32),
@@ -319,7 +328,7 @@
         cost_estimate=pl.CostEstimate(
             flops=4 * W * Q * Q, bytes_accessed=4 * Q * Q, transcendentals=0
         ),
-    )(*pin(live), shards, features, so_far, tests)
+    )(*pin(live), shards, *far, so_far, tests)
 
 
 def end_kernel(live_h, mine, a, b, c, out, live, sem):
@@ -344,18 +353,27 @@
 def body(u_train, y_train, sing, lambdas, lam_index, live, v_basis, x_test):
     sing = sing.reshape(1, F)
     small = (lambdas, lam_index, live, sing)
-    p_send, yt = start_call(*small, u_train, y_train)
-    come = send(p_send, PAIR_A)
-    p_b, p_own = rest_call(*small, u_train, yt)
+    *p_send, yt = start_call(*small, u_train, y_train)
+    come = [send(p, PAIR_A) for p in p_send]
+    v_basis = after(v_basis, yt)
     near = [send(v_basis, pairs) for pairs in FIRST]
+    p_b0, p_b1, p_own0, p_own1 = rest_call(*small, u_train, yt)
     row = row_call(v_basis, *near)
     below = send(row, UP)
     above = send(row, DOWN)
-    from_b = send((p_b + come[1].astype(F32)).astype(BF16), PAIR_B)
-    filtered = (p_own + come[0].astype(F32) + from_b.astype(F32)).astype(BF16)
-    f_b = send(filtered, PAIR_B)
-    below, above, f_b = lax.optimization_barrier((below, above, f_b))
-    f_far = pass_call(send(jnp.stack([filtered, f_b]), PAIR_A))
+    sum_0 = (p_b0 + come[0][1].astype(F32)).astype(BF16)
+    come[1] = after(come[1], sum_0)
+    sum_1 = (p_b1 + come[1][1].astype(F32)).astype(BF16)
+    from_0, from_1 = send(sum_0, PAIR_B), send(sum_1, PAIR_B)
+    own_0 = (p_own0 + come[0][0].astype(F32) + from_0.astype(F32)).astype(BF16)
+    from_1 = after(from_1, own_0)
+    own_1 = (p_own1 + come[1][0].astype(F32) + from_1.astype(F32)).astype(BF16)
+    other_0, other_1 = send(own_0, PAIR_B), send(own_1, PAIR_B)
+    both_0 = jnp.stack([own_0, other_0])
+    both_1 = jnp.stack([own_1, after(other_1, both_0)])
+    (far_0,) = pass_call(LITTLE_COST, send(both_0, PAIR_A))
+    far = pass_call(PASS_COST, far_0, send(both_1, PAIR_A))
+    below, above = after((below, above), both_1)
     far_a = send(below[:2], UP)
     far_b = send(above[2:], DOWN)
     early = jnp.concatenate([row, below, above])
@@ -363,8 +381,8 @@
     late = jnp.concatenate([far_a, far_b])
     late_other = send(late, SWAP)
     shards = jnp.concatenate([early, late, early_other, late_other])
-    so_far = half_call(shards, filtered, f_b)
-    weights, mine, to_a, to_b, opposite = last_call(live, shards, f_far, so_far, x_test)
+    so_far = half_call(shards, own_0, own_1, other_0, other_1)
+    weights, mine, to_a, to_b, opposite = last_call(live, shards, far, so_far, x_test)
     predictions = end_call(
         live, mine, send(opposite, OPPOSITE), send(to_a, PAIR_A), send(to_b, PAIR_B)
     )

time: 71.6 us -> 74.1 us (1.035)
  starting transfers between devices: 26.1 us -> 30.6 us
  waiting for transfers between devices: 30.9 us -> 28.7 us
    ppermute x16 -> x20, starting transfers between devices: 26.1 us -> 30.6 us  [send(): return lax.ppermute(value, ('tm', 'vox'), pairs)]
    ppermute x16 -> x20, waiting for transfers between devices: 30.9 us -> 28.7 us  [send(): return lax.ppermute(value, ('tm', 'vox'), pairs)]
    pallas_call x3 -> x4, Pallas kernels: 5.5 us -> 5.5 us  [the longest x1 2.87 us: start_call(): pl.pallas_call(start_kernel, out_shape=[jax.ShapeDtypeStruct((2, BLK, Q),...]
  transfers between devices with their start and end apart: 16 -> 20, of which waited for: 9 -> 8; matrix products, arithmetic and copies ran while one was open for 3% -> 3% of each run, Pallas kernels for 4% -> 4%
where the time goes in v5:
time: 74.1 us; the launch traced here: 73.8 us
  starting transfers between devices  30.6 us (41%)
  waiting for transfers between devices  28.7 us (39%)
  Pallas kernels  11.5 us (16%)
  local copies, waits for them, and re-layouts  1.12 us (2%)
  between operations  0.92 us (1%)
  other arithmetic  0.88 us (1%)
    ppermute x20, starting transfers between devices, send(): return lax.ppermute(value, ('tm', 'vox'), pairs)  30.6 us
    ppermute x20, waiting for transfers between devices, send(): return lax.ppermute(value, ('tm', 'vox'), pairs)  28.7 us
    pallas_call x1, Pallas kernels, last_call(): pl.pallas_call(last_kernel, out_shape=[jax.ShapeDtypeStruct((Q, VD), BF16...  3.28 us
    pallas_call x1, Pallas kernels, start_call(): pl.pallas_call(start_kernel, out_shape=[jax.ShapeDtypeStruct((2, BLK, Q),...  2.87 us
    pallas_call x1, Pallas kernels, rest_call(): pl.pallas_call(rest_kernel, out_shape=[jax.ShapeDtypeStruct((BLK, Q), F32...  2.63 us
  transfers between devices with their start and end apart: 20, of which 8 were waited for; matrix products, arithmetic and copies ran while one was open for 3% of the time, Pallas kernels for 4%

profile of v5, /device:TPU:0, one launch (start us, length us, event | category | flops | bytes accessed | tf_op | source)
XLA Modules:
  0.0 73.8 jit_solution(10919986824726012769)
XLA Ops:
  0.6 0.0 copy-start.1
  0.6 2.9 %shard_map.95 = (bf16[2,128,1024]{2,1,0:T(8,128)(2,1)S(1)}, bf16[2,128,1024]{2,1,0:T(8,128)(2,1)S(1)}, bf16[256,768]{1,0:T(8,128)(2,1)S(1)}) custom-call(f32[20]{0:T(128)} %lambdas_h.3, s32[3]{0:T(128)} %lam_index_h.3, s32[3]{0:T(128)} %live_h.7, f32[1,4096]{1,0:T(1,128)} %bitcast.25, bf16[768,4096]{1,0:T(8,128)(2,1)} %u.3, bf16[768,384]{1,0:T(8,128)(2,1)} %y.1), custom_call_target="tpu_custom_call" | custom-call | flops 805306368 | bytes 3145728 | tf_op jit(solution)/shard_map/pallas_call | solution.py:143
  3.5 1.7 %collective-permute-start.6 = (bf16[2,128,1024]{2,1,0:T(8,128)(2,1)S(1)}, bf16[2,128,1024]{2,1,0:T(8,128)(2,1)S(1)}, u32[]{:S(2)}, u32[]{:S(2)}) collective-permute-start(bf16[2,128,1024]{2,1,0:T(8,128)(2,1)S(1)} %get-tuple-element.27), channel_id=1, source_target_pairs={{0,32},{1,97},{2,34},{3,99},{4,36},{5,101},{6,38},{7,103},{8,40},{... | collective-permute-start | bytes 1572872 | tf_op jit(solution)/shard_map/ppermute | solution.py:59
  5.2 1.6 %collective-permute-start = (bf16[1024,128]{1,0:T(8,128)(2,1)}, bf16[1024,128]{1,0:T(8,128)(2,1)S(1)}, u32[]{:S(2)}, u32[]{:S(2)}) collective-permute-start(bf16[1024,128]{1,0:T(8,128)(2,1)} %a), channel_id=1, source_target_pairs={{0,8},{1,3},{2,10},{3,5},{4,12},{5,7},{6,14},{7,1},{8,16},{9,11},{... | collective-permute-start | bytes 786440 | tf_op jit(solution)/shard_map/ppermute | solution.py:59
  6.7 2.9 %collective-permute-start.1 = (bf16[1024,128]{1,0:T(8,128)(2,1)}, bf16[1024,128]{1,0:T(8,128)(2,1)S(1)}, u32[]{:S(2)}, u32[]{:S(2)}) collective-permute-start(bf16[1024,128]{1,0:T(8,128)(2,1)} %a), channel_id=1, source_target_pairs={{0,16},{1,5},{2,18},{3,7},{4,20},{5,1},{6,22},{7,3},{8,24},{9,13},... | collective-permute-start | bytes 786440 | tf_op jit(solution)/shard_map/ppermute | solution.py:59
  9.7 1.3 %collective-permute-start.2 = (bf16[1024,128]{1,0:T(8,128)(2,1)}, bf16[1024,128]{1,0:T(8,128)(2,1)S(1)}, u32[]{:S(2)}, u32[]{:S(2)}) collective-permute-start(bf16[1024,128]{1,0:T(8,128)(2,1)} %a), channel_id=1, source_target_pairs={{0,24},{1,7},{2,26},{3,1},{4,28},{5,3},{6,30},{7,5},{8,0},{9,15},{... | collective-permute-start | bytes 786440 | tf_op jit(solution)/shard_map/ppermute | solution.py:59
  11.0 0.5 collective-permute-start.5
  11.5 2.6 %shard_map.97 = (f32[128,1024]{1,0:T(8,128)S(1)}, f32[128,1024]{1,0:T(8,128)S(1)}, f32[128,1024]{1,0:T(8,128)S(1)}, f32[128,1024]{1,0:T(8,128)S(1)}) custom-call(f32[20]{0:T(128)} %lambdas_h.3, s32[3]{0:T(128)} %lam_index_h.3, s32[3]{0:T(128)} %live_h.7, f32[1,4096]{1,0:T(1,128)} %bitcast.26, bf16[768,4096]{1,0:T(8,128)(2,1)} %u.3, ...), custom_call_target="tpu_custom_call" | custom-call | flops 805306368 | bytes 3145728 | tf_op jit(solution)/shard_map/pallas_call | solution.py:179
  14.2 0.0 collective-permute-done.6
  14.2 0.1 fusion.5
  14.2 2.8 %collective-permute-start.8 = (bf16[128,1024]{1,0:T(8,128)(2,1)S(1)}, bf16[128,1024]{1,0:T(8,128)(2,1)S(1)}, u32[]{:S(2)}, u32[]{:S(2)}) collective-permute-start(bf16[128,1024]{1,0:T(8,128)(2,1)S(1)} %fusion.5), channel_id=1, source_target_pairs={{0,96},{1,33},{2,98},{3,35},{4,100},{5,37},{6,102},{7,39},{8,104},... | collective-permute-start | bytes 786440 | tf_op jit(solution)/shard_map/ppermute | solution.py:59
  17.1 0.0 collective-permute-done.b
  17.1 0.0 collective-permute-done.1.c
  17.1 0.0 collective-permute-done.2.d
  17.1 0.0 copy-done.1
  17.1 0.1 shard_map.96
  17.2 2.0 %collective-permute-start.3 = (bf16[4,1024,128]{2,1,0:T(8,128)(2,1)S(1)}, bf16[4,1024,128]{2,1,0:T(8,128)(2,1)S(1)}, u32[]{:S(2)}, u32[]{:S(2)}) collective-permute-start(bf16[4,1024,128]{2,1,0:T(8,128)(2,1)S(1)} %shard_map.96), channel_id=1, source_target_pairs={{0,2},{1,9},{2,4},{3,11},{4,6},{5,13},{6,0},{7,15},{8,10},{9,17},{... | collective-permute-start | bytes 3145736 | tf_op jit(solution)/shard_map/ppermute | solution.py:59
  19.2 2.2 %collective-permute-start.4 = (bf16[4,1024,128]{2,1,0:T(8,128)(2,1)S(1)}, bf16[4,1024,128]{2,1,0:T(8,128)(2,1)S(1)}, u32[]{:S(2)}, u32[]{:S(2)}) collective-permute-start(bf16[4,1024,128]{2,1,0:T(8,128)(2,1)S(1)} %shard_map.96), channel_id=1, source_target_pairs={{0,6},{1,25},{2,0},{3,27},{4,2},{5,29},{6,4},{7,31},{8,14},{9,1},{... | collective-permute-start | bytes 3145736 | tf_op jit(solution)/shard_map/ppermute | solution.py:59
  21.4 1.6 %collective-permute-done.5 = bf16[2,128,1024]{2,1,0:T(8,128)(2,1)S(1)} collective-permute-done((bf16[2,128,1024]{2,1,0:T(8,128)(2,1)S(1)}, bf16[2,128,1024]{2,1,0:T(8,128)(2,1)S(1)}, u32[]{:S(2)}, u32[]{:S(2)}) %collective-permute-start.5) | collective-permute-done | bytes 524320 | tf_op jit(solution)/shard_map/ppermute | solution.py:59
  23.0 0.1 fusion.2
  23.1 1.6 %collective-permute-start.7 = (bf16[128,1024]{1,0:T(8,128)(2,1)S(1)}, bf16[128,1024]{1,0:T(8,128)(2,1)S(1)}, u32[]{:S(2)}, u32[]{:S(2)}) collective-permute-start(bf16[128,1024]{1,0:T(8,128)(2,1)S(1)} %fusion.2), channel_id=1, source_target_pairs={{0,96},{1,33},{2,98},{3,35},{4,100},{5,37},{6,102},{7,39},{8,104},... | collective-permute-start | bytes 786440 | tf_op jit(solution)/shard_map/ppermute | solution.py:59
  24.6 0.0 collective-permute-done.8
  24.6 0.1 fusion.1.own_0
  24.7 1.8 %collective-permute-start.10 = (bf16[128,1024]{1,0:T(8,128)(2,1)S(1)}, bf16[128,1024]{1,0:T(8,128)(2,1)S(1)}, u32[]{:S(2)}, u32[]{:S(2)}) collective-permute-start(bf16[128,1024]{1,0:T(8,128)(2,1)S(1)} %fusion.1.own_0), channel_id=1, source_target_pairs={{0,96},{1,33},{2,98},{3,35},{4,100},{5,37},{6,102},{7,39},{8,104},... | collective-permute-start | bytes 786440 | tf_op jit(solution)/shard_map/ppermute | solution.py:59
  26.6 4.2 %collective-permute-done.7 = bf16[128,1024]{1,0:T(8,128)(2,1)S(1)} collective-permute-done((bf16[128,1024]{1,0:T(8,128)(2,1)S(1)}, bf16[128,1024]{1,0:T(8,128)(2,1)S(1)}, u32[]{:S(2)}, u32[]{:S(2)}) %collective-permute-start.7) | collective-permute-done | bytes 262176 | tf_op jit(solution)/shard_map/ppermute | solution.py:59
  30.7 0.1 fusion.4.own_1
  30.8 1.6 %collective-permute-start.9 = (bf16[128,1024]{1,0:T(8,128)(2,1)S(1)}, bf16[128,1024]{1,0:T(8,128)(2,1)S(1)}, u32[]{:S(2)}, u32[]{:S(2)}) collective-permute-start(bf16[128,1024]{1,0:T(8,128)(2,1)S(1)} %fusion.4.own_1), channel_id=1, source_target_pairs={{0,96},{1,33},{2,98},{3,35},{4,100},{5,37},{6,102},{7,39},{8,104},... | collective-permute-start | bytes 786440 | tf_op jit(solution)/shard_map/ppermute | solution.py:59
  32.4 0.1 constant_dynamic-update-slice_fusion.6
  32.5 1.1 %collective-permute-done.10.other_0 = bf16[128,1024]{1,0:T(8,128)(2,1)S(1)} collective-permute-done((bf16[128,1024]{1,0:T(8,128)(2,1)S(1)}, bf16[128,1024]{1,0:T(8,128)(2,1)S(1)}, u32[]{:S(2)}, u32[]{:S(2)}) %collective-permute-start.10) | collective-permute-done | bytes 262176 | tf_op jit(solution)/shard_map/ppermute | solution.py:59
  33.5 0.1 pad_maximum_fusion.2
  33.6 0.1 collective-permute-start.15
  33.7 7.6 %collective-permute-done.9.other_1 = bf16[128,1024]{1,0:T(8,128)(2,1)S(1)} collective-permute-done((bf16[128,1024]{1,0:T(8,128)(2,1)S(1)}, bf16[128,1024]{1,0:T(8,128)(2,1)S(1)}, u32[]{:S(2)}, u32[]{:S(2)}) %collective-permute-start.9) | collective-permute-done | bytes 262176 | tf_op jit(solution)/shard_map/ppermute | solution.py:59
  41.3 0.1 pad_maximum_fusion.3
  41.4 0.1 collective-permute-start.16
  41.4 0.0 collective-permute-done.3
  41.5 0.0 collective-permute-done.4
  41.5 2.1 %collective-permute-start.11 = (bf16[2,1024,128]{2,1,0:T(8,128)(2,1)S(1)}, bf16[2,1024,128]{2,1,0:T(8,128)(2,1)S(1)}, u32[]{:S(2)}, u32[]{:S(2)}) collective-permute-start(bf16[2,1024,128]{2,1,0:T(8,128)(2,1)S(1)} %slice.22), channel_id=1, source_target_pairs={{0,2},{1,9},{2,4},{3,11},{4,6},{5,13},{6,0},{7,15},{8,10},{9,17},{... | collective-permute-start | bytes 1572872 | tf_op jit(solution)/shard_map/ppermute | solution.py:59
  43.6 4.0 %collective-permute-start.12 = (bf16[2,1024,128]{2,1,0:T(8,128)(2,1)S(1)}, bf16[2,1024,128]{2,1,0:T(8,128)(2,1)S(1)}, u32[]{:S(2)}, u32[]{:S(2)}) collective-permute-start(bf16[2,1024,128]{2,1,0:T(8,128)(2,1)S(1)} %slice.23), channel_id=1, source_target_pairs={{0,6},{1,25},{2,0},{3,27},{4,2},{5,29},{6,4},{7,31},{8,14},{9,1},{... | collective-permute-start | bytes 1572872 | tf_op jit(solution)/shard_map/ppermute | solution.py:59
  47.6 0.4 pad_maximum_fusion
  48.0 0.1 collective-permute-start.13
  48.1 0.1 constant_dynamic-update-slice_fusion.5
  48.3 0.1 constant_dynamic-update-slice_fusion.4
  48.4 0.0 collective-permute-done.15.refs_0_
  48.4 6.3 %collective-permute-done.11 = bf16[2,1024,128]{2,1,0:T(8,128)(2,1)S(1)} collective-permute-done((bf16[2,1024,128]{2,1,0:T(8,128)(2,1)S(1)}, bf16[2,1024,128]{2,1,0:T(8,128)(2,1)S(1)}, u32[]{:S(2)}, u32[]{:S(2)}) %collective-permute-start.11) | collective-permute-done | bytes 524320 | tf_op jit(solution)/shard_map/ppermute | solution.py:59
  54.7 0.0 collective-permute-done.12
  54.7 0.1 pad_maximum_fusion.1
  54.8 0.1 collective-permute-start.14
  54.9 0.0 collective-permute-done.16.refs_1_
  54.9 0.1 constant_dynamic-update-slice_fusion.3
  55.0 0.1 constant_dynamic-update-slice_fusion.2
  55.0 0.0 copy-start
  55.1 0.0 collective-permute-done.13
  55.1 0.4 constant_dynamic-update-slice_fusion.1
  55.5 2.0 %collective-permute-done.14 = bf16[4,1024,128]{2,1,0:T(8,128)(2,1)S(1)} collective-permute-done((bf16[4,1024,128]{2,1,0:T(8,128)(2,1)S(1)}, bf16[4,1024,128]{2,1,0:T(8,128)(2,1)S(1)}, u32[]{:S(2)}, u32[]{:S(2)}) %collective-permute-start.14) | collective-permute-done | bytes 1048608 | tf_op jit(solution)/shard_map/ppermute | solution.py:59
  57.5 0.1 constant_dynamic-update-slice_fusion.shards
  57.7 1.3 %shard_map.100.so_far = f32[1024,256]{1,0:T(8,128)S(1)} custom-call(bf16[32,1024,128]{2,1,0:T(8,128)(2,1)S(1)} %constant_dynamic-update-slice_fusion.shards, bf16[128,1024]{1,0:T(8,128)(2,1)S(1)} %fusion.1.own_0, bf16[128,1024]{1,0:T(8,128)(2,1)S(1)} %fusion.4.own_1, bf16[128,1024]{1,0:T(8,128)(2,1)S(1)} %collective-permute-done.10.other_0, ...), custom_call_target="tpu_custom_call" | custom-call | flops 1073741824 | bytes 4194304 | tf_op jit(solution)/shard_map/pallas_call | solution.py:260
  58.9 3.3 %shard_map.101 = (bf16[1024,384]{1,0:T(8,128)(2,1)}, f32[256,256]{1,0:T(8,128)S(1)}, bf16[256,256]{1,0:T(8,128)(2,1)S(1)}, bf16[256,256]{1,0:T(8,128)(2,1)S(1)}, bf16[256,256]{1,0:T(8,128)(2,1)S(1)}) custom-call(s32[3]{0:T(128)} %live_h.7, bf16[32,1024,128]{2,1,0:T(8,128)(2,1)S(1)} %constant_dynamic-update-slice_fusion.shards, ...), custom_call_target="tpu_custom_call" | custom-call | flops 1073741824 | bytes 4194304 | tf_op jit(solution)/shard_map/pallas_call | solution.py:311
  62.2 2.9 %collective-permute-start.17 = (bf16[256,256]{1,0:T(8,128)(2,1)S(1)}, bf16[256,256]{1,0:T(8,128)(2,1)S(1)}, u32[]{:S(2)}, u32[]{:S(2)}) collective-permute-start(bf16[256,256]{1,0:T(8,128)(2,1)S(1)} %get-tuple-element.39), channel_id=1, source_target_pairs={{0,64},{1,65},{2,66},{3,67},{4,68},{5,69},{6,70},{7,71},{8,72},{9,... | collective-permute-start | bytes 393224 | tf_op jit(solution)/shard_map/ppermute | solution.py:59
  65.1 0.9 %collective-permute-start.18 = (bf16[256,256]{1,0:T(8,128)(2,1)S(1)}, bf16[256,256]{1,0:T(8,128)(2,1)S(1)}, u32[]{:S(2)}, u32[]{:S(2)}) collective-permute-start(bf16[256,256]{1,0:T(8,128)(2,1)S(1)} %get-tuple-element.40), channel_id=1, source_target_pairs={{0,32},{1,97},{2,34},{3,99},{4,36},{5,101},{6,38},{7,103},{8,40},{... | collective-permute-start | bytes 393224 | tf_op jit(solution)/shard_map/ppermute | solution.py:59
  66.1 0.3 collective-permute-start.19
  66.4 3.0 %collective-permute-done.17.a = bf16[256,256]{1,0:T(8,128)(2,1)S(1)} collective-permute-done((bf16[256,256]{1,0:T(8,128)(2,1)S(1)}, bf16[256,256]{1,0:T(8,128)(2,1)S(1)}, u32[]{:S(2)}, u32[]{:S(2)}) %collective-permute-start.17) | collective-permute-done | bytes 131104 | tf_op jit(solution)/shard_map/ppermute | solution.py:59
  69.4 3.0 %collective-permute-done.18.b = bf16[256,256]{1,0:T(8,128)(2,1)S(1)} collective-permute-done((bf16[256,256]{1,0:T(8,128)(2,1)S(1)}, bf16[256,256]{1,0:T(8,128)(2,1)S(1)}, u32[]{:S(2)}, u32[]{:S(2)}) %collective-permute-start.18) | collective-permute-done | bytes 131104 | tf_op jit(solution)/shard_map/ppermute | solution.py:59
  72.4 0.0 collective-permute-done.19.c
  72.4 1.4 %shard_map.102 = bf16[256,384]{1,0:T(8,128)(2,1)} custom-call(s32[3]{0:T(128)} %live_h.7, f32[256,256]{1,0:T(8,128)S(1)} %get-tuple-element.38.mine, bf16[256,256]{1,0:T(8,128)(2,1)S(1)} %collective-permute-done.17.a, bf16[256,256]{1,0:T(8,128)(2,1)S(1)} %collective-permute-done.18.b, bf16[256,256]{1,0:T(8,128)(2,1)S(1)} %collective-permute-done.19.c), custom_call_target="tpu_custom_call" | custom-call | tf_op jit(solution)/shard_map/pallas_call | solution.py:343
  (5 shorter events, 0.1 us)
Async XLA Ops:
  0.6 16.5 %copy-start.1 = (bf16[1024,128]{1,0:T(8,128)(2,1)S(1)}, bf16[1024,128]{1,0:T(8,128)(2,1)}, u32[]{:S(2)}) copy-start(bf16[1024,128]{1,0:T(8,128)(2,1)} %a) | copy-start | bytes 786436
  3.5 10.7 %collective-permute-start.6 = (bf16[2,128,1024]{2,1,0:T(8,128)(2,1)S(1)}, bf16[2,128,1024]{2,1,0:T(8,128)(2,1)S(1)}, u32[]{:S(2)}, u32[]{:S(2)}) collective-permute-start(bf16[2,128,1024]{2,1,0:T(8,128)(2,1)S(1)} %get-tuple-element.27), channel_id=1, source_target_pairs={{0,32},{1,97},{2,34},{3,99},{4,36},{5,101},{6,38},{7,103},{8,40},{... | collective-permute-start | bytes 1572872 | tf_op jit(solution)/shard_map/ppermute | solution.py:59
  5.2 11.9 %collective-permute-start = (bf16[1024,128]{1,0:T(8,128)(2,1)}, bf16[1024,128]{1,0:T(8,128)(2,1)S(1)}, u32[]{:S(2)}, u32[]{:S(2)}) collective-permute-start(bf16[1024,128]{1,0:T(8,128)(2,1)} %a), channel_id=1, source_target_pairs={{0,8},{1,3},{2,10},{3,5},{4,12},{5,7},{6,14},{7,1},{8,16},{9,11},{... | collective-permute-start | bytes 786440 | tf_op jit(solution)/shard_map/ppermute | solution.py:59
  6.7 10.3 %collective-permute-start.1 = (bf16[1024,128]{1,0:T(8,128)(2,1)}, bf16[1024,128]{1,0:T(8,128)(2,1)S(1)}, u32[]{:S(2)}, u32[]{:S(2)}) collective-permute-start(bf16[1024,128]{1,0:T(8,128)(2,1)} %a), channel_id=1, source_target_pairs={{0,16},{1,5},{2,18},{3,7},{4,20},{5,1},{6,22},{7,3},{8,24},{9,13},... | collective-permute-start | bytes 786440 | tf_op jit(solution)/shard_map/ppermute | solution.py:59
  9.7 7.4 %collective-permute-start.2 = (bf16[1024,128]{1,0:T(8,128)(2,1)}, bf16[1024,128]{1,0:T(8,128)(2,1)S(1)}, u32[]{:S(2)}, u32[]{:S(2)}) collective-permute-start(bf16[1024,128]{1,0:T(8,128)(2,1)} %a), channel_id=1, source_target_pairs={{0,24},{1,7},{2,26},{3,1},{4,28},{5,3},{6,30},{7,5},{8,0},{9,15},{... | collective-permute-start | bytes 786440 | tf_op jit(solution)/shard_map/ppermute | solution.py:59
  11.0 12.0 %collective-permute-start.5 = (bf16[2,128,1024]{2,1,0:T(8,128)(2,1)S(1)}, bf16[2,128,1024]{2,1,0:T(8,128)(2,1)S(1)}, u32[]{:S(2)}, u32[]{:S(2)}) collective-permute-start(bf16[2,128,1024]{2,1,0:T(8,128)(2,1)S(1)} %get-tuple-element.25), channel_id=1, source_target_pairs={{0,32},{1,97},{2,34},{3,99},{4,36},{5,101},{6,38},{7,103},{8,40},{... | collective-permute-start | bytes 1572872 | tf_op jit(solution)/shard_map/ppermute | solution.py:59
  14.2 10.4 %collective-permute-start.8 = (bf16[128,1024]{1,0:T(8,128)(2,1)S(1)}, bf16[128,1024]{1,0:T(8,128)(2,1)S(1)}, u32[]{:S(2)}, u32[]{:S(2)}) collective-permute-start(bf16[128,1024]{1,0:T(8,128)(2,1)S(1)} %fusion.5), channel_id=1, source_target_pairs={{0,96},{1,33},{2,98},{3,35},{4,100},{5,37},{6,102},{7,39},{8,104},... | collective-permute-start | bytes 786440 | tf_op jit(solution)/shard_map/ppermute | solution.py:59
  17.2 24.3 %collective-permute-start.3 = (bf16[4,1024,128]{2,1,0:T(8,128)(2,1)S(1)}, bf16[4,1024,128]{2,1,0:T(8,128)(2,1)S(1)}, u32[]{:S(2)}, u32[]{:S(2)}) collective-permute-start(bf16[4,1024,128]{2,1,0:T(8,128)(2,1)S(1)} %shard_map.96), channel_id=1, source_target_pairs={{0,2},{1,9},{2,4},{3,11},{4,6},{5,13},{6,0},{7,15},{8,10},{9,17},{... | collective-permute-start | bytes 3145736 | tf_op jit(solution)/shard_map/ppermute | solution.py:59
  19.2 22.3 %collective-permute-start.4 = (bf16[4,1024,128]{2,1,0:T(8,128)(2,1)S(1)}, bf16[4,1024,128]{2,1,0:T(8,128)(2,1)S(1)}, u32[]{:S(2)}, u32[]{:S(2)}) collective-permute-start(bf16[4,1024,128]{2,1,0:T(8,128)(2,1)S(1)} %shard_map.96), channel_id=1, source_target_pairs={{0,6},{1,25},{2,0},{3,27},{4,2},{5,29},{6,4},{7,31},{8,14},{9,1},{... | collective-permute-start | bytes 3145736 | tf_op jit(solution)/shard_map/ppermute | solution.py:59
  23.1 7.7 %collective-permute-start.7 = (bf16[128,1024]{1,0:T(8,128)(2,1)S(1)}, bf16[128,1024]{1,0:T(8,128)(2,1)S(1)}, u32[]{:S(2)}, u32[]{:S(2)}) collective-permute-start(bf16[128,1024]{1,0:T(8,128)(2,1)S(1)} %fusion.2), channel_id=1, source_target_pairs={{0,96},{1,33},{2,98},{3,35},{4,100},{5,37},{6,102},{7,39},{8,104},... | collective-permute-start | bytes 786440 | tf_op jit(solution)/shard_map/ppermute | solution.py:59
  24.7 8.8 %collective-permute-start.10 = (bf16[128,1024]{1,0:T(8,128)(2,1)S(1)}, bf16[128,1024]{1,0:T(8,128)(2,1)S(1)}, u32[]{:S(2)}, u32[]{:S(2)}) collective-permute-start(bf16[128,1024]{1,0:T(8,128)(2,1)S(1)} %fusion.1.own_0), channel_id=1, source_target_pairs={{0,96},{1,33},{2,98},{3,35},{4,100},{5,37},{6,102},{7,39},{8,104},... | collective-permute-start | bytes 786440 | tf_op jit(solution)/shard_map/ppermute | solution.py:59
  30.8 10.5 %collective-permute-start.9 = (bf16[128,1024]{1,0:T(8,128)(2,1)S(1)}, bf16[128,1024]{1,0:T(8,128)(2,1)S(1)}, u32[]{:S(2)}, u32[]{:S(2)}) collective-permute-start(bf16[128,1024]{1,0:T(8,128)(2,1)S(1)} %fusion.4.own_1), channel_id=1, source_target_pairs={{0,96},{1,33},{2,98},{3,35},{4,100},{5,37},{6,102},{7,39},{8,104},... | collective-permute-start | bytes 786440 | tf_op jit(solution)/shard_map/ppermute | solution.py:59
  33.6 14.8 %collective-permute-start.15 = (bf16[2,128,1024]{2,1,0:T(8,128)(2,1)S(1)}, bf16[2,128,1024]{2,1,0:T(8,128)(2,1)S(1)}, u32[]{:S(2)}, u32[]{:S(2)}) collective-permute-start(bf16[2,128,1024]{2,1,0:T(8,128)(2,1)S(1)} %pad_maximum_fusion.2), channel_id=1, source_target_pairs={{0,32},{1,97},{2,34},{3,99},{4,36},{5,101},{6,38},{7,103},{8,40},{... | collective-permute-start | bytes 1572872 | tf_op jit(solution)/shard_map/ppermute | solution.py:59
  41.4 13.5 %collective-permute-start.16 = (bf16[2,128,1024]{2,1,0:T(8,128)(2,1)S(1)}, bf16[2,128,1024]{2,1,0:T(8,128)(2,1)S(1)}, u32[]{:S(2)}, u32[]{:S(2)}) collective-permute-start(bf16[2,128,1024]{2,1,0:T(8,128)(2,1)S(1)} %pad_maximum_fusion.3), channel_id=1, source_target_pairs={{0,32},{1,97},{2,34},{3,99},{4,36},{5,101},{6,38},{7,103},{8,40},{... | collective-permute-start | bytes 1572872 | tf_op jit(solution)/shard_map/ppermute | solution.py:59
  41.5 13.2 %collective-permute-start.11 = (bf16[2,1024,128]{2,1,0:T(8,128)(2,1)S(1)}, bf16[2,1024,128]{2,1,0:T(8,128)(2,1)S(1)}, u32[]{:S(2)}, u32[]{:S(2)}) collective-permute-start(bf16[2,1024,128]{2,1,0:T(8,128)(2,1)S(1)} %slice.22), channel_id=1, source_target_pairs={{0,2},{1,9},{2,4},{3,11},{4,6},{5,13},{6,0},{7,15},{8,10},{9,17},{... | collective-permute-start | bytes 1572872 | tf_op jit(solution)/shard_map/ppermute | solution.py:59
  43.6 11.1 %collective-permute-start.12 = (bf16[2,1024,128]{2,1,0:T(8,128)(2,1)S(1)}, bf16[2,1024,128]{2,1,0:T(8,128)(2,1)S(1)}, u32[]{:S(2)}, u32[]{:S(2)}) collective-permute-start(bf16[2,1024,128]{2,1,0:T(8,128)(2,1)S(1)} %slice.23), channel_id=1, source_target_pairs={{0,6},{1,25},{2,0},{3,27},{4,2},{5,29},{6,4},{7,31},{8,14},{9,1},{... | collective-permute-start | bytes 1572872 | tf_op jit(solution)/shard_map/ppermute | solution.py:59
  48.0 7.0 %collective-permute-start.13 = (bf16[12,1024,128]{2,1,0:T(8,128)(2,1)S(1)}, bf16[12,1024,128]{2,1,0:T(8,128)(2,1)S(1)}, u32[]{:S(2)}, u32[]{:S(2)}) collective-permute-start(bf16[12,1024,128]{2,1,0:T(8,128)(2,1)S(1)} %pad_maximum_fusion), channel_id=1, source_target_pairs={{0,1},{1,0},{2,3},{3,2},{4,5},{5,4},{6,7},{7,6},{8,9},{9,8},{10,11... | collective-permute-start | bytes 9437192 | tf_op jit(solution)/shard_map/ppermute | solution.py:59
  54.8 2.7 %collective-permute-start.14 = (bf16[4,1024,128]{2,1,0:T(8,128)(2,1)S(1)}, bf16[4,1024,128]{2,1,0:T(8,128)(2,1)S(1)}, u32[]{:S(2)}, u32[]{:S(2)}) collective-permute-start(bf16[4,1024,128]{2,1,0:T(8,128)(2,1)S(1)} %pad_maximum_fusion.1), channel_id=1, source_target_pairs={{0,1},{1,0},{2,3},{3,2},{4,5},{5,4},{6,7},{7,6},{8,9},{9,8},{10,11... | collective-permute-start | bytes 3145736 | tf_op jit(solution)/shard_map/ppermute | solution.py:59
  55.0 3.9 %copy-start = (bf16[1024,1024]{1,0:T(8,128)(2,1)S(1)}, bf16[1024,1024]{1,0:T(8,128)(2,1)}, u32[]{:S(2)}) copy-start(bf16[1024,1024]{1,0:T(8,128)(2,1)} %tests.1) | copy-start | bytes 6291460
  62.2 7.2 %collective-permute-start.17 = (bf16[256,256]{1,0:T(8,128)(2,1)S(1)}, bf16[256,256]{1,0:T(8,128)(2,1)S(1)}, u32[]{:S(2)}, u32[]{:S(2)}) collective-permute-start(bf16[256,256]{1,0:T(8,128)(2,1)S(1)} %get-tuple-element.39), channel_id=1, source_target_pairs={{0,64},{1,65},{2,66},{3,67},{4,68},{5,69},{6,70},{7,71},{8,72},{9,... | collective-permute-start | bytes 393224 | tf_op jit(solution)/shard_map/ppermute | solution.py:59
  65.1 7.2 %collective-permute-start.18 = (bf16[256,256]{1,0:T(8,128)(2,1)S(1)}, bf16[256,256]{1,0:T(8,128)(2,1)S(1)}, u32[]{:S(2)}, u32[]{:S(2)}) collective-permute-start(bf16[256,256]{1,0:T(8,128)(2,1)S(1)} %get-tuple-element.40), channel_id=1, source_target_pairs={{0,32},{1,97},{2,34},{3,99},{4,36},{5,101},{6,38},{7,103},{8,40},{... | collective-permute-start | bytes 393224 | tf_op jit(solution)/shard_map/ppermute | solution.py:59
  66.1 6.3 %collective-permute-start.19 = (bf16[256,256]{1,0:T(8,128)(2,1)S(1)}, bf16[256,256]{1,0:T(8,128)(2,1)S(1)}, u32[]{:S(2)}, u32[]{:S(2)}) collective-permute-start(bf16[256,256]{1,0:T(8,128)(2,1)S(1)} %get-tuple-element.41), channel_id=1, source_target_pairs={{0,96},{1,33},{2,98},{3,35},{4,100},{5,37},{6,102},{7,39},{8,104},... | collective-permute-start | bytes 393224 | tf_op jit(solution)/shard_map/ppermute | solution.py:59

commit v6 on v5

--- a/solution.py
+++ b/solution.py
@@ -19,9 +19,7 @@
 T = 768
 Q = 1024
 W = NS * BLK
-ROW_COST = 10_000_000_000
-PASS_COST = 50_000_000_000
-LITTLE_COST = 500_000_000
+ROW_COST = 20000_000_000
 NX = NY = NZ = 4
 NC = 2
 SMEM = pl.BlockSpec(memory_space=pltpu.SMEM)
@@ -49,6 +47,9 @@
 FIRST = [moves(lambda x, y, z, c, d=d: (x, y + d * (1 - c), z + d * c, c)) for d in (1, 2, 3)]
 UP = moves(lambda x, y, z, c: (x, y + c, z + 1 - c, c))
 DOWN = moves(lambda x, y, z, c: (x, y - c, z - 1 + c, c))
+
+
+SECOND = [moves(lambda x, y, z, c, d=d: (x, y + d * c, z + d * (1 - c), c)) for d in (1, 3, 2)]
 
 
 def pin(*arrays):
@@ -211,7 +212,7 @@
     pass
 
 
-def pass_call(cost, *values):
+def hold(cost, *values):
     n = len(values)
     return pl.pallas_call(
         pass_kernel,
@@ -264,7 +265,7 @@
         out_specs=VMEM,
         compiler_params=pltpu.CompilerParams(vmem_limit_bytes=8 << 20),
         cost_estimate=pl.CostEstimate(
-            flops=2 * W * 2 * Q * Q, bytes_accessed=2 * Q * 2 * Q, transcendentals=0
+            flops=6000_000_000, bytes_accessed=2 * Q * 2 * Q, transcendentals=0
         ),
     )(shards, *features)
 
@@ -278,12 +279,9 @@
         out[rows, b * BLK : (b + 1) * BLK] = block.astype(out.dtype)
 
 
-def last_kernel(live_h, shards, far_0, far_1, so_far, tests, *rest):
-    weights, mine, to_a, to_b, opposite, live, packed, sem = rest
-    copy = pltpu.make_async_copy(live_h, live, sem)
-    copy.start()
+def last_kernel(shards, far_0, far_1, so_far, tests, *rest):
+    packed, mine, to_a, to_b, opposite = rest
     x, _, _, c = place()
-    copy.wait()
     for r in range(Q // CHUNK):
         rows = slice(r * CHUNK, (r + 1) * CHUNK)
         total = so_far[rows, :]
@@ -293,7 +291,6 @@
             )
         total = total.astype(BF16)
         packed[rows, :] = total
-        spread(weights, rows, total, live)
     count = TEST // NX
     for name, out in (
         ("opposite", opposite),
@@ -306,85 +303,101 @@
         out[...] = jnp.dot(part, packed[...], preferred_element_type=F32).astype(out.dtype)
 
 
-def last_call(live, shards, far, so_far, tests):
+def last_call(shards, far, so_far, tests):
     rows = TEST // NX
     return pl.pallas_call(
         last_kernel,
         out_shape=[
-            jax.ShapeDtypeStruct((Q, VD), BF16),
+            jax.ShapeDtypeStruct((Q, W), BF16),
             jax.ShapeDtypeStruct((rows, W), F32),
             jax.ShapeDtypeStruct((rows, W), BF16),
             jax.ShapeDtypeStruct((rows, W), BF16),
             jax.ShapeDtypeStruct((rows, W), BF16),
         ],
-        in_specs=[HBM] + [VMEM] * 5,
+        in_specs=[VMEM] * 5,
         out_specs=[VMEM] * 5,
-        scratch_shapes=[
-            pltpu.SMEM((NB,), jnp.int32),
-            pltpu.VMEM((Q, W), BF16),
-            pltpu.SemaphoreType.DMA,
-        ],
         compiler_params=pltpu.CompilerParams(vmem_limit_bytes=8 << 20),
         cost_estimate=pl.CostEstimate(
             flops=4 * W * Q * Q, bytes_accessed=4 * Q * Q, transcendentals=0
         ),
-    )(*pin(live), shards, *far, so_far, tests)
-
-
-def end_kernel(live_h, mine, a, b, c, out, live, sem):
+    )(shards, *far, so_far, tests)
+
+
+def spread_kernel(live_h, packed, out, picks, live, sem):
     copy = pltpu.make_async_copy(live_h, live, sem)
     copy.start()
-    total = mine[...] + a[...].astype(F32) + b[...].astype(F32) + c[...].astype(F32)
     copy.wait()
-    spread(out, slice(0, TEST // NX), total, live)
-
-
-def end_call(live, mine, a, b, c):
-    return pl.pallas_call(
-        end_kernel,
-        out_shape=jax.ShapeDtypeStruct((TEST // NX, VD), BF16),
-        in_specs=[HBM] + [VMEM] * 4,
-        out_specs=VMEM,
+    chosen = slots(live)
+    for i, slot in enumerate(chosen):
+        for b in range(NB):
+            here = jnp.where((slot == b) & (live[b] > 0), 1.0, 0.0)
+            picks[i, :, b * BLK : (b + 1) * BLK] = jnp.full((8, BLK), here, F32)
+    for r in range(Q // CHUNK):
+        rows = slice(r * CHUNK, (r + 1) * CHUNK)
+        spread(out, rows, packed[rows, :], live)
+
+
+def spread_call(live, packed):
+    return pl.pallas_call(
+        spread_kernel,
+        out_shape=[
+            jax.ShapeDtypeStruct((Q, VD), BF16),
+            jax.ShapeDtypeStruct((NS, 8, VD), F32),
+        ],
+        in_specs=[HBM, VMEM],
+        out_specs=[VMEM] * 2,
         scratch_shapes=[pltpu.SMEM((NB,), jnp.int32), pltpu.SemaphoreType.DMA],
         compiler_params=pltpu.CompilerParams(vmem_limit_bytes=4 << 20),
-    )(*pin(live), mine, a, b, c)
+        cost_estimate=pl.CostEstimate(
+            flops=1 << 20, bytes_accessed=4 << 20, transcendentals=0
+        ),
+    )(*pin(live), packed)
+
+
+def end_sum(picks, mine, *parts):
+    total = mine
+    for part in parts:
+        total = total + part.astype(F32)
+    left, right = (jnp.concatenate([h] * NB, axis=1) for h in jnp.split(total, 2, axis=1))
+    first, second = (picks[i, :1, :] > 0 for i in range(NS))
+    return jnp.where(first, left, jnp.where(second, right, 0.0)).astype(BF16)
 
 
 def body(u_train, y_train, sing, lambdas, lam_index, live, v_basis, x_test):
     sing = sing.reshape(1, F)
     small = (lambdas, lam_index, live, sing)
     *p_send, yt = start_call(*small, u_train, y_train)
-    come = [send(p, PAIR_A) for p in p_send]
-    v_basis = after(v_basis, yt)
-    near = [send(v_basis, pairs) for pairs in FIRST]
+    come_0, come_1 = [send(p, PAIR_A) for p in p_send]
+    near = [send(after(v_basis, yt), pairs) for pairs in FIRST]
     p_b0, p_b1, p_own0, p_own1 = rest_call(*small, u_train, yt)
     row = row_call(v_basis, *near)
-    below = send(row, UP)
-    above = send(row, DOWN)
-    sum_0 = (p_b0 + come[0][1].astype(F32)).astype(BF16)
-    come[1] = after(come[1], sum_0)
-    sum_1 = (p_b1 + come[1][1].astype(F32)).astype(BF16)
-    from_0, from_1 = send(sum_0, PAIR_B), send(sum_1, PAIR_B)
-    own_0 = (p_own0 + come[0][0].astype(F32) + from_0.astype(F32)).astype(BF16)
-    from_1 = after(from_1, own_0)
-    own_1 = (p_own1 + come[1][0].astype(F32) + from_1.astype(F32)).astype(BF16)
+    come_1 = after(come_1, row)
+    sum_0 = (p_b0 + come_0[1].astype(F32)).astype(BF16)
+    come_1 = after(come_1, sum_0)
+    sum_1 = (p_b1 + come_1[1].astype(F32)).astype(BF16)
+    from_0, from_b = send(sum_0, PAIR_B), send(sum_1, PAIR_B)
+    ahead = [send(row, pairs) for pairs in SECOND]
+    row_other = send(row, SWAP)
+    own_0 = (p_own0 + come_0[0].astype(F32) + from_0.astype(F32)).astype(BF16)
+    from_1 = after(from_b, own_0)
+    own_1 = (p_own1 + come_1[0].astype(F32) + from_1.astype(F32)).astype(BF16)
     other_0, other_1 = send(own_0, PAIR_B), send(own_1, PAIR_B)
     both_0 = jnp.stack([own_0, other_0])
-    both_1 = jnp.stack([own_1, after(other_1, both_0)])
-    (far_0,) = pass_call(LITTLE_COST, send(both_0, PAIR_A))
-    far = pass_call(PASS_COST, far_0, send(both_1, PAIR_A))
-    below, above = after((below, above), both_1)
-    far_a = send(below[:2], UP)
-    far_b = send(above[2:], DOWN)
-    early = jnp.concatenate([row, below, above])
-    early_other = send(early, SWAP)
-    late = jnp.concatenate([far_a, far_b])
-    late_other = send(late, SWAP)
-    shards = jnp.concatenate([early, late, early_other, late_other])
+    other_1 = after(other_1, both_0)
+    both_1 = jnp.stack([own_1, other_1])
+    (far_0,) = hold(500_000_000, send(both_0, PAIR_A))
+    far = hold(100000_000_000, far_0, send(both_1, PAIR_A))
+    pair = jnp.concatenate(after(ahead[:2], both_1))
+    far_row = after(ahead[2], pair)
+    (far_row,) = hold(25000_000_000, far_row)
+    pair_other = send(pair, SWAP)
+    far_other = send(far_row, SWAP)
+    shards = jnp.concatenate([row, pair, far_row, row_other, pair_other, far_other])
     so_far = half_call(shards, own_0, own_1, other_0, other_1)
-    weights, mine, to_a, to_b, opposite = last_call(live, shards, far, so_far, x_test)
-    predictions = end_call(
-        live, mine, send(opposite, OPPOSITE), send(to_a, PAIR_A), send(to_b, PAIR_B)
+    packed, mine, to_a, to_b, opposite = last_call(shards, far, so_far, x_test)
+    weights, picks = spread_call(live, packed)
+    predictions = end_sum(
+        picks, mine, send(opposite, OPPOSITE), send(to_a, PAIR_A), send(to_b, PAIR_B)
     )
     return weights, predictions
 

time: 74.1 us -> 68.8 us (0.928)
  waiting for transfers between devices: 28.7 us -> 22 us
  starting transfers between devices: 30.6 us -> 32 us
  Pallas kernels: 11.5 us -> 10.4 us
    ppermute x20, waiting for transfers between devices: 28.7 us -> 22 us  [send(): return lax.ppermute(value, ('tm', 'vox'), pairs)]
    ppermute x20, starting transfers between devices: 30.6 us -> 32 us  [send(): return lax.ppermute(value, ('tm', 'vox'), pairs)]
    pallas_call x4 -> x5, Pallas kernels: 4.68 us -> 3.53 us  [the longest x1 1.82 us: last_call(): pl.pallas_call(last_kernel, out_shape=[jax.ShapeDtypeStruct((Q, W), BF16)...]
  transfers between devices with their start and end apart: 20 -> 20, of which waited for: 8 -> 9; matrix products, arithmetic and copies ran while one was open for 3% -> 3% of each run, Pallas kernels for 4% -> 6%
where the time goes in v6:
time: 68.8 us; the launch traced here: 68.3 us
  starting transfers between devices  32 us (47%)
  waiting for transfers between devices  22 us (32%)
  Pallas kernels  10.4 us (15%)
  local copies, waits for them, and re-layouts  1.82 us (3%)
  other arithmetic  1.25 us (2%)
  between operations  0.85 us (1%)
    ppermute x20, starting transfers between devices, send(): return lax.ppermute(value, ('tm', 'vox'), pairs)  32 us
    ppermute x20, waiting for transfers between devices, send(): return lax.ppermute(value, ('tm', 'vox'), pairs)  22 us
    pallas_call x1, Pallas kernels, start_call(): pl.pallas_call(start_kernel, out_shape=[jax.ShapeDtypeStruct((2, BLK, Q),...  2.87 us
    pallas_call x1, Pallas kernels, rest_call(): pl.pallas_call(rest_kernel, out_shape=[jax.ShapeDtypeStruct((BLK, Q), F32...  2.63 us
    pallas_call x1, Pallas kernels, last_call(): pl.pallas_call(last_kernel, out_shape=[jax.ShapeDtypeStruct((Q, W), BF16)...  1.82 us
    pallas_call x1, Pallas kernels, spread_call(): pl.pallas_call(spread_kernel, out_shape=[jax.ShapeDtypeStruct((Q, VD), BF...  1.7 us
  transfers between devices with their start and end apart: 20, of which 9 were waited for; matrix products, arithmetic and copies ran while one was open for 3% of the time, Pallas kernels for 6%

profile of v6, /device:TPU:0, one launch (start us, length us, event | category | flops | bytes accessed | tf_op | source)
XLA Modules:
  0.0 68.3 jit_solution(3370386694561030155)
XLA Ops:
  0.6 0.0 copy-start.1
  0.6 2.9 %shard_map.95 = (bf16[2,128,1024]{2,1,0:T(8,128)(2,1)S(1)}, bf16[2,128,1024]{2,1,0:T(8,128)(2,1)S(1)}, bf16[256,768]{1,0:T(8,128)(2,1)S(1)}) custom-call(f32[20]{0:T(128)} %lambdas_h.3, s32[3]{0:T(128)} %lam_index_h.3, s32[3]{0:T(128)} %live_h.5, f32[1,4096]{1,0:T(1,128)} %bitcast.25, bf16[768,4096]{1,0:T(8,128)(2,1)} %u.3, bf16[768,384]{1,0:T(8,128)(2,1)} %y.1), custom_call_target="tpu_custom_call" | custom-call | flops 805306368 | bytes 3145728 | tf_op jit(solution)/shard_map/pallas_call | solution.py:144
  3.5 1.7 %collective-permute-start.6 = (bf16[2,128,1024]{2,1,0:T(8,128)(2,1)S(1)}, bf16[2,128,1024]{2,1,0:T(8,128)(2,1)S(1)}, u32[]{:S(2)}, u32[]{:S(2)}) collective-permute-start(bf16[2,128,1024]{2,1,0:T(8,128)(2,1)S(1)} %get-tuple-element.32), channel_id=1, source_target_pairs={{0,32},{1,97},{2,34},{3,99},{4,36},{5,101},{6,38},{7,103},{8,40},{... | collective-permute-start | bytes 1572872 | tf_op jit(solution)/shard_map/ppermute | solution.py:60
  5.2 1.6 %collective-permute-start = (bf16[1024,128]{1,0:T(8,128)(2,1)}, bf16[1024,128]{1,0:T(8,128)(2,1)S(1)}, u32[]{:S(2)}, u32[]{:S(2)}) collective-permute-start(bf16[1024,128]{1,0:T(8,128)(2,1)} %a.1), channel_id=1, source_target_pairs={{0,8},{1,3},{2,10},{3,5},{4,12},{5,7},{6,14},{7,1},{8,16},{9,11},{... | collective-permute-start | bytes 786440 | tf_op jit(solution)/shard_map/ppermute | solution.py:60
  6.7 2.9 %collective-permute-start.1 = (bf16[1024,128]{1,0:T(8,128)(2,1)}, bf16[1024,128]{1,0:T(8,128)(2,1)S(1)}, u32[]{:S(2)}, u32[]{:S(2)}) collective-permute-start(bf16[1024,128]{1,0:T(8,128)(2,1)} %a.1), channel_id=1, source_target_pairs={{0,16},{1,5},{2,18},{3,7},{4,20},{5,1},{6,22},{7,3},{8,24},{9,13},... | collective-permute-start | bytes 786440 | tf_op jit(solution)/shard_map/ppermute | solution.py:60
  9.7 1.3 %collective-permute-start.2 = (bf16[1024,128]{1,0:T(8,128)(2,1)}, bf16[1024,128]{1,0:T(8,128)(2,1)S(1)}, u32[]{:S(2)}, u32[]{:S(2)}) collective-permute-start(bf16[1024,128]{1,0:T(8,128)(2,1)} %a.1), channel_id=1, source_target_pairs={{0,24},{1,7},{2,26},{3,1},{4,28},{5,3},{6,30},{7,5},{8,0},{9,15},{... | collective-permute-start | bytes 786440 | tf_op jit(solution)/shard_map/ppermute | solution.py:60
  11.0 0.5 collective-permute-start.5
  11.5 2.6 %shard_map.97 = (f32[128,1024]{1,0:T(8,128)S(1)}, f32[128,1024]{1,0:T(8,128)S(1)}, f32[128,1024]{1,0:T(8,128)S(1)}, f32[128,1024]{1,0:T(8,128)S(1)}) custom-call(f32[20]{0:T(128)} %lambdas_h.3, s32[3]{0:T(128)} %lam_index_h.3, s32[3]{0:T(128)} %live_h.5, f32[1,4096]{1,0:T(1,128)} %bitcast.26, bf16[768,4096]{1,0:T(8,128)(2,1)} %u.3, ...), custom_call_target="tpu_custom_call" | custom-call | flops 805306368 | bytes 3145728 | tf_op jit(solution)/shard_map/pallas_call | solution.py:180
  14.2 0.0 collective-permute-done.6
  14.2 0.1 fusion.5
  14.2 2.8 %collective-permute-start.8 = (bf16[128,1024]{1,0:T(8,128)(2,1)S(1)}, bf16[128,1024]{1,0:T(8,128)(2,1)S(1)}, u32[]{:S(2)}, u32[]{:S(2)}) collective-permute-start(bf16[128,1024]{1,0:T(8,128)(2,1)S(1)} %fusion.5), channel_id=1, source_target_pairs={{0,96},{1,33},{2,98},{3,35},{4,100},{5,37},{6,102},{7,39},{8,104},... | collective-permute-start | bytes 786440 | tf_op jit(solution)/shard_map/ppermute | solution.py:60
  17.1 0.0 collective-permute-done.b
  17.1 0.0 collective-permute-done.1.c
  17.1 0.0 collective-permute-done.2.d
  17.1 0.1 shard_map.96
  17.2 2.0 %collective-permute-start.3 = (bf16[4,1024,128]{2,1,0:T(8,128)(2,1)S(1)}, bf16[4,1024,128]{2,1,0:T(8,128)(2,1)S(1)}, u32[]{:S(2)}, u32[]{:S(2)}) collective-permute-start(bf16[4,1024,128]{2,1,0:T(8,128)(2,1)S(1)} %shard_map.96), channel_id=1, source_target_pairs={{0,2},{1,9},{2,4},{3,11},{4,6},{5,13},{6,0},{7,15},{8,10},{9,17},{... | collective-permute-start | bytes 3145736 | tf_op jit(solution)/shard_map/ppermute | solution.py:60
  19.2 2.2 %collective-permute-start.4 = (bf16[4,1024,128]{2,1,0:T(8,128)(2,1)S(1)}, bf16[4,1024,128]{2,1,0:T(8,128)(2,1)S(1)}, u32[]{:S(2)}, u32[]{:S(2)}) collective-permute-start(bf16[4,1024,128]{2,1,0:T(8,128)(2,1)S(1)} %shard_map.96), channel_id=1, source_target_pairs={{0,6},{1,25},{2,0},{3,27},{4,2},{5,29},{6,4},{7,31},{8,14},{9,1},{... | collective-permute-start | bytes 3145736 | tf_op jit(solution)/shard_map/ppermute | solution.py:60
  21.4 1.6 %collective-permute-done.5 = bf16[2,128,1024]{2,1,0:T(8,128)(2,1)S(1)} collective-permute-done((bf16[2,128,1024]{2,1,0:T(8,128)(2,1)S(1)}, bf16[2,128,1024]{2,1,0:T(8,128)(2,1)S(1)}, u32[]{:S(2)}, u32[]{:S(2)}) %collective-permute-start.5) | collective-permute-done | bytes 524320 | tf_op jit(solution)/shard_map/ppermute | solution.py:60
  23.0 0.1 fusion.2
  23.1 1.6 %collective-permute-start.7 = (bf16[128,1024]{1,0:T(8,128)(2,1)S(1)}, bf16[128,1024]{1,0:T(8,128)(2,1)S(1)}, u32[]{:S(2)}, u32[]{:S(2)}) collective-permute-start(bf16[128,1024]{1,0:T(8,128)(2,1)S(1)} %fusion.2), channel_id=1, source_target_pairs={{0,96},{1,33},{2,98},{3,35},{4,100},{5,37},{6,102},{7,39},{8,104},... | collective-permute-start | bytes 786440 | tf_op jit(solution)/shard_map/ppermute | solution.py:60
  24.6 5.6 %collective-permute-start.11 = (bf16[4,1024,128]{2,1,0:T(8,128)(2,1)S(1)}, bf16[4,1024,128]{2,1,0:T(8,128)(2,1)S(1)}, u32[]{:S(2)}, u32[]{:S(2)}) collective-permute-start(bf16[4,1024,128]{2,1,0:T(8,128)(2,1)S(1)} %shard_map.96), channel_id=1, source_target_pairs={{0,4},{1,17},{2,6},{3,19},{4,0},{5,21},{6,2},{7,23},{8,12},{9,25},... | collective-permute-start | bytes 3145736 | tf_op jit(solution)/shard_map/ppermute | solution.py:60
  30.3 0.0 collective-permute-done.8
  30.3 0.1 fusion.1.own_0
  30.4 0.9 %collective-permute-start.10 = (bf16[128,1024]{1,0:T(8,128)(2,1)S(1)}, bf16[128,1024]{1,0:T(8,128)(2,1)S(1)}, u32[]{:S(2)}, u32[]{:S(2)}) collective-permute-start(bf16[128,1024]{1,0:T(8,128)(2,1)S(1)} %fusion.1.own_0), channel_id=1, source_target_pairs={{0,96},{1,33},{2,98},{3,35},{4,100},{5,37},{6,102},{7,39},{8,104},... | collective-permute-start | bytes 786440 | tf_op jit(solution)/shard_map/ppermute | solution.py:60
  31.3 0.0 collective-permute-done.7
  31.3 0.1 fusion.4.own_1
  31.4 2.5 %collective-permute-start.9 = (bf16[128,1024]{1,0:T(8,128)(2,1)S(1)}, bf16[128,1024]{1,0:T(8,128)(2,1)S(1)}, u32[]{:S(2)}, u32[]{:S(2)}) collective-permute-start(bf16[128,1024]{1,0:T(8,128)(2,1)S(1)} %fusion.4.own_1), channel_id=1, source_target_pairs={{0,96},{1,33},{2,98},{3,35},{4,100},{5,37},{6,102},{7,39},{8,104},... | collective-permute-start | bytes 786440 | tf_op jit(solution)/shard_map/ppermute | solution.py:60
  33.9 0.1 constant_dynamic-update-slice_fusion.8
  34.0 4.1 %collective-permute-done.10.other_0 = bf16[128,1024]{1,0:T(8,128)(2,1)S(1)} collective-permute-done((bf16[128,1024]{1,0:T(8,128)(2,1)S(1)}, bf16[128,1024]{1,0:T(8,128)(2,1)S(1)}, u32[]{:S(2)}, u32[]{:S(2)}) %collective-permute-start.10) | collective-permute-done | bytes 262176 | tf_op jit(solution)/shard_map/ppermute | solution.py:60
  38.0 0.0 collective-permute-start.12
  38.0 0.1 pad_maximum_fusion
  38.1 2.8 %collective-permute-done.9.other_1 = bf16[128,1024]{1,0:T(8,128)(2,1)S(1)} collective-permute-done((bf16[128,1024]{1,0:T(8,128)(2,1)S(1)}, bf16[128,1024]{1,0:T(8,128)(2,1)S(1)}, u32[]{:S(2)}, u32[]{:S(2)}) %collective-permute-start.9) | collective-permute-done | bytes 262176 | tf_op jit(solution)/shard_map/ppermute | solution.py:60
  40.8 0.3 collective-permute-start.15
  41.1 0.1 pad_maximum_fusion.1
  41.2 0.0 collective-permute-done.3
  41.2 1.8 %collective-permute-start.16 = (bf16[2,128,1024]{2,1,0:T(8,128)(2,1)S(1)}, bf16[2,128,1024]{2,1,0:T(8,128)(2,1)S(1)}, u32[]{:S(2)}, u32[]{:S(2)}) collective-permute-start(bf16[2,128,1024]{2,1,0:T(8,128)(2,1)S(1)} %pad_maximum_fusion.1), channel_id=1, source_target_pairs={{0,32},{1,97},{2,34},{3,99},{4,36},{5,101},{6,38},{7,103},{8,40},{... | collective-permute-start | bytes 1572872 | tf_op jit(solution)/shard_map/ppermute | solution.py:60
  43.0 1.9 %collective-permute-done.4 = bf16[4,1024,128]{2,1,0:T(8,128)(2,1)S(1)} collective-permute-done((bf16[4,1024,128]{2,1,0:T(8,128)(2,1)S(1)}, bf16[4,1024,128]{2,1,0:T(8,128)(2,1)S(1)}, u32[]{:S(2)}, u32[]{:S(2)}) %collective-permute-start.4) | collective-permute-done | bytes 1048608 | tf_op jit(solution)/shard_map/ppermute | solution.py:60
  45.0 0.3 constant_dynamic-update-slice_fusion.1
  45.3 0.4 constant_dynamic-update-slice_fusion
  45.7 0.1 collective-permute-start.13
  45.8 1.0 %collective-permute-done.11.refs_0_ = bf16[4,1024,128]{2,1,0:T(8,128)(2,1)S(1)} collective-permute-done((bf16[4,1024,128]{2,1,0:T(8,128)(2,1)S(1)}, bf16[4,1024,128]{2,1,0:T(8,128)(2,1)S(1)}, u32[]{:S(2)}, u32[]{:S(2)}) %collective-permute-start.11) | collective-permute-done | bytes 1048608 | tf_op jit(solution)/shard_map/ppermute | solution.py:60
  46.8 0.0 collective-permute-start.14
  46.8 0.1 constant_dynamic-update-slice_fusion.5
  46.9 0.0 collective-permute-done.12
  46.9 0.1 constant_dynamic-update-slice_fusion.4
  47.1 3.0 %collective-permute-done.15.refs_0_ = bf16[2,128,1024]{2,1,0:T(8,128)(2,1)S(1)} collective-permute-done((bf16[2,128,1024]{2,1,0:T(8,128)(2,1)S(1)}, bf16[2,128,1024]{2,1,0:T(8,128)(2,1)S(1)}, u32[]{:S(2)}, u32[]{:S(2)}) %collective-permute-start.15) | collective-permute-done | bytes 524320 | tf_op jit(solution)/shard_map/ppermute | solution.py:60
  50.0 5.6 %collective-permute-done.16.refs_1_ = bf16[2,128,1024]{2,1,0:T(8,128)(2,1)S(1)} collective-permute-done((bf16[2,128,1024]{2,1,0:T(8,128)(2,1)S(1)}, bf16[2,128,1024]{2,1,0:T(8,128)(2,1)S(1)}, u32[]{:S(2)}, u32[]{:S(2)}) %collective-permute-start.16) | collective-permute-done | bytes 524320 | tf_op jit(solution)/shard_map/ppermute | solution.py:60
  55.6 0.0 collective-permute-done.13
  55.6 0.3 constant_dynamic-update-slice_fusion.3
  55.9 0.0 collective-permute-done.14
  55.9 0.1 constant_dynamic-update-slice_fusion.2.shards
  56.1 0.0 copy-start
  56.1 1.3 %shard_map.101.so_far = f32[1024,256]{1,0:T(8,128)S(1)} custom-call(bf16[32,1024,128]{2,1,0:T(8,128)(2,1)S(1)} %constant_dynamic-update-slice_fusion.2.shards, bf16[128,1024]{1,0:T(8,128)(2,1)S(1)} %fusion.1.own_0, bf16[128,1024]{1,0:T(8,128)(2,1)S(1)} %fusion.4.own_1, bf16[128,1024]{1,0:T(8,128)(2,1)S(1)} %collective-permute-done.10.other_0, ...), custom_call_target="tpu_custom_call" | custom-call | flops 6000000000 | bytes 4194304 | tf_op jit(solution)/shard_map/pallas_call | solution.py:261
  57.4 0.3 copy-done
  57.7 1.8 %shard_map.102 = (bf16[1024,256]{1,0:T(8,128)(2,1)S(1)}, f32[256,256]{1,0:T(8,128)S(1)}, bf16[256,256]{1,0:T(8,128)(2,1)S(1)}, bf16[256,256]{1,0:T(8,128)(2,1)S(1)}, bf16[256,256]{1,0:T(8,128)(2,1)S(1)}) custom-call(bf16[32,1024,128]{2,1,0:T(8,128)(2,1)S(1)} %constant_dynamic-update-slice_fusion.2.shards, bf16[2,128,1024]{2,1,0:T(8,128)(2,1)S(1)} %get-tuple-element.41.far_0, ...), custom_call_target="tpu_custom_call" | custom-call | flops 1073741824 | bytes 4194304 | tf_op jit(solution)/shard_map/pallas_call | solution.py:308
  59.5 0.5 collective-permute-start.17
  60.0 1.3 %collective-permute-start.18 = (bf16[256,256]{1,0:T(8,128)(2,1)S(1)}, bf16[256,256]{1,0:T(8,128)(2,1)S(1)}, u32[]{:S(2)}, u32[]{:S(2)}) collective-permute-start(bf16[256,256]{1,0:T(8,128)(2,1)S(1)} %get-tuple-element.48), channel_id=1, source_target_pairs={{0,32},{1,97},{2,34},{3,99},{4,36},{5,101},{6,38},{7,103},{8,40},{... | collective-permute-start | bytes 393224 | tf_op jit(solution)/shard_map/ppermute | solution.py:60
  61.3 2.4 %collective-permute-start.19 = (bf16[256,256]{1,0:T(8,128)(2,1)S(1)}, bf16[256,256]{1,0:T(8,128)(2,1)S(1)}, u32[]{:S(2)}, u32[]{:S(2)}) collective-permute-start(bf16[256,256]{1,0:T(8,128)(2,1)S(1)} %get-tuple-element.49), channel_id=1, source_target_pairs={{0,96},{1,33},{2,98},{3,35},{4,100},{5,37},{6,102},{7,39},{8,104},... | collective-permute-start | bytes 393224 | tf_op jit(solution)/shard_map/ppermute | solution.py:60
  63.7 1.7 %shard_map.103 = (bf16[1024,384]{1,0:T(8,128)(2,1)}, f32[2,8,384]{2,1,0:T(8,128)S(1)}) custom-call(s32[3]{0:T(128)} %live_h.5, bf16[1024,256]{1,0:T(8,128)(2,1)S(1)} %get-tuple-element.43.packed), custom_call_target="tpu_custom_call" | custom-call | flops 1048576 | bytes 4194304 | tf_op jit(solution)/shard_map/pallas_call | solution.py:341
  65.4 0.6 collective-permute-done.17
  66.1 0.0 collective-permute-done.18
  66.1 1.4 %collective-permute-done.19 = bf16[256,256]{1,0:T(8,128)(2,1)S(1)} collective-permute-done((bf16[256,256]{1,0:T(8,128)(2,1)S(1)}, bf16[256,256]{1,0:T(8,128)(2,1)S(1)}, u32[]{:S(2)}, u32[]{:S(2)}) %collective-permute-start.19) | collective-permute-done | bytes 131104 | tf_op jit(solution)/shard_map/ppermute | solution.py:60
  67.5 0.1 convert_add_fusion.4
  67.6 0.7 %fusion.6 = bf16[256,384]{1,0:T(8,128)(2,1)} fusion(bf16[256,128]{1,0:T(8,128)(2,1)S(1)} %get-tuple-element.57, bf16[256,128]{1,0:T(8,128)(2,1)S(1)} %get-tuple-element.56, pred[384]{0:T(512)(128)(4,1)S(1)} %get-tuple-element.51, pred[384]{0:T(512)(128)(4,1)S(1)} %get-tuple-element.50), kind=kLoop, calls=%fused_computation.13 | loop fusion | flops 1376256 | bytes 328448 | tf_op jit(solution)/shard_map/convert_element_type | solution.py:363
  (6 shorter events, 0.0 us)
Async XLA Ops:
  0.6 16.5 %copy-start.1 = (bf16[1024,128]{1,0:T(8,128)(2,1)S(1)}, bf16[1024,128]{1,0:T(8,128)(2,1)}, u32[]{:S(2)}) copy-start(bf16[1024,128]{1,0:T(8,128)(2,1)} %a.1) | copy-start | bytes 786436
  3.5 10.7 %collective-permute-start.6 = (bf16[2,128,1024]{2,1,0:T(8,128)(2,1)S(1)}, bf16[2,128,1024]{2,1,0:T(8,128)(2,1)S(1)}, u32[]{:S(2)}, u32[]{:S(2)}) collective-permute-start(bf16[2,128,1024]{2,1,0:T(8,128)(2,1)S(1)} %get-tuple-element.32), channel_id=1, source_target_pairs={{0,32},{1,97},{2,34},{3,99},{4,36},{5,101},{6,38},{7,103},{8,40},{... | collective-permute-start | bytes 1572872 | tf_op jit(solution)/shard_map/ppermute | solution.py:60
  5.2 11.9 %collective-permute-start = (bf16[1024,128]{1,0:T(8,128)(2,1)}, bf16[1024,128]{1,0:T(8,128)(2,1)S(1)}, u32[]{:S(2)}, u32[]{:S(2)}) collective-permute-start(bf16[1024,128]{1,0:T(8,128)(2,1)} %a.1), channel_id=1, source_target_pairs={{0,8},{1,3},{2,10},{3,5},{4,12},{5,7},{6,14},{7,1},{8,16},{9,11},{... | collective-permute-start | bytes 786440 | tf_op jit(solution)/shard_map/ppermute | solution.py:60
  6.7 10.3 %collective-permute-start.1 = (bf16[1024,128]{1,0:T(8,128)(2,1)}, bf16[1024,128]{1,0:T(8,128)(2,1)S(1)}, u32[]{:S(2)}, u32[]{:S(2)}) collective-permute-start(bf16[1024,128]{1,0:T(8,128)(2,1)} %a.1), channel_id=1, source_target_pairs={{0,16},{1,5},{2,18},{3,7},{4,20},{5,1},{6,22},{7,3},{8,24},{9,13},... | collective-permute-start | bytes 786440 | tf_op jit(solution)/shard_map/ppermute | solution.py:60
  9.7 7.4 %collective-permute-start.2 = (bf16[1024,128]{1,0:T(8,128)(2,1)}, bf16[1024,128]{1,0:T(8,128)(2,1)S(1)}, u32[]{:S(2)}, u32[]{:S(2)}) collective-permute-start(bf16[1024,128]{1,0:T(8,128)(2,1)} %a.1), channel_id=1, source_target_pairs={{0,24},{1,7},{2,26},{3,1},{4,28},{5,3},{6,30},{7,5},{8,0},{9,15},{... | collective-permute-start | bytes 786440 | tf_op jit(solution)/shard_map/ppermute | solution.py:60
  11.0 12.0 %collective-permute-start.5 = (bf16[2,128,1024]{2,1,0:T(8,128)(2,1)S(1)}, bf16[2,128,1024]{2,1,0:T(8,128)(2,1)S(1)}, u32[]{:S(2)}, u32[]{:S(2)}) collective-permute-start(bf16[2,128,1024]{2,1,0:T(8,128)(2,1)S(1)} %get-tuple-element.29), channel_id=1, source_target_pairs={{0,32},{1,97},{2,34},{3,99},{4,36},{5,101},{6,38},{7,103},{8,40},{... | collective-permute-start | bytes 1572872 | tf_op jit(solution)/shard_map/ppermute | solution.py:60
  14.2 16.0 %collective-permute-start.8 = (bf16[128,1024]{1,0:T(8,128)(2,1)S(1)}, bf16[128,1024]{1,0:T(8,128)(2,1)S(1)}, u32[]{:S(2)}, u32[]{:S(2)}) collective-permute-start(bf16[128,1024]{1,0:T(8,128)(2,1)S(1)} %fusion.5), channel_id=1, source_target_pairs={{0,96},{1,33},{2,98},{3,35},{4,100},{5,37},{6,102},{7,39},{8,104},... | collective-permute-start | bytes 786440 | tf_op jit(solution)/shard_map/ppermute | solution.py:60
  17.2 24.0 %collective-permute-start.3 = (bf16[4,1024,128]{2,1,0:T(8,128)(2,1)S(1)}, bf16[4,1024,128]{2,1,0:T(8,128)(2,1)S(1)}, u32[]{:S(2)}, u32[]{:S(2)}) collective-permute-start(bf16[4,1024,128]{2,1,0:T(8,128)(2,1)S(1)} %shard_map.96), channel_id=1, source_target_pairs={{0,2},{1,9},{2,4},{3,11},{4,6},{5,13},{6,0},{7,15},{8,10},{9,17},{... | collective-permute-start | bytes 3145736 | tf_op jit(solution)/shard_map/ppermute | solution.py:60
  19.2 25.8 %collective-permute-start.4 = (bf16[4,1024,128]{2,1,0:T(8,128)(2,1)S(1)}, bf16[4,1024,128]{2,1,0:T(8,128)(2,1)S(1)}, u32[]{:S(2)}, u32[]{:S(2)}) collective-permute-start(bf16[4,1024,128]{2,1,0:T(8,128)(2,1)S(1)} %shard_map.96), channel_id=1, source_target_pairs={{0,6},{1,25},{2,0},{3,27},{4,2},{5,29},{6,4},{7,31},{8,14},{9,1},{... | collective-permute-start | bytes 3145736 | tf_op jit(solution)/shard_map/ppermute | solution.py:60
  23.1 8.2 %collective-permute-start.7 = (bf16[128,1024]{1,0:T(8,128)(2,1)S(1)}, bf16[128,1024]{1,0:T(8,128)(2,1)S(1)}, u32[]{:S(2)}, u32[]{:S(2)}) collective-permute-start(bf16[128,1024]{1,0:T(8,128)(2,1)S(1)} %fusion.2), channel_id=1, source_target_pairs={{0,96},{1,33},{2,98},{3,35},{4,100},{5,37},{6,102},{7,39},{8,104},... | collective-permute-start | bytes 786440 | tf_op jit(solution)/shard_map/ppermute | solution.py:60
  24.6 22.1 %collective-permute-start.11 = (bf16[4,1024,128]{2,1,0:T(8,128)(2,1)S(1)}, bf16[4,1024,128]{2,1,0:T(8,128)(2,1)S(1)}, u32[]{:S(2)}, u32[]{:S(2)}) collective-permute-start(bf16[4,1024,128]{2,1,0:T(8,128)(2,1)S(1)} %shard_map.96), channel_id=1, source_target_pairs={{0,4},{1,17},{2,6},{3,19},{4,0},{5,21},{6,2},{7,23},{8,12},{9,25},... | collective-permute-start | bytes 3145736 | tf_op jit(solution)/shard_map/ppermute | solution.py:60
  30.4 7.7 %collective-permute-start.10 = (bf16[128,1024]{1,0:T(8,128)(2,1)S(1)}, bf16[128,1024]{1,0:T(8,128)(2,1)S(1)}, u32[]{:S(2)}, u32[]{:S(2)}) collective-permute-start(bf16[128,1024]{1,0:T(8,128)(2,1)S(1)} %fusion.1.own_0), channel_id=1, source_target_pairs={{0,96},{1,33},{2,98},{3,35},{4,100},{5,37},{6,102},{7,39},{8,104},... | collective-permute-start | bytes 786440 | tf_op jit(solution)/shard_map/ppermute | solution.py:60
  31.4 9.4 %collective-permute-start.9 = (bf16[128,1024]{1,0:T(8,128)(2,1)S(1)}, bf16[128,1024]{1,0:T(8,128)(2,1)S(1)}, u32[]{:S(2)}, u32[]{:S(2)}) collective-permute-start(bf16[128,1024]{1,0:T(8,128)(2,1)S(1)} %fusion.4.own_1), channel_id=1, source_target_pairs={{0,96},{1,33},{2,98},{3,35},{4,100},{5,37},{6,102},{7,39},{8,104},... | collective-permute-start | bytes 786440 | tf_op jit(solution)/shard_map/ppermute | solution.py:60
  38.0 8.9 %collective-permute-start.12 = (bf16[4,1024,128]{2,1,0:T(8,128)(2,1)S(1)}, bf16[4,1024,128]{2,1,0:T(8,128)(2,1)S(1)}, u32[]{:S(2)}, u32[]{:S(2)}) collective-permute-start(bf16[4,1024,128]{2,1,0:T(8,128)(2,1)S(1)} %shard_map.96), channel_id=1, source_target_pairs={{0,1},{1,0},{2,3},{3,2},{4,5},{5,4},{6,7},{7,6},{8,9},{9,8},{10,11... | collective-permute-start | bytes 3145736 | tf_op jit(solution)/shard_map/ppermute | solution.py:60
  40.8 9.2 %collective-permute-start.15 = (bf16[2,128,1024]{2,1,0:T(8,128)(2,1)S(1)}, bf16[2,128,1024]{2,1,0:T(8,128)(2,1)S(1)}, u32[]{:S(2)}, u32[]{:S(2)}) collective-permute-start(bf16[2,128,1024]{2,1,0:T(8,128)(2,1)S(1)} %pad_maximum_fusion), channel_id=1, source_target_pairs={{0,32},{1,97},{2,34},{3,99},{4,36},{5,101},{6,38},{7,103},{8,40},{... | collective-permute-start | bytes 1572872 | tf_op jit(solution)/shard_map/ppermute | solution.py:60
  41.2 14.5 %collective-permute-start.16 = (bf16[2,128,1024]{2,1,0:T(8,128)(2,1)S(1)}, bf16[2,128,1024]{2,1,0:T(8,128)(2,1)S(1)}, u32[]{:S(2)}, u32[]{:S(2)}) collective-permute-start(bf16[2,128,1024]{2,1,0:T(8,128)(2,1)S(1)} %pad_maximum_fusion.1), channel_id=1, source_target_pairs={{0,32},{1,97},{2,34},{3,99},{4,36},{5,101},{6,38},{7,103},{8,40},{... | collective-permute-start | bytes 1572872 | tf_op jit(solution)/shard_map/ppermute | solution.py:60
  45.7 9.9 %collective-permute-start.13 = (bf16[8,1024,128]{2,1,0:T(8,128)(2,1)S(1)}, bf16[8,1024,128]{2,1,0:T(8,128)(2,1)S(1)}, u32[]{:S(2)}, u32[]{:S(2)}) collective-permute-start(bf16[8,1024,128]{2,1,0:T(8,128)(2,1)S(1)} %get-tuple-element.52), channel_id=1, source_target_pairs={{0,1},{1,0},{2,3},{3,2},{4,5},{5,4},{6,7},{7,6},{8,9},{9,8},{10,11... | collective-permute-start | bytes 6291464 | tf_op jit(solution)/shard_map/ppermute | solution.py:60
  46.8 9.2 %collective-permute-start.14 = (bf16[4,1024,128]{2,1,0:T(8,128)(2,1)S(1)}, bf16[4,1024,128]{2,1,0:T(8,128)(2,1)S(1)}, u32[]{:S(2)}, u32[]{:S(2)}) collective-permute-start(bf16[4,1024,128]{2,1,0:T(8,128)(2,1)S(1)} %shard_map.98), channel_id=1, source_target_pairs={{0,1},{1,0},{2,3},{3,2},{4,5},{5,4},{6,7},{7,6},{8,9},{9,8},{10,11... | collective-permute-start | bytes 3145736 | tf_op jit(solution)/shard_map/ppermute | solution.py:60
  56.1 1.6 %copy-start = (bf16[1024,1024]{1,0:T(8,128)(2,1)S(1)}, bf16[1024,1024]{1,0:T(8,128)(2,1)}, u32[]{:S(2)}) copy-start(bf16[1024,1024]{1,0:T(8,128)(2,1)} %tests.1) | copy-start | bytes 6291460
  59.5 6.6 %collective-permute-start.17 = (bf16[256,256]{1,0:T(8,128)(2,1)S(1)}, bf16[256,256]{1,0:T(8,128)(2,1)S(1)}, u32[]{:S(2)}, u32[]{:S(2)}) collective-permute-start(bf16[256,256]{1,0:T(8,128)(2,1)S(1)} %get-tuple-element.47), channel_id=1, source_target_pairs={{0,64},{1,65},{2,66},{3,67},{4,68},{5,69},{6,70},{7,71},{8,72},{9,... | collective-permute-start | bytes 393224 | tf_op jit(solution)/shard_map/ppermute | solution.py:60
  60.0 6.1 %collective-permute-start.18 = (bf16[256,256]{1,0:T(8,128)(2,1)S(1)}, bf16[256,256]{1,0:T(8,128)(2,1)S(1)}, u32[]{:S(2)}, u32[]{:S(2)}) collective-permute-start(bf16[256,256]{1,0:T(8,128)(2,1)S(1)} %get-tuple-element.48), channel_id=1, source_target_pairs={{0,32},{1,97},{2,34},{3,99},{4,36},{5,101},{6,38},{7,103},{8,40},{... | collective-permute-start | bytes 393224 | tf_op jit(solution)/shard_map/ppermute | solution.py:60
  61.3 6.2 %collective-permute-start.19 = (bf16[256,256]{1,0:T(8,128)(2,1)S(1)}, bf16[256,256]{1,0:T(8,128)(2,1)S(1)}, u32[]{:S(2)}, u32[]{:S(2)}) collective-permute-start(bf16[256,256]{1,0:T(8,128)(2,1)S(1)} %get-tuple-element.49), channel_id=1, source_target_pairs={{0,96},{1,33},{2,98},{3,35},{4,100},{5,37},{6,102},{7,39},{8,104},... | collective-permute-start | bytes 393224 | tf_op jit(solution)/shard_map/ppermute | solution.py:60

commit v7 on v6

--- a/solution.py
+++ b/solution.py
@@ -376,23 +376,23 @@
     come_1 = after(come_1, sum_0)
     sum_1 = (p_b1 + come_1[1].astype(F32)).astype(BF16)
     from_0, from_b = send(sum_0, PAIR_B), send(sum_1, PAIR_B)
-    ahead = [send(row, pairs) for pairs in SECOND]
-    row_other = send(row, SWAP)
+    ahead = [send(row, pairs) for pairs in SECOND[:2]]
     own_0 = (p_own0 + come_0[0].astype(F32) + from_0.astype(F32)).astype(BF16)
+    across = send(after(row, own_0), SECOND[2])
     from_1 = after(from_b, own_0)
     own_1 = (p_own1 + come_1[0].astype(F32) + from_1.astype(F32)).astype(BF16)
     other_0, other_1 = send(own_0, PAIR_B), send(own_1, PAIR_B)
     both_0 = jnp.stack([own_0, other_0])
     other_1 = after(other_1, both_0)
     both_1 = jnp.stack([own_1, other_1])
-    (far_0,) = hold(500_000_000, send(both_0, PAIR_A))
+    (far_0,) = hold(2000_000_000, send(both_0, PAIR_A))
     far = hold(100000_000_000, far_0, send(both_1, PAIR_A))
     pair = jnp.concatenate(after(ahead[:2], both_1))
-    far_row = after(ahead[2], pair)
-    (far_row,) = hold(25000_000_000, far_row)
-    pair_other = send(pair, SWAP)
+    far_row = after(across, pair)
+    early = jnp.concatenate([row, pair])
+    early_other = send(early, SWAP)
     far_other = send(far_row, SWAP)
-    shards = jnp.concatenate([row, pair, far_row, row_other, pair_other, far_other])
+    shards = jnp.concatenate([early, far_row, early_other, far_other])
     so_far = half_call(shards, own_0, own_1, other_0, other_1)
     packed, mine, to_a, to_b, opposite = last_call(shards, far, so_far, x_test)
     weights, picks = spread_call(live, packed)

time: 68.8 us -> 67.7 us (0.984)
  starting transfers between devices: 32 us -> 31.2 us
    ppermute x20 -> x19, starting transfers between devices: 32 us -> 31.2 us  [send(): return lax.ppermute(value, ('tm', 'vox'), pairs)]
    ppermute x20 -> x19, waiting for transfers between devices: 22 us -> 22.2 us  [send(): return lax.ppermute(value, ('tm', 'vox'), pairs)]
  transfers between devices with their start and end apart: 20 -> 19, of which waited for: 9 -> 7; matrix products, arithmetic and copies ran while one was open for 3% -> 3% of each run, Pallas kernels for 6% -> 7%
where the time goes in v7:
time: 67.7 us; the launch traced here: 67.6 us
  starting transfers between devices  31.2 us (46%)
  waiting for transfers between devices  22.2 us (33%)
  Pallas kernels  10.4 us (15%)
  other arithmetic  1.61 us (2%)
  local copies, waits for them, and re-layouts  1.37 us (2%)
  between operations  0.86 us (1%)
    ppermute x19, starting transfers between devices, send(): return lax.ppermute(value, ('tm', 'vox'), pairs)  31.2 us
    ppermute x19, waiting for transfers between devices, send(): return lax.ppermute(value, ('tm', 'vox'), pairs)  22.2 us
    pallas_call x1, Pallas kernels, start_call(): pl.pallas_call(start_kernel, out_shape=[jax.ShapeDtypeStruct((2, BLK, Q),...  2.87 us
    pallas_call x1, Pallas kernels, rest_call(): pl.pallas_call(rest_kernel, out_shape=[jax.ShapeDtypeStruct((BLK, Q), F32...  2.63 us
    pallas_call x1, Pallas kernels, last_call(): pl.pallas_call(last_kernel, out_shape=[jax.ShapeDtypeStruct((Q, W), BF16)...  1.82 us
    pallas_call x1, Pallas kernels, spread_call(): pl.pallas_call(spread_kernel, out_shape=[jax.ShapeDtypeStruct((Q, VD), BF...  1.7 us
  transfers between devices with their start and end apart: 19, of which 7 were waited for; matrix products, arithmetic and copies ran while one was open for 3% of the time, Pallas kernels for 7%

profile of v7, /device:TPU:0, one launch (start us, length us, event | category | flops | bytes accessed | tf_op | source)
XLA Modules:
  0.0 67.6 jit_solution(6364744491533940360)
XLA Ops:
  0.6 0.0 copy-start.1
  0.6 2.9 %shard_map.95 = (bf16[2,128,1024]{2,1,0:T(8,128)(2,1)S(1)}, bf16[2,128,1024]{2,1,0:T(8,128)(2,1)S(1)}, bf16[256,768]{1,0:T(8,128)(2,1)S(1)}) custom-call(f32[20]{0:T(128)} %lambdas_h.3, s32[3]{0:T(128)} %lam_index_h.3, s32[3]{0:T(128)} %live_h.5, f32[1,4096]{1,0:T(1,128)} %bitcast.25, bf16[768,4096]{1,0:T(8,128)(2,1)} %u.3, bf16[768,384]{1,0:T(8,128)(2,1)} %y.1), custom_call_target="tpu_custom_call" | custom-call | flops 805306368 | bytes 3145728 | tf_op jit(solution)/shard_map/pallas_call | solution.py:144
  3.5 1.7 %collective-permute-start.6 = (bf16[2,128,1024]{2,1,0:T(8,128)(2,1)S(1)}, bf16[2,128,1024]{2,1,0:T(8,128)(2,1)S(1)}, u32[]{:S(2)}, u32[]{:S(2)}) collective-permute-start(bf16[2,128,1024]{2,1,0:T(8,128)(2,1)S(1)} %get-tuple-element.32), channel_id=1, source_target_pairs={{0,32},{1,97},{2,34},{3,99},{4,36},{5,101},{6,38},{7,103},{8,40},{... | collective-permute-start | bytes 1572872 | tf_op jit(solution)/shard_map/ppermute | solution.py:60
  5.2 1.6 %collective-permute-start = (bf16[1024,128]{1,0:T(8,128)(2,1)}, bf16[1024,128]{1,0:T(8,128)(2,1)S(1)}, u32[]{:S(2)}, u32[]{:S(2)}) collective-permute-start(bf16[1024,128]{1,0:T(8,128)(2,1)} %a.1), channel_id=1, source_target_pairs={{0,8},{1,3},{2,10},{3,5},{4,12},{5,7},{6,14},{7,1},{8,16},{9,11},{... | collective-permute-start | bytes 786440 | tf_op jit(solution)/shard_map/ppermute | solution.py:60
  6.7 2.9 %collective-permute-start.1 = (bf16[1024,128]{1,0:T(8,128)(2,1)}, bf16[1024,128]{1,0:T(8,128)(2,1)S(1)}, u32[]{:S(2)}, u32[]{:S(2)}) collective-permute-start(bf16[1024,128]{1,0:T(8,128)(2,1)} %a.1), channel_id=1, source_target_pairs={{0,16},{1,5},{2,18},{3,7},{4,20},{5,1},{6,22},{7,3},{8,24},{9,13},... | collective-permute-start | bytes 786440 | tf_op jit(solution)/shard_map/ppermute | solution.py:60
  9.7 1.3 %collective-permute-start.2 = (bf16[1024,128]{1,0:T(8,128)(2,1)}, bf16[1024,128]{1,0:T(8,128)(2,1)S(1)}, u32[]{:S(2)}, u32[]{:S(2)}) collective-permute-start(bf16[1024,128]{1,0:T(8,128)(2,1)} %a.1), channel_id=1, source_target_pairs={{0,24},{1,7},{2,26},{3,1},{4,28},{5,3},{6,30},{7,5},{8,0},{9,15},{... | collective-permute-start | bytes 786440 | tf_op jit(solution)/shard_map/ppermute | solution.py:60
  11.0 0.5 collective-permute-start.5
  11.5 2.6 %shard_map.97 = (f32[128,1024]{1,0:T(8,128)S(1)}, f32[128,1024]{1,0:T(8,128)S(1)}, f32[128,1024]{1,0:T(8,128)S(1)}, f32[128,1024]{1,0:T(8,128)S(1)}) custom-call(f32[20]{0:T(128)} %lambdas_h.3, s32[3]{0:T(128)} %lam_index_h.3, s32[3]{0:T(128)} %live_h.5, f32[1,4096]{1,0:T(1,128)} %bitcast.26, bf16[768,4096]{1,0:T(8,128)(2,1)} %u.3, ...), custom_call_target="tpu_custom_call" | custom-call | flops 805306368 | bytes 3145728 | tf_op jit(solution)/shard_map/pallas_call | solution.py:180
  14.2 0.0 collective-permute-done.6
  14.2 0.1 fusion.5
  14.2 2.8 %collective-permute-start.8 = (bf16[128,1024]{1,0:T(8,128)(2,1)S(1)}, bf16[128,1024]{1,0:T(8,128)(2,1)S(1)}, u32[]{:S(2)}, u32[]{:S(2)}) collective-permute-start(bf16[128,1024]{1,0:T(8,128)(2,1)S(1)} %fusion.5), channel_id=1, source_target_pairs={{0,96},{1,33},{2,98},{3,35},{4,100},{5,37},{6,102},{7,39},{8,104},... | collective-permute-start | bytes 786440 | tf_op jit(solution)/shard_map/ppermute | solution.py:60
  17.1 0.0 collective-permute-done.b
  17.1 0.0 collective-permute-done.1.c
  17.1 0.0 collective-permute-done.2.d
  17.1 0.0 copy-done.1
  17.1 0.1 shard_map.96
  17.2 2.0 %collective-permute-start.3 = (bf16[4,1024,128]{2,1,0:T(8,128)(2,1)S(1)}, bf16[4,1024,128]{2,1,0:T(8,128)(2,1)S(1)}, u32[]{:S(2)}, u32[]{:S(2)}) collective-permute-start(bf16[4,1024,128]{2,1,0:T(8,128)(2,1)S(1)} %shard_map.96), channel_id=1, source_target_pairs={{0,2},{1,9},{2,4},{3,11},{4,6},{5,13},{6,0},{7,15},{8,10},{9,17},{... | collective-permute-start | bytes 3145736 | tf_op jit(solution)/shard_map/ppermute | solution.py:60
  19.2 2.2 %collective-permute-start.4 = (bf16[4,1024,128]{2,1,0:T(8,128)(2,1)S(1)}, bf16[4,1024,128]{2,1,0:T(8,128)(2,1)S(1)}, u32[]{:S(2)}, u32[]{:S(2)}) collective-permute-start(bf16[4,1024,128]{2,1,0:T(8,128)(2,1)S(1)} %shard_map.96), channel_id=1, source_target_pairs={{0,6},{1,25},{2,0},{3,27},{4,2},{5,29},{6,4},{7,31},{8,14},{9,1},{... | collective-permute-start | bytes 3145736 | tf_op jit(solution)/shard_map/ppermute | solution.py:60
  21.4 1.6 %collective-permute-done.5 = bf16[2,128,1024]{2,1,0:T(8,128)(2,1)S(1)} collective-permute-done((bf16[2,128,1024]{2,1,0:T(8,128)(2,1)S(1)}, bf16[2,128,1024]{2,1,0:T(8,128)(2,1)S(1)}, u32[]{:S(2)}, u32[]{:S(2)}) %collective-permute-start.5) | collective-permute-done | bytes 524320 | tf_op jit(solution)/shard_map/ppermute | solution.py:60
  23.0 0.1 fusion.2
  23.1 1.6 %collective-permute-start.7 = (bf16[128,1024]{1,0:T(8,128)(2,1)S(1)}, bf16[128,1024]{1,0:T(8,128)(2,1)S(1)}, u32[]{:S(2)}, u32[]{:S(2)}) collective-permute-start(bf16[128,1024]{1,0:T(8,128)(2,1)S(1)} %fusion.2), channel_id=1, source_target_pairs={{0,96},{1,33},{2,98},{3,35},{4,100},{5,37},{6,102},{7,39},{8,104},... | collective-permute-start | bytes 786440 | tf_op jit(solution)/shard_map/ppermute | solution.py:60
  24.6 0.0 collective-permute-done.8
  24.6 0.1 fusion.1.own_0
  24.7 1.8 %collective-permute-start.10 = (bf16[128,1024]{1,0:T(8,128)(2,1)S(1)}, bf16[128,1024]{1,0:T(8,128)(2,1)S(1)}, u32[]{:S(2)}, u32[]{:S(2)}) collective-permute-start(bf16[128,1024]{1,0:T(8,128)(2,1)S(1)} %fusion.1.own_0), channel_id=1, source_target_pairs={{0,96},{1,33},{2,98},{3,35},{4,100},{5,37},{6,102},{7,39},{8,104},... | collective-permute-start | bytes 786440 | tf_op jit(solution)/shard_map/ppermute | solution.py:60
  26.6 4.2 %collective-permute-done.7 = bf16[128,1024]{1,0:T(8,128)(2,1)S(1)} collective-permute-done((bf16[128,1024]{1,0:T(8,128)(2,1)S(1)}, bf16[128,1024]{1,0:T(8,128)(2,1)S(1)}, u32[]{:S(2)}, u32[]{:S(2)}) %collective-permute-start.7) | collective-permute-done | bytes 262176 | tf_op jit(solution)/shard_map/ppermute | solution.py:60
  30.7 0.1 fusion.4.own_1
  30.8 1.6 %collective-permute-start.9 = (bf16[128,1024]{1,0:T(8,128)(2,1)S(1)}, bf16[128,1024]{1,0:T(8,128)(2,1)S(1)}, u32[]{:S(2)}, u32[]{:S(2)}) collective-permute-start(bf16[128,1024]{1,0:T(8,128)(2,1)S(1)} %fusion.4.own_1), channel_id=1, source_target_pairs={{0,96},{1,33},{2,98},{3,35},{4,100},{5,37},{6,102},{7,39},{8,104},... | collective-permute-start | bytes 786440 | tf_op jit(solution)/shard_map/ppermute | solution.py:60
  32.4 5.6 %collective-permute-start.11 = (bf16[4,1024,128]{2,1,0:T(8,128)(2,1)S(1)}, bf16[4,1024,128]{2,1,0:T(8,128)(2,1)S(1)}, u32[]{:S(2)}, u32[]{:S(2)}) collective-permute-start(bf16[4,1024,128]{2,1,0:T(8,128)(2,1)S(1)} %shard_map.96), channel_id=1, source_target_pairs={{0,4},{1,17},{2,6},{3,19},{4,0},{5,21},{6,2},{7,23},{8,12},{9,25},... | collective-permute-start | bytes 3145736 | tf_op jit(solution)/shard_map/ppermute | solution.py:60
  38.0 0.1 constant_dynamic-update-slice_fusion.5
  38.1 0.0 collective-permute-done.10.other_0
  38.1 0.1 pad_maximum_fusion.1
  38.2 0.4 collective-permute-start.14
  38.5 1.5 %collective-permute-done.9.other_1 = bf16[128,1024]{1,0:T(8,128)(2,1)S(1)} collective-permute-done((bf16[128,1024]{1,0:T(8,128)(2,1)S(1)}, bf16[128,1024]{1,0:T(8,128)(2,1)S(1)}, u32[]{:S(2)}, u32[]{:S(2)}) %collective-permute-start.9) | collective-permute-done | bytes 262176 | tf_op jit(solution)/shard_map/ppermute | solution.py:60
  40.1 0.1 pad_maximum_fusion.2
  40.1 0.3 collective-permute-start.15
  40.4 0.0 collective-permute-done.3
  40.4 0.0 collective-permute-done.4
  40.4 0.4 pad_maximum_fusion
  40.8 0.1 collective-permute-start.12
  40.9 0.1 constant_dynamic-update-slice_fusion.4
  41.0 0.1 constant_dynamic-update-slice_fusion.3
  41.2 6.3 %collective-permute-done.14.refs_0_ = bf16[2,128,1024]{2,1,0:T(8,128)(2,1)S(1)} collective-permute-done((bf16[2,128,1024]{2,1,0:T(8,128)(2,1)S(1)}, bf16[2,128,1024]{2,1,0:T(8,128)(2,1)S(1)}, u32[]{:S(2)}, u32[]{:S(2)}) %collective-permute-start.14) | collective-permute-done | bytes 524320 | tf_op jit(solution)/shard_map/ppermute | solution.py:60
  47.4 3.4 %collective-permute-done.11 = bf16[4,1024,128]{2,1,0:T(8,128)(2,1)S(1)} collective-permute-done((bf16[4,1024,128]{2,1,0:T(8,128)(2,1)S(1)}, bf16[4,1024,128]{2,1,0:T(8,128)(2,1)S(1)}, u32[]{:S(2)}, u32[]{:S(2)}) %collective-permute-start.11) | collective-permute-done | bytes 1048608 | tf_op jit(solution)/shard_map/ppermute | solution.py:60
  50.8 0.0 collective-permute-start.13
  50.8 2.2 %collective-permute-done.15.refs_1_ = bf16[2,128,1024]{2,1,0:T(8,128)(2,1)S(1)} collective-permute-done((bf16[2,128,1024]{2,1,0:T(8,128)(2,1)S(1)}, bf16[2,128,1024]{2,1,0:T(8,128)(2,1)S(1)}, u32[]{:S(2)}, u32[]{:S(2)}) %collective-permute-start.15) | collective-permute-done | bytes 524320 | tf_op jit(solution)/shard_map/ppermute | solution.py:60
  53.1 0.1 constant_dynamic-update-slice_fusion.2
  53.2 0.0 collective-permute-done.12
  53.2 0.4 constant_dynamic-update-slice_fusion.1
  53.6 0.0 collective-permute-done.13
  53.6 0.1 constant_dynamic-update-slice_fusion.shards
  53.8 0.0 copy-start
  53.8 1.3 %shard_map.100.so_far = f32[1024,256]{1,0:T(8,128)S(1)} custom-call(bf16[32,1024,128]{2,1,0:T(8,128)(2,1)S(1)} %constant_dynamic-update-slice_fusion.shards, bf16[128,1024]{1,0:T(8,128)(2,1)S(1)} %fusion.1.own_0, bf16[128,1024]{1,0:T(8,128)(2,1)S(1)} %fusion.4.own_1, bf16[128,1024]{1,0:T(8,128)(2,1)S(1)} %collective-permute-done.10.other_0, ...), custom_call_target="tpu_custom_call" | custom-call | flops 6000000000 | bytes 4194304 | tf_op jit(solution)/shard_map/pallas_call | solution.py:261
  55.1 0.3 copy-done
  55.4 1.8 %shard_map.101 = (bf16[1024,256]{1,0:T(8,128)(2,1)S(1)}, f32[256,256]{1,0:T(8,128)S(1)}, bf16[256,256]{1,0:T(8,128)(2,1)S(1)}, bf16[256,256]{1,0:T(8,128)(2,1)S(1)}, bf16[256,256]{1,0:T(8,128)(2,1)S(1)}) custom-call(bf16[32,1024,128]{2,1,0:T(8,128)(2,1)S(1)} %constant_dynamic-update-slice_fusion.shards, bf16[2,128,1024]{2,1,0:T(8,128)(2,1)S(1)} %get-tuple-element.41.far_0, ...), custom_call_target="tpu_custom_call" | custom-call | flops 1073741824 | bytes 4194304 | tf_op jit(solution)/shard_map/pallas_call | solution.py:308
  57.2 0.9 %collective-permute-start.18 = (bf16[256,256]{1,0:T(8,128)(2,1)S(1)}, bf16[256,256]{1,0:T(8,128)(2,1)S(1)}, u32[]{:S(2)}, u32[]{:S(2)}) collective-permute-start(bf16[256,256]{1,0:T(8,128)(2,1)S(1)} %get-tuple-element.49), channel_id=1, source_target_pairs={{0,96},{1,33},{2,98},{3,35},{4,100},{5,37},{6,102},{7,39},{8,104},... | collective-permute-start | bytes 393224 | tf_op jit(solution)/shard_map/ppermute | solution.py:60
  58.1 0.0 collective-permute-start.17
  58.1 3.9 %collective-permute-start.16 = (bf16[256,256]{1,0:T(8,128)(2,1)S(1)}, bf16[256,256]{1,0:T(8,128)(2,1)S(1)}, u32[]{:S(2)}, u32[]{:S(2)}) collective-permute-start(bf16[256,256]{1,0:T(8,128)(2,1)S(1)} %get-tuple-element.47), channel_id=1, source_target_pairs={{0,64},{1,65},{2,66},{3,67},{4,68},{5,69},{6,70},{7,71},{8,72},{9,... | collective-permute-start | bytes 393224 | tf_op jit(solution)/shard_map/ppermute | solution.py:60
  62.0 1.7 %shard_map.102 = (bf16[1024,384]{1,0:T(8,128)(2,1)}, f32[2,8,384]{2,1,0:T(8,128)S(1)}) custom-call(s32[3]{0:T(128)} %live_h.5, bf16[1024,256]{1,0:T(8,128)(2,1)S(1)} %get-tuple-element.43.packed), custom_call_target="tpu_custom_call" | custom-call | flops 1048576 | bytes 4194304 | tf_op jit(solution)/shard_map/pallas_call | solution.py:341
  63.7 3.0 %collective-permute-done.18 = bf16[256,256]{1,0:T(8,128)(2,1)S(1)} collective-permute-done((bf16[256,256]{1,0:T(8,128)(2,1)S(1)}, bf16[256,256]{1,0:T(8,128)(2,1)S(1)}, u32[]{:S(2)}, u32[]{:S(2)}) %collective-permute-start.18) | collective-permute-done | bytes 131104 | tf_op jit(solution)/shard_map/ppermute | solution.py:60
  66.8 0.0 collective-permute-done.17
  66.8 0.0 collective-permute-done.16
  66.8 0.1 convert_add_fusion.4
  66.9 0.7 %fusion.6 = bf16[256,384]{1,0:T(8,128)(2,1)} fusion(bf16[256,128]{1,0:T(8,128)(2,1)S(1)} %get-tuple-element.53, bf16[256,128]{1,0:T(8,128)(2,1)S(1)} %get-tuple-element.52, pred[384]{0:T(512)(128)(4,1)S(1)} %get-tuple-element.51, pred[384]{0:T(512)(128)(4,1)S(1)} %get-tuple-element.50), kind=kLoop, calls=%fused_computation.14 | loop fusion | flops 1376256 | bytes 328448 | tf_op jit(solution)/shard_map/convert_element_type | solution.py:363
  (4 shorter events, 0.0 us)
Async XLA Ops:
  0.6 16.5 %copy-start.1 = (bf16[1024,128]{1,0:T(8,128)(2,1)S(1)}, bf16[1024,128]{1,0:T(8,128)(2,1)}, u32[]{:S(2)}) copy-start(bf16[1024,128]{1,0:T(8,128)(2,1)} %a.1) | copy-start | bytes 786436
  3.5 10.7 %collective-permute-start.6 = (bf16[2,128,1024]{2,1,0:T(8,128)(2,1)S(1)}, bf16[2,128,1024]{2,1,0:T(8,128)(2,1)S(1)}, u32[]{:S(2)}, u32[]{:S(2)}) collective-permute-start(bf16[2,128,1024]{2,1,0:T(8,128)(2,1)S(1)} %get-tuple-element.32), channel_id=1, source_target_pairs={{0,32},{1,97},{2,34},{3,99},{4,36},{5,101},{6,38},{7,103},{8,40},{... | collective-permute-start | bytes 1572872 | tf_op jit(solution)/shard_map/ppermute | solution.py:60
  5.2 11.9 %collective-permute-start = (bf16[1024,128]{1,0:T(8,128)(2,1)}, bf16[1024,128]{1,0:T(8,128)(2,1)S(1)}, u32[]{:S(2)}, u32[]{:S(2)}) collective-permute-start(bf16[1024,128]{1,0:T(8,128)(2,1)} %a.1), channel_id=1, source_target_pairs={{0,8},{1,3},{2,10},{3,5},{4,12},{5,7},{6,14},{7,1},{8,16},{9,11},{... | collective-permute-start | bytes 786440 | tf_op jit(solution)/shard_map/ppermute | solution.py:60
  6.7 10.3 %collective-permute-start.1 = (bf16[1024,128]{1,0:T(8,128)(2,1)}, bf16[1024,128]{1,0:T(8,128)(2,1)S(1)}, u32[]{:S(2)}, u32[]{:S(2)}) collective-permute-start(bf16[1024,128]{1,0:T(8,128)(2,1)} %a.1), channel_id=1, source_target_pairs={{0,16},{1,5},{2,18},{3,7},{4,20},{5,1},{6,22},{7,3},{8,24},{9,13},... | collective-permute-start | bytes 786440 | tf_op jit(solution)/shard_map/ppermute | solution.py:60
  9.7 7.4 %collective-permute-start.2 = (bf16[1024,128]{1,0:T(8,128)(2,1)}, bf16[1024,128]{1,0:T(8,128)(2,1)S(1)}, u32[]{:S(2)}, u32[]{:S(2)}) collective-permute-start(bf16[1024,128]{1,0:T(8,128)(2,1)} %a.1), channel_id=1, source_target_pairs={{0,24},{1,7},{2,26},{3,1},{4,28},{5,3},{6,30},{7,5},{8,0},{9,15},{... | collective-permute-start | bytes 786440 | tf_op jit(solution)/shard_map/ppermute | solution.py:60
  11.0 12.0 %collective-permute-start.5 = (bf16[2,128,1024]{2,1,0:T(8,128)(2,1)S(1)}, bf16[2,128,1024]{2,1,0:T(8,128)(2,1)S(1)}, u32[]{:S(2)}, u32[]{:S(2)}) collective-permute-start(bf16[2,128,1024]{2,1,0:T(8,128)(2,1)S(1)} %get-tuple-element.29), channel_id=1, source_target_pairs={{0,32},{1,97},{2,34},{3,99},{4,36},{5,101},{6,38},{7,103},{8,40},{... | collective-permute-start | bytes 1572872 | tf_op jit(solution)/shard_map/ppermute | solution.py:60
  14.2 10.4 %collective-permute-start.8 = (bf16[128,1024]{1,0:T(8,128)(2,1)S(1)}, bf16[128,1024]{1,0:T(8,128)(2,1)S(1)}, u32[]{:S(2)}, u32[]{:S(2)}) collective-permute-start(bf16[128,1024]{1,0:T(8,128)(2,1)S(1)} %fusion.5), channel_id=1, source_target_pairs={{0,96},{1,33},{2,98},{3,35},{4,100},{5,37},{6,102},{7,39},{8,104},... | collective-permute-start | bytes 786440 | tf_op jit(solution)/shard_map/ppermute | solution.py:60
  17.2 23.2 %collective-permute-start.3 = (bf16[4,1024,128]{2,1,0:T(8,128)(2,1)S(1)}, bf16[4,1024,128]{2,1,0:T(8,128)(2,1)S(1)}, u32[]{:S(2)}, u32[]{:S(2)}) collective-permute-start(bf16[4,1024,128]{2,1,0:T(8,128)(2,1)S(1)} %shard_map.96), channel_id=1, source_target_pairs={{0,2},{1,9},{2,4},{3,11},{4,6},{5,13},{6,0},{7,15},{8,10},{9,17},{... | collective-permute-start | bytes 3145736 | tf_op jit(solution)/shard_map/ppermute | solution.py:60
  19.2 21.2 %collective-permute-start.4 = (bf16[4,1024,128]{2,1,0:T(8,128)(2,1)S(1)}, bf16[4,1024,128]{2,1,0:T(8,128)(2,1)S(1)}, u32[]{:S(2)}, u32[]{:S(2)}) collective-permute-start(bf16[4,1024,128]{2,1,0:T(8,128)(2,1)S(1)} %shard_map.96), channel_id=1, source_target_pairs={{0,6},{1,25},{2,0},{3,27},{4,2},{5,29},{6,4},{7,31},{8,14},{9,1},{... | collective-permute-start | bytes 3145736 | tf_op jit(solution)/shard_map/ppermute | solution.py:60
  23.1 7.7 %collective-permute-start.7 = (bf16[128,1024]{1,0:T(8,128)(2,1)S(1)}, bf16[128,1024]{1,0:T(8,128)(2,1)S(1)}, u32[]{:S(2)}, u32[]{:S(2)}) collective-permute-start(bf16[128,1024]{1,0:T(8,128)(2,1)S(1)} %fusion.2), channel_id=1, source_target_pairs={{0,96},{1,33},{2,98},{3,35},{4,100},{5,37},{6,102},{7,39},{8,104},... | collective-permute-start | bytes 786440 | tf_op jit(solution)/shard_map/ppermute | solution.py:60
  24.7 13.4 %collective-permute-start.10 = (bf16[128,1024]{1,0:T(8,128)(2,1)S(1)}, bf16[128,1024]{1,0:T(8,128)(2,1)S(1)}, u32[]{:S(2)}, u32[]{:S(2)}) collective-permute-start(bf16[128,1024]{1,0:T(8,128)(2,1)S(1)} %fusion.1.own_0), channel_id=1, source_target_pairs={{0,96},{1,33},{2,98},{3,35},{4,100},{5,37},{6,102},{7,39},{8,104},... | collective-permute-start | bytes 786440 | tf_op jit(solution)/shard_map/ppermute | solution.py:60
  30.8 9.2 %collective-permute-start.9 = (bf16[128,1024]{1,0:T(8,128)(2,1)S(1)}, bf16[128,1024]{1,0:T(8,128)(2,1)S(1)}, u32[]{:S(2)}, u32[]{:S(2)}) collective-permute-start(bf16[128,1024]{1,0:T(8,128)(2,1)S(1)} %fusion.4.own_1), channel_id=1, source_target_pairs={{0,96},{1,33},{2,98},{3,35},{4,100},{5,37},{6,102},{7,39},{8,104},... | collective-permute-start | bytes 786440 | tf_op jit(solution)/shard_map/ppermute | solution.py:60
  32.4 18.4 %collective-permute-start.11 = (bf16[4,1024,128]{2,1,0:T(8,128)(2,1)S(1)}, bf16[4,1024,128]{2,1,0:T(8,128)(2,1)S(1)}, u32[]{:S(2)}, u32[]{:S(2)}) collective-permute-start(bf16[4,1024,128]{2,1,0:T(8,128)(2,1)S(1)} %shard_map.96), channel_id=1, source_target_pairs={{0,4},{1,17},{2,6},{3,19},{4,0},{5,21},{6,2},{7,23},{8,12},{9,25},... | collective-permute-start | bytes 3145736 | tf_op jit(solution)/shard_map/ppermute | solution.py:60
  38.2 9.3 %collective-permute-start.14 = (bf16[2,128,1024]{2,1,0:T(8,128)(2,1)S(1)}, bf16[2,128,1024]{2,1,0:T(8,128)(2,1)S(1)}, u32[]{:S(2)}, u32[]{:S(2)}) collective-permute-start(bf16[2,128,1024]{2,1,0:T(8,128)(2,1)S(1)} %pad_maximum_fusion.1), channel_id=1, source_target_pairs={{0,32},{1,97},{2,34},{3,99},{4,36},{5,101},{6,38},{7,103},{8,40},{... | collective-permute-start | bytes 1572872 | tf_op jit(solution)/shard_map/ppermute | solution.py:60
  40.1 12.9 %collective-permute-start.15 = (bf16[2,128,1024]{2,1,0:T(8,128)(2,1)S(1)}, bf16[2,128,1024]{2,1,0:T(8,128)(2,1)S(1)}, u32[]{:S(2)}, u32[]{:S(2)}) collective-permute-start(bf16[2,128,1024]{2,1,0:T(8,128)(2,1)S(1)} %pad_maximum_fusion.2), channel_id=1, source_target_pairs={{0,32},{1,97},{2,34},{3,99},{4,36},{5,101},{6,38},{7,103},{8,40},{... | collective-permute-start | bytes 1572872 | tf_op jit(solution)/shard_map/ppermute | solution.py:60
  40.8 12.4 %collective-permute-start.12 = (bf16[12,1024,128]{2,1,0:T(8,128)(2,1)S(1)}, bf16[12,1024,128]{2,1,0:T(8,128)(2,1)S(1)}, u32[]{:S(2)}, u32[]{:S(2)}) collective-permute-start(bf16[12,1024,128]{2,1,0:T(8,128)(2,1)S(1)} %pad_maximum_fusion), channel_id=1, source_target_pairs={{0,1},{1,0},{2,3},{3,2},{4,5},{5,4},{6,7},{7,6},{8,9},{9,8},{10,11... | collective-permute-start | bytes 9437192 | tf_op jit(solution)/shard_map/ppermute | solution.py:60
  50.8 2.8 %collective-permute-start.13 = (bf16[4,1024,128]{2,1,0:T(8,128)(2,1)S(1)}, bf16[4,1024,128]{2,1,0:T(8,128)(2,1)S(1)}, u32[]{:S(2)}, u32[]{:S(2)}) collective-permute-start(bf16[4,1024,128]{2,1,0:T(8,128)(2,1)S(1)} %collective-permute-done.11), channel_id=1, source_target_pairs={{0,1},{1,0},{2,3},{3,2},{4,5},{5,4},{6,7},{7,6},{8,9},{9,8},{10,11... | collective-permute-start | bytes 3145736 | tf_op jit(solution)/shard_map/ppermute | solution.py:60
  53.8 1.6 %copy-start = (bf16[1024,1024]{1,0:T(8,128)(2,1)S(1)}, bf16[1024,1024]{1,0:T(8,128)(2,1)}, u32[]{:S(2)}) copy-start(bf16[1024,1024]{1,0:T(8,128)(2,1)} %tests.1) | copy-start | bytes 6291460
  57.2 9.5 %collective-permute-start.18 = (bf16[256,256]{1,0:T(8,128)(2,1)S(1)}, bf16[256,256]{1,0:T(8,128)(2,1)S(1)}, u32[]{:S(2)}, u32[]{:S(2)}) collective-permute-start(bf16[256,256]{1,0:T(8,128)(2,1)S(1)} %get-tuple-element.49), channel_id=1, source_target_pairs={{0,96},{1,33},{2,98},{3,35},{4,100},{5,37},{6,102},{7,39},{8,104},... | collective-permute-start | bytes 393224 | tf_op jit(solution)/shard_map/ppermute | solution.py:60
  58.1 8.6 %collective-permute-start.17 = (bf16[256,256]{1,0:T(8,128)(2,1)S(1)}, bf16[256,256]{1,0:T(8,128)(2,1)S(1)}, u32[]{:S(2)}, u32[]{:S(2)}) collective-permute-start(bf16[256,256]{1,0:T(8,128)(2,1)S(1)} %get-tuple-element.48), channel_id=1, source_target_pairs={{0,32},{1,97},{2,34},{3,99},{4,36},{5,101},{6,38},{7,103},{8,40},{... | collective-permute-start | bytes 393224 | tf_op jit(solution)/shard_map/ppermute | solution.py:60
  58.1 8.6 %collective-permute-start.16 = (bf16[256,256]{1,0:T(8,128)(2,1)S(1)}, bf16[256,256]{1,0:T(8,128)(2,1)S(1)}, u32[]{:S(2)}, u32[]{:S(2)}) collective-permute-start(bf16[256,256]{1,0:T(8,128)(2,1)S(1)} %get-tuple-element.47), channel_id=1, source_target_pairs={{0,64},{1,65},{2,66},{3,67},{4,68},{5,69},{6,70},{7,71},{8,72},{9,... | collective-permute-start | bytes 393224 | tf_op jit(solution)/shard_map/ppermute | solution.py:60

commit v8 on v7

--- a/solution.py
+++ b/solution.py
@@ -248,28 +248,6 @@
     return total
 
 
-def half_kernel(shards, own_0, own_1, other_0, other_1, out):
-    x, _, _, c = place()
-    for r in range(Q // CHUNK):
-        rows = slice(r * CHUNK, (r + 1) * CHUNK)
-        out[rows, :] = multiply(x, rows, shards, (own_0, own_1)) + multiply(
-            quarter("b", x, c), rows, shards, (other_0, other_1)
-        )
-
-
-def half_call(shards, *features):
-    return pl.pallas_call(
-        half_kernel,
-        out_shape=jax.ShapeDtypeStruct((Q, W), F32),
-        in_specs=[VMEM] * 5,
-        out_specs=VMEM,
-        compiler_params=pltpu.CompilerParams(vmem_limit_bytes=8 << 20),
-        cost_estimate=pl.CostEstimate(
-            flops=6000_000_000, bytes_accessed=2 * Q * 2 * Q, transcendentals=0
-        ),
-    )(shards, *features)
-
-
 def spread(out, rows, values, live):
     first, second = slots(live)
     left, right = values[:, :BLK], values[:, BLK:]
@@ -279,12 +257,13 @@
         out[rows, b * BLK : (b + 1) * BLK] = block.astype(out.dtype)
 
 
-def last_kernel(shards, far_0, far_1, so_far, tests, *rest):
+def last_kernel(shards, far_0, far_1, own_0, own_1, other_0, other_1, tests, *rest):
     packed, mine, to_a, to_b, opposite = rest
     x, _, _, c = place()
     for r in range(Q // CHUNK):
         rows = slice(r * CHUNK, (r + 1) * CHUNK)
-        total = so_far[rows, :]
+        total = multiply(x, rows, shards, (own_0, own_1))
+        total = total + multiply(quarter("b", x, c), rows, shards, (other_0, other_1))
         for i, name in enumerate(("a", "opposite")):
             total = total + multiply(
                 quarter(name, x, c), rows, shards, (far_0.at[i], far_1.at[i])
@@ -303,7 +282,7 @@
         out[...] = jnp.dot(part, packed[...], preferred_element_type=F32).astype(out.dtype)
 
 
-def last_call(shards, far, so_far, tests):
+def last_call(shards, far, near, tests):
     rows = TEST // NX
     return pl.pallas_call(
         last_kernel,
@@ -314,13 +293,13 @@
             jax.ShapeDtypeStruct((rows, W), BF16),
             jax.ShapeDtypeStruct((rows, W), BF16),
         ],
-        in_specs=[VMEM] * 5,
+        in_specs=[VMEM] * 8,
         out_specs=[VMEM] * 5,
         compiler_params=pltpu.CompilerParams(vmem_limit_bytes=8 << 20),
         cost_estimate=pl.CostEstimate(
             flops=4 * W * Q * Q, bytes_accessed=4 * Q * Q, transcendentals=0
         ),
-    )(shards, *far, so_far, tests)
+    )(shards, *far, *near, tests)
 
 
 def spread_kernel(live_h, packed, out, picks, live, sem):
@@ -393,8 +372,7 @@
     early_other = send(early, SWAP)
     far_other = send(far_row, SWAP)
     shards = jnp.concatenate([early, far_row, early_other, far_other])
-    so_far = half_call(shards, own_0, own_1, other_0, other_1)
-    packed, mine, to_a, to_b, opposite = last_call(shards, far, so_far, x_test)
+    packed, mine, to_a, to_b, opposite = last_call(shards, far, (own_0, own_1, other_0, other_1), x_test)
     weights, picks = spread_call(live, packed)
     predictions = end_sum(
         picks, mine, send(opposite, OPPOSITE), send(to_a, PAIR_A), send(to_b, PAIR_B)

time: 67.7 us -> 67.6 us (level)
    pallas_call x1 -> x0, Pallas kernels: 1.27 us -> none  [half_call(): pl.pallas_call(half_kernel, out_shape=jax.ShapeDtypeStruct((Q, W), F32),...]
    pallas_call x1, Pallas kernels: 1.82 us -> 2.89 us  [last_call(): pl.pallas_call(last_kernel, out_shape=[jax.ShapeDtypeStruct((Q, W), BF16)...]
  transfers between devices with their start and end apart: 19 -> 19, of which waited for: 7 -> 8; matrix products, arithmetic and copies ran while one was open for 3% -> 3% of each run, Pallas kernels for 7% -> 7%
where the time goes in v8:
time: 67.6 us; the launch traced here: 67.5 us
  starting transfers between devices  31.2 us (46%)
  waiting for transfers between devices  21.8 us (32%)
  Pallas kernels  10.2 us (15%)
  local copies, waits for them, and re-layouts  1.91 us (3%)
  other arithmetic  1.6 us (2%)
  between operations  0.85 us (1%)
    ppermute x19, starting transfers between devices, send(): return lax.ppermute(value, ('tm', 'vox'), pairs)  31.2 us
    ppermute x19, waiting for transfers between devices, send(): return lax.ppermute(value, ('tm', 'vox'), pairs)  21.8 us
    pallas_call x1, Pallas kernels, last_call(): pl.pallas_call(last_kernel, out_shape=[jax.ShapeDtypeStruct((Q, W), BF16)...  2.89 us
    pallas_call x1, Pallas kernels, start_call(): pl.pallas_call(start_kernel, out_shape=[jax.ShapeDtypeStruct((2, BLK, Q),...  2.87 us
    pallas_call x1, Pallas kernels, rest_call(): pl.pallas_call(rest_kernel, out_shape=[jax.ShapeDtypeStruct((BLK, Q), F32...  2.63 us
    unnamed x9, local copies, waits for them, and re-layouts  1.76 us
    pallas_call x1, Pallas kernels, spread_call(): pl.pallas_call(spread_kernel, out_shape=[jax.ShapeDtypeStruct((Q, VD), BF...  1.7 us
  transfers between devices with their start and end apart: 19, of which 8 were waited for; matrix products, arithmetic and copies ran while one was open for 3% of the time, Pallas kernels for 7%

profile of v8, /device:TPU:0, one launch (start us, length us, event | category | flops | bytes accessed | tf_op | source)
XLA Modules:
  0.0 67.5 jit_solution(2781713191777473170)
XLA Ops:
  0.6 0.0 copy-start.1
  0.6 2.9 %shard_map.95 = (bf16[2,128,1024]{2,1,0:T(8,128)(2,1)S(1)}, bf16[2,128,1024]{2,1,0:T(8,128)(2,1)S(1)}, bf16[256,768]{1,0:T(8,128)(2,1)S(1)}) custom-call(f32[20]{0:T(128)} %lambdas_h.3, s32[3]{0:T(128)} %lam_index_h.3, s32[3]{0:T(128)} %live_h.5, f32[1,4096]{1,0:T(1,128)} %bitcast.25, bf16[768,4096]{1,0:T(8,128)(2,1)} %u.3, bf16[768,384]{1,0:T(8,128)(2,1)} %y.1), custom_call_target="tpu_custom_call" | custom-call | flops 805306368 | bytes 3145728 | tf_op jit(solution)/shard_map/pallas_call | solution.py:144
  3.5 1.7 %collective-permute-start.6 = (bf16[2,128,1024]{2,1,0:T(8,128)(2,1)S(1)}, bf16[2,128,1024]{2,1,0:T(8,128)(2,1)S(1)}, u32[]{:S(2)}, u32[]{:S(2)}) collective-permute-start(bf16[2,128,1024]{2,1,0:T(8,128)(2,1)S(1)} %get-tuple-element.32), channel_id=1, source_target_pairs={{0,32},{1,97},{2,34},{3,99},{4,36},{5,101},{6,38},{7,103},{8,40},{... | collective-permute-start | bytes 1572872 | tf_op jit(solution)/shard_map/ppermute | solution.py:60
  5.2 1.6 %collective-permute-start = (bf16[1024,128]{1,0:T(8,128)(2,1)}, bf16[1024,128]{1,0:T(8,128)(2,1)S(1)}, u32[]{:S(2)}, u32[]{:S(2)}) collective-permute-start(bf16[1024,128]{1,0:T(8,128)(2,1)} %a.1), channel_id=1, source_target_pairs={{0,8},{1,3},{2,10},{3,5},{4,12},{5,7},{6,14},{7,1},{8,16},{9,11},{... | collective-permute-start | bytes 786440 | tf_op jit(solution)/shard_map/ppermute | solution.py:60
  6.7 2.9 %collective-permute-start.1 = (bf16[1024,128]{1,0:T(8,128)(2,1)}, bf16[1024,128]{1,0:T(8,128)(2,1)S(1)}, u32[]{:S(2)}, u32[]{:S(2)}) collective-permute-start(bf16[1024,128]{1,0:T(8,128)(2,1)} %a.1), channel_id=1, source_target_pairs={{0,16},{1,5},{2,18},{3,7},{4,20},{5,1},{6,22},{7,3},{8,24},{9,13},... | collective-permute-start | bytes 786440 | tf_op jit(solution)/shard_map/ppermute | solution.py:60
  9.7 1.3 %collective-permute-start.2 = (bf16[1024,128]{1,0:T(8,128)(2,1)}, bf16[1024,128]{1,0:T(8,128)(2,1)S(1)}, u32[]{:S(2)}, u32[]{:S(2)}) collective-permute-start(bf16[1024,128]{1,0:T(8,128)(2,1)} %a.1), channel_id=1, source_target_pairs={{0,24},{1,7},{2,26},{3,1},{4,28},{5,3},{6,30},{7,5},{8,0},{9,15},{... | collective-permute-start | bytes 786440 | tf_op jit(solution)/shard_map/ppermute | solution.py:60
  11.0 0.5 collective-permute-start.5
  11.5 2.6 %shard_map.97 = (f32[128,1024]{1,0:T(8,128)S(1)}, f32[128,1024]{1,0:T(8,128)S(1)}, f32[128,1024]{1,0:T(8,128)S(1)}, f32[128,1024]{1,0:T(8,128)S(1)}) custom-call(f32[20]{0:T(128)} %lambdas_h.3, s32[3]{0:T(128)} %lam_index_h.3, s32[3]{0:T(128)} %live_h.5, f32[1,4096]{1,0:T(1,128)} %bitcast.26, bf16[768,4096]{1,0:T(8,128)(2,1)} %u.3, ...), custom_call_target="tpu_custom_call" | custom-call | flops 805306368 | bytes 3145728 | tf_op jit(solution)/shard_map/pallas_call | solution.py:180
  14.2 0.0 collective-permute-done.6
  14.2 0.1 fusion.5
  14.2 2.8 %collective-permute-start.8 = (bf16[128,1024]{1,0:T(8,128)(2,1)S(1)}, bf16[128,1024]{1,0:T(8,128)(2,1)S(1)}, u32[]{:S(2)}, u32[]{:S(2)}) collective-permute-start(bf16[128,1024]{1,0:T(8,128)(2,1)S(1)} %fusion.5), channel_id=1, source_target_pairs={{0,96},{1,33},{2,98},{3,35},{4,100},{5,37},{6,102},{7,39},{8,104},... | collective-permute-start | bytes 786440 | tf_op jit(solution)/shard_map/ppermute | solution.py:60
  17.1 0.0 collective-permute-done.b
  17.1 0.0 collective-permute-done.1.c
  17.1 0.0 collective-permute-done.2.d
  17.1 0.0 copy-done.1
  17.1 0.1 shard_map.96
  17.2 2.0 %collective-permute-start.3 = (bf16[4,1024,128]{2,1,0:T(8,128)(2,1)S(1)}, bf16[4,1024,128]{2,1,0:T(8,128)(2,1)S(1)}, u32[]{:S(2)}, u32[]{:S(2)}) collective-permute-start(bf16[4,1024,128]{2,1,0:T(8,128)(2,1)S(1)} %shard_map.96), channel_id=1, source_target_pairs={{0,2},{1,9},{2,4},{3,11},{4,6},{5,13},{6,0},{7,15},{8,10},{9,17},{... | collective-permute-start | bytes 3145736 | tf_op jit(solution)/shard_map/ppermute | solution.py:60
  19.2 2.2 %collective-permute-start.4 = (bf16[4,1024,128]{2,1,0:T(8,128)(2,1)S(1)}, bf16[4,1024,128]{2,1,0:T(8,128)(2,1)S(1)}, u32[]{:S(2)}, u32[]{:S(2)}) collective-permute-start(bf16[4,1024,128]{2,1,0:T(8,128)(2,1)S(1)} %shard_map.96), channel_id=1, source_target_pairs={{0,6},{1,25},{2,0},{3,27},{4,2},{5,29},{6,4},{7,31},{8,14},{9,1},{... | collective-permute-start | bytes 3145736 | tf_op jit(solution)/shard_map/ppermute | solution.py:60
  21.4 1.6 %collective-permute-done.5 = bf16[2,128,1024]{2,1,0:T(8,128)(2,1)S(1)} collective-permute-done((bf16[2,128,1024]{2,1,0:T(8,128)(2,1)S(1)}, bf16[2,128,1024]{2,1,0:T(8,128)(2,1)S(1)}, u32[]{:S(2)}, u32[]{:S(2)}) %collective-permute-start.5) | collective-permute-done | bytes 524320 | tf_op jit(solution)/shard_map/ppermute | solution.py:60
  23.0 0.1 fusion.2
  23.1 1.6 %collective-permute-start.7 = (bf16[128,1024]{1,0:T(8,128)(2,1)S(1)}, bf16[128,1024]{1,0:T(8,128)(2,1)S(1)}, u32[]{:S(2)}, u32[]{:S(2)}) collective-permute-start(bf16[128,1024]{1,0:T(8,128)(2,1)S(1)} %fusion.2), channel_id=1, source_target_pairs={{0,96},{1,33},{2,98},{3,35},{4,100},{5,37},{6,102},{7,39},{8,104},... | collective-permute-start | bytes 786440 | tf_op jit(solution)/shard_map/ppermute | solution.py:60
  24.6 0.0 collective-permute-done.8
  24.6 0.1 fusion.1.own_0
  24.7 1.8 %collective-permute-start.10 = (bf16[128,1024]{1,0:T(8,128)(2,1)S(1)}, bf16[128,1024]{1,0:T(8,128)(2,1)S(1)}, u32[]{:S(2)}, u32[]{:S(2)}) collective-permute-start(bf16[128,1024]{1,0:T(8,128)(2,1)S(1)} %fusion.1.own_0), channel_id=1, source_target_pairs={{0,96},{1,33},{2,98},{3,35},{4,100},{5,37},{6,102},{7,39},{8,104},... | collective-permute-start | bytes 786440 | tf_op jit(solution)/shard_map/ppermute | solution.py:60
  26.6 4.2 %collective-permute-done.7 = bf16[128,1024]{1,0:T(8,128)(2,1)S(1)} collective-permute-done((bf16[128,1024]{1,0:T(8,128)(2,1)S(1)}, bf16[128,1024]{1,0:T(8,128)(2,1)S(1)}, u32[]{:S(2)}, u32[]{:S(2)}) %collective-permute-start.7) | collective-permute-done | bytes 262176 | tf_op jit(solution)/shard_map/ppermute | solution.py:60
  30.7 0.1 fusion.4.own_1
  30.8 1.6 %collective-permute-start.9 = (bf16[128,1024]{1,0:T(8,128)(2,1)S(1)}, bf16[128,1024]{1,0:T(8,128)(2,1)S(1)}, u32[]{:S(2)}, u32[]{:S(2)}) collective-permute-start(bf16[128,1024]{1,0:T(8,128)(2,1)S(1)} %fusion.4.own_1), channel_id=1, source_target_pairs={{0,96},{1,33},{2,98},{3,35},{4,100},{5,37},{6,102},{7,39},{8,104},... | collective-permute-start | bytes 786440 | tf_op jit(solution)/shard_map/ppermute | solution.py:60
  32.4 5.6 %collective-permute-start.11 = (bf16[4,1024,128]{2,1,0:T(8,128)(2,1)S(1)}, bf16[4,1024,128]{2,1,0:T(8,128)(2,1)S(1)}, u32[]{:S(2)}, u32[]{:S(2)}) collective-permute-start(bf16[4,1024,128]{2,1,0:T(8,128)(2,1)S(1)} %shard_map.96), channel_id=1, source_target_pairs={{0,4},{1,17},{2,6},{3,19},{4,0},{5,21},{6,2},{7,23},{8,12},{9,25},... | collective-permute-start | bytes 3145736 | tf_op jit(solution)/shard_map/ppermute | solution.py:60
  38.0 0.1 constant_dynamic-update-slice_fusion.5
  38.1 0.0 collective-permute-done.10.other_0
  38.1 0.1 pad_maximum_fusion.1
  38.2 0.4 collective-permute-start.14
  38.5 1.5 %collective-permute-done.9.other_1 = bf16[128,1024]{1,0:T(8,128)(2,1)S(1)} collective-permute-done((bf16[128,1024]{1,0:T(8,128)(2,1)S(1)}, bf16[128,1024]{1,0:T(8,128)(2,1)S(1)}, u32[]{:S(2)}, u32[]{:S(2)}) %collective-permute-start.9) | collective-permute-done | bytes 262176 | tf_op jit(solution)/shard_map/ppermute | solution.py:60
  40.1 0.1 pad_maximum_fusion.2
  40.1 0.3 collective-permute-start.15
  40.4 0.0 collective-permute-done.3
  40.4 0.0 collective-permute-done.4
  40.4 0.4 pad_maximum_fusion
  40.8 0.1 collective-permute-start.12
  40.9 0.1 constant_dynamic-update-slice_fusion.4
  41.0 0.1 constant_dynamic-update-slice_fusion.3
  41.2 6.3 %collective-permute-done.14.refs_0_ = bf16[2,128,1024]{2,1,0:T(8,128)(2,1)S(1)} collective-permute-done((bf16[2,128,1024]{2,1,0:T(8,128)(2,1)S(1)}, bf16[2,128,1024]{2,1,0:T(8,128)(2,1)S(1)}, u32[]{:S(2)}, u32[]{:S(2)}) %collective-permute-start.14) | collective-permute-done | bytes 524320 | tf_op jit(solution)/shard_map/ppermute | solution.py:60
  47.4 3.4 %collective-permute-done.11 = bf16[4,1024,128]{2,1,0:T(8,128)(2,1)S(1)} collective-permute-done((bf16[4,1024,128]{2,1,0:T(8,128)(2,1)S(1)}, bf16[4,1024,128]{2,1,0:T(8,128)(2,1)S(1)}, u32[]{:S(2)}, u32[]{:S(2)}) %collective-permute-start.11) | collective-permute-done | bytes 1048608 | tf_op jit(solution)/shard_map/ppermute | solution.py:60
  50.8 0.0 collective-permute-start.13
  50.8 2.2 %collective-permute-done.15.refs_1_ = bf16[2,128,1024]{2,1,0:T(8,128)(2,1)S(1)} collective-permute-done((bf16[2,128,1024]{2,1,0:T(8,128)(2,1)S(1)}, bf16[2,128,1024]{2,1,0:T(8,128)(2,1)S(1)}, u32[]{:S(2)}, u32[]{:S(2)}) %collective-permute-start.15) | collective-permute-done | bytes 524320 | tf_op jit(solution)/shard_map/ppermute | solution.py:60
  53.1 0.0 copy-start
  53.1 0.1 constant_dynamic-update-slice_fusion.2
  53.2 0.0 collective-permute-done.12
  53.2 0.4 constant_dynamic-update-slice_fusion.1
  53.6 0.0 collective-permute-done.13
  53.6 0.1 constant_dynamic-update-slice_fusion.shards
  53.8 0.9 %copy-done = bf16[1024,1024]{1,0:T(8,128)(2,1)S(1)} copy-done((bf16[1024,1024]{1,0:T(8,128)(2,1)S(1)}, bf16[1024,1024]{1,0:T(8,128)(2,1)}, u32[]{:S(2)}) %copy-start) | copy-done | bytes 2097176
  54.6 2.9 %shard_map.100 = (bf16[1024,256]{1,0:T(8,128)(2,1)S(1)}, f32[256,256]{1,0:T(8,128)S(1)}, bf16[256,256]{1,0:T(8,128)(2,1)S(1)}, bf16[256,256]{1,0:T(8,128)(2,1)S(1)}, bf16[256,256]{1,0:T(8,128)(2,1)S(1)}) custom-call(bf16[32,1024,128]{2,1,0:T(8,128)(2,1)S(1)} %constant_dynamic-update-slice_fusion.shards, bf16[2,128,1024]{2,1,0:T(8,128)(2,1)S(1)} %get-tuple-element.41.far_0, ...), custom_call_target="tpu_custom_call" | custom-call | flops 1073741824 | bytes 4194304 | tf_op jit(solution)/shard_map/pallas_call | solution.py:287
  57.5 0.9 %collective-permute-start.18 = (bf16[256,256]{1,0:T(8,128)(2,1)S(1)}, bf16[256,256]{1,0:T(8,128)(2,1)S(1)}, u32[]{:S(2)}, u32[]{:S(2)}) collective-permute-start(bf16[256,256]{1,0:T(8,128)(2,1)S(1)} %get-tuple-element.49), channel_id=1, source_target_pairs={{0,96},{1,33},{2,98},{3,35},{4,100},{5,37},{6,102},{7,39},{8,104},... | collective-permute-start | bytes 393224 | tf_op jit(solution)/shard_map/ppermute | solution.py:60
  58.5 0.0 collective-permute-start.17
  58.5 3.8 %collective-permute-start.16 = (bf16[256,256]{1,0:T(8,128)(2,1)S(1)}, bf16[256,256]{1,0:T(8,128)(2,1)S(1)}, u32[]{:S(2)}, u32[]{:S(2)}) collective-permute-start(bf16[256,256]{1,0:T(8,128)(2,1)S(1)} %get-tuple-element.47), channel_id=1, source_target_pairs={{0,64},{1,65},{2,66},{3,67},{4,68},{5,69},{6,70},{7,71},{8,72},{9,... | collective-permute-start | bytes 393224 | tf_op jit(solution)/shard_map/ppermute | solution.py:60
  62.3 1.7 %shard_map.101 = (bf16[1024,384]{1,0:T(8,128)(2,1)}, f32[2,8,384]{2,1,0:T(8,128)S(1)}) custom-call(s32[3]{0:T(128)} %live_h.5, bf16[1024,256]{1,0:T(8,128)(2,1)S(1)} %get-tuple-element.43.packed), custom_call_target="tpu_custom_call" | custom-call | flops 1048576 | bytes 4194304 | tf_op jit(solution)/shard_map/pallas_call | solution.py:320
  64.1 0.8 %collective-permute-done.18 = bf16[256,256]{1,0:T(8,128)(2,1)S(1)} collective-permute-done((bf16[256,256]{1,0:T(8,128)(2,1)S(1)}, bf16[256,256]{1,0:T(8,128)(2,1)S(1)}, u32[]{:S(2)}, u32[]{:S(2)}) %collective-permute-start.18) | collective-permute-done | bytes 131104 | tf_op jit(solution)/shard_map/ppermute | solution.py:60
  64.8 0.0 collective-permute-done.17
  64.8 1.8 %collective-permute-done.16 = bf16[256,256]{1,0:T(8,128)(2,1)S(1)} collective-permute-done((bf16[256,256]{1,0:T(8,128)(2,1)S(1)}, bf16[256,256]{1,0:T(8,128)(2,1)S(1)}, u32[]{:S(2)}, u32[]{:S(2)}) %collective-permute-start.16) | collective-permute-done | bytes 131104 | tf_op jit(solution)/shard_map/ppermute | solution.py:60
  66.7 0.1 convert_add_fusion.4
  66.8 0.7 %fusion.6 = bf16[256,384]{1,0:T(8,128)(2,1)} fusion(bf16[256,128]{1,0:T(8,128)(2,1)S(1)} %get-tuple-element.53, bf16[256,128]{1,0:T(8,128)(2,1)S(1)} %get-tuple-element.52, pred[384]{0:T(512)(128)(4,1)S(1)} %get-tuple-element.51, pred[384]{0:T(512)(128)(4,1)S(1)} %get-tuple-element.50), kind=kLoop, calls=%fused_computation.14 | loop fusion | flops 1376256 | bytes 328448 | tf_op jit(solution)/shard_map/convert_element_type | solution.py:342
  (4 shorter events, 0.0 us)
Async XLA Ops:
  0.6 16.5 %copy-start.1 = (bf16[1024,128]{1,0:T(8,128)(2,1)S(1)}, bf16[1024,128]{1,0:T(8,128)(2,1)}, u32[]{:S(2)}) copy-start(bf16[1024,128]{1,0:T(8,128)(2,1)} %a.1) | copy-start | bytes 786436
  3.5 10.7 %collective-permute-start.6 = (bf16[2,128,1024]{2,1,0:T(8,128)(2,1)S(1)}, bf16[2,128,1024]{2,1,0:T(8,128)(2,1)S(1)}, u32[]{:S(2)}, u32[]{:S(2)}) collective-permute-start(bf16[2,128,1024]{2,1,0:T(8,128)(2,1)S(1)} %get-tuple-element.32), channel_id=1, source_target_pairs={{0,32},{1,97},{2,34},{3,99},{4,36},{5,101},{6,38},{7,103},{8,40},{... | collective-permute-start | bytes 1572872 | tf_op jit(solution)/shard_map/ppermute | solution.py:60
  5.2 11.9 %collective-permute-start = (bf16[1024,128]{1,0:T(8,128)(2,1)}, bf16[1024,128]{1,0:T(8,128)(2,1)S(1)}, u32[]{:S(2)}, u32[]{:S(2)}) collective-permute-start(bf16[1024,128]{1,0:T(8,128)(2,1)} %a.1), channel_id=1, source_target_pairs={{0,8},{1,3},{2,10},{3,5},{4,12},{5,7},{6,14},{7,1},{8,16},{9,11},{... | collective-permute-start | bytes 786440 | tf_op jit(solution)/shard_map/ppermute | solution.py:60
  6.7 10.3 %collective-permute-start.1 = (bf16[1024,128]{1,0:T(8,128)(2,1)}, bf16[1024,128]{1,0:T(8,128)(2,1)S(1)}, u32[]{:S(2)}, u32[]{:S(2)}) collective-permute-start(bf16[1024,128]{1,0:T(8,128)(2,1)} %a.1), channel_id=1, source_target_pairs={{0,16},{1,5},{2,18},{3,7},{4,20},{5,1},{6,22},{7,3},{8,24},{9,13},... | collective-permute-start | bytes 786440 | tf_op jit(solution)/shard_map/ppermute | solution.py:60
  9.7 7.4 %collective-permute-start.2 = (bf16[1024,128]{1,0:T(8,128)(2,1)}, bf16[1024,128]{1,0:T(8,128)(2,1)S(1)}, u32[]{:S(2)}, u32[]{:S(2)}) collective-permute-start(bf16[1024,128]{1,0:T(8,128)(2,1)} %a.1), channel_id=1, source_target_pairs={{0,24},{1,7},{2,26},{3,1},{4,28},{5,3},{6,30},{7,5},{8,0},{9,15},{... | collective-permute-start | bytes 786440 | tf_op jit(solution)/shard_map/ppermute | solution.py:60
  11.0 12.0 %collective-permute-start.5 = (bf16[2,128,1024]{2,1,0:T(8,128)(2,1)S(1)}, bf16[2,128,1024]{2,1,0:T(8,128)(2,1)S(1)}, u32[]{:S(2)}, u32[]{:S(2)}) collective-permute-start(bf16[2,128,1024]{2,1,0:T(8,128)(2,1)S(1)} %get-tuple-element.29), channel_id=1, source_target_pairs={{0,32},{1,97},{2,34},{3,99},{4,36},{5,101},{6,38},{7,103},{8,40},{... | collective-permute-start | bytes 1572872 | tf_op jit(solution)/shard_map/ppermute | solution.py:60
  14.2 10.4 %collective-permute-start.8 = (bf16[128,1024]{1,0:T(8,128)(2,1)S(1)}, bf16[128,1024]{1,0:T(8,128)(2,1)S(1)}, u32[]{:S(2)}, u32[]{:S(2)}) collective-permute-start(bf16[128,1024]{1,0:T(8,128)(2,1)S(1)} %fusion.5), channel_id=1, source_target_pairs={{0,96},{1,33},{2,98},{3,35},{4,100},{5,37},{6,102},{7,39},{8,104},... | collective-permute-start | bytes 786440 | tf_op jit(solution)/shard_map/ppermute | solution.py:60
  17.2 23.2 %collective-permute-start.3 = (bf16[4,1024,128]{2,1,0:T(8,128)(2,1)S(1)}, bf16[4,1024,128]{2,1,0:T(8,128)(2,1)S(1)}, u32[]{:S(2)}, u32[]{:S(2)}) collective-permute-start(bf16[4,1024,128]{2,1,0:T(8,128)(2,1)S(1)} %shard_map.96), channel_id=1, source_target_pairs={{0,2},{1,9},{2,4},{3,11},{4,6},{5,13},{6,0},{7,15},{8,10},{9,17},{... | collective-permute-start | bytes 3145736 | tf_op jit(solution)/shard_map/ppermute | solution.py:60
  19.2 21.2 %collective-permute-start.4 = (bf16[4,1024,128]{2,1,0:T(8,128)(2,1)S(1)}, bf16[4,1024,128]{2,1,0:T(8,128)(2,1)S(1)}, u32[]{:S(2)}, u32[]{:S(2)}) collective-permute-start(bf16[4,1024,128]{2,1,0:T(8,128)(2,1)S(1)} %shard_map.96), channel_id=1, source_target_pairs={{0,6},{1,25},{2,0},{3,27},{4,2},{5,29},{6,4},{7,31},{8,14},{9,1},{... | collective-permute-start | bytes 3145736 | tf_op jit(solution)/shard_map/ppermute | solution.py:60
  23.1 7.7 %collective-permute-start.7 = (bf16[128,1024]{1,0:T(8,128)(2,1)S(1)}, bf16[128,1024]{1,0:T(8,128)(2,1)S(1)}, u32[]{:S(2)}, u32[]{:S(2)}) collective-permute-start(bf16[128,1024]{1,0:T(8,128)(2,1)S(1)} %fusion.2), channel_id=1, source_target_pairs={{0,96},{1,33},{2,98},{3,35},{4,100},{5,37},{6,102},{7,39},{8,104},... | collective-permute-start | bytes 786440 | tf_op jit(solution)/shard_map/ppermute | solution.py:60
  24.7 13.4 %collective-permute-start.10 = (bf16[128,1024]{1,0:T(8,128)(2,1)S(1)}, bf16[128,1024]{1,0:T(8,128)(2,1)S(1)}, u32[]{:S(2)}, u32[]{:S(2)}) collective-permute-start(bf16[128,1024]{1,0:T(8,128)(2,1)S(1)} %fusion.1.own_0), channel_id=1, source_target_pairs={{0,96},{1,33},{2,98},{3,35},{4,100},{5,37},{6,102},{7,39},{8,104},... | collective-permute-start | bytes 786440 | tf_op jit(solution)/shard_map/ppermute | solution.py:60
  30.8 9.2 %collective-permute-start.9 = (bf16[128,1024]{1,0:T(8,128)(2,1)S(1)}, bf16[128,1024]{1,0:T(8,128)(2,1)S(1)}, u32[]{:S(2)}, u32[]{:S(2)}) collective-permute-start(bf16[128,1024]{1,0:T(8,128)(2,1)S(1)} %fusion.4.own_1), channel_id=1, source_target_pairs={{0,96},{1,33},{2,98},{3,35},{4,100},{5,37},{6,102},{7,39},{8,104},... | collective-permute-start | bytes 786440 | tf_op jit(solution)/shard_map/ppermute | solution.py:60
  32.4 18.4 %collective-permute-start.11 = (bf16[4,1024,128]{2,1,0:T(8,128)(2,1)S(1)}, bf16[4,1024,128]{2,1,0:T(8,128)(2,1)S(1)}, u32[]{:S(2)}, u32[]{:S(2)}) collective-permute-start(bf16[4,1024,128]{2,1,0:T(8,128)(2,1)S(1)} %shard_map.96), channel_id=1, source_target_pairs={{0,4},{1,17},{2,6},{3,19},{4,0},{5,21},{6,2},{7,23},{8,12},{9,25},... | collective-permute-start | bytes 3145736 | tf_op jit(solution)/shard_map/ppermute | solution.py:60
  38.2 9.3 %collective-permute-start.14 = (bf16[2,128,1024]{2,1,0:T(8,128)(2,1)S(1)}, bf16[2,128,1024]{2,1,0:T(8,128)(2,1)S(1)}, u32[]{:S(2)}, u32[]{:S(2)}) collective-permute-start(bf16[2,128,1024]{2,1,0:T(8,128)(2,1)S(1)} %pad_maximum_fusion.1), channel_id=1, source_target_pairs={{0,32},{1,97},{2,34},{3,99},{4,36},{5,101},{6,38},{7,103},{8,40},{... | collective-permute-start | bytes 1572872 | tf_op jit(solution)/shard_map/ppermute | solution.py:60
  40.1 12.9 %collective-permute-start.15 = (bf16[2,128,1024]{2,1,0:T(8,128)(2,1)S(1)}, bf16[2,128,1024]{2,1,0:T(8,128)(2,1)S(1)}, u32[]{:S(2)}, u32[]{:S(2)}) collective-permute-start(bf16[2,128,1024]{2,1,0:T(8,128)(2,1)S(1)} %pad_maximum_fusion.2), channel_id=1, source_target_pairs={{0,32},{1,97},{2,34},{3,99},{4,36},{5,101},{6,38},{7,103},{8,40},{... | collective-permute-start | bytes 1572872 | tf_op jit(solution)/shard_map/ppermute | solution.py:60
  40.8 12.4 %collective-permute-start.12 = (bf16[12,1024,128]{2,1,0:T(8,128)(2,1)S(1)}, bf16[12,1024,128]{2,1,0:T(8,128)(2,1)S(1)}, u32[]{:S(2)}, u32[]{:S(2)}) collective-permute-start(bf16[12,1024,128]{2,1,0:T(8,128)(2,1)S(1)} %pad_maximum_fusion), channel_id=1, source_target_pairs={{0,1},{1,0},{2,3},{3,2},{4,5},{5,4},{6,7},{7,6},{8,9},{9,8},{10,11... | collective-permute-start | bytes 9437192 | tf_op jit(solution)/shard_map/ppermute | solution.py:60
  50.8 2.8 %collective-permute-start.13 = (bf16[4,1024,128]{2,1,0:T(8,128)(2,1)S(1)}, bf16[4,1024,128]{2,1,0:T(8,128)(2,1)S(1)}, u32[]{:S(2)}, u32[]{:S(2)}) collective-permute-start(bf16[4,1024,128]{2,1,0:T(8,128)(2,1)S(1)} %collective-permute-done.11), channel_id=1, source_target_pairs={{0,1},{1,0},{2,3},{3,2},{4,5},{5,4},{6,7},{7,6},{8,9},{9,8},{10,11... | collective-permute-start | bytes 3145736 | tf_op jit(solution)/shard_map/ppermute | solution.py:60
  53.1 1.6 %copy-start = (bf16[1024,1024]{1,0:T(8,128)(2,1)S(1)}, bf16[1024,1024]{1,0:T(8,128)(2,1)}, u32[]{:S(2)}) copy-start(bf16[1024,1024]{1,0:T(8,128)(2,1)} %tests.1) | copy-start | bytes 6291460
  57.5 7.3 %collective-permute-start.18 = (bf16[256,256]{1,0:T(8,128)(2,1)S(1)}, bf16[256,256]{1,0:T(8,128)(2,1)S(1)}, u32[]{:S(2)}, u32[]{:S(2)}) collective-permute-start(bf16[256,256]{1,0:T(8,128)(2,1)S(1)} %get-tuple-element.49), channel_id=1, source_target_pairs={{0,96},{1,33},{2,98},{3,35},{4,100},{5,37},{6,102},{7,39},{8,104},... | collective-permute-start | bytes 393224 | tf_op jit(solution)/shard_map/ppermute | solution.py:60
  58.5 6.4 %collective-permute-start.17 = (bf16[256,256]{1,0:T(8,128)(2,1)S(1)}, bf16[256,256]{1,0:T(8,128)(2,1)S(1)}, u32[]{:S(2)}, u32[]{:S(2)}) collective-permute-start(bf16[256,256]{1,0:T(8,128)(2,1)S(1)} %get-tuple-element.48), channel_id=1, source_target_pairs={{0,32},{1,97},{2,34},{3,99},{4,36},{5,101},{6,38},{7,103},{8,40},{... | collective-permute-start | bytes 393224 | tf_op jit(solution)/shard_map/ppermute | solution.py:60
  58.5 8.2 %collective-permute-start.16 = (bf16[256,256]{1,0:T(8,128)(2,1)S(1)}, bf16[256,256]{1,0:T(8,128)(2,1)S(1)}, u32[]{:S(2)}, u32[]{:S(2)}) collective-permute-start(bf16[256,256]{1,0:T(8,128)(2,1)S(1)} %get-tuple-element.47), channel_id=1, source_target_pairs={{0,64},{1,65},{2,66},{3,67},{4,68},{5,69},{6,70},{7,71},{8,72},{9,... | collective-permute-start | bytes 393224 | tf_op jit(solution)/shard_map/ppermute | solution.py:60

commit v9 on v8

--- a/solution.py
+++ b/solution.py
@@ -375,7 +375,7 @@
     packed, mine, to_a, to_b, opposite = last_call(shards, far, (own_0, own_1, other_0, other_1), x_test)
     weights, picks = spread_call(live, packed)
     predictions = end_sum(
-        picks, mine, send(opposite, OPPOSITE), send(to_a, PAIR_A), send(to_b, PAIR_B)
+        picks, mine, send(to_b, PAIR_B), send(to_a, PAIR_A), send(opposite, OPPOSITE)
     )
     return weights, predictions
 

time: 67.6 us -> 67.3 us (level)
  no operation moved by 1% of the time
where the time goes in v9:
time: 67.3 us; the launch traced here: 67.1 us
  starting transfers between devices  30.6 us (45%)
  waiting for transfers between devices  22 us (33%)
  Pallas kernels  10.2 us (15%)
  local copies, waits for them, and re-layouts  1.91 us (3%)
  other arithmetic  1.6 us (2%)
  between operations  0.85 us (1%)
    ppermute x19, starting transfers between devices, send(): return lax.ppermute(value, ('tm', 'vox'), pairs)  30.6 us
    ppermute x19, waiting for transfers between devices, send(): return lax.ppermute(value, ('tm', 'vox'), pairs)  22 us
    pallas_call x1, Pallas kernels, last_call(): pl.pallas_call(last_kernel, out_shape=[jax.ShapeDtypeStruct((Q, W), BF16)...  2.89 us
    pallas_call x1, Pallas kernels, start_call(): pl.pallas_call(start_kernel, out_shape=[jax.ShapeDtypeStruct((2, BLK, Q),...  2.87 us
    pallas_call x1, Pallas kernels, rest_call(): pl.pallas_call(rest_kernel, out_shape=[jax.ShapeDtypeStruct((BLK, Q), F32...  2.63 us
    unnamed x9, local copies, waits for them, and re-layouts  1.76 us
    pallas_call x1, Pallas kernels, spread_call(): pl.pallas_call(spread_kernel, out_shape=[jax.ShapeDtypeStruct((Q, VD), BF...  1.7 us
  transfers between devices with their start and end apart: 19, of which 8 were waited for; matrix products, arithmetic and copies ran while one was open for 3% of the time, Pallas kernels for 7%

profile of v9, /device:TPU:0, one launch (start us, length us, event | category | flops | bytes accessed | tf_op | source)
XLA Modules:
  0.0 67.1 jit_solution(2524055384355752207)
XLA Ops:
  0.6 0.0 copy-start.1
  0.6 2.9 %shard_map.95 = (bf16[2,128,1024]{2,1,0:T(8,128)(2,1)S(1)}, bf16[2,128,1024]{2,1,0:T(8,128)(2,1)S(1)}, bf16[256,768]{1,0:T(8,128)(2,1)S(1)}) custom-call(f32[20]{0:T(128)} %lambdas_h.3, s32[3]{0:T(128)} %lam_index_h.3, s32[3]{0:T(128)} %live_h.5, f32[1,4096]{1,0:T(1,128)} %bitcast.25, bf16[768,4096]{1,0:T(8,128)(2,1)} %u.3, bf16[768,384]{1,0:T(8,128)(2,1)} %y.1), custom_call_target="tpu_custom_call" | custom-call | flops 805306368 | bytes 3145728 | tf_op jit(solution)/shard_map/pallas_call | solution.py:144
  3.5 1.7 %collective-permute-start.6 = (bf16[2,128,1024]{2,1,0:T(8,128)(2,1)S(1)}, bf16[2,128,1024]{2,1,0:T(8,128)(2,1)S(1)}, u32[]{:S(2)}, u32[]{:S(2)}) collective-permute-start(bf16[2,128,1024]{2,1,0:T(8,128)(2,1)S(1)} %get-tuple-element.32), channel_id=1, source_target_pairs={{0,32},{1,97},{2,34},{3,99},{4,36},{5,101},{6,38},{7,103},{8,40},{... | collective-permute-start | bytes 1572872 | tf_op jit(solution)/shard_map/ppermute | solution.py:60
  5.2 1.6 %collective-permute-start = (bf16[1024,128]{1,0:T(8,128)(2,1)}, bf16[1024,128]{1,0:T(8,128)(2,1)S(1)}, u32[]{:S(2)}, u32[]{:S(2)}) collective-permute-start(bf16[1024,128]{1,0:T(8,128)(2,1)} %a.1), channel_id=1, source_target_pairs={{0,8},{1,3},{2,10},{3,5},{4,12},{5,7},{6,14},{7,1},{8,16},{9,11},{... | collective-permute-start | bytes 786440 | tf_op jit(solution)/shard_map/ppermute | solution.py:60
  6.7 2.9 %collective-permute-start.1 = (bf16[1024,128]{1,0:T(8,128)(2,1)}, bf16[1024,128]{1,0:T(8,128)(2,1)S(1)}, u32[]{:S(2)}, u32[]{:S(2)}) collective-permute-start(bf16[1024,128]{1,0:T(8,128)(2,1)} %a.1), channel_id=1, source_target_pairs={{0,16},{1,5},{2,18},{3,7},{4,20},{5,1},{6,22},{7,3},{8,24},{9,13},... | collective-permute-start | bytes 786440 | tf_op jit(solution)/shard_map/ppermute | solution.py:60
  9.7 1.3 %collective-permute-start.2 = (bf16[1024,128]{1,0:T(8,128)(2,1)}, bf16[1024,128]{1,0:T(8,128)(2,1)S(1)}, u32[]{:S(2)}, u32[]{:S(2)}) collective-permute-start(bf16[1024,128]{1,0:T(8,128)(2,1)} %a.1), channel_id=1, source_target_pairs={{0,24},{1,7},{2,26},{3,1},{4,28},{5,3},{6,30},{7,5},{8,0},{9,15},{... | collective-permute-start | bytes 786440 | tf_op jit(solution)/shard_map/ppermute | solution.py:60
  11.0 0.5 collective-permute-start.5
  11.5 2.6 %shard_map.97 = (f32[128,1024]{1,0:T(8,128)S(1)}, f32[128,1024]{1,0:T(8,128)S(1)}, f32[128,1024]{1,0:T(8,128)S(1)}, f32[128,1024]{1,0:T(8,128)S(1)}) custom-call(f32[20]{0:T(128)} %lambdas_h.3, s32[3]{0:T(128)} %lam_index_h.3, s32[3]{0:T(128)} %live_h.5, f32[1,4096]{1,0:T(1,128)} %bitcast.26, bf16[768,4096]{1,0:T(8,128)(2,1)} %u.3, ...), custom_call_target="tpu_custom_call" | custom-call | flops 805306368 | bytes 3145728 | tf_op jit(solution)/shard_map/pallas_call | solution.py:180
  14.2 0.0 collective-permute-done.6
  14.2 0.1 fusion.5
  14.2 2.8 %collective-permute-start.8 = (bf16[128,1024]{1,0:T(8,128)(2,1)S(1)}, bf16[128,1024]{1,0:T(8,128)(2,1)S(1)}, u32[]{:S(2)}, u32[]{:S(2)}) collective-permute-start(bf16[128,1024]{1,0:T(8,128)(2,1)S(1)} %fusion.5), channel_id=1, source_target_pairs={{0,96},{1,33},{2,98},{3,35},{4,100},{5,37},{6,102},{7,39},{8,104},... | collective-permute-start | bytes 786440 | tf_op jit(solution)/shard_map/ppermute | solution.py:60
  17.1 0.0 collective-permute-done.b
  17.1 0.0 collective-permute-done.1.c
  17.1 0.0 collective-permute-done.2.d
  17.1 0.0 copy-done.1
  17.1 0.1 shard_map.96
  17.2 2.0 %collective-permute-start.3 = (bf16[4,1024,128]{2,1,0:T(8,128)(2,1)S(1)}, bf16[4,1024,128]{2,1,0:T(8,128)(2,1)S(1)}, u32[]{:S(2)}, u32[]{:S(2)}) collective-permute-start(bf16[4,1024,128]{2,1,0:T(8,128)(2,1)S(1)} %shard_map.96), channel_id=1, source_target_pairs={{0,2},{1,9},{2,4},{3,11},{4,6},{5,13},{6,0},{7,15},{8,10},{9,17},{... | collective-permute-start | bytes 3145736 | tf_op jit(solution)/shard_map/ppermute | solution.py:60
  19.2 2.2 %collective-permute-start.4 = (bf16[4,1024,128]{2,1,0:T(8,128)(2,1)S(1)}, bf16[4,1024,128]{2,1,0:T(8,128)(2,1)S(1)}, u32[]{:S(2)}, u32[]{:S(2)}) collective-permute-start(bf16[4,1024,128]{2,1,0:T(8,128)(2,1)S(1)} %shard_map.96), channel_id=1, source_target_pairs={{0,6},{1,25},{2,0},{3,27},{4,2},{5,29},{6,4},{7,31},{8,14},{9,1},{... | collective-permute-start | bytes 3145736 | tf_op jit(solution)/shard_map/ppermute | solution.py:60
  21.4 1.6 %collective-permute-done.5 = bf16[2,128,1024]{2,1,0:T(8,128)(2,1)S(1)} collective-permute-done((bf16[2,128,1024]{2,1,0:T(8,128)(2,1)S(1)}, bf16[2,128,1024]{2,1,0:T(8,128)(2,1)S(1)}, u32[]{:S(2)}, u32[]{:S(2)}) %collective-permute-start.5) | collective-permute-done | bytes 524320 | tf_op jit(solution)/shard_map/ppermute | solution.py:60
  23.0 0.1 fusion.2
  23.1 1.6 %collective-permute-start.7 = (bf16[128,1024]{1,0:T(8,128)(2,1)S(1)}, bf16[128,1024]{1,0:T(8,128)(2,1)S(1)}, u32[]{:S(2)}, u32[]{:S(2)}) collective-permute-start(bf16[128,1024]{1,0:T(8,128)(2,1)S(1)} %fusion.2), channel_id=1, source_target_pairs={{0,96},{1,33},{2,98},{3,35},{4,100},{5,37},{6,102},{7,39},{8,104},... | collective-permute-start | bytes 786440 | tf_op jit(solution)/shard_map/ppermute | solution.py:60
  24.6 0.0 collective-permute-done.8
  24.6 0.1 fusion.1.own_0
  24.7 1.8 %collective-permute-start.10 = (bf16[128,1024]{1,0:T(8,128)(2,1)S(1)}, bf16[128,1024]{1,0:T(8,128)(2,1)S(1)}, u32[]{:S(2)}, u32[]{:S(2)}) collective-permute-start(bf16[128,1024]{1,0:T(8,128)(2,1)S(1)} %fusion.1.own_0), channel_id=1, source_target_pairs={{0,96},{1,33},{2,98},{3,35},{4,100},{5,37},{6,102},{7,39},{8,104},... | collective-permute-start | bytes 786440 | tf_op jit(solution)/shard_map/ppermute | solution.py:60
  26.6 4.2 %collective-permute-done.7 = bf16[128,1024]{1,0:T(8,128)(2,1)S(1)} collective-permute-done((bf16[128,1024]{1,0:T(8,128)(2,1)S(1)}, bf16[128,1024]{1,0:T(8,128)(2,1)S(1)}, u32[]{:S(2)}, u32[]{:S(2)}) %collective-permute-start.7) | collective-permute-done | bytes 262176 | tf_op jit(solution)/shard_map/ppermute | solution.py:60
  30.7 0.1 fusion.4.own_1
  30.8 1.6 %collective-permute-start.9 = (bf16[128,1024]{1,0:T(8,128)(2,1)S(1)}, bf16[128,1024]{1,0:T(8,128)(2,1)S(1)}, u32[]{:S(2)}, u32[]{:S(2)}) collective-permute-start(bf16[128,1024]{1,0:T(8,128)(2,1)S(1)} %fusion.4.own_1), channel_id=1, source_target_pairs={{0,96},{1,33},{2,98},{3,35},{4,100},{5,37},{6,102},{7,39},{8,104},... | collective-permute-start | bytes 786440 | tf_op jit(solution)/shard_map/ppermute | solution.py:60
  32.4 5.6 %collective-permute-start.11 = (bf16[4,1024,128]{2,1,0:T(8,128)(2,1)S(1)}, bf16[4,1024,128]{2,1,0:T(8,128)(2,1)S(1)}, u32[]{:S(2)}, u32[]{:S(2)}) collective-permute-start(bf16[4,1024,128]{2,1,0:T(8,128)(2,1)S(1)} %shard_map.96), channel_id=1, source_target_pairs={{0,4},{1,17},{2,6},{3,19},{4,0},{5,21},{6,2},{7,23},{8,12},{9,25},... | collective-permute-start | bytes 3145736 | tf_op jit(solution)/shard_map/ppermute | solution.py:60
  38.0 0.1 constant_dynamic-update-slice_fusion.5
  38.1 0.0 collective-permute-done.10.other_0
  38.1 0.1 pad_maximum_fusion.1
  38.2 0.4 collective-permute-start.14
  38.5 1.5 %collective-permute-done.9.other_1 = bf16[128,1024]{1,0:T(8,128)(2,1)S(1)} collective-permute-done((bf16[128,1024]{1,0:T(8,128)(2,1)S(1)}, bf16[128,1024]{1,0:T(8,128)(2,1)S(1)}, u32[]{:S(2)}, u32[]{:S(2)}) %collective-permute-start.9) | collective-permute-done | bytes 262176 | tf_op jit(solution)/shard_map/ppermute | solution.py:60
  40.1 0.1 pad_maximum_fusion.2
  40.1 0.3 collective-permute-start.15
  40.4 0.0 collective-permute-done.3
  40.4 0.0 collective-permute-done.4
  40.4 0.4 pad_maximum_fusion
  40.8 0.1 collective-permute-start.12
  40.9 0.1 constant_dynamic-update-slice_fusion.4
  41.0 0.1 constant_dynamic-update-slice_fusion.3
  41.2 6.3 %collective-permute-done.14.refs_0_ = bf16[2,128,1024]{2,1,0:T(8,128)(2,1)S(1)} collective-permute-done((bf16[2,128,1024]{2,1,0:T(8,128)(2,1)S(1)}, bf16[2,128,1024]{2,1,0:T(8,128)(2,1)S(1)}, u32[]{:S(2)}, u32[]{:S(2)}) %collective-permute-start.14) | collective-permute-done | bytes 524320 | tf_op jit(solution)/shard_map/ppermute | solution.py:60
  47.4 3.4 %collective-permute-done.11 = bf16[4,1024,128]{2,1,0:T(8,128)(2,1)S(1)} collective-permute-done((bf16[4,1024,128]{2,1,0:T(8,128)(2,1)S(1)}, bf16[4,1024,128]{2,1,0:T(8,128)(2,1)S(1)}, u32[]{:S(2)}, u32[]{:S(2)}) %collective-permute-start.11) | collective-permute-done | bytes 1048608 | tf_op jit(solution)/shard_map/ppermute | solution.py:60
  50.8 0.0 collective-permute-start.13
  50.8 2.2 %collective-permute-done.15.refs_1_ = bf16[2,128,1024]{2,1,0:T(8,128)(2,1)S(1)} collective-permute-done((bf16[2,128,1024]{2,1,0:T(8,128)(2,1)S(1)}, bf16[2,128,1024]{2,1,0:T(8,128)(2,1)S(1)}, u32[]{:S(2)}, u32[]{:S(2)}) %collective-permute-start.15) | collective-permute-done | bytes 524320 | tf_op jit(solution)/shard_map/ppermute | solution.py:60
  53.1 0.0 copy-start
  53.1 0.1 constant_dynamic-update-slice_fusion.2
  53.2 0.0 collective-permute-done.12
  53.2 0.4 constant_dynamic-update-slice_fusion.1
  53.6 0.0 collective-permute-done.13
  53.6 0.1 constant_dynamic-update-slice_fusion.shards
  53.8 0.9 %copy-done = bf16[1024,1024]{1,0:T(8,128)(2,1)S(1)} copy-done((bf16[1024,1024]{1,0:T(8,128)(2,1)S(1)}, bf16[1024,1024]{1,0:T(8,128)(2,1)}, u32[]{:S(2)}) %copy-start) | copy-done | bytes 2097176
  54.6 2.9 %shard_map.100 = (bf16[1024,256]{1,0:T(8,128)(2,1)S(1)}, f32[256,256]{1,0:T(8,128)S(1)}, bf16[256,256]{1,0:T(8,128)(2,1)S(1)}, bf16[256,256]{1,0:T(8,128)(2,1)S(1)}, bf16[256,256]{1,0:T(8,128)(2,1)S(1)}) custom-call(bf16[32,1024,128]{2,1,0:T(8,128)(2,1)S(1)} %constant_dynamic-update-slice_fusion.shards, bf16[2,128,1024]{2,1,0:T(8,128)(2,1)S(1)} %get-tuple-element.41.far_0, ...), custom_call_target="tpu_custom_call" | custom-call | flops 1073741824 | bytes 4194304 | tf_op jit(solution)/shard_map/pallas_call | solution.py:287
  57.5 0.5 collective-permute-start.18
  58.0 1.3 %collective-permute-start.17 = (bf16[256,256]{1,0:T(8,128)(2,1)S(1)}, bf16[256,256]{1,0:T(8,128)(2,1)S(1)}, u32[]{:S(2)}, u32[]{:S(2)}) collective-permute-start(bf16[256,256]{1,0:T(8,128)(2,1)S(1)} %get-tuple-element.48), channel_id=1, source_target_pairs={{0,32},{1,97},{2,34},{3,99},{4,36},{5,101},{6,38},{7,103},{8,40},{... | collective-permute-start | bytes 393224 | tf_op jit(solution)/shard_map/ppermute | solution.py:60
  59.3 2.4 %collective-permute-start.16 = (bf16[256,256]{1,0:T(8,128)(2,1)S(1)}, bf16[256,256]{1,0:T(8,128)(2,1)S(1)}, u32[]{:S(2)}, u32[]{:S(2)}) collective-permute-start(bf16[256,256]{1,0:T(8,128)(2,1)S(1)} %get-tuple-element.47), channel_id=1, source_target_pairs={{0,96},{1,33},{2,98},{3,35},{4,100},{5,37},{6,102},{7,39},{8,104},... | collective-permute-start | bytes 393224 | tf_op jit(solution)/shard_map/ppermute | solution.py:60
  61.7 1.7 %shard_map.101 = (bf16[1024,384]{1,0:T(8,128)(2,1)}, f32[2,8,384]{2,1,0:T(8,128)S(1)}) custom-call(s32[3]{0:T(128)} %live_h.5, bf16[1024,256]{1,0:T(8,128)(2,1)S(1)} %get-tuple-element.43.packed), custom_call_target="tpu_custom_call" | custom-call | flops 1048576 | bytes 4194304 | tf_op jit(solution)/shard_map/pallas_call | solution.py:320
  63.5 1.7 %collective-permute-done.18 = bf16[256,256]{1,0:T(8,128)(2,1)S(1)} collective-permute-done((bf16[256,256]{1,0:T(8,128)(2,1)S(1)}, bf16[256,256]{1,0:T(8,128)(2,1)S(1)}, u32[]{:S(2)}, u32[]{:S(2)}) %collective-permute-start.18) | collective-permute-done | bytes 131104 | tf_op jit(solution)/shard_map/ppermute | solution.py:60
  65.1 0.0 collective-permute-done.17
  65.1 1.2 %collective-permute-done.16 = bf16[256,256]{1,0:T(8,128)(2,1)S(1)} collective-permute-done((bf16[256,256]{1,0:T(8,128)(2,1)S(1)}, bf16[256,256]{1,0:T(8,128)(2,1)S(1)}, u32[]{:S(2)}, u32[]{:S(2)}) %collective-permute-start.16) | collective-permute-done | bytes 131104 | tf_op jit(solution)/shard_map/ppermute | solution.py:60
  66.3 0.1 convert_add_fusion.4
  66.4 0.7 %fusion.6 = bf16[256,384]{1,0:T(8,128)(2,1)} fusion(bf16[256,128]{1,0:T(8,128)(2,1)S(1)} %get-tuple-element.53, bf16[256,128]{1,0:T(8,128)(2,1)S(1)} %get-tuple-element.52, pred[384]{0:T(512)(128)(4,1)S(1)} %get-tuple-element.51, pred[384]{0:T(512)(128)(4,1)S(1)} %get-tuple-element.50), kind=kLoop, calls=%fused_computation.14 | loop fusion | flops 1376256 | bytes 328448 | tf_op jit(solution)/shard_map/convert_element_type | solution.py:342
  (4 shorter events, 0.0 us)
Async XLA Ops:
  0.6 16.5 %copy-start.1 = (bf16[1024,128]{1,0:T(8,128)(2,1)S(1)}, bf16[1024,128]{1,0:T(8,128)(2,1)}, u32[]{:S(2)}) copy-start(bf16[1024,128]{1,0:T(8,128)(2,1)} %a.1) | copy-start | bytes 786436
  3.5 10.7 %collective-permute-start.6 = (bf16[2,128,1024]{2,1,0:T(8,128)(2,1)S(1)}, bf16[2,128,1024]{2,1,0:T(8,128)(2,1)S(1)}, u32[]{:S(2)}, u32[]{:S(2)}) collective-permute-start(bf16[2,128,1024]{2,1,0:T(8,128)(2,1)S(1)} %get-tuple-element.32), channel_id=1, source_target_pairs={{0,32},{1,97},{2,34},{3,99},{4,36},{5,101},{6,38},{7,103},{8,40},{... | collective-permute-start | bytes 1572872 | tf_op jit(solution)/shard_map/ppermute | solution.py:60
  5.2 11.9 %collective-permute-start = (bf16[1024,128]{1,0:T(8,128)(2,1)}, bf16[1024,128]{1,0:T(8,128)(2,1)S(1)}, u32[]{:S(2)}, u32[]{:S(2)}) collective-permute-start(bf16[1024,128]{1,0:T(8,128)(2,1)} %a.1), channel_id=1, source_target_pairs={{0,8},{1,3},{2,10},{3,5},{4,12},{5,7},{6,14},{7,1},{8,16},{9,11},{... | collective-permute-start | bytes 786440 | tf_op jit(solution)/shard_map/ppermute | solution.py:60
  6.7 10.3 %collective-permute-start.1 = (bf16[1024,128]{1,0:T(8,128)(2,1)}, bf16[1024,128]{1,0:T(8,128)(2,1)S(1)}, u32[]{:S(2)}, u32[]{:S(2)}) collective-permute-start(bf16[1024,128]{1,0:T(8,128)(2,1)} %a.1), channel_id=1, source_target_pairs={{0,16},{1,5},{2,18},{3,7},{4,20},{5,1},{6,22},{7,3},{8,24},{9,13},... | collective-permute-start | bytes 786440 | tf_op jit(solution)/shard_map/ppermute | solution.py:60
  9.7 7.4 %collective-permute-start.2 = (bf16[1024,128]{1,0:T(8,128)(2,1)}, bf16[1024,128]{1,0:T(8,128)(2,1)S(1)}, u32[]{:S(2)}, u32[]{:S(2)}) collective-permute-start(bf16[1024,128]{1,0:T(8,128)(2,1)} %a.1), channel_id=1, source_target_pairs={{0,24},{1,7},{2,26},{3,1},{4,28},{5,3},{6,30},{7,5},{8,0},{9,15},{... | collective-permute-start | bytes 786440 | tf_op jit(solution)/shard_map/ppermute | solution.py:60
  11.0 12.0 %collective-permute-start.5 = (bf16[2,128,1024]{2,1,0:T(8,128)(2,1)S(1)}, bf16[2,128,1024]{2,1,0:T(8,128)(2,1)S(1)}, u32[]{:S(2)}, u32[]{:S(2)}) collective-permute-start(bf16[2,128,1024]{2,1,0:T(8,128)(2,1)S(1)} %get-tuple-element.29), channel_id=1, source_target_pairs={{0,32},{1,97},{2,34},{3,99},{4,36},{5,101},{6,38},{7,103},{8,40},{... | collective-permute-start | bytes 1572872 | tf_op jit(solution)/shard_map/ppermute | solution.py:60
  14.2 10.4 %collective-permute-start.8 = (bf16[128,1024]{1,0:T(8,128)(2,1)S(1)}, bf16[128,1024]{1,0:T(8,128)(2,1)S(1)}, u32[]{:S(2)}, u32[]{:S(2)}) collective-permute-start(bf16[128,1024]{1,0:T(8,128)(2,1)S(1)} %fusion.5), channel_id=1, source_target_pairs={{0,96},{1,33},{2,98},{3,35},{4,100},{5,37},{6,102},{7,39},{8,104},... | collective-permute-start | bytes 786440 | tf_op jit(solution)/shard_map/ppermute | solution.py:60
  17.2 23.2 %collective-permute-start.3 = (bf16[4,1024,128]{2,1,0:T(8,128)(2,1)S(1)}, bf16[4,1024,128]{2,1,0:T(8,128)(2,1)S(1)}, u32[]{:S(2)}, u32[]{:S(2)}) collective-permute-start(bf16[4,1024,128]{2,1,0:T(8,128)(2,1)S(1)} %shard_map.96), channel_id=1, source_target_pairs={{0,2},{1,9},{2,4},{3,11},{4,6},{5,13},{6,0},{7,15},{8,10},{9,17},{... | collective-permute-start | bytes 3145736 | tf_op jit(solution)/shard_map/ppermute | solution.py:60
  19.2 21.2 %collective-permute-start.4 = (bf16[4,1024,128]{2,1,0:T(8,128)(2,1)S(1)}, bf16[4,1024,128]{2,1,0:T(8,128)(2,1)S(1)}, u32[]{:S(2)}, u32[]{:S(2)}) collective-permute-start(bf16[4,1024,128]{2,1,0:T(8,128)(2,1)S(1)} %shard_map.96), channel_id=1, source_target_pairs={{0,6},{1,25},{2,0},{3,27},{4,2},{5,29},{6,4},{7,31},{8,14},{9,1},{... | collective-permute-start | bytes 3145736 | tf_op jit(solution)/shard_map/ppermute | solution.py:60
  23.1 7.7 %collective-permute-start.7 = (bf16[128,1024]{1,0:T(8,128)(2,1)S(1)}, bf16[128,1024]{1,0:T(8,128)(2,1)S(1)}, u32[]{:S(2)}, u32[]{:S(2)}) collective-permute-start(bf16[128,1024]{1,0:T(8,128)(2,1)S(1)} %fusion.2), channel_id=1, source_target_pairs={{0,96},{1,33},{2,98},{3,35},{4,100},{5,37},{6,102},{7,39},{8,104},... | collective-permute-start | bytes 786440 | tf_op jit(solution)/shard_map/ppermute | solution.py:60
  24.7 13.4 %collective-permute-start.10 = (bf16[128,1024]{1,0:T(8,128)(2,1)S(1)}, bf16[128,1024]{1,0:T(8,128)(2,1)S(1)}, u32[]{:S(2)}, u32[]{:S(2)}) collective-permute-start(bf16[128,1024]{1,0:T(8,128)(2,1)S(1)} %fusion.1.own_0), channel_id=1, source_target_pairs={{0,96},{1,33},{2,98},{3,35},{4,100},{5,37},{6,102},{7,39},{8,104},... | collective-permute-start | bytes 786440 | tf_op jit(solution)/shard_map/ppermute | solution.py:60
  30.8 9.2 %collective-permute-start.9 = (bf16[128,1024]{1,0:T(8,128)(2,1)S(1)}, bf16[128,1024]{1,0:T(8,128)(2,1)S(1)}, u32[]{:S(2)}, u32[]{:S(2)}) collective-permute-start(bf16[128,1024]{1,0:T(8,128)(2,1)S(1)} %fusion.4.own_1), channel_id=1, source_target_pairs={{0,96},{1,33},{2,98},{3,35},{4,100},{5,37},{6,102},{7,39},{8,104},... | collective-permute-start | bytes 786440 | tf_op jit(solution)/shard_map/ppermute | solution.py:60
  32.4 18.4 %collective-permute-start.11 = (bf16[4,1024,128]{2,1,0:T(8,128)(2,1)S(1)}, bf16[4,1024,128]{2,1,0:T(8,128)(2,1)S(1)}, u32[]{:S(2)}, u32[]{:S(2)}) collective-permute-start(bf16[4,1024,128]{2,1,0:T(8,128)(2,1)S(1)} %shard_map.96), channel_id=1, source_target_pairs={{0,4},{1,17},{2,6},{3,19},{4,0},{5,21},{6,2},{7,23},{8,12},{9,25},... | collective-permute-start | bytes 3145736 | tf_op jit(solution)/shard_map/ppermute | solution.py:60
  38.2 9.3 %collective-permute-start.14 = (bf16[2,128,1024]{2,1,0:T(8,128)(2,1)S(1)}, bf16[2,128,1024]{2,1,0:T(8,128)(2,1)S(1)}, u32[]{:S(2)}, u32[]{:S(2)}) collective-permute-start(bf16[2,128,1024]{2,1,0:T(8,128)(2,1)S(1)} %pad_maximum_fusion.1), channel_id=1, source_target_pairs={{0,32},{1,97},{2,34},{3,99},{4,36},{5,101},{6,38},{7,103},{8,40},{... | collective-permute-start | bytes 1572872 | tf_op jit(solution)/shard_map/ppermute | solution.py:60
  40.1 12.9 %collective-permute-start.15 = (bf16[2,128,1024]{2,1,0:T(8,128)(2,1)S(1)}, bf16[2,128,1024]{2,1,0:T(8,128)(2,1)S(1)}, u32[]{:S(2)}, u32[]{:S(2)}) collective-permute-start(bf16[2,128,1024]{2,1,0:T(8,128)(2,1)S(1)} %pad_maximum_fusion.2), channel_id=1, source_target_pairs={{0,32},{1,97},{2,34},{3,99},{4,36},{5,101},{6,38},{7,103},{8,40},{... | collective-permute-start | bytes 1572872 | tf_op jit(solution)/shard_map/ppermute | solution.py:60
  40.8 12.4 %collective-permute-start.12 = (bf16[12,1024,128]{2,1,0:T(8,128)(2,1)S(1)}, bf16[12,1024,128]{2,1,0:T(8,128)(2,1)S(1)}, u32[]{:S(2)}, u32[]{:S(2)}) collective-permute-start(bf16[12,1024,128]{2,1,0:T(8,128)(2,1)S(1)} %pad_maximum_fusion), channel_id=1, source_target_pairs={{0,1},{1,0},{2,3},{3,2},{4,5},{5,4},{6,7},{7,6},{8,9},{9,8},{10,11... | collective-permute-start | bytes 9437192 | tf_op jit(solution)/shard_map/ppermute | solution.py:60
  50.8 2.8 %collective-permute-start.13 = (bf16[4,1024,128]{2,1,0:T(8,128)(2,1)S(1)}, bf16[4,1024,128]{2,1,0:T(8,128)(2,1)S(1)}, u32[]{:S(2)}, u32[]{:S(2)}) collective-permute-start(bf16[4,1024,128]{2,1,0:T(8,128)(2,1)S(1)} %collective-permute-done.11), channel_id=1, source_target_pairs={{0,1},{1,0},{2,3},{3,2},{4,5},{5,4},{6,7},{7,6},{8,9},{9,8},{10,11... | collective-permute-start | bytes 3145736 | tf_op jit(solution)/shard_map/ppermute | solution.py:60
  53.1 1.6 %copy-start = (bf16[1024,1024]{1,0:T(8,128)(2,1)S(1)}, bf16[1024,1024]{1,0:T(8,128)(2,1)}, u32[]{:S(2)}) copy-start(bf16[1024,1024]{1,0:T(8,128)(2,1)} %tests.1) | copy-start | bytes 6291460
  57.5 7.6 %collective-permute-start.18 = (bf16[256,256]{1,0:T(8,128)(2,1)S(1)}, bf16[256,256]{1,0:T(8,128)(2,1)S(1)}, u32[]{:S(2)}, u32[]{:S(2)}) collective-permute-start(bf16[256,256]{1,0:T(8,128)(2,1)S(1)} %get-tuple-element.49), channel_id=1, source_target_pairs={{0,64},{1,65},{2,66},{3,67},{4,68},{5,69},{6,70},{7,71},{8,72},{9,... | collective-permute-start | bytes 393224 | tf_op jit(solution)/shard_map/ppermute | solution.py:60
  58.0 7.1 %collective-permute-start.17 = (bf16[256,256]{1,0:T(8,128)(2,1)S(1)}, bf16[256,256]{1,0:T(8,128)(2,1)S(1)}, u32[]{:S(2)}, u32[]{:S(2)}) collective-permute-start(bf16[256,256]{1,0:T(8,128)(2,1)S(1)} %get-tuple-element.48), channel_id=1, source_target_pairs={{0,32},{1,97},{2,34},{3,99},{4,36},{5,101},{6,38},{7,103},{8,40},{... | collective-permute-start | bytes 393224 | tf_op jit(solution)/shard_map/ppermute | solution.py:60
  59.3 7.0 %collective-permute-start.16 = (bf16[256,256]{1,0:T(8,128)(2,1)S(1)}, bf16[256,256]{1,0:T(8,128)(2,1)S(1)}, u32[]{:S(2)}, u32[]{:S(2)}) collective-permute-start(bf16[256,256]{1,0:T(8,128)(2,1)S(1)} %get-tuple-element.47), channel_id=1, source_target_pairs={{0,96},{1,33},{2,98},{3,35},{4,100},{5,37},{6,102},{7,39},{8,104},... | collective-permute-start | bytes 393224 | tf_op jit(solution)/shard_map/ppermute | solution.py:60

commit v10 on v8

--- a/solution.py
+++ b/solution.py
@@ -366,7 +366,7 @@
     both_1 = jnp.stack([own_1, other_1])
     (far_0,) = hold(2000_000_000, send(both_0, PAIR_A))
     far = hold(100000_000_000, far_0, send(both_1, PAIR_A))
-    pair = jnp.concatenate(after(ahead[:2], both_1))
+    pair = jnp.concatenate(after(ahead[:2], both_0))
     far_row = after(across, pair)
     early = jnp.concatenate([row, pair])
     early_other = send(early, SWAP)

time: 67.6 us -> 67.3 us (level)
  local copies, waits for them, and re-layouts: 1.91 us -> 1.08 us
    unnamed x9, local copies, waits for them, and re-layouts: 1.76 us -> 0.94 us
where the time goes in v10:
time: 67.3 us; the launch traced here: 67 us
  starting transfers between devices  31 us (46%)
  waiting for transfers between devices  22.3 us (33%)
  Pallas kernels  10.2 us (15%)
  other arithmetic  1.6 us (2%)
  local copies, waits for them, and re-layouts  1.08 us (2%)
  between operations  0.86 us (1%)
    ppermute x19, starting transfers between devices, send(): return lax.ppermute(value, ('tm', 'vox'), pairs)  31 us
    ppermute x19, waiting for transfers between devices, send(): return lax.ppermute(value, ('tm', 'vox'), pairs)  22.3 us
    pallas_call x1, Pallas kernels, last_call(): pl.pallas_call(last_kernel, out_shape=[jax.ShapeDtypeStruct((Q, W), BF16)...  2.9 us
    pallas_call x1, Pallas kernels, start_call(): pl.pallas_call(start_kernel, out_shape=[jax.ShapeDtypeStruct((2, BLK, Q),...  2.87 us
    pallas_call x1, Pallas kernels, rest_call(): pl.pallas_call(rest_kernel, out_shape=[jax.ShapeDtypeStruct((BLK, Q), F32...  2.63 us
    pallas_call x1, Pallas kernels, spread_call(): pl.pallas_call(spread_kernel, out_shape=[jax.ShapeDtypeStruct((Q, VD), BF...  1.7 us
  transfers between devices with their start and end apart: 19, of which 8 were waited for; matrix products, arithmetic and copies ran while one was open for 3% of the time, Pallas kernels for 7%

profile of v10, /device:TPU:0, one launch (start us, length us, event | category | flops | bytes accessed | tf_op | source)
XLA Modules:
  0.0 67.0 jit_solution(12919426978548401528)
XLA Ops:
  0.6 0.0 copy-start.1
  0.6 2.9 %shard_map.95 = (bf16[2,128,1024]{2,1,0:T(8,128)(2,1)S(1)}, bf16[2,128,1024]{2,1,0:T(8,128)(2,1)S(1)}, bf16[256,768]{1,0:T(8,128)(2,1)S(1)}) custom-call(f32[20]{0:T(128)} %lambdas_h.3, s32[3]{0:T(128)} %lam_index_h.3, s32[3]{0:T(128)} %live_h.5, f32[1,4096]{1,0:T(1,128)} %bitcast.25, bf16[768,4096]{1,0:T(8,128)(2,1)} %u.3, bf16[768,384]{1,0:T(8,128)(2,1)} %y.1), custom_call_target="tpu_custom_call" | custom-call | flops 805306368 | bytes 3145728 | tf_op jit(solution)/shard_map/pallas_call | solution.py:144
  3.5 1.7 %collective-permute-start.5 = (bf16[2,128,1024]{2,1,0:T(8,128)(2,1)S(1)}, bf16[2,128,1024]{2,1,0:T(8,128)(2,1)S(1)}, u32[]{:S(2)}, u32[]{:S(2)}) collective-permute-start(bf16[2,128,1024]{2,1,0:T(8,128)(2,1)S(1)} %get-tuple-element.29), channel_id=1, source_target_pairs={{0,32},{1,97},{2,34},{3,99},{4,36},{5,101},{6,38},{7,103},{8,40},{... | collective-permute-start | bytes 1572872 | tf_op jit(solution)/shard_map/ppermute | solution.py:60
  5.2 1.6 %collective-permute-start = (bf16[1024,128]{1,0:T(8,128)(2,1)}, bf16[1024,128]{1,0:T(8,128)(2,1)S(1)}, u32[]{:S(2)}, u32[]{:S(2)}) collective-permute-start(bf16[1024,128]{1,0:T(8,128)(2,1)} %a.1), channel_id=1, source_target_pairs={{0,8},{1,3},{2,10},{3,5},{4,12},{5,7},{6,14},{7,1},{8,16},{9,11},{... | collective-permute-start | bytes 786440 | tf_op jit(solution)/shard_map/ppermute | solution.py:60
  6.7 2.9 %collective-permute-start.1 = (bf16[1024,128]{1,0:T(8,128)(2,1)}, bf16[1024,128]{1,0:T(8,128)(2,1)S(1)}, u32[]{:S(2)}, u32[]{:S(2)}) collective-permute-start(bf16[1024,128]{1,0:T(8,128)(2,1)} %a.1), channel_id=1, source_target_pairs={{0,16},{1,5},{2,18},{3,7},{4,20},{5,1},{6,22},{7,3},{8,24},{9,13},... | collective-permute-start | bytes 786440 | tf_op jit(solution)/shard_map/ppermute | solution.py:60
  9.7 1.3 %collective-permute-start.2 = (bf16[1024,128]{1,0:T(8,128)(2,1)}, bf16[1024,128]{1,0:T(8,128)(2,1)S(1)}, u32[]{:S(2)}, u32[]{:S(2)}) collective-permute-start(bf16[1024,128]{1,0:T(8,128)(2,1)} %a.1), channel_id=1, source_target_pairs={{0,24},{1,7},{2,26},{3,1},{4,28},{5,3},{6,30},{7,5},{8,0},{9,15},{... | collective-permute-start | bytes 786440 | tf_op jit(solution)/shard_map/ppermute | solution.py:60
  11.0 0.5 collective-permute-start.12
  11.5 2.6 %shard_map.97 = (f32[128,1024]{1,0:T(8,128)S(1)}, f32[128,1024]{1,0:T(8,128)S(1)}, f32[128,1024]{1,0:T(8,128)S(1)}, f32[128,1024]{1,0:T(8,128)S(1)}) custom-call(f32[20]{0:T(128)} %lambdas_h.3, s32[3]{0:T(128)} %lam_index_h.3, s32[3]{0:T(128)} %live_h.5, f32[1,4096]{1,0:T(1,128)} %bitcast.26, bf16[768,4096]{1,0:T(8,128)(2,1)} %u.3, ...), custom_call_target="tpu_custom_call" | custom-call | flops 805306368 | bytes 3145728 | tf_op jit(solution)/shard_map/pallas_call | solution.py:180
  14.2 0.0 collective-permute-done.5
  14.2 0.1 fusion.3
  14.2 2.8 %collective-permute-start.6 = (bf16[128,1024]{1,0:T(8,128)(2,1)S(1)}, bf16[128,1024]{1,0:T(8,128)(2,1)S(1)}, u32[]{:S(2)}, u32[]{:S(2)}) collective-permute-start(bf16[128,1024]{1,0:T(8,128)(2,1)S(1)} %fusion.3), channel_id=1, source_target_pairs={{0,96},{1,33},{2,98},{3,35},{4,100},{5,37},{6,102},{7,39},{8,104},... | collective-permute-start | bytes 786440 | tf_op jit(solution)/shard_map/ppermute | solution.py:60
  17.1 0.0 collective-permute-done.b
  17.1 0.0 collective-permute-done.1.c
  17.1 0.0 collective-permute-done.2.d
  17.1 0.0 copy-done.1
  17.1 0.1 shard_map.96
  17.2 2.0 %collective-permute-start.3 = (bf16[4,1024,128]{2,1,0:T(8,128)(2,1)S(1)}, bf16[4,1024,128]{2,1,0:T(8,128)(2,1)S(1)}, u32[]{:S(2)}, u32[]{:S(2)}) collective-permute-start(bf16[4,1024,128]{2,1,0:T(8,128)(2,1)S(1)} %shard_map.96), channel_id=1, source_target_pairs={{0,2},{1,9},{2,4},{3,11},{4,6},{5,13},{6,0},{7,15},{8,10},{9,17},{... | collective-permute-start | bytes 3145736 | tf_op jit(solution)/shard_map/ppermute | solution.py:60
  19.2 2.2 %collective-permute-start.4 = (bf16[4,1024,128]{2,1,0:T(8,128)(2,1)S(1)}, bf16[4,1024,128]{2,1,0:T(8,128)(2,1)S(1)}, u32[]{:S(2)}, u32[]{:S(2)}) collective-permute-start(bf16[4,1024,128]{2,1,0:T(8,128)(2,1)S(1)} %shard_map.96), channel_id=1, source_target_pairs={{0,6},{1,25},{2,0},{3,27},{4,2},{5,29},{6,4},{7,31},{8,14},{9,1},{... | collective-permute-start | bytes 3145736 | tf_op jit(solution)/shard_map/ppermute | solution.py:60
  21.4 1.6 %collective-permute-done.12 = bf16[2,128,1024]{2,1,0:T(8,128)(2,1)S(1)} collective-permute-done((bf16[2,128,1024]{2,1,0:T(8,128)(2,1)S(1)}, bf16[2,128,1024]{2,1,0:T(8,128)(2,1)S(1)}, u32[]{:S(2)}, u32[]{:S(2)}) %collective-permute-start.12) | collective-permute-done | bytes 524320 | tf_op jit(solution)/shard_map/ppermute | solution.py:60
  23.0 0.1 fusion
  23.1 1.6 %collective-permute-start.13 = (bf16[128,1024]{1,0:T(8,128)(2,1)S(1)}, bf16[128,1024]{1,0:T(8,128)(2,1)S(1)}, u32[]{:S(2)}, u32[]{:S(2)}) collective-permute-start(bf16[128,1024]{1,0:T(8,128)(2,1)S(1)} %fusion), channel_id=1, source_target_pairs={{0,96},{1,33},{2,98},{3,35},{4,100},{5,37},{6,102},{7,39},{8,104},... | collective-permute-start | bytes 786440 | tf_op jit(solution)/shard_map/ppermute | solution.py:60
  24.6 0.0 collective-permute-done.6
  24.6 0.1 fusion.5.own_0
  24.7 1.8 %collective-permute-start.7 = (bf16[128,1024]{1,0:T(8,128)(2,1)S(1)}, bf16[128,1024]{1,0:T(8,128)(2,1)S(1)}, u32[]{:S(2)}, u32[]{:S(2)}) collective-permute-start(bf16[128,1024]{1,0:T(8,128)(2,1)S(1)} %fusion.5.own_0), channel_id=1, source_target_pairs={{0,96},{1,33},{2,98},{3,35},{4,100},{5,37},{6,102},{7,39},{8,104},... | collective-permute-start | bytes 786440 | tf_op jit(solution)/shard_map/ppermute | solution.py:60
  26.6 4.7 %collective-permute-start.8 = (bf16[4,1024,128]{2,1,0:T(8,128)(2,1)S(1)}, bf16[4,1024,128]{2,1,0:T(8,128)(2,1)S(1)}, u32[]{:S(2)}, u32[]{:S(2)}) collective-permute-start(bf16[4,1024,128]{2,1,0:T(8,128)(2,1)S(1)} %shard_map.96), channel_id=1, source_target_pairs={{0,4},{1,17},{2,6},{3,19},{4,0},{5,21},{6,2},{7,23},{8,12},{9,25},... | collective-permute-start | bytes 3145736 | tf_op jit(solution)/shard_map/ppermute | solution.py:60
  31.3 0.0 collective-permute-done.13
  31.3 0.1 fusion.2.own_1
  31.4 2.5 %collective-permute-start.14 = (bf16[128,1024]{1,0:T(8,128)(2,1)S(1)}, bf16[128,1024]{1,0:T(8,128)(2,1)S(1)}, u32[]{:S(2)}, u32[]{:S(2)}) collective-permute-start(bf16[128,1024]{1,0:T(8,128)(2,1)S(1)} %fusion.2.own_1), channel_id=1, source_target_pairs={{0,96},{1,33},{2,98},{3,35},{4,100},{5,37},{6,102},{7,39},{8,104},... | collective-permute-start | bytes 786440 | tf_op jit(solution)/shard_map/ppermute | solution.py:60
  33.9 0.1 constant_dynamic-update-slice_fusion.5
  34.0 0.0 collective-permute-done.7.other_0
  34.0 0.1 pad_maximum_fusion.1
  34.0 0.4 collective-permute-start.11
  34.4 7.4 %collective-permute-done.14.other_1 = bf16[128,1024]{1,0:T(8,128)(2,1)S(1)} collective-permute-done((bf16[128,1024]{1,0:T(8,128)(2,1)S(1)}, bf16[128,1024]{1,0:T(8,128)(2,1)S(1)}, u32[]{:S(2)}, u32[]{:S(2)}) %collective-permute-start.14) | collective-permute-done | bytes 262176 | tf_op jit(solution)/shard_map/ppermute | solution.py:60
  41.8 0.1 pad_maximum_fusion.2
  41.9 0.1 collective-permute-start.15
  42.0 0.0 collective-permute-done.3
  42.0 3.0 %collective-permute-done.4 = bf16[4,1024,128]{2,1,0:T(8,128)(2,1)S(1)} collective-permute-done((bf16[4,1024,128]{2,1,0:T(8,128)(2,1)S(1)}, bf16[4,1024,128]{2,1,0:T(8,128)(2,1)S(1)}, u32[]{:S(2)}, u32[]{:S(2)}) %collective-permute-start.4) | collective-permute-done | bytes 1048608 | tf_op jit(solution)/shard_map/ppermute | solution.py:60
  45.0 0.4 pad_maximum_fusion
  45.3 0.1 collective-permute-start.9
  45.4 0.1 constant_dynamic-update-slice_fusion.4
  45.6 0.1 constant_dynamic-update-slice_fusion.3
  45.7 0.0 collective-permute-done.11.refs_0_
  45.7 1.0 %collective-permute-done.8 = bf16[4,1024,128]{2,1,0:T(8,128)(2,1)S(1)} collective-permute-done((bf16[4,1024,128]{2,1,0:T(8,128)(2,1)S(1)}, bf16[4,1024,128]{2,1,0:T(8,128)(2,1)S(1)}, u32[]{:S(2)}, u32[]{:S(2)}) %collective-permute-start.8) | collective-permute-done | bytes 1048608 | tf_op jit(solution)/shard_map/ppermute | solution.py:60
  46.8 0.0 collective-permute-start.10
  46.8 4.4 %collective-permute-done.15.refs_1_ = bf16[2,128,1024]{2,1,0:T(8,128)(2,1)S(1)} collective-permute-done((bf16[2,128,1024]{2,1,0:T(8,128)(2,1)S(1)}, bf16[2,128,1024]{2,1,0:T(8,128)(2,1)S(1)}, u32[]{:S(2)}, u32[]{:S(2)}) %collective-permute-start.15) | collective-permute-done | bytes 524320 | tf_op jit(solution)/shard_map/ppermute | solution.py:60
  51.2 0.0 copy-start
  51.2 0.1 constant_dynamic-update-slice_fusion.2
  51.3 0.0 collective-permute-done.9
  51.3 0.4 constant_dynamic-update-slice_fusion.1
  51.7 0.8 %collective-permute-done.10 = bf16[4,1024,128]{2,1,0:T(8,128)(2,1)S(1)} collective-permute-done((bf16[4,1024,128]{2,1,0:T(8,128)(2,1)S(1)}, bf16[4,1024,128]{2,1,0:T(8,128)(2,1)S(1)}, u32[]{:S(2)}, u32[]{:S(2)}) %collective-permute-start.10) | collective-permute-done | bytes 1048608 | tf_op jit(solution)/shard_map/ppermute | solution.py:60
  52.6 0.1 constant_dynamic-update-slice_fusion.shards
  52.7 0.0 copy-done
  52.7 2.9 %shard_map.100 = (bf16[1024,256]{1,0:T(8,128)(2,1)S(1)}, f32[256,256]{1,0:T(8,128)S(1)}, bf16[256,256]{1,0:T(8,128)(2,1)S(1)}, bf16[256,256]{1,0:T(8,128)(2,1)S(1)}, bf16[256,256]{1,0:T(8,128)(2,1)S(1)}) custom-call(bf16[32,1024,128]{2,1,0:T(8,128)(2,1)S(1)} %constant_dynamic-update-slice_fusion.shards, bf16[2,128,1024]{2,1,0:T(8,128)(2,1)S(1)} %get-tuple-element.41.far_0, ...), custom_call_target="tpu_custom_call" | custom-call | flops 1073741824 | bytes 4194304 | tf_op jit(solution)/shard_map/pallas_call | solution.py:287
  55.7 2.6 %collective-permute-start.18 = (bf16[256,256]{1,0:T(8,128)(2,1)S(1)}, bf16[256,256]{1,0:T(8,128)(2,1)S(1)}, u32[]{:S(2)}, u32[]{:S(2)}) collective-permute-start(bf16[256,256]{1,0:T(8,128)(2,1)S(1)} %get-tuple-element.49), channel_id=1, source_target_pairs={{0,96},{1,33},{2,98},{3,35},{4,100},{5,37},{6,102},{7,39},{8,104},... | collective-permute-start | bytes 393224 | tf_op jit(solution)/shard_map/ppermute | solution.py:60
  58.2 0.1 collective-permute-start.17
  58.3 2.1 %collective-permute-start.16 = (bf16[256,256]{1,0:T(8,128)(2,1)S(1)}, bf16[256,256]{1,0:T(8,128)(2,1)S(1)}, u32[]{:S(2)}, u32[]{:S(2)}) collective-permute-start(bf16[256,256]{1,0:T(8,128)(2,1)S(1)} %get-tuple-element.47), channel_id=1, source_target_pairs={{0,64},{1,65},{2,66},{3,67},{4,68},{5,69},{6,70},{7,71},{8,72},{9,... | collective-permute-start | bytes 393224 | tf_op jit(solution)/shard_map/ppermute | solution.py:60
  60.4 1.7 %shard_map.101 = (bf16[1024,384]{1,0:T(8,128)(2,1)}, f32[2,8,384]{2,1,0:T(8,128)S(1)}) custom-call(s32[3]{0:T(128)} %live_h.5, bf16[1024,256]{1,0:T(8,128)(2,1)S(1)} %get-tuple-element.43.packed), custom_call_target="tpu_custom_call" | custom-call | flops 1048576 | bytes 4194304 | tf_op jit(solution)/shard_map/pallas_call | solution.py:320
  62.2 2.4 %collective-permute-done.18 = bf16[256,256]{1,0:T(8,128)(2,1)S(1)} collective-permute-done((bf16[256,256]{1,0:T(8,128)(2,1)S(1)}, bf16[256,256]{1,0:T(8,128)(2,1)S(1)}, u32[]{:S(2)}, u32[]{:S(2)}) %collective-permute-start.18) | collective-permute-done | bytes 131104 | tf_op jit(solution)/shard_map/ppermute | solution.py:60
  64.5 0.0 collective-permute-done.17
  64.5 1.7 %collective-permute-done.16 = bf16[256,256]{1,0:T(8,128)(2,1)S(1)} collective-permute-done((bf16[256,256]{1,0:T(8,128)(2,1)S(1)}, bf16[256,256]{1,0:T(8,128)(2,1)S(1)}, u32[]{:S(2)}, u32[]{:S(2)}) %collective-permute-start.16) | collective-permute-done | bytes 131104 | tf_op jit(solution)/shard_map/ppermute | solution.py:60
  66.2 0.1 convert_add_fusion.4
  66.3 0.7 %fusion.6 = bf16[256,384]{1,0:T(8,128)(2,1)} fusion(bf16[256,128]{1,0:T(8,128)(2,1)S(1)} %get-tuple-element.53, bf16[256,128]{1,0:T(8,128)(2,1)S(1)} %get-tuple-element.52, pred[384]{0:T(512)(128)(4,1)S(1)} %get-tuple-element.51, pred[384]{0:T(512)(128)(4,1)S(1)} %get-tuple-element.50), kind=kLoop, calls=%fused_computation.14 | loop fusion | flops 1376256 | bytes 328448 | tf_op jit(solution)/shard_map/convert_element_type | solution.py:342
  (4 shorter events, 0.0 us)
Async XLA Ops:
  0.6 16.5 %copy-start.1 = (bf16[1024,128]{1,0:T(8,128)(2,1)S(1)}, bf16[1024,128]{1,0:T(8,128)(2,1)}, u32[]{:S(2)}) copy-start(bf16[1024,128]{1,0:T(8,128)(2,1)} %a.1) | copy-start | bytes 786436
  3.5 10.7 %collective-permute-start.5 = (bf16[2,128,1024]{2,1,0:T(8,128)(2,1)S(1)}, bf16[2,128,1024]{2,1,0:T(8,128)(2,1)S(1)}, u32[]{:S(2)}, u32[]{:S(2)}) collective-permute-start(bf16[2,128,1024]{2,1,0:T(8,128)(2,1)S(1)} %get-tuple-element.29), channel_id=1, source_target_pairs={{0,32},{1,97},{2,34},{3,99},{4,36},{5,101},{6,38},{7,103},{8,40},{... | collective-permute-start | bytes 1572872 | tf_op jit(solution)/shard_map/ppermute | solution.py:60
  5.2 11.9 %collective-permute-start = (bf16[1024,128]{1,0:T(8,128)(2,1)}, bf16[1024,128]{1,0:T(8,128)(2,1)S(1)}, u32[]{:S(2)}, u32[]{:S(2)}) collective-permute-start(bf16[1024,128]{1,0:T(8,128)(2,1)} %a.1), channel_id=1, source_target_pairs={{0,8},{1,3},{2,10},{3,5},{4,12},{5,7},{6,14},{7,1},{8,16},{9,11},{... | collective-permute-start | bytes 786440 | tf_op jit(solution)/shard_map/ppermute | solution.py:60
  6.7 10.3 %collective-permute-start.1 = (bf16[1024,128]{1,0:T(8,128)(2,1)}, bf16[1024,128]{1,0:T(8,128)(2,1)S(1)}, u32[]{:S(2)}, u32[]{:S(2)}) collective-permute-start(bf16[1024,128]{1,0:T(8,128)(2,1)} %a.1), channel_id=1, source_target_pairs={{0,16},{1,5},{2,18},{3,7},{4,20},{5,1},{6,22},{7,3},{8,24},{9,13},... | collective-permute-start | bytes 786440 | tf_op jit(solution)/shard_map/ppermute | solution.py:60
  9.7 7.4 %collective-permute-start.2 = (bf16[1024,128]{1,0:T(8,128)(2,1)}, bf16[1024,128]{1,0:T(8,128)(2,1)S(1)}, u32[]{:S(2)}, u32[]{:S(2)}) collective-permute-start(bf16[1024,128]{1,0:T(8,128)(2,1)} %a.1), channel_id=1, source_target_pairs={{0,24},{1,7},{2,26},{3,1},{4,28},{5,3},{6,30},{7,5},{8,0},{9,15},{... | collective-permute-start | bytes 786440 | tf_op jit(solution)/shard_map/ppermute | solution.py:60
  11.0 12.0 %collective-permute-start.12 = (bf16[2,128,1024]{2,1,0:T(8,128)(2,1)S(1)}, bf16[2,128,1024]{2,1,0:T(8,128)(2,1)S(1)}, u32[]{:S(2)}, u32[]{:S(2)}) collective-permute-start(bf16[2,128,1024]{2,1,0:T(8,128)(2,1)S(1)} %get-tuple-element.35), channel_id=1, source_target_pairs={{0,32},{1,97},{2,34},{3,99},{4,36},{5,101},{6,38},{7,103},{8,40},{... | collective-permute-start | bytes 1572872 | tf_op jit(solution)/shard_map/ppermute | solution.py:60
  14.2 10.4 %collective-permute-start.6 = (bf16[128,1024]{1,0:T(8,128)(2,1)S(1)}, bf16[128,1024]{1,0:T(8,128)(2,1)S(1)}, u32[]{:S(2)}, u32[]{:S(2)}) collective-permute-start(bf16[128,1024]{1,0:T(8,128)(2,1)S(1)} %fusion.3), channel_id=1, source_target_pairs={{0,96},{1,33},{2,98},{3,35},{4,100},{5,37},{6,102},{7,39},{8,104},... | collective-permute-start | bytes 786440 | tf_op jit(solution)/shard_map/ppermute | solution.py:60
  17.2 24.8 %collective-permute-start.3 = (bf16[4,1024,128]{2,1,0:T(8,128)(2,1)S(1)}, bf16[4,1024,128]{2,1,0:T(8,128)(2,1)S(1)}, u32[]{:S(2)}, u32[]{:S(2)}) collective-permute-start(bf16[4,1024,128]{2,1,0:T(8,128)(2,1)S(1)} %shard_map.96), channel_id=1, source_target_pairs={{0,2},{1,9},{2,4},{3,11},{4,6},{5,13},{6,0},{7,15},{8,10},{9,17},{... | collective-permute-start | bytes 3145736 | tf_op jit(solution)/shard_map/ppermute | solution.py:60
  19.2 25.8 %collective-permute-start.4 = (bf16[4,1024,128]{2,1,0:T(8,128)(2,1)S(1)}, bf16[4,1024,128]{2,1,0:T(8,128)(2,1)S(1)}, u32[]{:S(2)}, u32[]{:S(2)}) collective-permute-start(bf16[4,1024,128]{2,1,0:T(8,128)(2,1)S(1)} %shard_map.96), channel_id=1, source_target_pairs={{0,6},{1,25},{2,0},{3,27},{4,2},{5,29},{6,4},{7,31},{8,14},{9,1},{... | collective-permute-start | bytes 3145736 | tf_op jit(solution)/shard_map/ppermute | solution.py:60
  23.1 8.2 %collective-permute-start.13 = (bf16[128,1024]{1,0:T(8,128)(2,1)S(1)}, bf16[128,1024]{1,0:T(8,128)(2,1)S(1)}, u32[]{:S(2)}, u32[]{:S(2)}) collective-permute-start(bf16[128,1024]{1,0:T(8,128)(2,1)S(1)} %fusion), channel_id=1, source_target_pairs={{0,96},{1,33},{2,98},{3,35},{4,100},{5,37},{6,102},{7,39},{8,104},... | collective-permute-start | bytes 786440 | tf_op jit(solution)/shard_map/ppermute | solution.py:60
  24.7 9.2 %collective-permute-start.7 = (bf16[128,1024]{1,0:T(8,128)(2,1)S(1)}, bf16[128,1024]{1,0:T(8,128)(2,1)S(1)}, u32[]{:S(2)}, u32[]{:S(2)}) collective-permute-start(bf16[128,1024]{1,0:T(8,128)(2,1)S(1)} %fusion.5.own_0), channel_id=1, source_target_pairs={{0,96},{1,33},{2,98},{3,35},{4,100},{5,37},{6,102},{7,39},{8,104},... | collective-permute-start | bytes 786440 | tf_op jit(solution)/shard_map/ppermute | solution.py:60
  26.6 20.2 %collective-permute-start.8 = (bf16[4,1024,128]{2,1,0:T(8,128)(2,1)S(1)}, bf16[4,1024,128]{2,1,0:T(8,128)(2,1)S(1)}, u32[]{:S(2)}, u32[]{:S(2)}) collective-permute-start(bf16[4,1024,128]{2,1,0:T(8,128)(2,1)S(1)} %shard_map.96), channel_id=1, source_target_pairs={{0,4},{1,17},{2,6},{3,19},{4,0},{5,21},{6,2},{7,23},{8,12},{9,25},... | collective-permute-start | bytes 3145736 | tf_op jit(solution)/shard_map/ppermute | solution.py:60
  31.4 10.4 %collective-permute-start.14 = (bf16[128,1024]{1,0:T(8,128)(2,1)S(1)}, bf16[128,1024]{1,0:T(8,128)(2,1)S(1)}, u32[]{:S(2)}, u32[]{:S(2)}) collective-permute-start(bf16[128,1024]{1,0:T(8,128)(2,1)S(1)} %fusion.2.own_1), channel_id=1, source_target_pairs={{0,96},{1,33},{2,98},{3,35},{4,100},{5,37},{6,102},{7,39},{8,104},... | collective-permute-start | bytes 786440 | tf_op jit(solution)/shard_map/ppermute | solution.py:60
  34.0 11.7 %collective-permute-start.11 = (bf16[2,128,1024]{2,1,0:T(8,128)(2,1)S(1)}, bf16[2,128,1024]{2,1,0:T(8,128)(2,1)S(1)}, u32[]{:S(2)}, u32[]{:S(2)}) collective-permute-start(bf16[2,128,1024]{2,1,0:T(8,128)(2,1)S(1)} %pad_maximum_fusion.1), channel_id=1, source_target_pairs={{0,32},{1,97},{2,34},{3,99},{4,36},{5,101},{6,38},{7,103},{8,40},{... | collective-permute-start | bytes 1572872 | tf_op jit(solution)/shard_map/ppermute | solution.py:60
  41.9 9.3 %collective-permute-start.15 = (bf16[2,128,1024]{2,1,0:T(8,128)(2,1)S(1)}, bf16[2,128,1024]{2,1,0:T(8,128)(2,1)S(1)}, u32[]{:S(2)}, u32[]{:S(2)}) collective-permute-start(bf16[2,128,1024]{2,1,0:T(8,128)(2,1)S(1)} %pad_maximum_fusion.2), channel_id=1, source_target_pairs={{0,32},{1,97},{2,34},{3,99},{4,36},{5,101},{6,38},{7,103},{8,40},{... | collective-permute-start | bytes 1572872 | tf_op jit(solution)/shard_map/ppermute | solution.py:60
  45.3 6.0 %collective-permute-start.9 = (bf16[12,1024,128]{2,1,0:T(8,128)(2,1)S(1)}, bf16[12,1024,128]{2,1,0:T(8,128)(2,1)S(1)}, u32[]{:S(2)}, u32[]{:S(2)}) collective-permute-start(bf16[12,1024,128]{2,1,0:T(8,128)(2,1)S(1)} %pad_maximum_fusion), channel_id=1, source_target_pairs={{0,1},{1,0},{2,3},{3,2},{4,5},{5,4},{6,7},{7,6},{8,9},{9,8},{10,11... | collective-permute-start | bytes 9437192 | tf_op jit(solution)/shard_map/ppermute | solution.py:60
  46.8 5.8 %collective-permute-start.10 = (bf16[4,1024,128]{2,1,0:T(8,128)(2,1)S(1)}, bf16[4,1024,128]{2,1,0:T(8,128)(2,1)S(1)}, u32[]{:S(2)}, u32[]{:S(2)}) collective-permute-start(bf16[4,1024,128]{2,1,0:T(8,128)(2,1)S(1)} %collective-permute-done.8), channel_id=1, source_target_pairs={{0,1},{1,0},{2,3},{3,2},{4,5},{5,4},{6,7},{7,6},{8,9},{9,8},{10,11... | collective-permute-start | bytes 3145736 | tf_op jit(solution)/shard_map/ppermute | solution.py:60
  51.2 1.6 %copy-start = (bf16[1024,1024]{1,0:T(8,128)(2,1)S(1)}, bf16[1024,1024]{1,0:T(8,128)(2,1)}, u32[]{:S(2)}) copy-start(bf16[1024,1024]{1,0:T(8,128)(2,1)} %tests.1) | copy-start | bytes 6291460
  55.7 8.9 %collective-permute-start.18 = (bf16[256,256]{1,0:T(8,128)(2,1)S(1)}, bf16[256,256]{1,0:T(8,128)(2,1)S(1)}, u32[]{:S(2)}, u32[]{:S(2)}) collective-permute-start(bf16[256,256]{1,0:T(8,128)(2,1)S(1)} %get-tuple-element.49), channel_id=1, source_target_pairs={{0,96},{1,33},{2,98},{3,35},{4,100},{5,37},{6,102},{7,39},{8,104},... | collective-permute-start | bytes 393224 | tf_op jit(solution)/shard_map/ppermute | solution.py:60
  58.2 6.3 %collective-permute-start.17 = (bf16[256,256]{1,0:T(8,128)(2,1)S(1)}, bf16[256,256]{1,0:T(8,128)(2,1)S(1)}, u32[]{:S(2)}, u32[]{:S(2)}) collective-permute-start(bf16[256,256]{1,0:T(8,128)(2,1)S(1)} %get-tuple-element.48), channel_id=1, source_target_pairs={{0,32},{1,97},{2,34},{3,99},{4,36},{5,101},{6,38},{7,103},{8,40},{... | collective-permute-start | bytes 393224 | tf_op jit(solution)/shard_map/ppermute | solution.py:60
  58.3 7.9 %collective-permute-start.16 = (bf16[256,256]{1,0:T(8,128)(2,1)S(1)}, bf16[256,256]{1,0:T(8,128)(2,1)S(1)}, u32[]{:S(2)}, u32[]{:S(2)}) collective-permute-start(bf16[256,256]{1,0:T(8,128)(2,1)S(1)} %get-tuple-element.47), channel_id=1, source_target_pairs={{0,64},{1,65},{2,66},{3,67},{4,68},{5,69},{6,70},{7,71},{8,72},{9,... | collective-permute-start | bytes 393224 | tf_op jit(solution)/shard_map/ppermute | solution.py:60
